TPU v7x, 32 devices: a whole 2x2x4 slice. The times are simulated.
32 devices in a mesh: groups: 2 (over x), tp: 16 (over z, y, core).
Axes of the slice: x: 2, y: 2, z: 4, core: 2. Of those that a mesh axis runs over, the one named last changes fastest.
Arguments:
- query_rows: bfloat16 [2048, 16384], P(('groups', 'tp')), parts along dimension 0, may hold values from -96 to 96
- key_rows: bfloat16 [2048, 1024], P(('groups', 'tp')), parts along dimension 0, may hold values from -4.5 to 4.5
- value_rows: bfloat16 [2048, 1024], P(('groups', 'tp')), parts along dimension 0, may hold values from -6 to 6
Outputs:
- attended: bfloat16 [2048, 16384], P(('groups', 'tp')), parts along dimension 0
There are 2 independent parts, one for each index of `groups`. A program takes and returns all parts, laid end to end along the dimension named above; each array names one. Nothing has to cross between parts.
All inputs are finite; a program needn't handle non-finite values.
Results may differ from a plain program's by a relative error of at most 0.0044.
Values may be sent and summed in bfloat16 or wider, within the bound.
No kernel may reach another device: no remote copies, remote signals or barrier semaphores. Data moves between devices by JAX's collectives and lax.ppermute only.
A program may use at most 128 MiB of HBM per device.

v0:
```python
import jax
import jax.numpy as jnp
from jax import lax
from jax.sharding import PartitionSpec as P

HEADS = 128
KV_HEADS = 8


masked_score = -1e30


def cycle_attend(query_rows, key_rows, value_rows):
    tok_rows = query_rows.shape[0]
    head_dim = key_rows.shape[1] // KV_HEADS
    group = HEADS // KV_HEADS
    scaling = head_dim ** (-0.5)
    grouped = query_rows.reshape(tok_rows, KV_HEADS, group, head_dim)
    first_pos = lax.axis_index("tp") * tok_rows
    query_pos = first_pos + jnp.arange(tok_rows, dtype=jnp.int32)
    last_pos = first_pos + tok_rows - 1

    def absorb(running, key_block, value_block, block_start):

        def compute(partial_value):
            row_max, denominator, numerator = partial_value
            scores = (
                jnp.einsum("tgqd,ngd->tgqn", grouped, key_block, preferred_element_type=jnp.float32)
                * scaling
            )
            key_pos = block_start + jnp.arange(key_block.shape[0], dtype=jnp.int32)
            allowed = (key_pos[None, :] <= query_pos[:, None])[:, None, None, :]
            scores = jnp.where(allowed, scores, masked_score)
            new_max = jnp.maximum(row_max, jnp.max(scores, axis=-1))
            factor = jnp.exp(row_max - new_max)
            weights = jnp.where(allowed, jnp.exp(scores - new_max[..., None]), 0.0)
            denominator = denominator * factor + jnp.sum(weights, axis=-1)
            blended = jnp.einsum(
                "tgqn,ngd->tgqd",
                weights.astype(jnp.bfloat16),
                value_block,
                preferred_element_type=jnp.float32,
            )
            return (new_max, denominator, numerator * factor[..., None] + blended)

        return lax.cond(
            block_start <= last_pos, compute, lambda partial_value: partial_value, running
        )

    initial = (
        jnp.full((tok_rows, KV_HEADS, group), masked_score, jnp.float32),
        jnp.zeros((tok_rows, KV_HEADS, group), jnp.float32),
        jnp.zeros((tok_rows, KV_HEADS, group, head_dim), jnp.float32),
    )
    running = initial
    key_piece = lax.all_gather(key_rows, "tp", axis=0, tiled=True)
    value_piece = lax.all_gather(value_rows, "tp", axis=0, tiled=True)
    shards = key_piece.shape[0] // tok_rows
    width = max(1, min(shards, 512 // tok_rows))
    while shards % width:
        width -= 1
    block_keys = width * tok_rows
    key_split = key_piece.reshape(shards // width, block_keys, KV_HEADS, head_dim)
    value_split = value_piece.reshape(shards // width, block_keys, KV_HEADS, head_dim)
    block_starts = block_keys * jnp.arange(shards // width, dtype=jnp.int32)

    def scan_block(partial_value, payload):
        key_block, value_block, block_start = payload
        return (absorb(partial_value, key_block, value_block, block_start), None)

    running, ignored = lax.scan(scan_block, running, (key_split, value_split, block_starts))
    row_max, denominator, numerator = running
    finished = (numerator / denominator[..., None]).astype(jnp.bfloat16)
    return finished.reshape(tok_rows, HEADS * head_dim)


def body(query_rows, key_rows, value_rows):
    return cycle_attend(query_rows, key_rows, value_rows)


def solution(mesh):
    return jax.shard_map(
        body,
        mesh=mesh,
        in_specs=(P(("groups", "tp"), None), P(("groups", "tp"), None), P(("groups", "tp"), None)),
        out_specs=P(("groups", "tp"), None),
        check_vma=False,
    )
```

profile of v0, /device:TPU:25, one launch (start us, length us, event | category | flops | bytes accessed | tf_op | source)
XLA Modules:
  0.0 161.0 jit_solution(16707163165189685091)
XLA Ops:
  6.5 0.7 all-gather.3.cloned.1.call-update
  7.3 0.7 all-gather.5.cloned.1.call-update
  8.0 2.2 %copy.18 = bf16[8,8,128,128]{3,2,1,0:T(8,128)(2,1)S(1)} copy(bf16[8,8,128,128]{3,1,2,0:T(8,128)(2,1)} %bitcast.48) | data formatting | bytes 4194304
  10.2 1.4 copy.11
  11.6 39.6 %all-gather.3.cloned.1.call-done = bf16[1024,1024]{1,0:T(8,128)(2,1)} async-done(((bf16[64,1024]{1,0:T(8,128)(2,1)}), bf16[1024,1024]{1,0:T(8,128)(2,1)}) %all-gather.3.cloned.1.call-update) | async-done | bytes 2097168 | tf_op jit(solution)/shard_map/all_gather | solution.py:56
  51.1 2.2 %copy.17 = bf16[128,8,8,128]{3,2,1,0:T(8,128)(2,1)S(1)} copy(bf16[128,8,8,128]{3,1,2,0:T(8,128)(2,1)} %bitcast.49) | data formatting | bytes 4194304
  53.3 1.7 %copy.10 = bf16[2,512,8,128]{3,1,2,0:T(8,128)(2,1)} copy(bf16[2,512,8,128]{3,2,1,0:T(8,128)(2,1)S(1)} %bitcast.44) | data formatting | bytes 4194304
  55.0 38.4 %all-gather.5.cloned.1.call-done = bf16[1024,1024]{1,0:T(8,128)(2,1)} async-done(((bf16[64,1024]{1,0:T(8,128)(2,1)}), bf16[1024,1024]{1,0:T(8,128)(2,1)}) %all-gather.5.cloned.1.call-update) | async-done | bytes 2097168 | tf_op jit(solution)/shard_map/all_gather | solution.py:57
  93.5 2.2 %copy.19 = bf16[128,8,8,128]{3,2,1,0:T(8,128)(2,1)S(1)} copy(bf16[128,8,8,128]{3,1,2,0:T(8,128)(2,1)} %bitcast.50) | data formatting | bytes 4194304
  95.7 1.7 %copy.12 = bf16[2,512,8,128]{3,1,2,0:T(8,128)(2,1)} copy(bf16[2,512,8,128]{3,2,1,0:T(8,128)(2,1)S(1)} %bitcast.45) | data formatting | bytes 4194304
  97.4 2.3 %broadcast_in_dim.42 = f32[64,8,16,128]{3,2,0,1:T(8,128)} broadcast(f32[]{:T(128)} %constant.44.clone.1), dimensions={} | broadcast | bytes 4194308 | tf_op jit(solution)/shard_map/broadcast_in_dim | solution.py:53
  99.8 48.1 %while.15 = (s32[]{:T(128)}, f32[64,8,16]{0,2,1:T(8,128)S(1)}, f32[64,8,16]{0,2,1:T(8,128)S(1)}, f32[64,8,16,128]{3,2,0,1:T(8,128)}, s32[2]{0:T(128)S(1)}, /*ind...) while((s32[]{:T(128)}, f32[64,8,16]{0,2,1:T(8,128)S(1)}, ...), condition=%wide.region_5.6_spmd.clone, body=%wide.region_0.5_spmd.clone.sunk | while | flops 2187379200 | bytes 63576344 | solution.py:71
  100.0 0.6 dynamic_slice.33
  101.1 22.8 %conditional.3 = ((f32[64,8,16]{0,2,1:T(8,128)S(1)}, f32[64,8,16]{0,2,1:T(8,128)S(1)}, f32[64,8,16,128]{3,2,0,1:T(8,128)})) conditional(s32[]{:T(128)} %convert_element_type.16, (f32[64,8,16]{0,2,1:T(8,128)S(1)}, f32[64,8,16]{0,2,1:T(8,128)S(1)}, f32[64,8,16,128]{3,2,0,1:T(8,128)}) %tuple.40, (s32[]{:T(128)}, s32[]{:T(128)}, ...), branch_computations={%region_1.1_spmd, %region_2.4_spmd} | conditional | flops 2187379200 | bytes 63575848 | solution.py:46
  101.1 0.6 iota_add_fusion
  101.7 0.1 broadcast_compare_fusion
  101.8 3.7 %fusion.2 = (f32[64,8,16]{0,2,1:T(8,128)S(1)}, f32[8,512,64,16]{1,2,3,0:T(8,128)S(1)}) fusion(pred[64,512]{1,0:T(8,128)(4,1)S(1)} %broadcast_compare_fusion, bf16[64,8,16,128]{3,0,2,1:T(8,128)(2,1)S(1)} %get-tuple-element.121, bf16[2,512,8,128]{3,1,2,0:T(8,128)(2,1)} %get-tuple-element.119, s32[]{:T(128)} %get-tuple-element.120), kind=kOutput, calls=%fused_computation.3 | convolution fusion | flops 1086316544 | bytes 19988992 | tf_op jit(solution)/shard_map/while/body/eval_jaxpr/cond/branch_1_fun/tgqd,ngd->tgqn/dot_general | solution.py:28
  105.5 6.9 %fusion.3 = (bf16[64,8,16,512]{3,0,2,1:T(8,128)(2,1)}, f32[64,8,16]{0,2,1:T(8,128)S(1)}) fusion(f32[8,512,64,16]{1,2,3,0:T(8,128)S(1)} %get-tuple-element.207, f32[64,8,16]{0,2,1:T(8,128)S(1)} %max.4, pred[64,512]{1,0:T(8,128)(4,1)S(1)} %broadcast_compare_fusion), kind=kLoop, calls=%fused_computation.4 | loop fusion | flops 25157632 | bytes 25264128 | tf_op jit(solution)/shard_map/while/body/eval_jaxpr/cond/branch_1_fun/convert_element_type | solution.py:40
  112.5 0.1 copy.8
  112.6 11.2 %bitcast_add_fusion = f32[64,8,16,128]{3,2,0,1:T(8,128)} fusion(f32[64,8,16,128]{3,2,0,1:T(8,128)} %get-tuple-element.123, bf16[64,8,16,512]{3,0,2,1:T(8,128)(2,1)} %get-tuple-element.204, f32[64,8,16]{2,0,1:T(8,128)S(1)} %copy.8, bf16[2,512,8,128]{3,1,2,0:T(8,128)(2,1)} %get-tuple-element.124, s32[]{:T(128)} %get-tuple-element.120), kind=kOutput, calls=%fused_computation.8 | convolution fusion | flops 1075838976 | bytes 17859072 | tf_op jit(solution)/shard_map/while/body/eval_jaxpr/cond/branch_1_fun/tgqn,ngd->tgqd/dot_general | solution.py:38
  123.9 0.6 dynamic_slice.33
  125.0 22.8 %conditional.3 = ((f32[64,8,16]{0,2,1:T(8,128)S(1)}, f32[64,8,16]{0,2,1:T(8,128)S(1)}, f32[64,8,16,128]{3,2,0,1:T(8,128)})) conditional(s32[]{:T(128)} %convert_element_type.16, (f32[64,8,16]{0,2,1:T(8,128)S(1)}, f32[64,8,16]{0,2,1:T(8,128)S(1)}, f32[64,8,16,128]{3,2,0,1:T(8,128)}) %tuple.40, (s32[]{:T(128)}, s32[]{:T(128)}, ...), branch_computations={%region_1.1_spmd, %region_2.4_spmd} | conditional | flops 2187379200 | bytes 63575848 | solution.py:46
  125.1 0.6 iota_add_fusion
  125.6 0.1 broadcast_compare_fusion
  125.7 3.7 %fusion.2 = (f32[64,8,16]{0,2,1:T(8,128)S(1)}, f32[8,512,64,16]{1,2,3,0:T(8,128)S(1)}) fusion(pred[64,512]{1,0:T(8,128)(4,1)S(1)} %broadcast_compare_fusion, bf16[64,8,16,128]{3,0,2,1:T(8,128)(2,1)S(1)} %get-tuple-element.121, bf16[2,512,8,128]{3,1,2,0:T(8,128)(2,1)} %get-tuple-element.119, s32[]{:T(128)} %get-tuple-element.120), kind=kOutput, calls=%fused_computation.3 | convolution fusion | flops 1086316544 | bytes 19988992 | tf_op jit(solution)/shard_map/while/body/eval_jaxpr/cond/branch_1_fun/tgqd,ngd->tgqn/dot_general | solution.py:28
  129.4 6.9 %fusion.3 = (bf16[64,8,16,512]{3,0,2,1:T(8,128)(2,1)}, f32[64,8,16]{0,2,1:T(8,128)S(1)}) fusion(f32[8,512,64,16]{1,2,3,0:T(8,128)S(1)} %get-tuple-element.207, f32[64,8,16]{0,2,1:T(8,128)S(1)} %max.4, pred[64,512]{1,0:T(8,128)(4,1)S(1)} %broadcast_compare_fusion), kind=kLoop, calls=%fused_computation.4 | loop fusion | flops 25157632 | bytes 25264128 | tf_op jit(solution)/shard_map/while/body/eval_jaxpr/cond/branch_1_fun/convert_element_type | solution.py:40
  136.4 0.1 copy.8
  136.6 11.2 %bitcast_add_fusion = f32[64,8,16,128]{3,2,0,1:T(8,128)} fusion(f32[64,8,16,128]{3,2,0,1:T(8,128)} %get-tuple-element.123, bf16[64,8,16,512]{3,0,2,1:T(8,128)(2,1)} %get-tuple-element.204, f32[64,8,16]{2,0,1:T(8,128)S(1)} %copy.8, bf16[2,512,8,128]{3,1,2,0:T(8,128)(2,1)} %get-tuple-element.124, s32[]{:T(128)} %get-tuple-element.120), kind=kOutput, calls=%fused_computation.8 | convolution fusion | flops 1075838976 | bytes 17859072 | tf_op jit(solution)/shard_map/while/body/eval_jaxpr/cond/branch_1_fun/tgqn,ngd->tgqd/dot_general | solution.py:38
  147.8 0.1 copy.13
  147.9 2.9 %divide_convert_fusion = bf16[64,8,16,128]{3,2,0,1:T(8,128)(2,1)S(1)} fusion(f32[64,8,16,128]{3,2,0,1:T(8,128)} %get-tuple-element.141, f32[64,8,16]{2,0,1:T(8,128)S(1)} %copy.13), kind=kLoop, calls=%fused_computation.21 | loop fusion | flops 2097152 | bytes 6324224 | tf_op jit(solution)/shard_map/convert_element_type | solution.py:73
  150.8 0.6 copy.14
  151.4 2.8 %copy.26 = bf16[8,8,128,128]{3,1,2,0:T(8,128)(2,1)} copy(bf16[8,8,128,128]{3,2,1,0:T(8,128)(2,1)S(1)} %bitcast.46) | data formatting | bytes 4194304
  (15 shorter events, 0.2 us)
Async XLA Ops:
  6.5 44.6 %all-gather.3.cloned.1.call-start = ((), (), s32[]{:S(2)}) async-start(), calls=%async_computation | async-start | bytes 2228224 | tf_op jit(solution)/shard_map/all_gather | solution.py:56
  7.3 86.2 %all-gather.5.cloned.1.call-start = ((), (), s32[]{:S(2)}) async-start(), calls=%async_computation.1 | async-start | bytes 2228224 | tf_op jit(solution)/shard_map/all_gather | solution.py:57
Sparse Core Ops, SparseCore 0:
  9.5 41.5 all-gather.2
  53.3 40.1 all-gather.4
where the time goes:
time: 161 us
  waiting for transfers between devices  79.4 us (49%)
  matrix products  29.8 us (19%)
  local copies, waits for them, and re-layouts  18.6 us (12%)
  other arithmetic  18.2 us (11%)
  between operations  13.5 us (8%)
    all_gather x1, waiting for transfers between devices, cycle_attend(): key_piece = lax.all_gather(key_rows, 'tp', axis=0, tiled=True)  39.6 us
    all_gather x1, waiting for transfers between devices, cycle_attend(): value_piece = lax.all_gather(value_rows, 'tp', axis=0, tiled=True)  38.4 us
    dot_general x2, matrix products, compute(): jnp.einsum('tgqn,ngd->tgqd', weights.astype(jnp.bfloat16), value_block, p...  22.5 us
    unnamed x7, local copies, waits for them, and re-layouts  14.1 us
    convert_element_type x2, other arithmetic, compute(): weights.astype(jnp.bfloat16)  13.9 us
    dot_general x2, matrix products, compute(): jnp.einsum('tgqd,ngd->tgqn', grouped, key_block, preferred_element_type=j...  7.38 us
  transfers between devices with their start and end apart: 2, of which 2 were waited for; matrix products, arithmetic and copies ran while one was open for 5% of the time, Pallas kernels for 0%

commit v1 on v0

v1 whole, which is shorter than its diff:
```python
import functools
import math

import jax
import jax.numpy as jnp
from jax import lax
from jax.experimental import pallas as pl
from jax.experimental.pallas import tpu as pltpu
from jax.sharding import PartitionSpec as P

HEADS = 128
KV_HEADS = 8
GROUP = HEADS // KV_HEADS

masked_score = -1e30


def chip_grid(devices):
    if devices % 2:
        return devices, 1, 1
    chips = devices // 2
    if chips % 2 or chips > 8:
        return chips, 1, 2
    return chips // 2, 2, 2


def collect(own, grid):
    depth, width, cores = grid

    def index(z, y, c):
        return (z * width + y) * cores + c

    def move(block, pairs):
        return lax.ppermute(block, "tp", pairs)

    places = [(y, c) for y in range(width) for c in range(cores)]
    blocks = {(0, 0, 0): own}
    for dz in range(1, depth):
        blocks[dz, 0, 0] = move(
            blocks[dz - 1, 0, 0],
            [(index(z - 1, y, c), index(z, y, c)) for z in range(dz, depth) for y, c in places],
        )
    if width == 2:
        for dz in range(depth):
            blocks[dz, 1, 0] = move(
                blocks[dz, 0, 0],
                [
                    (index(z, y, c), index(z, 1 - y, c))
                    for z in range(dz, depth)
                    for y, c in places
                    if dz or y == 0
                ],
            )
    if cores == 2:
        for dz in range(depth):
            for dy in range(width):
                blocks[dz, dy, 1] = move(
                    blocks[dz, dy, 0],
                    [
                        (index(z, y, c), index(z, y, 1 - c))
                        for z in range(dz, depth)
                        for y, c in places
                        if dz or (dy and y == 1) or (not dy and c == 0)
                    ],
                )
    return blocks


def attend_kernel(keys, grid, order, chunk, *refs):
    depth, width, cores = grid
    count = len(order)
    query_ref = refs[0]
    block_refs = refs[1 : 1 + count]
    out_ref, held, sems, total, peak = refs[1 + count :]
    tok = query_ref.shape[0]
    dim = held.shape[1] // (2 * KV_HEADS)
    rows = GROUP * tok
    head = pl.program_id(0)
    me = lax.axis_index("tp")
    zz, yy, cc = me // (width * cores), (me // cores) % width, me % cores

    @pl.when(head == 0)
    def _():
        copies = []
        for place, (dz, dy, dc) in enumerate(order):
            source_z = jnp.where(zz >= dz, zz - dz, zz - dz + depth)
            source_y = jnp.where(yy >= dy, yy - dy, yy - dy + width)
            source_c = jnp.where(cc >= dc, cc - dc, cc - dc + cores)
            source = (source_z * width + source_y) * cores + source_c
            start = pl.multiple_of(source * tok, tok)
            copies.append(
                pltpu.make_async_copy(
                    block_refs[place], held.at[pl.ds(start, tok)], sems.at[place]
                )
            )
        for copy in copies:
            copy.start()
        for copy in copies:
            copy.wait()

    query = jnp.concatenate([query_ref[:, q * dim : (q + 1) * dim] for q in range(GROUP)], axis=0)
    factor = dim ** (-0.5) * math.log2(math.e)
    key_column = pl.ds(pl.multiple_of(head * dim, dim), dim)
    value_column = pl.ds(pl.multiple_of((KV_HEADS + head) * dim, dim), dim)
    ones = jnp.where(lax.broadcasted_iota(jnp.int32, (chunk, dim), 1) == 0, 1.0, 0.0).astype(
        jnp.bfloat16
    )
    parts = 4
    part_rows = rows // parts

    def absorb(start, first, allowed):
        span = pl.ds(pl.multiple_of(start, chunk), chunk)
        key_block = held[span, key_column]
        value_block = jnp.concatenate([held[span, value_column], ones], axis=1)
        for part in range(parts):
            here = slice(part * part_rows, (part + 1) * part_rows)
            scores = lax.dot_general(
                query[here],
                key_block,
                (((1,), (1,)), ((), ())),
                preferred_element_type=jnp.float32,
            )
            if allowed is not None:
                scores = jnp.where(allowed, scores, masked_score)
            top = jnp.max(scores, axis=1, keepdims=True)
            if not first:
                before = peak[here]
                top = jnp.maximum(before, top)
            weights = jnp.exp2((scores - top) * factor).astype(jnp.bfloat16)
            fresh = jnp.dot(weights, value_block, preferred_element_type=jnp.float32)
            if not first:
                fresh = total[here] * jnp.exp2((before - top) * factor) + fresh
            total[here] = fresh
            peak[here] = top

    first_pos = me * tok
    full = first_pos // chunk
    start = full * chunk
    row = lax.broadcasted_iota(jnp.int32, (part_rows, chunk), 0)
    column = lax.broadcasted_iota(jnp.int32, (part_rows, chunk), 1)
    allowed = column + start <= first_pos + row % tok
    absorb(start, True, allowed)

    @pl.loop(0, full)
    def _(block):
        absorb(block * chunk, False, None)

    for q in range(GROUP):
        here = slice(q * tok, (q + 1) * tok)
        out_ref[:, q * dim : (q + 1) * dim] = (
            total[here, :dim] / total[here, dim : dim + 1]
        ).astype(out_ref.dtype)


def attend(query_rows, blocks, grid):
    tok, width = query_rows.shape
    order = sorted(blocks)
    keys = tok * len(order)
    packed = blocks[order[0]].shape[1]
    dim = packed // (2 * KV_HEADS)
    chunk = math.gcd(keys, 512)
    columns = width // KV_HEADS
    return pl.pallas_call(
        functools.partial(attend_kernel, keys, grid, order, chunk),
        out_shape=jax.ShapeDtypeStruct(query_rows.shape, query_rows.dtype),
        grid=(KV_HEADS,),
        in_specs=[pl.BlockSpec((tok, columns), lambda head: (0, head))]
        + [pl.BlockSpec(memory_space=pl.ANY)] * len(order),
        out_specs=pl.BlockSpec((tok, columns), lambda head: (0, head)),
        scratch_shapes=[
            pltpu.VMEM((keys, packed), jnp.bfloat16),
            pltpu.SemaphoreType.DMA((len(order),)),
            pltpu.VMEM((GROUP * tok, 2 * dim), jnp.float32),
            pltpu.VMEM((GROUP * tok, 1), jnp.float32),
        ],
        compiler_params=pltpu.CompilerParams(vmem_limit_bytes=48 * 2**20),
        name="attend",
    )(query_rows, *[blocks[place] for place in order])


def solution(mesh):
    grid = chip_grid(mesh.shape["tp"])

    def body(query_rows, key_rows, value_rows):
        own = jnp.concatenate([key_rows, value_rows], axis=1)
        return attend(query_rows, collect(own, grid), grid)

    spec = P(("groups", "tp"), None)
    return jax.shard_map(
        body, mesh=mesh, in_specs=(spec, spec, spec), out_specs=spec, check_vma=False
    )
```

time: 161 us -> 71.8 us (0.45)
  waiting for transfers between devices: 79.4 us -> 12.2 us
  starting transfers between devices: 0.04 us -> 33.9 us
  matrix products: 29.8 us -> 0 us
  Pallas kernels: 0 us -> 22.9 us
  other arithmetic: 18.2 us -> 0 us
  local copies, waits for them, and re-layouts: 18.6 us -> 1.83 us
  between operations: 13.5 us -> 0.21 us
    all_gather x2 -> x0, waiting for transfers between devices: 78 us -> none  [the longest x1 39.6 us: cycle_attend(): key_piece = lax.all_gather(key_rows, 'tp', axis=0, tiled=True)]
    ppermute x0 -> x15, starting transfers between devices: none -> 33.9 us  [move(): return lax.ppermute(block, 'tp', pairs)]
    dot_general x4 -> x0, matrix products: 29.8 us -> none  [the longest x2 22.5 us: compute(): jnp.einsum('tgqn,ngd->tgqd', weights.astype(jnp.bfloat16), value_block, p...]
    pallas_call x0 -> x1, Pallas kernels: none -> 22.9 us  [attend(): pl.pallas_call(functools.partial(attend_kernel, keys, grid, order, chunk)...]
    convert_element_type x3 -> x0, other arithmetic: 16.7 us -> none  [the longest x2 13.9 us: compute(): weights.astype(jnp.bfloat16)]
    unnamed x7 -> x1, local copies, waits for them, and re-layouts: 14.1 us -> 0.91 us
    ppermute x0 -> x15, waiting for transfers between devices: none -> 12.2 us  [move(): return lax.ppermute(block, 'tp', pairs)]
    broadcast_in_dim x3 -> x0, local copies, waits for them, and re-layouts: 2.33 us -> none  [the longest x1 2.32 us: cycle_attend(): jnp.zeros((tok_rows, KV_HEADS, group, head_dim), jnp.float32)]
  transfers between devices with their start and end apart: 2 -> 15, of which waited for: 2 -> 4; matrix products, arithmetic and copies ran while one was open for 5% -> 0% of each run, Pallas kernels for 0% -> 0%
where the time goes in v1:
time: 71.8 us; the launch traced here: 71.1 us
  starting transfers between devices  33.9 us (47%)
  Pallas kernels  22.9 us (32%)
  waiting for transfers between devices  12.2 us (17%)
  local copies, waits for them, and re-layouts  1.83 us (3%)
    ppermute x15, starting transfers between devices, move(): return lax.ppermute(block, 'tp', pairs)  33.9 us
    pallas_call x1, Pallas kernels, attend(): pl.pallas_call(functools.partial(attend_kernel, keys, grid, order, chunk)...  22.9 us
    ppermute x15, waiting for transfers between devices, move(): return lax.ppermute(block, 'tp', pairs)  12.2 us
  transfers between devices with their start and end apart: 15, of which 4 were waited for; matrix products, arithmetic and copies ran while one was open for 0% of the time, Pallas kernels for 0%

profile of v1, /device:TPU:25, one launch (start us, length us, event | category | flops | bytes accessed | tf_op | source)
XLA Modules:
  0.0 71.1 jit_solution(13435006518624335084)
XLA Ops:
  0.0 0.9 %constant_dynamic-update-slice_fusion.1 = bf16[64,2048]{1,0:T(8,128)(2,1)S(1)} fusion(bf16[64,1024]{1,0:T(8,128)(2,1)} %param.4), kind=kLoop, calls=%fused_computation.1 | loop fusion | bytes 262144
  0.9 0.9 %constant_dynamic-update-slice_fusion.refs_1_ = bf16[64,2048]{1,0:T(8,128)(2,1)S(1)} fusion(bf16[64,2048]{1,0:T(8,128)(2,1)S(1)} %constant_dynamic-update-slice_fusion.1, bf16[64,1024]{1,0:T(8,128)(2,1)} %param.5), kind=kLoop, calls=%fused_computation | loop fusion | bytes 262144 | tf_op jit(solution)/shard_map/concatenate | solution.py:185
  1.8 1.3 %collective-permute-start.3 = (bf16[64,2048]{1,0:T(8,128)(2,1)S(1)}, bf16[64,2048]{1,0:T(8,128)(2,1)S(1)}, u32[]{:S(2)}, u32[]{:S(2)}) collective-permute-start(bf16[64,2048]{1,0:T(8,128)(2,1)S(1)} %constant_dynamic-update-slice_fusion.refs_1_), channel_id=1, source_target_pairs={{0,4},{1,5},{2,6},{3,7},{4,8},{5,9},{6,10},{7,11},{8,12},{9,13},{1... | collective-permute-start | bytes 786440 | tf_op jit(solution)/shard_map/ppermute | solution.py:34
  3.1 7.8 %collective-permute-done.3.refs_5_ = bf16[64,2048]{1,0:T(8,128)(2,1)S(1)} collective-permute-done((bf16[64,2048]{1,0:T(8,128)(2,1)S(1)}, bf16[64,2048]{1,0:T(8,128)(2,1)S(1)}, u32[]{:S(2)}, u32[]{:S(2)}) %collective-permute-start.3) | collective-permute-done | bytes 262176 | tf_op jit(solution)/shard_map/ppermute | solution.py:34
  10.9 1.3 %collective-permute-start.7 = (bf16[64,2048]{1,0:T(8,128)(2,1)S(1)}, bf16[64,2048]{1,0:T(8,128)(2,1)S(1)}, u32[]{:S(2)}, u32[]{:S(2)}) collective-permute-start(bf16[64,2048]{1,0:T(8,128)(2,1)S(1)} %collective-permute-done.3.refs_5_), channel_id=1, source_target_pairs={{4,8},{5,9},{6,10},{7,11},{8,12},{9,13},{10,14},{11,15},{20,24},{2... | collective-permute-start | bytes 786440 | tf_op jit(solution)/shard_map/ppermute | solution.py:34
  12.2 3.2 %collective-permute-start.1 = (bf16[64,2048]{1,0:T(8,128)(2,1)S(1)}, bf16[64,2048]{1,0:T(8,128)(2,1)S(1)}, u32[]{:S(2)}, u32[]{:S(2)}) collective-permute-start(bf16[64,2048]{1,0:T(8,128)(2,1)S(1)} %constant_dynamic-update-slice_fusion.refs_1_), channel_id=1, source_target_pairs={{0,2},{1,3},{4,6},{5,7},{8,10},{9,11},{12,14},{13,15},{16,18},{17,... | collective-permute-start | bytes 786440 | tf_op jit(solution)/shard_map/ppermute | solution.py:34
  15.4 1.3 %collective-permute-start = (bf16[64,2048]{1,0:T(8,128)(2,1)S(1)}, bf16[64,2048]{1,0:T(8,128)(2,1)S(1)}, u32[]{:S(2)}, u32[]{:S(2)}) collective-permute-start(bf16[64,2048]{1,0:T(8,128)(2,1)S(1)} %constant_dynamic-update-slice_fusion.refs_1_), channel_id=1, source_target_pairs={{0,1},{2,3},{4,5},{6,7},{8,9},{10,11},{12,13},{14,15},{16,17},{18,... | collective-permute-start | bytes 786440 | tf_op jit(solution)/shard_map/ppermute | solution.py:34
  16.7 2.4 %collective-permute-done.7.refs_9_ = bf16[64,2048]{1,0:T(8,128)(2,1)S(1)} collective-permute-done((bf16[64,2048]{1,0:T(8,128)(2,1)S(1)}, bf16[64,2048]{1,0:T(8,128)(2,1)S(1)}, u32[]{:S(2)}, u32[]{:S(2)}) %collective-permute-start.7) | collective-permute-done | bytes 262176 | tf_op jit(solution)/shard_map/ppermute | solution.py:34
  19.0 1.3 %collective-permute-start.11 = (bf16[64,2048]{1,0:T(8,128)(2,1)S(1)}, bf16[64,2048]{1,0:T(8,128)(2,1)S(1)}, u32[]{:S(2)}, u32[]{:S(2)}) collective-permute-start(bf16[64,2048]{1,0:T(8,128)(2,1)S(1)} %collective-permute-done.7.refs_9_), channel_id=1, source_target_pairs={{8,12},{9,13},{10,14},{11,15},{24,28},{25,29},{26,30},{27,31}} | collective-permute-start | bytes 786440 | tf_op jit(solution)/shard_map/ppermute | solution.py:34
  20.3 3.1 %collective-permute-start.5 = (bf16[64,2048]{1,0:T(8,128)(2,1)S(1)}, bf16[64,2048]{1,0:T(8,128)(2,1)S(1)}, u32[]{:S(2)}, u32[]{:S(2)}) collective-permute-start(bf16[64,2048]{1,0:T(8,128)(2,1)S(1)} %collective-permute-done.3.refs_5_), channel_id=1, source_target_pairs={{4,6},{5,7},{6,4},{7,5},{8,10},{9,11},{10,8},{11,9},{12,14},{13,15... | collective-permute-start | bytes 786440 | tf_op jit(solution)/shard_map/ppermute | solution.py:34
  23.5 4.7 %collective-permute-start.4 = (bf16[64,2048]{1,0:T(8,128)(2,1)S(1)}, bf16[64,2048]{1,0:T(8,128)(2,1)S(1)}, u32[]{:S(2)}, u32[]{:S(2)}) collective-permute-start(bf16[64,2048]{1,0:T(8,128)(2,1)S(1)} %collective-permute-done.3.refs_5_), channel_id=1, source_target_pairs={{4,5},{5,4},{6,7},{7,6},{8,9},{9,8},{10,11},{11,10},{12,13},{13,12... | collective-permute-start | bytes 786440 | tf_op jit(solution)/shard_map/ppermute | solution.py:34
  28.1 0.0 collective-permute-done.1.refs_3_
  28.2 0.7 collective-permute-start.2
  28.8 0.0 collective-permute-done.refs_2_
  28.9 3.4 %collective-permute-start.9 = (bf16[64,2048]{1,0:T(8,128)(2,1)S(1)}, bf16[64,2048]{1,0:T(8,128)(2,1)S(1)}, u32[]{:S(2)}, u32[]{:S(2)}) collective-permute-start(bf16[64,2048]{1,0:T(8,128)(2,1)S(1)} %collective-permute-done.7.refs_9_), channel_id=1, source_target_pairs={{8,10},{9,11},{10,8},{11,9},{12,14},{13,15},{14,12},{15,13},{24,26... | collective-permute-start | bytes 786440 | tf_op jit(solution)/shard_map/ppermute | solution.py:34
  32.2 0.0 collective-permute-done.11.refs_13_
  32.3 1.9 %collective-permute-start.13 = (bf16[64,2048]{1,0:T(8,128)(2,1)S(1)}, bf16[64,2048]{1,0:T(8,128)(2,1)S(1)}, u32[]{:S(2)}, u32[]{:S(2)}) collective-permute-start(bf16[64,2048]{1,0:T(8,128)(2,1)S(1)} %collective-permute-done.11.refs_13_), channel_id=1, source_target_pairs={{12,14},{13,15},{14,12},{15,13},{28,30},{29,31},{30,28},{31,29}} | collective-permute-start | bytes 786440 | tf_op jit(solution)/shard_map/ppermute | solution.py:34
  34.2 0.0 collective-permute-done.5.refs_7_
  34.2 2.7 %collective-permute-start.8 = (bf16[64,2048]{1,0:T(8,128)(2,1)S(1)}, bf16[64,2048]{1,0:T(8,128)(2,1)S(1)}, u32[]{:S(2)}, u32[]{:S(2)}) collective-permute-start(bf16[64,2048]{1,0:T(8,128)(2,1)S(1)} %collective-permute-done.7.refs_9_), channel_id=1, source_target_pairs={{8,9},{9,8},{10,11},{11,10},{12,13},{13,12},{14,15},{15,14},{24,25... | collective-permute-start | bytes 786440 | tf_op jit(solution)/shard_map/ppermute | solution.py:34
  36.9 0.0 collective-permute-done.4.refs_6_
  36.9 1.9 %collective-permute-start.6 = (bf16[64,2048]{1,0:T(8,128)(2,1)S(1)}, bf16[64,2048]{1,0:T(8,128)(2,1)S(1)}, u32[]{:S(2)}, u32[]{:S(2)}) collective-permute-start(bf16[64,2048]{1,0:T(8,128)(2,1)S(1)} %collective-permute-done.5.refs_7_), channel_id=1, source_target_pairs={{4,5},{5,4},{6,7},{7,6},{8,9},{9,8},{10,11},{11,10},{12,13},{13,12... | collective-permute-start | bytes 786440 | tf_op jit(solution)/shard_map/ppermute | solution.py:34
  38.8 0.0 collective-permute-done.2.refs_4_
  38.8 2.4 %collective-permute-start.12 = (bf16[64,2048]{1,0:T(8,128)(2,1)S(1)}, bf16[64,2048]{1,0:T(8,128)(2,1)S(1)}, u32[]{:S(2)}, u32[]{:S(2)}) collective-permute-start(bf16[64,2048]{1,0:T(8,128)(2,1)S(1)} %collective-permute-done.11.refs_13_), channel_id=1, source_target_pairs={{12,13},{13,12},{14,15},{15,14},{28,29},{29,28},{30,31},{31,30}} | collective-permute-start | bytes 786440 | tf_op jit(solution)/shard_map/ppermute | solution.py:34
  41.2 0.0 collective-permute-done.9.refs_11_
  41.3 1.9 %collective-permute-start.10 = (bf16[64,2048]{1,0:T(8,128)(2,1)S(1)}, bf16[64,2048]{1,0:T(8,128)(2,1)S(1)}, u32[]{:S(2)}, u32[]{:S(2)}) collective-permute-start(bf16[64,2048]{1,0:T(8,128)(2,1)S(1)} %collective-permute-done.9.refs_11_), channel_id=1, source_target_pairs={{8,9},{9,8},{10,11},{11,10},{12,13},{13,12},{14,15},{15,14},{24,25... | collective-permute-start | bytes 786440 | tf_op jit(solution)/shard_map/ppermute | solution.py:34
  43.2 0.9 %collective-permute-done.13.refs_15_ = bf16[64,2048]{1,0:T(8,128)(2,1)S(1)} collective-permute-done((bf16[64,2048]{1,0:T(8,128)(2,1)S(1)}, bf16[64,2048]{1,0:T(8,128)(2,1)S(1)}, u32[]{:S(2)}, u32[]{:S(2)}) %collective-permute-start.13) | collective-permute-done | bytes 262176 | tf_op jit(solution)/shard_map/ppermute | solution.py:34
  44.1 2.9 %collective-permute-start.14 = (bf16[64,2048]{1,0:T(8,128)(2,1)S(1)}, bf16[64,2048]{1,0:T(8,128)(2,1)S(1)}, u32[]{:S(2)}, u32[]{:S(2)}) collective-permute-start(bf16[64,2048]{1,0:T(8,128)(2,1)S(1)} %collective-permute-done.13.refs_15_), channel_id=1, source_target_pairs={{12,13},{13,12},{14,15},{15,14},{28,29},{29,28},{30,31},{31,30}} | collective-permute-start | bytes 786440 | tf_op jit(solution)/shard_map/ppermute | solution.py:34
  47.0 0.0 collective-permute-done.8.refs_10_
  47.0 0.0 collective-permute-done.6.refs_8_
  47.0 0.0 collective-permute-done.12.refs_14_
  47.0 1.1 %collective-permute-done.14.refs_16_ = bf16[64,2048]{1,0:T(8,128)(2,1)S(1)} collective-permute-done((bf16[64,2048]{1,0:T(8,128)(2,1)S(1)}, bf16[64,2048]{1,0:T(8,128)(2,1)S(1)}, u32[]{:S(2)}, u32[]{:S(2)}) %collective-permute-start.14) | collective-permute-done | bytes 262176 | tf_op jit(solution)/shard_map/ppermute | solution.py:34
  48.1 22.9 %attend.1 = bf16[64,16384]{1,0:T(8,128)(2,1)} custom-call(bf16[64,16384]{1,0:T(8,128)(2,1)} %refs_0_.1, bf16[64,2048]{1,0:T(8,128)(2,1)S(1)} %constant_dynamic-update-slice_fusion.refs_1_, bf16[64,2048]{1,0:T(8,128)(2,1)S(1)} %collective-permute-done.refs_2_, bf16[64,2048]{1,0:T(8,128)(2,1)S(1)} %collective-permute-done.1.refs_3_, ...), custom_call_target="tpu_custom_call" | custom-call | tf_op jit(solution)/shard_map/attend/pallas_call | solution.py:163
  (1 shorter events, 0.0 us)
Async XLA Ops:
  1.8 9.1 %collective-permute-start.3 = (bf16[64,2048]{1,0:T(8,128)(2,1)S(1)}, bf16[64,2048]{1,0:T(8,128)(2,1)S(1)}, u32[]{:S(2)}, u32[]{:S(2)}) collective-permute-start(bf16[64,2048]{1,0:T(8,128)(2,1)S(1)} %constant_dynamic-update-slice_fusion.refs_1_), channel_id=1, source_target_pairs={{0,4},{1,5},{2,6},{3,7},{4,8},{5,9},{6,10},{7,11},{8,12},{9,13},{1... | collective-permute-start | bytes 786440 | tf_op jit(solution)/shard_map/ppermute | solution.py:34
  10.9 8.1 %collective-permute-start.7 = (bf16[64,2048]{1,0:T(8,128)(2,1)S(1)}, bf16[64,2048]{1,0:T(8,128)(2,1)S(1)}, u32[]{:S(2)}, u32[]{:S(2)}) collective-permute-start(bf16[64,2048]{1,0:T(8,128)(2,1)S(1)} %collective-permute-done.3.refs_5_), channel_id=1, source_target_pairs={{4,8},{5,9},{6,10},{7,11},{8,12},{9,13},{10,14},{11,15},{20,24},{2... | collective-permute-start | bytes 786440 | tf_op jit(solution)/shard_map/ppermute | solution.py:34
  12.2 16.0 %collective-permute-start.1 = (bf16[64,2048]{1,0:T(8,128)(2,1)S(1)}, bf16[64,2048]{1,0:T(8,128)(2,1)S(1)}, u32[]{:S(2)}, u32[]{:S(2)}) collective-permute-start(bf16[64,2048]{1,0:T(8,128)(2,1)S(1)} %constant_dynamic-update-slice_fusion.refs_1_), channel_id=1, source_target_pairs={{0,2},{1,3},{4,6},{5,7},{8,10},{9,11},{12,14},{13,15},{16,18},{17,... | collective-permute-start | bytes 786440 | tf_op jit(solution)/shard_map/ppermute | solution.py:34
  15.4 13.5 %collective-permute-start = (bf16[64,2048]{1,0:T(8,128)(2,1)S(1)}, bf16[64,2048]{1,0:T(8,128)(2,1)S(1)}, u32[]{:S(2)}, u32[]{:S(2)}) collective-permute-start(bf16[64,2048]{1,0:T(8,128)(2,1)S(1)} %constant_dynamic-update-slice_fusion.refs_1_), channel_id=1, source_target_pairs={{0,1},{2,3},{4,5},{6,7},{8,9},{10,11},{12,13},{14,15},{16,17},{18,... | collective-permute-start | bytes 786440 | tf_op jit(solution)/shard_map/ppermute | solution.py:34
  19.0 13.2 %collective-permute-start.11 = (bf16[64,2048]{1,0:T(8,128)(2,1)S(1)}, bf16[64,2048]{1,0:T(8,128)(2,1)S(1)}, u32[]{:S(2)}, u32[]{:S(2)}) collective-permute-start(bf16[64,2048]{1,0:T(8,128)(2,1)S(1)} %collective-permute-done.7.refs_9_), channel_id=1, source_target_pairs={{8,12},{9,13},{10,14},{11,15},{24,28},{25,29},{26,30},{27,31}} | collective-permute-start | bytes 786440 | tf_op jit(solution)/shard_map/ppermute | solution.py:34
  20.3 13.9 %collective-permute-start.5 = (bf16[64,2048]{1,0:T(8,128)(2,1)S(1)}, bf16[64,2048]{1,0:T(8,128)(2,1)S(1)}, u32[]{:S(2)}, u32[]{:S(2)}) collective-permute-start(bf16[64,2048]{1,0:T(8,128)(2,1)S(1)} %collective-permute-done.3.refs_5_), channel_id=1, source_target_pairs={{4,6},{5,7},{6,4},{7,5},{8,10},{9,11},{10,8},{11,9},{12,14},{13,15... | collective-permute-start | bytes 786440 | tf_op jit(solution)/shard_map/ppermute | solution.py:34
  23.5 13.4 %collective-permute-start.4 = (bf16[64,2048]{1,0:T(8,128)(2,1)S(1)}, bf16[64,2048]{1,0:T(8,128)(2,1)S(1)}, u32[]{:S(2)}, u32[]{:S(2)}) collective-permute-start(bf16[64,2048]{1,0:T(8,128)(2,1)S(1)} %collective-permute-done.3.refs_5_), channel_id=1, source_target_pairs={{4,5},{5,4},{6,7},{7,6},{8,9},{9,8},{10,11},{11,10},{12,13},{13,12... | collective-permute-start | bytes 786440 | tf_op jit(solution)/shard_map/ppermute | solution.py:34
  28.2 10.7 %collective-permute-start.2 = (bf16[64,2048]{1,0:T(8,128)(2,1)S(1)}, bf16[64,2048]{1,0:T(8,128)(2,1)S(1)}, u32[]{:S(2)}, u32[]{:S(2)}) collective-permute-start(bf16[64,2048]{1,0:T(8,128)(2,1)S(1)} %collective-permute-done.1.refs_3_), channel_id=1, source_target_pairs={{2,3},{3,2},{6,7},{7,6},{10,11},{11,10},{14,15},{15,14},{18,19},{1... | collective-permute-start | bytes 786440 | tf_op jit(solution)/shard_map/ppermute | solution.py:34
  28.9 12.4 %collective-permute-start.9 = (bf16[64,2048]{1,0:T(8,128)(2,1)S(1)}, bf16[64,2048]{1,0:T(8,128)(2,1)S(1)}, u32[]{:S(2)}, u32[]{:S(2)}) collective-permute-start(bf16[64,2048]{1,0:T(8,128)(2,1)S(1)} %collective-permute-done.7.refs_9_), channel_id=1, source_target_pairs={{8,10},{9,11},{10,8},{11,9},{12,14},{13,15},{14,12},{15,13},{24,26... | collective-permute-start | bytes 786440 | tf_op jit(solution)/shard_map/ppermute | solution.py:34
  32.3 11.8 %collective-permute-start.13 = (bf16[64,2048]{1,0:T(8,128)(2,1)S(1)}, bf16[64,2048]{1,0:T(8,128)(2,1)S(1)}, u32[]{:S(2)}, u32[]{:S(2)}) collective-permute-start(bf16[64,2048]{1,0:T(8,128)(2,1)S(1)} %collective-permute-done.11.refs_13_), channel_id=1, source_target_pairs={{12,14},{13,15},{14,12},{15,13},{28,30},{29,31},{30,28},{31,29}} | collective-permute-start | bytes 786440 | tf_op jit(solution)/shard_map/ppermute | solution.py:34
  34.2 12.8 %collective-permute-start.8 = (bf16[64,2048]{1,0:T(8,128)(2,1)S(1)}, bf16[64,2048]{1,0:T(8,128)(2,1)S(1)}, u32[]{:S(2)}, u32[]{:S(2)}) collective-permute-start(bf16[64,2048]{1,0:T(8,128)(2,1)S(1)} %collective-permute-done.7.refs_9_), channel_id=1, source_target_pairs={{8,9},{9,8},{10,11},{11,10},{12,13},{13,12},{14,15},{15,14},{24,25... | collective-permute-start | bytes 786440 | tf_op jit(solution)/shard_map/ppermute | solution.py:34
  36.9 10.1 %collective-permute-start.6 = (bf16[64,2048]{1,0:T(8,128)(2,1)S(1)}, bf16[64,2048]{1,0:T(8,128)(2,1)S(1)}, u32[]{:S(2)}, u32[]{:S(2)}) collective-permute-start(bf16[64,2048]{1,0:T(8,128)(2,1)S(1)} %collective-permute-done.5.refs_7_), channel_id=1, source_target_pairs={{4,5},{5,4},{6,7},{7,6},{8,9},{9,8},{10,11},{11,10},{12,13},{13,12... | collective-permute-start | bytes 786440 | tf_op jit(solution)/shard_map/ppermute | solution.py:34
  38.8 8.2 %collective-permute-start.12 = (bf16[64,2048]{1,0:T(8,128)(2,1)S(1)}, bf16[64,2048]{1,0:T(8,128)(2,1)S(1)}, u32[]{:S(2)}, u32[]{:S(2)}) collective-permute-start(bf16[64,2048]{1,0:T(8,128)(2,1)S(1)} %collective-permute-done.11.refs_13_), channel_id=1, source_target_pairs={{12,13},{13,12},{14,15},{15,14},{28,29},{29,28},{30,31},{31,30}} | collective-permute-start | bytes 786440 | tf_op jit(solution)/shard_map/ppermute | solution.py:34
  41.3 5.8 %collective-permute-start.10 = (bf16[64,2048]{1,0:T(8,128)(2,1)S(1)}, bf16[64,2048]{1,0:T(8,128)(2,1)S(1)}, u32[]{:S(2)}, u32[]{:S(2)}) collective-permute-start(bf16[64,2048]{1,0:T(8,128)(2,1)S(1)} %collective-permute-done.9.refs_11_), channel_id=1, source_target_pairs={{8,9},{9,8},{10,11},{11,10},{12,13},{13,12},{14,15},{15,14},{24,25... | collective-permute-start | bytes 786440 | tf_op jit(solution)/shard_map/ppermute | solution.py:34
  44.1 4.1 %collective-permute-start.14 = (bf16[64,2048]{1,0:T(8,128)(2,1)S(1)}, bf16[64,2048]{1,0:T(8,128)(2,1)S(1)}, u32[]{:S(2)}, u32[]{:S(2)}) collective-permute-start(bf16[64,2048]{1,0:T(8,128)(2,1)S(1)} %collective-permute-done.13.refs_15_), channel_id=1, source_target_pairs={{12,13},{13,12},{14,15},{15,14},{28,29},{29,28},{30,31},{31,30}} | collective-permute-start | bytes 786440 | tf_op jit(solution)/shard_map/ppermute | solution.py:34

commit v2 on v0

v2 whole, which is shorter than its diff:
```python
import functools
import math

import jax
import jax.numpy as jnp
from jax import lax
from jax.experimental import pallas as pl
from jax.experimental.pallas import tpu as pltpu
from jax.sharding import PartitionSpec as P

HEADS = 128
KV_HEADS = 8
GROUP = HEADS // KV_HEADS
PARTS = 4

masked_score = -1e30


def chip_grid(devices):
    if devices % 2:
        return devices, 1, 1
    chips = devices // 2
    if chips % 2 or chips > 8:
        return chips, 1, 2
    return chips // 2, 2, 2


def place(grid):
    depth, width, cores = grid
    me = lax.axis_index("tp")
    return me // (width * cores), (me // cores) % width, me % cores


def stack(arrays, name, source=pl.ANY):
    rows, columns = arrays[0].shape

    def kernel(*refs):
        sems = refs[-1]
        out_ref = refs[-2]
        copies = [
            pltpu.make_async_copy(ref, out_ref.at[at], sems.at[at])
            for at, ref in enumerate(refs[:-2])
        ]
        for copy in copies:
            copy.start()
        for copy in copies:
            copy.wait()

    count = len(arrays)
    return pl.pallas_call(
        kernel,
        out_shape=jax.ShapeDtypeStruct((count, rows, columns), arrays[0].dtype),
        in_specs=[pl.BlockSpec(memory_space=source)] * count,
        out_specs=pl.BlockSpec(memory_space=pl.ANY),
        scratch_shapes=[pltpu.SemaphoreType.DMA((count,))],
        name=name,
    )(*arrays)


def z_move(own, grid, dz):
    depth, width, cores = grid
    side = width * cores
    pairs = [(at - dz * side, at) for at in range(dz * side, depth * side)]
    return lax.ppermute(own, "tp", pairs)


def y_swap(block, grid, dz):
    depth, width, cores = grid
    pairs = []
    for at in range(dz * width * cores, depth * width * cores):
        y = (at // cores) % width
        other = at + (1 - 2 * y) * cores
        if dz or other > at:
            pairs.append((at, other))
    return lax.ppermute(block, "tp", pairs)


def core_swap(blocks, grid):
    depth, width, cores = grid
    pairs = [(at, at ^ 1) for at in range(depth * width * cores)]
    return lax.ppermute(blocks, "tp", pairs)


def queries_of(query_ref, dim):
    return jnp.concatenate([query_ref[:, q * dim : (q + 1) * dim] for q in range(GROUP)], axis=0)


def keys_of(block, tok):
    count, _, _, dim = block.shape
    return block[:, 0].reshape(count * tok, dim), block[:, 1].reshape(count * tok, dim)


def with_ones(values):
    ones = jnp.where(lax.broadcasted_iota(jnp.int32, values.shape, 1) == 0, 1.0, 0.0)
    return jnp.concatenate([values, ones.astype(values.dtype)], axis=1)


def absorb(query, keys, values, bias, state, emit):
    rows, dim = query.shape
    factor = dim ** (-0.5) * math.log2(math.e)
    part_rows = rows // PARTS
    value_block = with_ones(values)
    lane = lax.broadcasted_iota(jnp.int32, (part_rows, 2 * dim), 1)
    for part in range(PARTS):
        here = slice(part * part_rows, (part + 1) * part_rows)
        scores = lax.dot_general(
            query[here], keys, (((1,), (1,)), ((), ())), preferred_element_type=jnp.float32
        )
        if bias is not None:
            repeats = part_rows // bias.shape[0]
            scores = (
                scores.reshape(repeats, bias.shape[0], scores.shape[1]) + bias[None]
            ).reshape(scores.shape)
        top = jnp.max(scores, axis=1, keepdims=True)
        if state is not None:
            before = state[here, dim + 1 : dim + 2]
            top = jnp.maximum(before, top)
        weights = jnp.exp2((scores - top) * factor).astype(jnp.bfloat16)
        fresh = jnp.dot(weights, value_block, preferred_element_type=jnp.float32)
        if state is not None:
            fresh = state[here, :] * jnp.exp2((before - top) * factor) + fresh
        emit(part, here, fresh, top, lane)


def first_kernel(grid, near, far, query_ref, near_ref, near_core_ref, far_ref, far_core_ref, state_ref, bias_ref):
    tok = query_ref.shape[0]
    dim = near_ref.shape[-1]
    zz, yy, cc = place(grid)
    width = grid[1]
    near_count = near_ref.shape[0]

    @pl.when(pl.program_id(0) == 0)
    def _():
        row = lax.broadcasted_iota(jnp.int32, bias_ref.shape, 0)
        column = lax.broadcasted_iota(jnp.int32, bias_ref.shape, 1)
        block, key = column // tok, column % tok
        other_y, other_c = block % width, block // near_count
        after_y = jnp.where(yy == 1, 0, tok)
        after_c = jnp.where(cc == 1, 0, tok)
        from_row = jnp.where(other_y == 1, after_y, jnp.where(other_c == 1, after_c, key))
        bias_ref[...] = jnp.where(from_row <= row, 0.0, masked_score)

    query = queries_of(query_ref, dim)

    def emit(part, here, fresh, top, lane):
        state_ref[here, :] = jnp.where(lane == dim + 1, top, fresh)

    near_keys, near_values = keys_of(
        jnp.concatenate([near_ref[...], near_core_ref[...]], axis=0), tok
    )

    if far:

        @pl.when(zz >= far)
        def _():
            far_keys, far_values = keys_of(
                jnp.concatenate([far_ref[...], far_core_ref[...]], axis=0), tok
            )
            bias = jnp.concatenate(
                [bias_ref[...], jnp.zeros((tok, far_keys.shape[0]), jnp.float32)], axis=1
            )
            absorb(
                query,
                jnp.concatenate([near_keys, far_keys], axis=0),
                jnp.concatenate([near_values, far_values], axis=0),
                bias,
                None,
                emit,
            )

    @pl.when(zz < far if far else zz >= 0)
    def _():
        absorb(query, near_keys, near_values, bias_ref[...], None, emit)


def later_kernel(grid, rows_below, last, query_ref, blocks_ref, state_ref, out_ref):
    tok = query_ref.shape[0]
    dim = blocks_ref.shape[-1]
    zz, _, _ = place(grid)
    query = queries_of(query_ref, dim)
    keys, values = keys_of(blocks_ref[...], tok)

    def emit(part, here, fresh, top, lane):
        if not last:
            out_ref[here, :] = jnp.where(lane == dim + 1, top, fresh)
            return
        done = (fresh[:, :dim] / fresh[:, dim : dim + 1]).astype(out_ref.dtype)
        heads = done.shape[0] // tok
        for head in range(heads):
            at = (part * heads + head) * dim
            out_ref[:, at : at + dim] = done[head * tok : (head + 1) * tok]

    state = state_ref
    all_there = zz >= max(rows_below)

    @pl.when(all_there)
    def _():
        absorb(query, keys, values, None, state, emit)

    @pl.when(jnp.logical_not(all_there))
    def _():
        block = lax.broadcasted_iota(jnp.int32, (tok, keys.shape[0]), 1) // tok
        bias = jnp.zeros(block.shape, jnp.float32)
        for at, below in enumerate(rows_below):
            bias = jnp.where(block == at, jnp.where(zz < below, masked_score, 0.0), bias)
        absorb(query, keys, values, bias, state, emit)


def solution(mesh):
    grid = chip_grid(mesh.shape["tp"])
    depth, width, cores = grid
    assert cores == 2 and depth > 2

    def body(query_rows, key_rows, value_rows):
        tok, columns = query_rows.shape
        dim = key_rows.shape[1] // KV_HEADS
        rows = GROUP * tok
        query_rows, key_rows, value_rows = (
            pltpu.with_memory_space_constraint(array, pltpu.HBM)
            for array in (query_rows, key_rows, value_rows)
        )
        own = stack([key_rows, value_rows], "pack", pltpu.HBM)

        def block_pair(block, dz):
            return [block, y_swap(block, grid, dz)] if width == 2 else [block]

        below = [depth - 1] + list(range(1, depth - 1))[::-1]
        moved = {dz: z_move(own, grid, dz) for dz in below}
        near = block_pair(own, 0)
        far = block_pair(moved[depth - 1], depth - 1)
        middle, rows_below = [], []
        for dz in below[1:]:
            pair = block_pair(moved[dz], dz)
            middle += pair
            rows_below += [dz] * len(pair)

        def pile(blocks, name):
            flat = [block.reshape(2 * tok, -1) for block in blocks]
            return stack(flat, name).reshape(len(blocks), 2, tok, -1)

        near, far, moved = lax.optimization_barrier((near, far, moved))
        early = pile(near + far, "early")
        early_core = core_swap(early, grid)
        query_spec = pl.BlockSpec((tok, columns // KV_HEADS), lambda head: (0, head))
        state_spec = pl.BlockSpec((None, rows, 2 * dim), lambda head: (head, 0, 0))
        state_shape = jax.ShapeDtypeStruct((KV_HEADS, rows, 2 * dim), jnp.float32)

        def blocks_spec(count, at):
            return pl.BlockSpec((count, 2, tok, dim), lambda head: (at, 0, 0, head))

        def cost(keys):
            return pl.CostEstimate(
                flops=4 * HEADS * tok * keys * dim,
                bytes_accessed=4 * HEADS * tok * dim,
                transcendentals=HEADS * tok * keys,
            )

        params = pltpu.CompilerParams(vmem_limit_bytes=32 * 2**20)
        count = len(near)
        state = pl.pallas_call(
            functools.partial(first_kernel, grid, 0, depth - 1),
            out_shape=state_shape,
            grid=(KV_HEADS,),
            in_specs=[
                query_spec,
                blocks_spec(count, 0),
                blocks_spec(count, 0),
                blocks_spec(count, 1),
                blocks_spec(count, 1),
            ],
            out_specs=state_spec,
            scratch_shapes=[pltpu.VMEM((tok, 2 * count * tok), jnp.float32)],
            compiler_params=params,
            cost_estimate=cost(4 * count * tok),
            name="attend_first",
        )(query_rows, early, early_core, early, early_core)
        middle, state = lax.optimization_barrier((middle, state))
        late = pile(middle, "late")
        late_core = core_swap(late, grid)
        for blocks, last in ((late, False), (late_core, True)):
            state = pl.pallas_call(
                functools.partial(later_kernel, grid, tuple(rows_below), last),
                out_shape=query_rows if last else state_shape,
                grid=(KV_HEADS,),
                in_specs=[query_spec, blocks_spec(len(middle), 0), state_spec],
                out_specs=query_spec if last else state_spec,
                compiler_params=params,
                cost_estimate=cost(len(middle) * tok),
                name="attend_last" if last else "attend_middle",
            )(query_rows, blocks, state)
        return state

    spec = P(("groups", "tp"), None)
    return jax.shard_map(
        body, mesh=mesh, in_specs=(spec, spec, spec), out_specs=spec, check_vma=False
    )
```

time: 161 us -> 165 us (1.025)
  Pallas kernels: 0 us -> 118 us
  waiting for transfers between devices: 79.4 us -> 18.7 us
  matrix products: 29.8 us -> 0 us
  other arithmetic: 18.2 us -> 0 us
  starting transfers between devices: 0.04 us -> 16.7 us
  between operations: 13.5 us -> 0.19 us
  local copies, waits for them, and re-layouts: 18.6 us -> 10.6 us
    pallas_call x0 -> x6, Pallas kernels: none -> 118 us  [the longest x3 74.9 us: stack(): pl.pallas_call(kernel, out_shape=jax.ShapeDtypeStruct((count, rows, colum...]
    all_gather x2 -> x0, waiting for transfers between devices: 78 us -> none  [the longest x1 39.6 us: cycle_attend(): key_piece = lax.all_gather(key_rows, 'tp', axis=0, tiled=True)]
    dot_general x4 -> x0, matrix products: 29.8 us -> none  [the longest x2 22.5 us: compute(): jnp.einsum('tgqn,ngd->tgqd', weights.astype(jnp.bfloat16), value_block, p...]
    ppermute x0 -> x9, waiting for transfers between devices: none -> 18.7 us  [the longest x3 18.7 us: z_move(): return lax.ppermute(own, 'tp', pairs)]
    convert_element_type x3 -> x0, other arithmetic: 16.7 us -> none  [the longest x2 13.9 us: compute(): weights.astype(jnp.bfloat16)]
    ppermute x0 -> x9, starting transfers between devices: none -> 16.7 us  [the longest x4 11.6 us: y_swap(): return lax.ppermute(block, 'tp', pairs)]
    unnamed x7 -> x22, local copies, waits for them, and re-layouts: 14.1 us -> 10.6 us
    broadcast_in_dim x3 -> x0, local copies, waits for them, and re-layouts: 2.33 us -> none  [the longest x1 2.32 us: cycle_attend(): jnp.zeros((tok_rows, KV_HEADS, group, head_dim), jnp.float32)]
  transfers between devices with their start and end apart: 2 -> 9, of which waited for: 2 -> 3; matrix products, arithmetic and copies ran while one was open for 5% -> 0% of each run, Pallas kernels for 0% -> 16%
where the time goes in v2:
time: 165 us
  Pallas kernels  118 us (72%)
  waiting for transfers between devices  18.7 us (11%)
  starting transfers between devices  16.7 us (10%)
  local copies, waits for them, and re-layouts  10.6 us (6%)
    pallas_call x3, Pallas kernels, stack(): pl.pallas_call(kernel, out_shape=jax.ShapeDtypeStruct((count, rows, colum...  74.9 us
    pallas_call x2, Pallas kernels, body(): pl.pallas_call(functools.partial(later_kernel, grid, tuple(rows_below), l...  33.6 us
    ppermute x3, waiting for transfers between devices, z_move(): return lax.ppermute(own, 'tp', pairs)  18.7 us
    ppermute x4, starting transfers between devices, y_swap(): return lax.ppermute(block, 'tp', pairs)  11.6 us
    unnamed x22, local copies, waits for them, and re-layouts  10.6 us
    pallas_call x1, Pallas kernels, body(): pl.pallas_call(functools.partial(first_kernel, grid, 0, depth - 1), out_s...  9.93 us
    ppermute x3, starting transfers between devices, z_move(): return lax.ppermute(own, 'tp', pairs)  3.88 us
  transfers between devices with their start and end apart: 9, of which 3 were waited for; matrix products, arithmetic and copies ran while one was open for 0% of the time, Pallas kernels for 16%

profile of v2, /device:TPU:25, one launch (start us, length us, event | category | flops | bytes accessed | tf_op | source)
XLA Modules:
  0.0 164.6 jit_solution(12431038168105511912)
XLA Ops:
  0.0 9.1 %pack.1 = bf16[2,64,1024]{2,1,0:T(8,128)(2,1)} custom-call(bf16[64,1024]{1,0:T(8,128)(2,1)} %refs_0_.1, bf16[64,1024]{1,0:T(8,128)(2,1)} %refs_1_.1), custom_call_target="tpu_custom_call" | custom-call | tf_op jit(solution)/shard_map/pack/pallas_call | solution.py:50
  9.1 1.3 collective-permute-start.5
  10.4 3.2 %collective-permute-start.4 = (bf16[2,64,1024]{2,1,0:T(8,128)(2,1)}, bf16[2,64,1024]{2,1,0:T(8,128)(2,1)S(1)}, u32[]{:S(2)}, u32[]{:S(2)}) collective-permute-start(bf16[2,64,1024]{2,1,0:T(8,128)(2,1)} %pack.1), channel_id=1, source_target_pairs={{0,2},{1,3},{4,6},{5,7},{8,10},{9,11},{12,14},{13,15},{16,18},{17,... | collective-permute-start | bytes 786440 | tf_op jit(solution)/shard_map/ppermute | solution.py:75
  13.5 1.3 collective-permute-start.2
  14.8 1.3 collective-permute-start
  16.1 4.1 %collective-permute-done.5 = bf16[2,64,1024]{2,1,0:T(8,128)(2,1)S(1)} collective-permute-done((bf16[2,64,1024]{2,1,0:T(8,128)(2,1)}, bf16[2,64,1024]{2,1,0:T(8,128)(2,1)S(1)}, u32[]{:S(2)}, u32[]{:S(2)}) %collective-permute-start.5) | collective-permute-done | bytes 262176 | tf_op jit(solution)/shard_map/ppermute | solution.py:64
  20.2 3.2 %collective-permute-start.6 = (bf16[2,64,1024]{2,1,0:T(8,128)(2,1)S(1)}, bf16[2,64,1024]{2,1,0:T(8,128)(2,1)S(1)}, u32[]{:S(2)}, u32[]{:S(2)}) collective-permute-start(bf16[2,64,1024]{2,1,0:T(8,128)(2,1)S(1)} %collective-permute-done.5), channel_id=1, source_target_pairs={{12,14},{13,15},{14,12},{15,13},{28,30},{29,31},{30,28},{31,29}} | collective-permute-start | bytes 786440 | tf_op jit(solution)/shard_map/ppermute | solution.py:75
  23.3 0.0 collective-permute-done.4
  23.4 3.5 %collective-permute-done.2 = bf16[2,64,1024]{2,1,0:T(8,128)(2,1)S(1)} collective-permute-done((bf16[2,64,1024]{2,1,0:T(8,128)(2,1)}, bf16[2,64,1024]{2,1,0:T(8,128)(2,1)S(1)}, u32[]{:S(2)}, u32[]{:S(2)}) %collective-permute-start.2) | collective-permute-done | bytes 262176 | tf_op jit(solution)/shard_map/ppermute | solution.py:64
  26.9 11.2 %collective-permute-done = bf16[2,64,1024]{2,1,0:T(8,128)(2,1)S(1)} collective-permute-done((bf16[2,64,1024]{2,1,0:T(8,128)(2,1)}, bf16[2,64,1024]{2,1,0:T(8,128)(2,1)S(1)}, u32[]{:S(2)}, u32[]{:S(2)}) %collective-permute-start) | collective-permute-done | bytes 262176 | tf_op jit(solution)/shard_map/ppermute | solution.py:64
  38.1 0.0 collective-permute-done.6
  38.1 0.7 copy-done.9
  38.8 32.9 %early.1 = bf16[4,128,1024]{2,1,0:T(8,128)(2,1)} custom-call(bf16[128,1024]{1,0:T(8,128)(2,1)} %bitcast.15, bf16[128,1024]{1,0:T(8,128)(2,1)} %bitcast.19, bf16[128,1024]{1,0:T(8,128)(2,1)} %bitcast.18, bf16[128,1024]{1,0:T(8,128)(2,1)} %bitcast.21), custom_call_target="tpu_custom_call" | custom-call | tf_op jit(solution)/shard_map/early/pallas_call | solution.py:50
  71.7 0.6 collective-permute-start.7
  72.3 3.1 %collective-permute-start.3 = (bf16[2,64,1024]{2,1,0:T(8,128)(2,1)S(1)}, bf16[2,64,1024]{2,1,0:T(8,128)(2,1)S(1)}, u32[]{:S(2)}, u32[]{:S(2)}) collective-permute-start(bf16[2,64,1024]{2,1,0:T(8,128)(2,1)S(1)} %collective-permute-done.2), channel_id=1, source_target_pairs={{4,6},{5,7},{6,4},{7,5},{8,10},{9,11},{10,8},{11,9},{12,14},{13,15... | collective-permute-start | bytes 786440 | tf_op jit(solution)/shard_map/ppermute | solution.py:75
  75.4 2.1 %collective-permute-start.1 = (bf16[2,64,1024]{2,1,0:T(8,128)(2,1)S(1)}, bf16[2,64,1024]{2,1,0:T(8,128)(2,1)S(1)}, u32[]{:S(2)}, u32[]{:S(2)}) collective-permute-start(bf16[2,64,1024]{2,1,0:T(8,128)(2,1)S(1)} %collective-permute-done), channel_id=1, source_target_pairs={{8,10},{9,11},{10,8},{11,9},{12,14},{13,15},{14,12},{15,13},{24,26... | collective-permute-start | bytes 786440 | tf_op jit(solution)/shard_map/ppermute | solution.py:75
  77.6 0.0 collective-permute-done.7.near_core_ref.far_core_ref
  77.6 0.0 copy-start.2
  77.6 1.2 copy-done.2
  78.8 9.9 %attend_first.1.state_ref = f32[8,1024,256]{2,1,0:T(8,128)S(1)} custom-call(bf16[64,16384]{1,0:T(8,128)(2,1)} %query_ref.5, bf16[4,2,64,1024]{3,2,1,0:T(8,128)(2,1)S(1)} %bitcast.11, bf16[4,2,64,1024]{3,2,1,0:T(8,128)(2,1)S(1)} %collective-permute-done.7.near_core_ref.far_core_ref, bf16[4,2,64,1024]{3,2,1,0:T(8,128)(2,1)S(1)} %bitcast.12, ...), custom_call_target="tpu_custom_call" | custom-call | flops 2147483648 | bytes 4194304 | tf_op jit(solution)/shard_map/attend_first/pallas_call | solution.py:260
  88.8 3.2 %copy-done = f32[8,1024,256]{2,1,0:T(8,128)} copy-done((f32[8,1024,256]{2,1,0:T(8,128)}, f32[8,1024,256]{2,1,0:T(8,128)S(1)}, u32[]{:S(2)}) %copy-start) | copy-done | bytes 8388632
  92.0 0.0 collective-permute-done.3
  92.0 0.0 collective-permute-done.1
  92.0 0.7 copy-done.8
  92.7 0.1 copy-done.10
  92.8 32.9 %late.1 = bf16[4,128,1024]{2,1,0:T(8,128)(2,1)} custom-call(bf16[128,1024]{1,0:T(8,128)(2,1)} %bitcast.17, bf16[128,1024]{1,0:T(8,128)(2,1)} %bitcast.22, bf16[128,1024]{1,0:T(8,128)(2,1)} %bitcast.16, bf16[128,1024]{1,0:T(8,128)(2,1)} %bitcast.20), custom_call_target="tpu_custom_call" | custom-call | tf_op jit(solution)/shard_map/late/pallas_call | solution.py:50
  125.7 0.7 collective-permute-start.8
  126.4 3.4 %copy-done.1 = f32[8,1024,256]{2,1,0:T(8,128)S(1)} copy-done((f32[8,1024,256]{2,1,0:T(8,128)S(1)}, f32[8,1024,256]{2,1,0:T(8,128)}, u32[]{:S(2)}) %copy-start.1) | copy-done | bytes 8388632
  129.8 1.2 copy-done.3
  131.0 16.3 %attend_middle.1.state_ref = f32[8,1024,256]{2,1,0:T(8,128)S(1)} custom-call(bf16[64,16384]{1,0:T(8,128)(2,1)} %query_ref.5, bf16[4,2,64,1024]{3,2,1,0:T(8,128)(2,1)S(1)} %bitcast.14, f32[8,1024,256]{2,1,0:T(8,128)S(1)} %copy-done.1), custom_call_target="tpu_custom_call" | custom-call | flops 1073741824 | bytes 4194304 | tf_op jit(solution)/shard_map/attend_middle/pallas_call | solution.py:281
  147.3 0.0 collective-permute-done.8.blocks_ref
  147.3 17.3 %attend_last.1 = bf16[64,16384]{1,0:T(8,128)(2,1)} custom-call(bf16[64,16384]{1,0:T(8,128)(2,1)} %query_ref.5, bf16[4,2,64,1024]{3,2,1,0:T(8,128)(2,1)S(1)} %collective-permute-done.8.blocks_ref, f32[8,1024,256]{2,1,0:T(8,128)S(1)} %attend_middle.1.state_ref), custom_call_target="tpu_custom_call" | custom-call | flops 1073741824 | bytes 4194304 | tf_op jit(solution)/shard_map/attend_last/pallas_call | solution.py:281
  (14 shorter events, 0.0 us)
Async XLA Ops:
  9.1 11.1 %collective-permute-start.5 = (bf16[2,64,1024]{2,1,0:T(8,128)(2,1)}, bf16[2,64,1024]{2,1,0:T(8,128)(2,1)S(1)}, u32[]{:S(2)}, u32[]{:S(2)}) collective-permute-start(bf16[2,64,1024]{2,1,0:T(8,128)(2,1)} %pack.1), channel_id=1, source_target_pairs={{0,12},{1,13},{2,14},{3,15},{16,28},{17,29},{18,30},{19,31}} | collective-permute-start | bytes 786440 | tf_op jit(solution)/shard_map/ppermute | solution.py:64
  10.4 13.0 %collective-permute-start.4 = (bf16[2,64,1024]{2,1,0:T(8,128)(2,1)}, bf16[2,64,1024]{2,1,0:T(8,128)(2,1)S(1)}, u32[]{:S(2)}, u32[]{:S(2)}) collective-permute-start(bf16[2,64,1024]{2,1,0:T(8,128)(2,1)} %pack.1), channel_id=1, source_target_pairs={{0,2},{1,3},{4,6},{5,7},{8,10},{9,11},{12,14},{13,15},{16,18},{17,... | collective-permute-start | bytes 786440 | tf_op jit(solution)/shard_map/ppermute | solution.py:75
  13.5 13.4 %collective-permute-start.2 = (bf16[2,64,1024]{2,1,0:T(8,128)(2,1)}, bf16[2,64,1024]{2,1,0:T(8,128)(2,1)S(1)}, u32[]{:S(2)}, u32[]{:S(2)}) collective-permute-start(bf16[2,64,1024]{2,1,0:T(8,128)(2,1)} %pack.1), channel_id=1, source_target_pairs={{0,4},{1,5},{2,6},{3,7},{4,8},{5,9},{6,10},{7,11},{8,12},{9,13},{1... | collective-permute-start | bytes 786440 | tf_op jit(solution)/shard_map/ppermute | solution.py:64
  14.8 23.2 %collective-permute-start = (bf16[2,64,1024]{2,1,0:T(8,128)(2,1)}, bf16[2,64,1024]{2,1,0:T(8,128)(2,1)S(1)}, u32[]{:S(2)}, u32[]{:S(2)}) collective-permute-start(bf16[2,64,1024]{2,1,0:T(8,128)(2,1)} %pack.1), channel_id=1, source_target_pairs={{0,8},{1,9},{2,10},{3,11},{4,12},{5,13},{6,14},{7,15},{16,24},{17,... | collective-permute-start | bytes 786440 | tf_op jit(solution)/shard_map/ppermute | solution.py:64
  20.2 17.9 %copy-start.6 = (bf16[2,64,1024]{2,1,0:T(8,128)(2,1)}, bf16[2,64,1024]{2,1,0:T(8,128)(2,1)S(1)}, u32[]{:S(2)}) copy-start(bf16[2,64,1024]{2,1,0:T(8,128)(2,1)S(1)} %collective-permute-done.5) | copy-start | bytes 786436
  20.2 17.9 %collective-permute-start.6 = (bf16[2,64,1024]{2,1,0:T(8,128)(2,1)S(1)}, bf16[2,64,1024]{2,1,0:T(8,128)(2,1)S(1)}, u32[]{:S(2)}, u32[]{:S(2)}) collective-permute-start(bf16[2,64,1024]{2,1,0:T(8,128)(2,1)S(1)} %collective-permute-done.5), channel_id=1, source_target_pairs={{12,14},{13,15},{14,12},{15,13},{28,30},{29,31},{30,28},{31,29}} | collective-permute-start | bytes 786440 | tf_op jit(solution)/shard_map/ppermute | solution.py:75
  23.4 14.7 %copy-start.7 = (bf16[2,64,1024]{2,1,0:T(8,128)(2,1)}, bf16[2,64,1024]{2,1,0:T(8,128)(2,1)S(1)}, u32[]{:S(2)}) copy-start(bf16[2,64,1024]{2,1,0:T(8,128)(2,1)S(1)} %collective-permute-done.4) | copy-start | bytes 786436
  26.9 61.8 %copy-start.4 = (bf16[2,64,1024]{2,1,0:T(8,128)(2,1)}, bf16[2,64,1024]{2,1,0:T(8,128)(2,1)S(1)}, u32[]{:S(2)}) copy-start(bf16[2,64,1024]{2,1,0:T(8,128)(2,1)S(1)} %collective-permute-done.2) | copy-start | bytes 786436
  38.0 50.7 %copy-start.5 = (bf16[2,64,1024]{2,1,0:T(8,128)(2,1)}, bf16[2,64,1024]{2,1,0:T(8,128)(2,1)S(1)}, u32[]{:S(2)}) copy-start(bf16[2,64,1024]{2,1,0:T(8,128)(2,1)S(1)} %collective-permute-done) | copy-start | bytes 786436
  38.1 0.7 copy-start.9
  71.7 5.8 %collective-permute-start.7 = (bf16[4,2,64,1024]{3,2,1,0:T(8,128)(2,1)}, bf16[4,2,64,1024]{3,2,1,0:T(8,128)(2,1)S(1)}, u32[]{:S(2)}, u32[]{:S(2)}) collective-permute-start(bf16[4,2,64,1024]{3,2,1,0:T(8,128)(2,1)} %bitcast.10), channel_id=1, source_target_pairs={{0,1},{1,0},{2,3},{3,2},{4,5},{5,4},{6,7},{7,6},{8,9},{9,8},{10,11... | collective-permute-start | bytes 3145736 | tf_op jit(solution)/shard_map/ppermute | solution.py:81
  72.3 19.7 %collective-permute-start.3 = (bf16[2,64,1024]{2,1,0:T(8,128)(2,1)S(1)}, bf16[2,64,1024]{2,1,0:T(8,128)(2,1)S(1)}, u32[]{:S(2)}, u32[]{:S(2)}) collective-permute-start(bf16[2,64,1024]{2,1,0:T(8,128)(2,1)S(1)} %collective-permute-done.2), channel_id=1, source_target_pairs={{4,6},{5,7},{6,4},{7,5},{8,10},{9,11},{10,8},{11,9},{12,14},{13,15... | collective-permute-start | bytes 786440 | tf_op jit(solution)/shard_map/ppermute | solution.py:75
  75.4 16.6 %collective-permute-start.1 = (bf16[2,64,1024]{2,1,0:T(8,128)(2,1)S(1)}, bf16[2,64,1024]{2,1,0:T(8,128)(2,1)S(1)}, u32[]{:S(2)}, u32[]{:S(2)}) collective-permute-start(bf16[2,64,1024]{2,1,0:T(8,128)(2,1)S(1)} %collective-permute-done), channel_id=1, source_target_pairs={{8,10},{9,11},{10,8},{11,9},{12,14},{13,15},{14,12},{15,13},{24,26... | collective-permute-start | bytes 786440 | tf_op jit(solution)/shard_map/ppermute | solution.py:75
  77.6 1.2 copy-start.2
  88.8 3.2 %copy-start = (f32[8,1024,256]{2,1,0:T(8,128)}, f32[8,1024,256]{2,1,0:T(8,128)S(1)}, u32[]{:S(2)}) copy-start(f32[8,1024,256]{2,1,0:T(8,128)S(1)} %attend_first.1.state_ref) | copy-start | bytes 25165828
  92.0 0.7 copy-start.8
  92.0 0.8 copy-start.10
  125.7 21.6 %collective-permute-start.8 = (bf16[4,2,64,1024]{3,2,1,0:T(8,128)(2,1)}, bf16[4,2,64,1024]{3,2,1,0:T(8,128)(2,1)S(1)}, u32[]{:S(2)}, u32[]{:S(2)}) collective-permute-start(bf16[4,2,64,1024]{3,2,1,0:T(8,128)(2,1)} %bitcast.13), channel_id=1, source_target_pairs={{0,1},{1,0},{2,3},{3,2},{4,5},{5,4},{6,7},{7,6},{8,9},{9,8},{10,11... | collective-permute-start | bytes 3145736 | tf_op jit(solution)/shard_map/ppermute | solution.py:81
  126.4 3.4 %copy-start.1 = (f32[8,1024,256]{2,1,0:T(8,128)S(1)}, f32[8,1024,256]{2,1,0:T(8,128)}, u32[]{:S(2)}) copy-start(f32[8,1024,256]{2,1,0:T(8,128)} %copy-done) | copy-start | bytes 25165828
  129.8 1.2 copy-start.3

commit v3 on v0

v3 whole, which is shorter than its diff:
```python
import functools
import math

import jax
import jax.numpy as jnp
from jax import lax
from jax.experimental import pallas as pl
from jax.experimental.pallas import tpu as pltpu
from jax.sharding import PartitionSpec as P

HEADS = 128
KV_HEADS = 8
GROUP = HEADS // KV_HEADS
PARTS = 4

masked_score = -1e30


def chip_grid(devices):
    if devices % 2:
        return devices, 1, 1
    chips = devices // 2
    if chips % 2 or chips > 8:
        return chips, 1, 2
    return chips // 2, 2, 2


def place(grid):
    depth, width, cores = grid
    me = lax.axis_index("tp")
    return me // (width * cores), (me // cores) % width, me % cores


def stack(arrays, name):
    def kernel(*refs):
        for at, ref in enumerate(refs[:-1]):
            refs[-1][at] = ref[...]

    count = len(arrays)
    return pl.pallas_call(
        kernel,
        out_shape=jax.ShapeDtypeStruct((count, *arrays[0].shape), arrays[0].dtype),
        in_specs=[pl.BlockSpec(memory_space=pltpu.VMEM)] * count,
        out_specs=pl.BlockSpec(memory_space=pltpu.VMEM),
        compiler_params=pltpu.CompilerParams(vmem_limit_bytes=32 * 2**20),
        name=name,
    )(*arrays)


def z_forward(block, grid, dz):
    depth, width, cores = grid
    side = width * cores
    pairs = [(at - side, at) for at in range(dz * side, depth * side)]
    return lax.ppermute(block, "tp", pairs)


def y_swap(block, grid, dz):
    depth, width, cores = grid
    pairs = []
    for at in range(dz * width * cores, depth * width * cores):
        y = (at // cores) % width
        other = at + (1 - 2 * y) * cores
        if dz or other > at:
            pairs.append((at, other))
    return lax.ppermute(block, "tp", pairs)


def core_swap(blocks, grid, dz):
    depth, width, cores = grid
    pairs = [(at, at ^ 1) for at in range(dz * width * cores, depth * width * cores)]
    return lax.ppermute(blocks, "tp", pairs)


def keys_of(blocks):
    count, _, tok, dim = blocks.shape
    return blocks[:, 0].reshape(count * tok, dim), blocks[:, 1].reshape(count * tok, dim)


def attend_kernel(grid, groups, query_ref, *refs):
    depth, width, cores = grid
    out_ref, bias_ref = refs[-2:]
    blocks_refs = refs[:-2]
    tok = query_ref.shape[0]
    dim = blocks_refs[0].shape[-1]
    rows = GROUP * tok
    factor = dim ** (-0.5) * math.log2(math.e)
    zz, yy, cc = place(grid)

    pieces, origin = [], []
    for (below, own_ref, core_ref) in zip(groups, blocks_refs[::2], blocks_refs[1::2]):
        for dc, ref in ((0, own_ref), (1, core_ref)):
            for at, dz in enumerate(below):
                pieces.append((dz, dc, below[:at].count(dz), ref, at))
    pieces.sort(key=lambda piece: piece[:3])
    near = width * cores * tok

    @pl.when(pl.program_id(0) == 0)
    def _():
        row = lax.broadcasted_iota(jnp.int32, (tok, tok), 0)
        key = lax.broadcasted_iota(jnp.int32, (tok, tok), 1)
        for at, (dz, dc, dy, _, _) in enumerate(pieces):
            if dz:
                limit = jnp.where(zz >= dz, 0, tok) + 0 * key
            elif dy:
                limit = jnp.where(yy == 1, 0, tok) + 0 * key
            elif dc:
                limit = jnp.where(cc == 1, 0, tok) + 0 * key
            else:
                limit = key
            bias_ref[:, at * tok : (at + 1) * tok] = jnp.where(limit <= row, 0.0, masked_score)

    def attend(bias):
        query = jnp.concatenate(
            [query_ref[:, q * dim : (q + 1) * dim] for q in range(GROUP)], axis=0
        )
        keys = jnp.concatenate([ref[at, 0] for _, _, _, ref, at in pieces], axis=0)
        values = jnp.concatenate([ref[at, 1] for _, _, _, ref, at in pieces], axis=0)
        ones = jnp.where(lax.broadcasted_iota(jnp.int32, values.shape, 1) == 0, 1.0, 0.0)
        values = jnp.concatenate([values, ones.astype(values.dtype)], axis=1)
        part_rows = rows // PARTS
        heads = part_rows // tok
        for part in range(PARTS):
            scores = lax.dot_general(
                query[part * part_rows : (part + 1) * part_rows],
                keys,
                (((1,), (1,)), ((), ())),
                preferred_element_type=jnp.float32,
            )
            span = bias.shape[1]
            first = scores[:, :span].reshape(heads, tok, span) + bias[None]
            first = first.reshape(part_rows, span)
            if span < scores.shape[1]:
                first = jnp.concatenate([first, scores[:, span:]], axis=1)
            scores = first
            top = jnp.max(scores, axis=1, keepdims=True)
            weights = jnp.exp2((scores - top) * factor).astype(jnp.bfloat16)
            sums = jnp.dot(weights, values, preferred_element_type=jnp.float32)
            done = (sums[:, :dim] / sums[:, dim : dim + 1]).astype(out_ref.dtype)
            for head in range(heads):
                at = (part * heads + head) * dim
                out_ref[:, at : at + dim] = done[head * tok : (head + 1) * tok]

    @pl.when(zz == depth - 1)
    def _():
        attend(bias_ref[:, :near])

    @pl.when(zz < depth - 1)
    def _():
        attend(bias_ref[...])


def solution(mesh):
    grid = chip_grid(mesh.shape["tp"])
    depth, width, cores = grid
    assert cores == 2 and depth > 2

    def body(query_rows, key_rows, value_rows):
        tok, columns = query_rows.shape
        dim = key_rows.shape[1] // KV_HEADS
        query_rows, key_rows, value_rows = (
            pltpu.with_memory_space_constraint(array, pltpu.HBM)
            for array in (query_rows, key_rows, value_rows)
        )
        block = stack([key_rows, value_rows], "pack")

        def with_swap(block, dz):
            return [block, y_swap(block, grid, dz)] if width == 2 else [block]

        rows_of = []
        for dz in range(depth):
            rows_of.append(with_swap(block, dz))
            if dz + 1 < depth:
                block = z_forward(block, grid, dz + 1)
                block, rows_of[dz] = lax.optimization_barrier((block, rows_of[dz]))

        spans = [range(0, 2), range(2, depth - 1), range(depth - 1, depth)]
        groups, operands = [], []
        for span in spans:
            blocks = [block for dz in span for block in rows_of[dz]]
            if not blocks:
                continue
            groups.append([dz for dz in span for _ in rows_of[dz]])
            merged = stack(blocks, "merge")
            operands += [merged, core_swap(merged, grid, span[0])]

        query_spec = pl.BlockSpec((tok, columns // KV_HEADS), lambda head: (0, head))
        keys = tok * depth * width * cores
        return pl.pallas_call(
            functools.partial(attend_kernel, grid, groups),
            out_shape=query_rows,
            grid=(KV_HEADS,),
            in_specs=[query_spec]
            + [
                pl.BlockSpec((operand.shape[0], 2, tok, dim), lambda head: (0, 0, 0, head))
                for operand in operands
            ],
            out_specs=query_spec,
            scratch_shapes=[pltpu.VMEM((tok, keys), jnp.float32)],
            compiler_params=pltpu.CompilerParams(vmem_limit_bytes=32 * 2**20),
            cost_estimate=pl.CostEstimate(
                flops=4 * HEADS * tok * keys * dim,
                bytes_accessed=4 * HEADS * tok * dim,
                transcendentals=HEADS * tok * keys,
            ),
            name="attend",
        )(query_rows, *operands)

    spec = P(("groups", "tp"), None)
    return jax.shard_map(
        body, mesh=mesh, in_specs=(spec, spec, spec), out_specs=spec, check_vma=False
    )
```

time: 161 us -> 66.6 us (0.41)
  waiting for transfers between devices: 79.4 us -> 18.1 us
  matrix products: 29.8 us -> 0 us
  starting transfers between devices: 0.04 us -> 29.7 us
  local copies, waits for them, and re-layouts: 18.6 us -> 0 us
  Pallas kernels: 0 us -> 18.3 us
  other arithmetic: 18.2 us -> 0 us
  between operations: 13.5 us -> 0.12 us
    all_gather x2 -> x0, waiting for transfers between devices: 78 us -> none  [the longest x1 39.6 us: cycle_attend(): key_piece = lax.all_gather(key_rows, 'tp', axis=0, tiled=True)]
    dot_general x4 -> x0, matrix products: 29.8 us -> none  [the longest x2 22.5 us: compute(): jnp.einsum('tgqn,ngd->tgqd', weights.astype(jnp.bfloat16), value_block, p...]
    ppermute x0 -> x10, starting transfers between devices: none -> 29.7 us  [the longest x3 15.5 us: core_swap(): return lax.ppermute(blocks, 'tp', pairs)]
    pallas_call x0 -> x5, Pallas kernels: none -> 18.3 us  [the longest x1 17.2 us: body(): pl.pallas_call(functools.partial(attend_kernel, grid, groups), out_shape=...]
    ppermute x0 -> x10, waiting for transfers between devices: none -> 18.1 us  [the longest x3 8.35 us: z_forward(): return lax.ppermute(block, 'tp', pairs)]
    convert_element_type x3 -> x0, other arithmetic: 16.7 us -> none  [the longest x2 13.9 us: compute(): weights.astype(jnp.bfloat16)]
    unnamed x7 -> x0, local copies, waits for them, and re-layouts: 14.1 us -> none
    broadcast_in_dim x3 -> x0, local copies, waits for them, and re-layouts: 2.33 us -> none  [the longest x1 2.32 us: cycle_attend(): jnp.zeros((tok_rows, KV_HEADS, group, head_dim), jnp.float32)]
  transfers between devices with their start and end apart: 2 -> 10, of which waited for: 2 -> 6; matrix products, arithmetic and copies ran while one was open for 5% -> 0% of each run, Pallas kernels for 0% -> 0%
where the time goes in v3:
time: 66.6 us; the launch traced here: 66.2 us
  starting transfers between devices  29.7 us (45%)
  Pallas kernels  18.3 us (27%)
  waiting for transfers between devices  18.1 us (27%)
    pallas_call x1, Pallas kernels, body(): pl.pallas_call(functools.partial(attend_kernel, grid, groups), out_shape=...  17.2 us
    ppermute x3, starting transfers between devices, core_swap(): return lax.ppermute(blocks, 'tp', pairs)  15.5 us
    ppermute x4, starting transfers between devices, y_swap(): return lax.ppermute(block, 'tp', pairs)  10.3 us
    ppermute x3, waiting for transfers between devices, z_forward(): return lax.ppermute(block, 'tp', pairs)  8.35 us
    ppermute x4, waiting for transfers between devices, y_swap(): return lax.ppermute(block, 'tp', pairs)  8.24 us
    ppermute x3, starting transfers between devices, z_forward(): return lax.ppermute(block, 'tp', pairs)  3.88 us
    ppermute x3, waiting for transfers between devices, core_swap(): return lax.ppermute(blocks, 'tp', pairs)  1.51 us
  transfers between devices with their start and end apart: 10, of which 6 were waited for; matrix products, arithmetic and copies ran while one was open for 0% of the time, Pallas kernels for 0%

profile of v3, /device:TPU:25, one launch (start us, length us, event | category | flops | bytes accessed | tf_op | source)
XLA Modules:
  0.0 66.2 jit_solution(12642315822162297837)
XLA Ops:
  0.0 1.0 %pack.1.refs_0_ = bf16[2,64,1024]{2,1,0:T(8,128)(2,1)S(1)} custom-call(bf16[64,1024]{1,0:T(8,128)(2,1)} %refs_0_.1, bf16[64,1024]{1,0:T(8,128)(2,1)} %refs_1_.1), custom_call_target="tpu_custom_call" | custom-call | tf_op jit(solution)/shard_map/pack/pallas_call | solution.py:40
  1.0 3.2 %collective-permute-start.1 = (bf16[2,64,1024]{2,1,0:T(8,128)(2,1)S(1)}, bf16[2,64,1024]{2,1,0:T(8,128)(2,1)S(1)}, u32[]{:S(2)}, u32[]{:S(2)}) collective-permute-start(bf16[2,64,1024]{2,1,0:T(8,128)(2,1)S(1)} %pack.1.refs_0_), channel_id=1, source_target_pairs={{0,2},{1,3},{4,6},{5,7},{8,10},{9,11},{12,14},{13,15},{16,18},{17,... | collective-permute-start | bytes 786440 | tf_op jit(solution)/shard_map/ppermute | solution.py:65
  4.2 1.3 %collective-permute-start = (bf16[2,64,1024]{2,1,0:T(8,128)(2,1)S(1)}, bf16[2,64,1024]{2,1,0:T(8,128)(2,1)S(1)}, u32[]{:S(2)}, u32[]{:S(2)}) collective-permute-start(bf16[2,64,1024]{2,1,0:T(8,128)(2,1)S(1)} %pack.1.refs_0_), channel_id=1, source_target_pairs={{0,4},{1,5},{2,6},{3,7},{4,8},{5,9},{6,10},{7,11},{8,12},{9,13},{1... | collective-permute-start | bytes 786440 | tf_op jit(solution)/shard_map/ppermute | solution.py:54
  5.5 3.6 %collective-permute-done.1.refs_1_ = bf16[2,64,1024]{2,1,0:T(8,128)(2,1)S(1)} collective-permute-done((bf16[2,64,1024]{2,1,0:T(8,128)(2,1)S(1)}, bf16[2,64,1024]{2,1,0:T(8,128)(2,1)S(1)}, u32[]{:S(2)}, u32[]{:S(2)}) %collective-permute-start.1) | collective-permute-done | bytes 262176 | tf_op jit(solution)/shard_map/ppermute | solution.py:65
  9.1 3.8 %collective-permute-done.refs_2_ = bf16[2,64,1024]{2,1,0:T(8,128)(2,1)S(1)} collective-permute-done((bf16[2,64,1024]{2,1,0:T(8,128)(2,1)S(1)}, bf16[2,64,1024]{2,1,0:T(8,128)(2,1)S(1)}, u32[]{:S(2)}, u32[]{:S(2)}) %collective-permute-start) | collective-permute-done | bytes 262176 | tf_op jit(solution)/shard_map/ppermute | solution.py:54
  12.9 1.9 %collective-permute-start.3 = (bf16[2,64,1024]{2,1,0:T(8,128)(2,1)S(1)}, bf16[2,64,1024]{2,1,0:T(8,128)(2,1)S(1)}, u32[]{:S(2)}, u32[]{:S(2)}) collective-permute-start(bf16[2,64,1024]{2,1,0:T(8,128)(2,1)S(1)} %collective-permute-done.refs_2_), channel_id=1, source_target_pairs={{4,6},{5,7},{6,4},{7,5},{8,10},{9,11},{10,8},{11,9},{12,14},{13,15... | collective-permute-start | bytes 786440 | tf_op jit(solution)/shard_map/ppermute | solution.py:65
  14.8 1.3 %collective-permute-start.2 = (bf16[2,64,1024]{2,1,0:T(8,128)(2,1)S(1)}, bf16[2,64,1024]{2,1,0:T(8,128)(2,1)S(1)}, u32[]{:S(2)}, u32[]{:S(2)}) collective-permute-start(bf16[2,64,1024]{2,1,0:T(8,128)(2,1)S(1)} %collective-permute-done.refs_2_), channel_id=1, source_target_pairs={{4,8},{5,9},{6,10},{7,11},{8,12},{9,13},{10,14},{11,15},{20,24},{2... | collective-permute-start | bytes 786440 | tf_op jit(solution)/shard_map/ppermute | solution.py:54
  16.1 4.6 %collective-permute-done.3.refs_3_ = bf16[2,64,1024]{2,1,0:T(8,128)(2,1)S(1)} collective-permute-done((bf16[2,64,1024]{2,1,0:T(8,128)(2,1)S(1)}, bf16[2,64,1024]{2,1,0:T(8,128)(2,1)S(1)}, u32[]{:S(2)}, u32[]{:S(2)}) %collective-permute-start.3) | collective-permute-done | bytes 262176 | tf_op jit(solution)/shard_map/ppermute | solution.py:65
  20.7 1.9 %collective-permute-done.2.refs_0_ = bf16[2,64,1024]{2,1,0:T(8,128)(2,1)S(1)} collective-permute-done((bf16[2,64,1024]{2,1,0:T(8,128)(2,1)S(1)}, bf16[2,64,1024]{2,1,0:T(8,128)(2,1)S(1)}, u32[]{:S(2)}, u32[]{:S(2)}) %collective-permute-start.2) | collective-permute-done | bytes 262176 | tf_op jit(solution)/shard_map/ppermute | solution.py:54
  22.7 3.1 %collective-permute-start.6 = (bf16[2,64,1024]{2,1,0:T(8,128)(2,1)S(1)}, bf16[2,64,1024]{2,1,0:T(8,128)(2,1)S(1)}, u32[]{:S(2)}, u32[]{:S(2)}) collective-permute-start(bf16[2,64,1024]{2,1,0:T(8,128)(2,1)S(1)} %collective-permute-done.2.refs_0_), channel_id=1, source_target_pairs={{8,10},{9,11},{10,8},{11,9},{12,14},{13,15},{14,12},{15,13},{24,26... | collective-permute-start | bytes 786440 | tf_op jit(solution)/shard_map/ppermute | solution.py:65
  25.7 1.3 %collective-permute-start.5 = (bf16[2,64,1024]{2,1,0:T(8,128)(2,1)S(1)}, bf16[2,64,1024]{2,1,0:T(8,128)(2,1)S(1)}, u32[]{:S(2)}, u32[]{:S(2)}) collective-permute-start(bf16[2,64,1024]{2,1,0:T(8,128)(2,1)S(1)} %collective-permute-done.2.refs_0_), channel_id=1, source_target_pairs={{8,12},{9,13},{10,14},{11,15},{24,28},{25,29},{26,30},{27,31}} | collective-permute-start | bytes 786440 | tf_op jit(solution)/shard_map/ppermute | solution.py:54
  27.0 0.1 merge.3.refs_0_
  27.1 3.4 %collective-permute-start.4 = (bf16[4,2,64,1024]{3,2,1,0:T(8,128)(2,1)S(1)}, bf16[4,2,64,1024]{3,2,1,0:T(8,128)(2,1)S(1)}, u32[]{:S(2)}, u32[]{:S(2)}) collective-permute-start(bf16[4,2,64,1024]{3,2,1,0:T(8,128)(2,1)S(1)} %merge.3.refs_0_), channel_id=1, source_target_pairs={{0,1},{1,0},{2,3},{3,2},{4,5},{5,4},{6,7},{7,6},{8,9},{9,8},{10,11... | collective-permute-start | bytes 3145736 | tf_op jit(solution)/shard_map/ppermute | solution.py:71
  30.5 0.0 collective-permute-done.6.refs_1_
  30.5 2.6 %collective-permute-done.5.refs_0_ = bf16[2,64,1024]{2,1,0:T(8,128)(2,1)S(1)} collective-permute-done((bf16[2,64,1024]{2,1,0:T(8,128)(2,1)S(1)}, bf16[2,64,1024]{2,1,0:T(8,128)(2,1)S(1)}, u32[]{:S(2)}, u32[]{:S(2)}) %collective-permute-start.5) | collective-permute-done | bytes 262176 | tf_op jit(solution)/shard_map/ppermute | solution.py:54
  33.1 2.2 %collective-permute-start.8 = (bf16[2,64,1024]{2,1,0:T(8,128)(2,1)S(1)}, bf16[2,64,1024]{2,1,0:T(8,128)(2,1)S(1)}, u32[]{:S(2)}, u32[]{:S(2)}) collective-permute-start(bf16[2,64,1024]{2,1,0:T(8,128)(2,1)S(1)} %collective-permute-done.5.refs_0_), channel_id=1, source_target_pairs={{12,14},{13,15},{14,12},{15,13},{28,30},{29,31},{30,28},{31,29}} | collective-permute-start | bytes 786440 | tf_op jit(solution)/shard_map/ppermute | solution.py:65
  35.4 6.1 %collective-permute-start.7 = (bf16[2,2,64,1024]{3,2,1,0:T(8,128)(2,1)S(1)}, bf16[2,2,64,1024]{3,2,1,0:T(8,128)(2,1)S(1)}, u32[]{:S(2)}, u32[]{:S(2)}) collective-permute-start(bf16[2,2,64,1024]{3,2,1,0:T(8,128)(2,1)S(1)} %merge.4.refs_2_), channel_id=1, source_target_pairs={{8,9},{9,8},{10,11},{11,10},{12,13},{13,12},{14,15},{15,14},{24,25... | collective-permute-start | bytes 1572872 | tf_op jit(solution)/shard_map/ppermute | solution.py:71
  41.5 0.0 collective-permute-done.8.refs_1_
  41.6 6.0 %collective-permute-start.9 = (bf16[2,2,64,1024]{3,2,1,0:T(8,128)(2,1)S(1)}, bf16[2,2,64,1024]{3,2,1,0:T(8,128)(2,1)S(1)}, u32[]{:S(2)}, u32[]{:S(2)}) collective-permute-start(bf16[2,2,64,1024]{3,2,1,0:T(8,128)(2,1)S(1)} %merge.5.refs_4_), channel_id=1, source_target_pairs={{12,13},{13,12},{14,15},{15,14},{28,29},{29,28},{30,31},{31,30}} | collective-permute-start | bytes 1572872 | tf_op jit(solution)/shard_map/ppermute | solution.py:71
  47.6 0.0 collective-permute-done.7.refs_3_
  47.6 1.5 %collective-permute-done.9.refs_5_ = bf16[2,2,64,1024]{3,2,1,0:T(8,128)(2,1)S(1)} collective-permute-done((bf16[2,2,64,1024]{3,2,1,0:T(8,128)(2,1)S(1)}, bf16[2,2,64,1024]{3,2,1,0:T(8,128)(2,1)S(1)}, u32[]{:S(2)}, u32[]{:S(2)}) %collective-permute-start.9) | collective-permute-done | bytes 524320 | tf_op jit(solution)/shard_map/ppermute | solution.py:71
  49.1 0.0 collective-permute-done.4.refs_1_
  49.1 17.2 %attend.1 = bf16[64,16384]{1,0:T(8,128)(2,1)} custom-call(bf16[64,16384]{1,0:T(8,128)(2,1)} %query_ref.1, bf16[4,2,64,1024]{3,2,1,0:T(8,128)(2,1)S(1)} %merge.3.refs_0_, bf16[4,2,64,1024]{3,2,1,0:T(8,128)(2,1)S(1)} %collective-permute-done.4.refs_1_, bf16[2,2,64,1024]{3,2,1,0:T(8,128)(2,1)S(1)} %merge.4.refs_2_, ...), custom_call_target="tpu_custom_call" | custom-call | flops 4294967296 | bytes 4194304 | tf_op jit(solution)/shard_map/attend/pallas_call | solution.py:188
  (2 shorter events, 0.1 us)
Async XLA Ops:
  1.0 8.1 %collective-permute-start.1 = (bf16[2,64,1024]{2,1,0:T(8,128)(2,1)S(1)}, bf16[2,64,1024]{2,1,0:T(8,128)(2,1)S(1)}, u32[]{:S(2)}, u32[]{:S(2)}) collective-permute-start(bf16[2,64,1024]{2,1,0:T(8,128)(2,1)S(1)} %pack.1.refs_0_), channel_id=1, source_target_pairs={{0,2},{1,3},{4,6},{5,7},{8,10},{9,11},{12,14},{13,15},{16,18},{17,... | collective-permute-start | bytes 786440 | tf_op jit(solution)/shard_map/ppermute | solution.py:65
  4.2 8.8 %collective-permute-start = (bf16[2,64,1024]{2,1,0:T(8,128)(2,1)S(1)}, bf16[2,64,1024]{2,1,0:T(8,128)(2,1)S(1)}, u32[]{:S(2)}, u32[]{:S(2)}) collective-permute-start(bf16[2,64,1024]{2,1,0:T(8,128)(2,1)S(1)} %pack.1.refs_0_), channel_id=1, source_target_pairs={{0,4},{1,5},{2,6},{3,7},{4,8},{5,9},{6,10},{7,11},{8,12},{9,13},{1... | collective-permute-start | bytes 786440 | tf_op jit(solution)/shard_map/ppermute | solution.py:54
  12.9 7.8 %collective-permute-start.3 = (bf16[2,64,1024]{2,1,0:T(8,128)(2,1)S(1)}, bf16[2,64,1024]{2,1,0:T(8,128)(2,1)S(1)}, u32[]{:S(2)}, u32[]{:S(2)}) collective-permute-start(bf16[2,64,1024]{2,1,0:T(8,128)(2,1)S(1)} %collective-permute-done.refs_2_), channel_id=1, source_target_pairs={{4,6},{5,7},{6,4},{7,5},{8,10},{9,11},{10,8},{11,9},{12,14},{13,15... | collective-permute-start | bytes 786440 | tf_op jit(solution)/shard_map/ppermute | solution.py:65
  14.8 7.8 %collective-permute-start.2 = (bf16[2,64,1024]{2,1,0:T(8,128)(2,1)S(1)}, bf16[2,64,1024]{2,1,0:T(8,128)(2,1)S(1)}, u32[]{:S(2)}, u32[]{:S(2)}) collective-permute-start(bf16[2,64,1024]{2,1,0:T(8,128)(2,1)S(1)} %collective-permute-done.refs_2_), channel_id=1, source_target_pairs={{4,8},{5,9},{6,10},{7,11},{8,12},{9,13},{10,14},{11,15},{20,24},{2... | collective-permute-start | bytes 786440 | tf_op jit(solution)/shard_map/ppermute | solution.py:54
  22.7 7.9 %collective-permute-start.6 = (bf16[2,64,1024]{2,1,0:T(8,128)(2,1)S(1)}, bf16[2,64,1024]{2,1,0:T(8,128)(2,1)S(1)}, u32[]{:S(2)}, u32[]{:S(2)}) collective-permute-start(bf16[2,64,1024]{2,1,0:T(8,128)(2,1)S(1)} %collective-permute-done.2.refs_0_), channel_id=1, source_target_pairs={{8,10},{9,11},{10,8},{11,9},{12,14},{13,15},{14,12},{15,13},{24,26... | collective-permute-start | bytes 786440 | tf_op jit(solution)/shard_map/ppermute | solution.py:65
  25.7 7.4 %collective-permute-start.5 = (bf16[2,64,1024]{2,1,0:T(8,128)(2,1)S(1)}, bf16[2,64,1024]{2,1,0:T(8,128)(2,1)S(1)}, u32[]{:S(2)}, u32[]{:S(2)}) collective-permute-start(bf16[2,64,1024]{2,1,0:T(8,128)(2,1)S(1)} %collective-permute-done.2.refs_0_), channel_id=1, source_target_pairs={{8,12},{9,13},{10,14},{11,15},{24,28},{25,29},{26,30},{27,31}} | collective-permute-start | bytes 786440 | tf_op jit(solution)/shard_map/ppermute | solution.py:54
  27.1 22.0 %collective-permute-start.4 = (bf16[4,2,64,1024]{3,2,1,0:T(8,128)(2,1)S(1)}, bf16[4,2,64,1024]{3,2,1,0:T(8,128)(2,1)S(1)}, u32[]{:S(2)}, u32[]{:S(2)}) collective-permute-start(bf16[4,2,64,1024]{3,2,1,0:T(8,128)(2,1)S(1)} %merge.3.refs_0_), channel_id=1, source_target_pairs={{0,1},{1,0},{2,3},{3,2},{4,5},{5,4},{6,7},{7,6},{8,9},{9,8},{10,11... | collective-permute-start | bytes 3145736 | tf_op jit(solution)/shard_map/ppermute | solution.py:71
  33.1 8.4 %collective-permute-start.8 = (bf16[2,64,1024]{2,1,0:T(8,128)(2,1)S(1)}, bf16[2,64,1024]{2,1,0:T(8,128)(2,1)S(1)}, u32[]{:S(2)}, u32[]{:S(2)}) collective-permute-start(bf16[2,64,1024]{2,1,0:T(8,128)(2,1)S(1)} %collective-permute-done.5.refs_0_), channel_id=1, source_target_pairs={{12,14},{13,15},{14,12},{15,13},{28,30},{29,31},{30,28},{31,29}} | collective-permute-start | bytes 786440 | tf_op jit(solution)/shard_map/ppermute | solution.py:65
  35.4 12.2 %collective-permute-start.7 = (bf16[2,2,64,1024]{3,2,1,0:T(8,128)(2,1)S(1)}, bf16[2,2,64,1024]{3,2,1,0:T(8,128)(2,1)S(1)}, u32[]{:S(2)}, u32[]{:S(2)}) collective-permute-start(bf16[2,2,64,1024]{3,2,1,0:T(8,128)(2,1)S(1)} %merge.4.refs_2_), channel_id=1, source_target_pairs={{8,9},{9,8},{10,11},{11,10},{12,13},{13,12},{14,15},{15,14},{24,25... | collective-permute-start | bytes 1572872 | tf_op jit(solution)/shard_map/ppermute | solution.py:71
  41.6 7.5 %collective-permute-start.9 = (bf16[2,2,64,1024]{3,2,1,0:T(8,128)(2,1)S(1)}, bf16[2,2,64,1024]{3,2,1,0:T(8,128)(2,1)S(1)}, u32[]{:S(2)}, u32[]{:S(2)}) collective-permute-start(bf16[2,2,64,1024]{3,2,1,0:T(8,128)(2,1)S(1)} %merge.5.refs_4_), channel_id=1, source_target_pairs={{12,13},{13,12},{14,15},{15,14},{28,29},{29,28},{30,31},{31,30}} | collective-permute-start | bytes 1572872 | tf_op jit(solution)/shard_map/ppermute | solution.py:71

commit v4 on v3

--- a/solution.py
+++ b/solution.py
@@ -12,6 +12,7 @@
 KV_HEADS = 8
 GROUP = HEADS // KV_HEADS
 PARTS = 4
+CHUNKS = 2
 
 masked_score = -1e30
 
@@ -47,28 +48,43 @@
     )(*arrays)
 
 
-def z_forward(block, grid, dz):
-    depth, width, cores = grid
-    side = width * cores
-    pairs = [(at - side, at) for at in range(dz * side, depth * side)]
-    return lax.ppermute(block, "tp", pairs)
-
-
-def y_swap(block, grid, dz):
-    depth, width, cores = grid
-    pairs = []
-    for at in range(dz * width * cores, depth * width * cores):
-        y = (at // cores) % width
-        other = at + (1 - 2 * y) * cores
-        if dz or other > at:
-            pairs.append((at, other))
-    return lax.ppermute(block, "tp", pairs)
-
-
-def core_swap(blocks, grid, dz):
-    depth, width, cores = grid
-    pairs = [(at, at ^ 1) for at in range(dz * width * cores, depth * width * cores)]
-    return lax.ppermute(blocks, "tp", pairs)
+def pack(key_rows, value_rows, chunks):
+    tok, columns = key_rows.shape
+    columns //= chunks
+
+    def kernel(key_ref, value_ref, *out_refs):
+        for chunk, out_ref in enumerate(out_refs):
+            span = slice(chunk * columns, (chunk + 1) * columns)
+            out_ref[0] = key_ref[:, span]
+            out_ref[1] = value_ref[:, span]
+
+    return pl.pallas_call(
+        kernel,
+        out_shape=[jax.ShapeDtypeStruct((2, tok, columns), key_rows.dtype)] * chunks,
+        in_specs=[pl.BlockSpec(memory_space=pltpu.VMEM)] * 2,
+        out_specs=[pl.BlockSpec(memory_space=pltpu.VMEM)] * chunks,
+        name="pack",
+    )(key_rows, value_rows)
+
+
+def z_forward(block, grid):
+    depth, width, cores = grid
+    count = depth * width * cores
+    return lax.ppermute(
+        block, "tp", [(at, (at + width * cores) % count) for at in range(count)]
+    )
+
+
+def y_swap(block, grid):
+    depth, width, cores = grid
+    return lax.ppermute(
+        block, "tp", [(at, at ^ cores) for at in range(depth * width * cores)]
+    )
+
+
+def core_swap(blocks, grid):
+    depth, width, cores = grid
+    return lax.ppermute(blocks, "tp", [(at, at ^ 1) for at in range(depth * width * cores)])
 
 
 def keys_of(blocks):
@@ -79,7 +95,7 @@
 def attend_kernel(grid, groups, query_ref, *refs):
     depth, width, cores = grid
     out_ref, bias_ref = refs[-2:]
-    blocks_refs = refs[:-2]
+    blocks_refs = refs[: 2 * len(groups)]
     tok = query_ref.shape[0]
     dim = blocks_refs[0].shape[-1]
     rows = GROUP * tok
@@ -119,14 +135,21 @@
         values = jnp.concatenate([values, ones.astype(values.dtype)], axis=1)
         part_rows = rows // PARTS
         heads = part_rows // tok
-        for part in range(PARTS):
-            scores = lax.dot_general(
+        span = bias.shape[1]
+
+        def scores_of(part):
+            return lax.dot_general(
                 query[part * part_rows : (part + 1) * part_rows],
                 keys,
                 (((1,), (1,)), ((), ())),
                 preferred_element_type=jnp.float32,
             )
-            span = bias.shape[1]
+
+        following = scores_of(0)
+        for part in range(PARTS):
+            scores = following
+            if part + 1 < PARTS:
+                following = scores_of(part + 1)
             first = scores[:, :span].reshape(heads, tok, span) + bias[None]
             first = first.reshape(part_rows, span)
             if span < scores.shape[1]:
@@ -161,49 +184,53 @@
             pltpu.with_memory_space_constraint(array, pltpu.HBM)
             for array in (query_rows, key_rows, value_rows)
         )
-        block = stack([key_rows, value_rows], "pack")
-
-        def with_swap(block, dz):
-            return [block, y_swap(block, grid, dz)] if width == 2 else [block]
-
-        rows_of = []
+        blocks = list(pack(key_rows, value_rows, CHUNKS))
+        rows_of = [[] for _ in range(CHUNKS)]
         for dz in range(depth):
-            rows_of.append(with_swap(block, dz))
-            if dz + 1 < depth:
-                block = z_forward(block, grid, dz + 1)
-                block, rows_of[dz] = lax.optimization_barrier((block, rows_of[dz]))
+            for chunk in range(CHUNKS):
+                block = blocks[chunk]
+                row = [block, y_swap(block, grid)] if width == 2 else [block]
+                if dz + 1 < depth:
+                    following = z_forward(block, grid)
+                    blocks[chunk], row = lax.optimization_barrier((following, row))
+                rows_of[chunk].append(row)
 
         spans = [range(0, 2), range(2, depth - 1), range(depth - 1, depth)]
-        groups, operands = [], []
-        for span in spans:
-            blocks = [block for dz in span for block in rows_of[dz]]
-            if not blocks:
-                continue
-            groups.append([dz for dz in span for _ in rows_of[dz]])
-            merged = stack(blocks, "merge")
-            operands += [merged, core_swap(merged, grid, span[0])]
-
-        query_spec = pl.BlockSpec((tok, columns // KV_HEADS), lambda head: (0, head))
+        spans = [span for span in spans if len(span)]
+        groups = [[dz for dz in span for _ in range(width)] for span in spans]
         keys = tok * depth * width * cores
-        return pl.pallas_call(
-            functools.partial(attend_kernel, grid, groups),
-            out_shape=query_rows,
-            grid=(KV_HEADS,),
-            in_specs=[query_spec]
-            + [
-                pl.BlockSpec((operand.shape[0], 2, tok, dim), lambda head: (0, 0, 0, head))
-                for operand in operands
-            ],
-            out_specs=query_spec,
-            scratch_shapes=[pltpu.VMEM((tok, keys), jnp.float32)],
-            compiler_params=pltpu.CompilerParams(vmem_limit_bytes=32 * 2**20),
-            cost_estimate=pl.CostEstimate(
-                flops=4 * HEADS * tok * keys * dim,
-                bytes_accessed=4 * HEADS * tok * dim,
-                transcendentals=HEADS * tok * keys,
-            ),
-            name="attend",
-        )(query_rows, *operands)
+        heads = KV_HEADS // CHUNKS
+        result = None
+        for chunk in range(CHUNKS):
+            operands = []
+            for span in spans:
+                merged = stack([block for dz in span for block in rows_of[chunk][dz]], "merge")
+                operands += [merged, core_swap(merged, grid)]
+            query_spec = pl.BlockSpec(
+                (tok, columns // KV_HEADS), lambda head, chunk=chunk: (0, chunk * heads + head)
+            )
+            result = pl.pallas_call(
+                functools.partial(attend_kernel, grid, groups),
+                out_shape=query_rows,
+                grid=(heads,),
+                in_specs=[query_spec]
+                + [
+                    pl.BlockSpec((operand.shape[0], 2, tok, dim), lambda head: (0, 0, 0, head))
+                    for operand in operands
+                ]
+                + [pl.BlockSpec(memory_space=pl.ANY)] * (chunk > 0),
+                out_specs=query_spec,
+                scratch_shapes=[pltpu.VMEM((tok, keys), jnp.float32)],
+                input_output_aliases={1 + len(operands): 0} if chunk else {},
+                compiler_params=pltpu.CompilerParams(vmem_limit_bytes=32 * 2**20),
+                cost_estimate=pl.CostEstimate(
+                    flops=4 * HEADS * tok * keys * dim // CHUNKS,
+                    bytes_accessed=4 * HEADS * tok * dim // CHUNKS,
+                    transcendentals=HEADS * tok * keys // CHUNKS,
+                ),
+                name="attend",
+            )(query_rows, *operands, *([result] if chunk else []))
+        return result
 
     spec = P(("groups", "tp"), None)
     return jax.shard_map(

time: 66.6 us -> 60.8 us (0.913)
  the two profiles are of different devices: /device:TPU:25 before, /device:TPU:0 now
where the time goes in v4:
time: 60.8 us; the launch traced here: 60.6 us
  waiting for transfers between devices  24.4 us (40%)
  Pallas kernels  20.4 us (34%)
  starting transfers between devices  13.9 us (23%)
  local copies, waits for them, and re-layouts  1.81 us (3%)
    pallas_call x2, Pallas kernels, body(): pl.pallas_call(functools.partial(attend_kernel, grid, groups), out_shape=...  18.6 us
    ppermute x8, waiting for transfers between devices, y_swap(): lax.ppermute(block, 'tp', [(at, at ^ cores) for at in range(depth * width...  12.4 us
    ppermute x6, waiting for transfers between devices, z_forward(): lax.ppermute(block, 'tp', [(at, (at + width * cores) % count) for at in r...  12 us
    ppermute x8, starting transfers between devices, y_swap(): lax.ppermute(block, 'tp', [(at, at ^ cores) for at in range(depth * width...  10.4 us
    ppermute x6, starting transfers between devices, z_forward(): lax.ppermute(block, 'tp', [(at, (at + width * cores) % count) for at in r...  2.86 us
    unnamed x4, local copies, waits for them, and re-layouts  1.81 us
    pallas_call x1, Pallas kernels, pack(): pl.pallas_call(kernel, out_shape=[jax.ShapeDtypeStruct((2, tok, columns),...  1.67 us
  transfers between devices with their start and end apart: 20, of which 12 were waited for; matrix products, arithmetic and copies ran while one was open for 0% of the time, Pallas kernels for 16%

profile of v4, /device:TPU:0, one launch (start us, length us, event | category | flops | bytes accessed | tf_op | source)
XLA Modules:
  0.0 60.6 jit_solution(14411767652580544427)
XLA Ops:
  0.0 1.7 %pack.1 = (bf16[2,64,512]{2,1,0:T(8,128)(2,1)}, bf16[2,64,512]{2,1,0:T(8,128)(2,1)}) custom-call(bf16[64,1024]{1,0:T(8,128)(2,1)} %key_ref.1, bf16[64,1024]{1,0:T(8,128)(2,1)} %value_ref.1), custom_call_target="tpu_custom_call" | custom-call | tf_op jit(solution)/shard_map/pack/pallas_call | solution.py:61
  1.7 3.0 %collective-permute-start.11 = (bf16[2,64,512]{2,1,0:T(8,128)(2,1)}, bf16[2,64,512]{2,1,0:T(8,128)(2,1)S(1)}, u32[]{:S(2)}, u32[]{:S(2)}) collective-permute-start(bf16[2,64,512]{2,1,0:T(8,128)(2,1)} %get-tuple-element.36.refs_0_), channel_id=1, source_target_pairs={{0,2},{1,3},{2,0},{3,1},{4,6},{5,7},{6,4},{7,5},{8,10},{9,11},{10,... | collective-permute-start | bytes 393224 | tf_op jit(solution)/shard_map/ppermute | solution.py:80
  4.6 1.6 %collective-permute-start.10 = (bf16[2,64,512]{2,1,0:T(8,128)(2,1)}, bf16[2,64,512]{2,1,0:T(8,128)(2,1)S(1)}, u32[]{:S(2)}, u32[]{:S(2)}) collective-permute-start(bf16[2,64,512]{2,1,0:T(8,128)(2,1)} %get-tuple-element.36.refs_0_), channel_id=1, source_target_pairs={{0,4},{1,5},{2,6},{3,7},{4,8},{5,9},{6,10},{7,11},{8,12},{9,13},{1... | collective-permute-start | bytes 393224 | tf_op jit(solution)/shard_map/ppermute | solution.py:73
  6.2 2.1 %collective-permute-done.11.refs_1_ = bf16[2,64,512]{2,1,0:T(8,128)(2,1)S(1)} collective-permute-done((bf16[2,64,512]{2,1,0:T(8,128)(2,1)}, bf16[2,64,512]{2,1,0:T(8,128)(2,1)S(1)}, u32[]{:S(2)}, u32[]{:S(2)}) %collective-permute-start.11) | collective-permute-done | bytes 131104 | tf_op jit(solution)/shard_map/ppermute | solution.py:80
  8.3 3.4 %collective-permute-done.10.refs_2_ = bf16[2,64,512]{2,1,0:T(8,128)(2,1)S(1)} collective-permute-done((bf16[2,64,512]{2,1,0:T(8,128)(2,1)}, bf16[2,64,512]{2,1,0:T(8,128)(2,1)S(1)}, u32[]{:S(2)}, u32[]{:S(2)}) %collective-permute-start.10) | collective-permute-done | bytes 131104 | tf_op jit(solution)/shard_map/ppermute | solution.py:73
  11.7 0.5 collective-permute-start.13
  12.2 0.0 collective-permute-start.12
  12.2 1.5 %collective-permute-start.1 = (bf16[2,64,512]{2,1,0:T(8,128)(2,1)}, bf16[2,64,512]{2,1,0:T(8,128)(2,1)S(1)}, u32[]{:S(2)}, u32[]{:S(2)}) collective-permute-start(bf16[2,64,512]{2,1,0:T(8,128)(2,1)} %get-tuple-element.26.refs_0_), channel_id=1, source_target_pairs={{0,2},{1,3},{2,0},{3,1},{4,6},{5,7},{6,4},{7,5},{8,10},{9,11},{10,... | collective-permute-start | bytes 393224 | tf_op jit(solution)/shard_map/ppermute | solution.py:80
  13.7 1.3 %collective-permute-start = (bf16[2,64,512]{2,1,0:T(8,128)(2,1)}, bf16[2,64,512]{2,1,0:T(8,128)(2,1)S(1)}, u32[]{:S(2)}, u32[]{:S(2)}) collective-permute-start(bf16[2,64,512]{2,1,0:T(8,128)(2,1)} %get-tuple-element.26.refs_0_), channel_id=1, source_target_pairs={{0,4},{1,5},{2,6},{3,7},{4,8},{5,9},{6,10},{7,11},{8,12},{9,13},{1... | collective-permute-start | bytes 393224 | tf_op jit(solution)/shard_map/ppermute | solution.py:73
  15.0 2.3 %collective-permute-done.13.refs_3_ = bf16[2,64,512]{2,1,0:T(8,128)(2,1)S(1)} collective-permute-done((bf16[2,64,512]{2,1,0:T(8,128)(2,1)S(1)}, bf16[2,64,512]{2,1,0:T(8,128)(2,1)S(1)}, u32[]{:S(2)}, u32[]{:S(2)}) %collective-permute-start.13) | collective-permute-done | bytes 131104 | tf_op jit(solution)/shard_map/ppermute | solution.py:80
  17.3 2.2 %collective-permute-done.12.refs_0_ = bf16[2,64,512]{2,1,0:T(8,128)(2,1)S(1)} collective-permute-done((bf16[2,64,512]{2,1,0:T(8,128)(2,1)S(1)}, bf16[2,64,512]{2,1,0:T(8,128)(2,1)S(1)}, u32[]{:S(2)}, u32[]{:S(2)}) %collective-permute-start.12) | collective-permute-done | bytes 131104 | tf_op jit(solution)/shard_map/ppermute | solution.py:73
  19.5 1.3 %collective-permute-start.16 = (bf16[2,64,512]{2,1,0:T(8,128)(2,1)S(1)}, bf16[2,64,512]{2,1,0:T(8,128)(2,1)S(1)}, u32[]{:S(2)}, u32[]{:S(2)}) collective-permute-start(bf16[2,64,512]{2,1,0:T(8,128)(2,1)S(1)} %collective-permute-done.12.refs_0_), channel_id=1, source_target_pairs={{0,2},{1,3},{2,0},{3,1},{4,6},{5,7},{6,4},{7,5},{8,10},{9,11},{10,... | collective-permute-start | bytes 393224 | tf_op jit(solution)/shard_map/ppermute | solution.py:80
  20.8 0.0 collective-permute-start.15
  20.8 0.1 collective-permute-done.refs_2_
  20.9 1.3 %collective-permute-start.3 = (bf16[2,64,512]{2,1,0:T(8,128)(2,1)S(1)}, bf16[2,64,512]{2,1,0:T(8,128)(2,1)S(1)}, u32[]{:S(2)}, u32[]{:S(2)}) collective-permute-start(bf16[2,64,512]{2,1,0:T(8,128)(2,1)S(1)} %collective-permute-done.refs_2_), channel_id=1, source_target_pairs={{0,2},{1,3},{2,0},{3,1},{4,6},{5,7},{6,4},{7,5},{8,10},{9,11},{10,... | collective-permute-start | bytes 393224 | tf_op jit(solution)/shard_map/ppermute | solution.py:80
  22.2 0.9 %copy-done.1 = bf16[2,64,512]{2,1,0:T(8,128)(2,1)S(1)} copy-done((bf16[2,64,512]{2,1,0:T(8,128)(2,1)S(1)}, bf16[2,64,512]{2,1,0:T(8,128)(2,1)}, u32[]{:S(2)}) %copy-start.1) | copy-done | bytes 131096
  23.1 0.1 collective-permute-start.14
  23.2 1.2 %collective-permute-done.16.refs_1_ = bf16[2,64,512]{2,1,0:T(8,128)(2,1)S(1)} collective-permute-done((bf16[2,64,512]{2,1,0:T(8,128)(2,1)S(1)}, bf16[2,64,512]{2,1,0:T(8,128)(2,1)S(1)}, u32[]{:S(2)}, u32[]{:S(2)}) %collective-permute-start.16) | collective-permute-done | bytes 131104 | tf_op jit(solution)/shard_map/ppermute | solution.py:80
  24.5 3.1 %collective-permute-done.15.refs_0_ = bf16[2,64,512]{2,1,0:T(8,128)(2,1)S(1)} collective-permute-done((bf16[2,64,512]{2,1,0:T(8,128)(2,1)S(1)}, bf16[2,64,512]{2,1,0:T(8,128)(2,1)S(1)}, u32[]{:S(2)}, u32[]{:S(2)}) %collective-permute-start.15) | collective-permute-done | bytes 131104 | tf_op jit(solution)/shard_map/ppermute | solution.py:73
  27.6 0.7 %collective-permute-start.18 = (bf16[2,64,512]{2,1,0:T(8,128)(2,1)S(1)}, bf16[2,64,512]{2,1,0:T(8,128)(2,1)S(1)}, u32[]{:S(2)}, u32[]{:S(2)}) collective-permute-start(bf16[2,64,512]{2,1,0:T(8,128)(2,1)S(1)} %collective-permute-done.15.refs_0_), channel_id=1, source_target_pairs={{0,2},{1,3},{2,0},{3,1},{4,6},{5,7},{6,4},{7,5},{8,10},{9,11},{10,... | collective-permute-start | bytes 393224 | tf_op jit(solution)/shard_map/ppermute | solution.py:80
  28.3 0.7 %collective-permute-done.2.refs_0_ = bf16[2,64,512]{2,1,0:T(8,128)(2,1)S(1)} collective-permute-done((bf16[2,64,512]{2,1,0:T(8,128)(2,1)S(1)}, bf16[2,64,512]{2,1,0:T(8,128)(2,1)S(1)}, u32[]{:S(2)}, u32[]{:S(2)}) %collective-permute-start.2) | collective-permute-done | bytes 131104 | tf_op jit(solution)/shard_map/ppermute | solution.py:73
  29.0 0.7 %collective-permute-start.6 = (bf16[2,64,512]{2,1,0:T(8,128)(2,1)S(1)}, bf16[2,64,512]{2,1,0:T(8,128)(2,1)S(1)}, u32[]{:S(2)}, u32[]{:S(2)}) collective-permute-start(bf16[2,64,512]{2,1,0:T(8,128)(2,1)S(1)} %collective-permute-done.2.refs_0_), channel_id=1, source_target_pairs={{0,2},{1,3},{2,0},{3,1},{4,6},{5,7},{6,4},{7,5},{8,10},{9,11},{10,... | collective-permute-start | bytes 393224 | tf_op jit(solution)/shard_map/ppermute | solution.py:80
  29.7 0.9 %copy-done = bf16[2,64,512]{2,1,0:T(8,128)(2,1)S(1)} copy-done((bf16[2,64,512]{2,1,0:T(8,128)(2,1)S(1)}, bf16[2,64,512]{2,1,0:T(8,128)(2,1)}, u32[]{:S(2)}) %copy-start) | copy-done | bytes 131096
  30.7 0.1 collective-permute-start.17
  30.7 1.8 %collective-permute-done.18.refs_1_ = bf16[2,64,512]{2,1,0:T(8,128)(2,1)S(1)} collective-permute-done((bf16[2,64,512]{2,1,0:T(8,128)(2,1)S(1)}, bf16[2,64,512]{2,1,0:T(8,128)(2,1)S(1)}, u32[]{:S(2)}, u32[]{:S(2)}) %collective-permute-start.18) | collective-permute-done | bytes 131104 | tf_op jit(solution)/shard_map/ppermute | solution.py:80
  32.6 1.4 %collective-permute-done.6.refs_1_ = bf16[2,64,512]{2,1,0:T(8,128)(2,1)S(1)} collective-permute-done((bf16[2,64,512]{2,1,0:T(8,128)(2,1)S(1)}, bf16[2,64,512]{2,1,0:T(8,128)(2,1)S(1)}, u32[]{:S(2)}, u32[]{:S(2)}) %collective-permute-start.6) | collective-permute-done | bytes 131104 | tf_op jit(solution)/shard_map/ppermute | solution.py:80
  33.9 2.5 %collective-permute-done.5.refs_0_ = bf16[2,64,512]{2,1,0:T(8,128)(2,1)S(1)} collective-permute-done((bf16[2,64,512]{2,1,0:T(8,128)(2,1)S(1)}, bf16[2,64,512]{2,1,0:T(8,128)(2,1)S(1)}, u32[]{:S(2)}, u32[]{:S(2)}) %collective-permute-start.5) | collective-permute-done | bytes 131104 | tf_op jit(solution)/shard_map/ppermute | solution.py:73
  36.5 1.3 %collective-permute-start.8 = (bf16[2,64,512]{2,1,0:T(8,128)(2,1)S(1)}, bf16[2,64,512]{2,1,0:T(8,128)(2,1)S(1)}, u32[]{:S(2)}, u32[]{:S(2)}) collective-permute-start(bf16[2,64,512]{2,1,0:T(8,128)(2,1)S(1)} %collective-permute-done.5.refs_0_), channel_id=1, source_target_pairs={{0,2},{1,3},{2,0},{3,1},{4,6},{5,7},{6,4},{7,5},{8,10},{9,11},{10,... | collective-permute-start | bytes 393224 | tf_op jit(solution)/shard_map/ppermute | solution.py:80
  37.8 3.6 %collective-permute-done.8.refs_1_ = bf16[2,64,512]{2,1,0:T(8,128)(2,1)S(1)} collective-permute-done((bf16[2,64,512]{2,1,0:T(8,128)(2,1)S(1)}, bf16[2,64,512]{2,1,0:T(8,128)(2,1)S(1)}, u32[]{:S(2)}, u32[]{:S(2)}) %collective-permute-start.8) | collective-permute-done | bytes 131104 | tf_op jit(solution)/shard_map/ppermute | solution.py:80
  41.5 0.6 collective-permute-start.9
  42.0 9.3 %attend.2.refs_6_ = bf16[64,16384]{1,0:T(8,128)(2,1)} custom-call(bf16[64,16384]{1,0:T(8,128)(2,1)} %query_ref.3, bf16[4,2,64,512]{3,2,1,0:T(8,128)(2,1)S(1)} %merge.9.refs_0_, bf16[4,2,64,512]{3,2,1,0:T(8,128)(2,1)S(1)} %collective-permute-done.14.refs_1_, bf16[2,2,64,512]{3,2,1,0:T(8,128)(2,1)S(1)} %merge.10.refs_2_, ...), custom_call_target="tpu_custom_call" | custom-call | flops 2147483648 | bytes 2097152 | tf_op jit(solution)/shard_map/attend/pallas_call | solution.py:212
  51.3 9.3 %attend.3 = bf16[64,16384]{1,0:T(8,128)(2,1)} custom-call(bf16[64,16384]{1,0:T(8,128)(2,1)} %query_ref.3, bf16[4,2,64,512]{3,2,1,0:T(8,128)(2,1)S(1)} %merge.6.refs_0_, bf16[4,2,64,512]{3,2,1,0:T(8,128)(2,1)S(1)} %collective-permute-done.4.refs_1_, bf16[2,2,64,512]{3,2,1,0:T(8,128)(2,1)S(1)} %merge.7.refs_2_, ...), custom_call_target="tpu_custom_call", output_to_operand_aliasing={{}: (7, {})} | custom-call | flops 2147483648 | bytes 2097152 | tf_op jit(solution)/shard_map/attend/pallas_call | solution.py:212
  (21 shorter events, 0.2 us)
Async XLA Ops:
  1.7 6.7 %collective-permute-start.11 = (bf16[2,64,512]{2,1,0:T(8,128)(2,1)}, bf16[2,64,512]{2,1,0:T(8,128)(2,1)S(1)}, u32[]{:S(2)}, u32[]{:S(2)}) collective-permute-start(bf16[2,64,512]{2,1,0:T(8,128)(2,1)} %get-tuple-element.36.refs_0_), channel_id=1, source_target_pairs={{0,2},{1,3},{2,0},{3,1},{4,6},{5,7},{6,4},{7,5},{8,10},{9,11},{10,... | collective-permute-start | bytes 393224 | tf_op jit(solution)/shard_map/ppermute | solution.py:80
  4.6 7.1 %collective-permute-start.10 = (bf16[2,64,512]{2,1,0:T(8,128)(2,1)}, bf16[2,64,512]{2,1,0:T(8,128)(2,1)S(1)}, u32[]{:S(2)}, u32[]{:S(2)}) collective-permute-start(bf16[2,64,512]{2,1,0:T(8,128)(2,1)} %get-tuple-element.36.refs_0_), channel_id=1, source_target_pairs={{0,4},{1,5},{2,6},{3,7},{4,8},{5,9},{6,10},{7,11},{8,12},{9,13},{1... | collective-permute-start | bytes 393224 | tf_op jit(solution)/shard_map/ppermute | solution.py:73
  11.7 5.6 %collective-permute-start.13 = (bf16[2,64,512]{2,1,0:T(8,128)(2,1)S(1)}, bf16[2,64,512]{2,1,0:T(8,128)(2,1)S(1)}, u32[]{:S(2)}, u32[]{:S(2)}) collective-permute-start(bf16[2,64,512]{2,1,0:T(8,128)(2,1)S(1)} %collective-permute-done.10.refs_2_), channel_id=1, source_target_pairs={{0,2},{1,3},{2,0},{3,1},{4,6},{5,7},{6,4},{7,5},{8,10},{9,11},{10,... | collective-permute-start | bytes 393224 | tf_op jit(solution)/shard_map/ppermute | solution.py:80
  12.2 7.3 %collective-permute-start.12 = (bf16[2,64,512]{2,1,0:T(8,128)(2,1)S(1)}, bf16[2,64,512]{2,1,0:T(8,128)(2,1)S(1)}, u32[]{:S(2)}, u32[]{:S(2)}) collective-permute-start(bf16[2,64,512]{2,1,0:T(8,128)(2,1)S(1)} %collective-permute-done.10.refs_2_), channel_id=1, source_target_pairs={{0,4},{1,5},{2,6},{3,7},{4,8},{5,9},{6,10},{7,11},{8,12},{9,13},{1... | collective-permute-start | bytes 393224 | tf_op jit(solution)/shard_map/ppermute | solution.py:73
  12.2 8.6 %collective-permute-start.1 = (bf16[2,64,512]{2,1,0:T(8,128)(2,1)}, bf16[2,64,512]{2,1,0:T(8,128)(2,1)S(1)}, u32[]{:S(2)}, u32[]{:S(2)}) collective-permute-start(bf16[2,64,512]{2,1,0:T(8,128)(2,1)} %get-tuple-element.26.refs_0_), channel_id=1, source_target_pairs={{0,2},{1,3},{2,0},{3,1},{4,6},{5,7},{6,4},{7,5},{8,10},{9,11},{10,... | collective-permute-start | bytes 393224 | tf_op jit(solution)/shard_map/ppermute | solution.py:80
  13.7 7.2 %collective-permute-start = (bf16[2,64,512]{2,1,0:T(8,128)(2,1)}, bf16[2,64,512]{2,1,0:T(8,128)(2,1)S(1)}, u32[]{:S(2)}, u32[]{:S(2)}) collective-permute-start(bf16[2,64,512]{2,1,0:T(8,128)(2,1)} %get-tuple-element.26.refs_0_), channel_id=1, source_target_pairs={{0,4},{1,5},{2,6},{3,7},{4,8},{5,9},{6,10},{7,11},{8,12},{9,13},{1... | collective-permute-start | bytes 393224 | tf_op jit(solution)/shard_map/ppermute | solution.py:73
  19.5 5.0 %collective-permute-start.16 = (bf16[2,64,512]{2,1,0:T(8,128)(2,1)S(1)}, bf16[2,64,512]{2,1,0:T(8,128)(2,1)S(1)}, u32[]{:S(2)}, u32[]{:S(2)}) collective-permute-start(bf16[2,64,512]{2,1,0:T(8,128)(2,1)S(1)} %collective-permute-done.12.refs_0_), channel_id=1, source_target_pairs={{0,2},{1,3},{2,0},{3,1},{4,6},{5,7},{6,4},{7,5},{8,10},{9,11},{10,... | collective-permute-start | bytes 393224 | tf_op jit(solution)/shard_map/ppermute | solution.py:80
  20.8 6.8 %collective-permute-start.15 = (bf16[2,64,512]{2,1,0:T(8,128)(2,1)S(1)}, bf16[2,64,512]{2,1,0:T(8,128)(2,1)S(1)}, u32[]{:S(2)}, u32[]{:S(2)}) collective-permute-start(bf16[2,64,512]{2,1,0:T(8,128)(2,1)S(1)} %collective-permute-done.12.refs_0_), channel_id=1, source_target_pairs={{0,4},{1,5},{2,6},{3,7},{4,8},{5,9},{6,10},{7,11},{8,12},{9,13},{1... | collective-permute-start | bytes 393224 | tf_op jit(solution)/shard_map/ppermute | solution.py:73
  20.9 7.4 %collective-permute-start.3 = (bf16[2,64,512]{2,1,0:T(8,128)(2,1)S(1)}, bf16[2,64,512]{2,1,0:T(8,128)(2,1)S(1)}, u32[]{:S(2)}, u32[]{:S(2)}) collective-permute-start(bf16[2,64,512]{2,1,0:T(8,128)(2,1)S(1)} %collective-permute-done.refs_2_), channel_id=1, source_target_pairs={{0,2},{1,3},{2,0},{3,1},{4,6},{5,7},{6,4},{7,5},{8,10},{9,11},{10,... | collective-permute-start | bytes 393224 | tf_op jit(solution)/shard_map/ppermute | solution.py:80
  22.2 6.8 %collective-permute-start.2 = (bf16[2,64,512]{2,1,0:T(8,128)(2,1)S(1)}, bf16[2,64,512]{2,1,0:T(8,128)(2,1)S(1)}, u32[]{:S(2)}, u32[]{:S(2)}) collective-permute-start(bf16[2,64,512]{2,1,0:T(8,128)(2,1)S(1)} %collective-permute-done.refs_2_), channel_id=1, source_target_pairs={{0,4},{1,5},{2,6},{3,7},{4,8},{5,9},{6,10},{7,11},{8,12},{9,13},{1... | collective-permute-start | bytes 393224 | tf_op jit(solution)/shard_map/ppermute | solution.py:73
  22.2 0.9 %copy-start.1 = (bf16[2,64,512]{2,1,0:T(8,128)(2,1)S(1)}, bf16[2,64,512]{2,1,0:T(8,128)(2,1)}, u32[]{:S(2)}) copy-start(bf16[2,64,512]{2,1,0:T(8,128)(2,1)} %get-tuple-element.36.refs_0_) | copy-start | bytes 393220
  23.1 18.9 %collective-permute-start.14 = (bf16[4,2,64,512]{3,2,1,0:T(8,128)(2,1)S(1)}, bf16[4,2,64,512]{3,2,1,0:T(8,128)(2,1)S(1)}, u32[]{:S(2)}, u32[]{:S(2)}) collective-permute-start(bf16[4,2,64,512]{3,2,1,0:T(8,128)(2,1)S(1)} %merge.9.refs_0_), channel_id=1, source_target_pairs={{0,1},{1,0},{2,3},{3,2},{4,5},{5,4},{6,7},{7,6},{8,9},{9,8},{10,11... | collective-permute-start | bytes 1572872 | tf_op jit(solution)/shard_map/ppermute | solution.py:87
  27.6 5.0 %collective-permute-start.18 = (bf16[2,64,512]{2,1,0:T(8,128)(2,1)S(1)}, bf16[2,64,512]{2,1,0:T(8,128)(2,1)S(1)}, u32[]{:S(2)}, u32[]{:S(2)}) collective-permute-start(bf16[2,64,512]{2,1,0:T(8,128)(2,1)S(1)} %collective-permute-done.15.refs_0_), channel_id=1, source_target_pairs={{0,2},{1,3},{2,0},{3,1},{4,6},{5,7},{6,4},{7,5},{8,10},{9,11},{10,... | collective-permute-start | bytes 393224 | tf_op jit(solution)/shard_map/ppermute | solution.py:80
  29.0 5.0 %collective-permute-start.6 = (bf16[2,64,512]{2,1,0:T(8,128)(2,1)S(1)}, bf16[2,64,512]{2,1,0:T(8,128)(2,1)S(1)}, u32[]{:S(2)}, u32[]{:S(2)}) collective-permute-start(bf16[2,64,512]{2,1,0:T(8,128)(2,1)S(1)} %collective-permute-done.2.refs_0_), channel_id=1, source_target_pairs={{0,2},{1,3},{2,0},{3,1},{4,6},{5,7},{6,4},{7,5},{8,10},{9,11},{10,... | collective-permute-start | bytes 393224 | tf_op jit(solution)/shard_map/ppermute | solution.py:80
  29.7 6.8 %collective-permute-start.5 = (bf16[2,64,512]{2,1,0:T(8,128)(2,1)S(1)}, bf16[2,64,512]{2,1,0:T(8,128)(2,1)S(1)}, u32[]{:S(2)}, u32[]{:S(2)}) collective-permute-start(bf16[2,64,512]{2,1,0:T(8,128)(2,1)S(1)} %collective-permute-done.2.refs_0_), channel_id=1, source_target_pairs={{0,4},{1,5},{2,6},{3,7},{4,8},{5,9},{6,10},{7,11},{8,12},{9,13},{1... | collective-permute-start | bytes 393224 | tf_op jit(solution)/shard_map/ppermute | solution.py:73
  29.7 0.9 %copy-start = (bf16[2,64,512]{2,1,0:T(8,128)(2,1)S(1)}, bf16[2,64,512]{2,1,0:T(8,128)(2,1)}, u32[]{:S(2)}) copy-start(bf16[2,64,512]{2,1,0:T(8,128)(2,1)} %get-tuple-element.26.refs_0_) | copy-start | bytes 393220
  30.7 10.8 %collective-permute-start.17 = (bf16[2,2,64,512]{3,2,1,0:T(8,128)(2,1)S(1)}, bf16[2,2,64,512]{3,2,1,0:T(8,128)(2,1)S(1)}, u32[]{:S(2)}, u32[]{:S(2)}) collective-permute-start(bf16[2,2,64,512]{3,2,1,0:T(8,128)(2,1)S(1)} %merge.10.refs_2_), channel_id=1, source_target_pairs={{0,1},{1,0},{2,3},{3,2},{4,5},{5,4},{6,7},{7,6},{8,9},{9,8},{10,11... | collective-permute-start | bytes 786440 | tf_op jit(solution)/shard_map/ppermute | solution.py:87
  32.5 18.8 %collective-permute-start.4 = (bf16[4,2,64,512]{3,2,1,0:T(8,128)(2,1)S(1)}, bf16[4,2,64,512]{3,2,1,0:T(8,128)(2,1)S(1)}, u32[]{:S(2)}, u32[]{:S(2)}) collective-permute-start(bf16[4,2,64,512]{3,2,1,0:T(8,128)(2,1)S(1)} %merge.6.refs_0_), channel_id=1, source_target_pairs={{0,1},{1,0},{2,3},{3,2},{4,5},{5,4},{6,7},{7,6},{8,9},{9,8},{10,11... | collective-permute-start | bytes 1572872 | tf_op jit(solution)/shard_map/ppermute | solution.py:87
  33.9 8.1 %collective-permute-start.19 = (bf16[2,2,64,512]{3,2,1,0:T(8,128)(2,1)S(1)}, bf16[2,2,64,512]{3,2,1,0:T(8,128)(2,1)S(1)}, u32[]{:S(2)}, u32[]{:S(2)}) collective-permute-start(bf16[2,2,64,512]{3,2,1,0:T(8,128)(2,1)S(1)} %merge.11.refs_4_), channel_id=1, source_target_pairs={{0,1},{1,0},{2,3},{3,2},{4,5},{5,4},{6,7},{7,6},{8,9},{9,8},{10,11... | collective-permute-start | bytes 786440 | tf_op jit(solution)/shard_map/ppermute | solution.py:87
  36.5 5.0 %collective-permute-start.8 = (bf16[2,64,512]{2,1,0:T(8,128)(2,1)S(1)}, bf16[2,64,512]{2,1,0:T(8,128)(2,1)S(1)}, u32[]{:S(2)}, u32[]{:S(2)}) collective-permute-start(bf16[2,64,512]{2,1,0:T(8,128)(2,1)S(1)} %collective-permute-done.5.refs_0_), channel_id=1, source_target_pairs={{0,2},{1,3},{2,0},{3,1},{4,6},{5,7},{6,4},{7,5},{8,10},{9,11},{10,... | collective-permute-start | bytes 393224 | tf_op jit(solution)/shard_map/ppermute | solution.py:80
  41.4 9.9 %collective-permute-start.7 = (bf16[2,2,64,512]{3,2,1,0:T(8,128)(2,1)S(1)}, bf16[2,2,64,512]{3,2,1,0:T(8,128)(2,1)S(1)}, u32[]{:S(2)}, u32[]{:S(2)}) collective-permute-start(bf16[2,2,64,512]{3,2,1,0:T(8,128)(2,1)S(1)} %merge.7.refs_2_), channel_id=1, source_target_pairs={{0,1},{1,0},{2,3},{3,2},{4,5},{5,4},{6,7},{7,6},{8,9},{9,8},{10,11... | collective-permute-start | bytes 786440 | tf_op jit(solution)/shard_map/ppermute | solution.py:87
  41.5 9.9 %collective-permute-start.9 = (bf16[2,2,64,512]{3,2,1,0:T(8,128)(2,1)S(1)}, bf16[2,2,64,512]{3,2,1,0:T(8,128)(2,1)S(1)}, u32[]{:S(2)}, u32[]{:S(2)}) collective-permute-start(bf16[2,2,64,512]{3,2,1,0:T(8,128)(2,1)S(1)} %merge.8.refs_4_), channel_id=1, source_target_pairs={{0,1},{1,0},{2,3},{3,2},{4,5},{5,4},{6,7},{7,6},{8,9},{9,8},{10,11... | collective-permute-start | bytes 786440 | tf_op jit(solution)/shard_map/ppermute | solution.py:87

commit v5 on v4

v5 whole, which is shorter than its diff:
```python
import functools
import math

import jax
import jax.numpy as jnp
from jax import lax
from jax.experimental import pallas as pl
from jax.experimental.pallas import tpu as pltpu
from jax.sharding import PartitionSpec as P

HEADS = 128
KV_HEADS = 8
GROUP = HEADS // KV_HEADS
PARTS = 4
STEP_HEADS = 2

masked_score = -1e30


def chip_grid(devices):
    if devices % 2:
        return devices, 1, 1
    chips = devices // 2
    if chips % 2 or chips > 8:
        return chips, 1, 2
    return chips // 2, 2, 2


def place(grid):
    depth, width, cores = grid
    me = lax.axis_index("tp")
    return me // (width * cores), (me // cores) % width, me % cores


def stack(arrays, name):
    def kernel(*refs):
        for at, ref in enumerate(refs[:-1]):
            refs[-1][at] = ref[...]

    count = len(arrays)
    return pl.pallas_call(
        kernel,
        out_shape=jax.ShapeDtypeStruct((count, *arrays[0].shape), arrays[0].dtype),
        in_specs=[pl.BlockSpec(memory_space=pltpu.VMEM)] * count,
        out_specs=pl.BlockSpec(memory_space=pltpu.VMEM),
        compiler_params=pltpu.CompilerParams(vmem_limit_bytes=32 * 2**20),
        name=name,
    )(*arrays)


def z_forward(block, grid):
    depth, width, cores = grid
    count = depth * width * cores
    return lax.ppermute(
        block, "tp", [(at, (at + width * cores) % count) for at in range(count)]
    )


def y_swap(block, grid):
    depth, width, cores = grid
    return lax.ppermute(
        block, "tp", [(at, at ^ cores) for at in range(depth * width * cores)]
    )


def core_swap(blocks, grid):
    depth, width, cores = grid
    return lax.ppermute(blocks, "tp", [(at, at ^ 1) for at in range(depth * width * cores)])


def reciprocal(x):
    guess = pl.reciprocal(x, approx=True)
    return guess * (2.0 - x * guess)


def attend_kernel(grid, groups, kept, last, query_ref, *refs):
    depth, width, cores = grid
    blocks_refs, refs = refs[: 2 * len(groups)], refs[2 * len(groups) :]
    kept_refs, refs = refs[: 2 * kept], refs[2 * kept :]
    out_refs, scratch = refs[: 2 - last], refs[2 - last :]
    tok = query_ref.shape[0]
    dim = blocks_refs[0].shape[-1] // STEP_HEADS
    rows = GROUP * tok
    part_rows = rows // PARTS
    heads = part_rows // tok
    factor = dim ** (-0.5) * math.log2(math.e)
    zz, yy, cc = place(grid)

    pieces = []
    for below, own_ref, core_ref in zip(groups, blocks_refs[::2], blocks_refs[1::2]):
        for dc, ref in ((0, own_ref), (1, core_ref)):
            for at, dz in enumerate(below):
                pieces.append((dz, dc, below[:at].count(dz), ref, at))
    pieces.sort(key=lambda piece: piece[:3])
    lowest, highest = pieces[0][0], pieces[-1][0]

    if scratch:
        bias_ref = scratch[0]

        @pl.when(pl.program_id(0) == 0)
        def _():
            row = lax.broadcasted_iota(jnp.int32, (tok, tok), 0)
            key = lax.broadcasted_iota(jnp.int32, (tok, tok), 1)
            for at, (dz, dc, dy, _, _) in enumerate(pieces):
                if dz:
                    limit = jnp.where(zz >= dz, 0, tok) + 0 * key
                elif dy:
                    limit = jnp.where(yy == 1, 0, tok) + 0 * key
                elif dc:
                    limit = jnp.where(cc == 1, 0, tok) + 0 * key
                else:
                    limit = key
                bias_ref[:, at * tok : (at + 1) * tok] = jnp.where(
                    limit <= row, 0.0, masked_score
                )

    def emit(head, part, result, level):
        here = slice(part * part_rows, (part + 1) * part_rows)
        if not last:
            out_refs[0][head, here, :] = result
            out_refs[1][head, here, :] = level()
            return
        result = result.astype(out_refs[0].dtype)
        for index in range(heads):
            at = ((head * PARTS + part) * heads + index) * dim
            out_refs[0][:, at : at + dim] = result[index * tok : (index + 1) * tok]

    def attend(used, span):
        for head in range(STEP_HEADS):
            column = slice(head * dim, (head + 1) * dim)
            keys = jnp.concatenate([ref[at, 0, :, column] for _, _, _, ref, at in used], axis=0)
            values = jnp.concatenate([ref[at, 1, :, column] for _, _, _, ref, at in used], axis=0)
            values = jnp.concatenate([values, jnp.ones_like(values)], axis=1)
            first_head = head * GROUP
            for part in range(PARTS):
                here = slice(part * part_rows, (part + 1) * part_rows)
                query = jnp.concatenate(
                    [
                        query_ref[:, at * dim : (at + 1) * dim]
                        for at in range(first_head + part * heads, first_head + (part + 1) * heads)
                    ],
                    axis=0,
                )
                scores = lax.dot_general(
                    query, keys, (((1,), (1,)), ((), ())), preferred_element_type=jnp.float32
                )
                if span:
                    first = scores[:, :span].reshape(heads, tok, span) + bias_ref[:, :span][None]
                    first = first.reshape(part_rows, span)
                    if span < scores.shape[1]:
                        first = jnp.concatenate([first, scores[:, span:]], axis=1)
                    scores = first
                peak = jnp.max(scores, axis=1, keepdims=True) * factor
                if kept:
                    before = kept_refs[1][head, here, :]
                    peak = jnp.maximum(jnp.broadcast_to(peak, before.shape), before)
                    shifted = jnp.concatenate(
                        [
                            scores[:, at : at + dim] * factor - peak
                            for at in range(0, scores.shape[1], dim)
                        ],
                        axis=1,
                    )
                else:
                    shifted = scores * factor - peak
                weights = jnp.exp2(shifted).astype(jnp.bfloat16)
                sums = jnp.dot(weights, values, preferred_element_type=jnp.float32)
                numerator, denominator = sums[:, :dim], sums[:, dim:]
                if kept:
                    carry = jnp.exp2(before - peak)
                    numerator = numerator + carry * kept_refs[0][head, here, :]
                    denominator = denominator + carry
                emit(
                    head,
                    part,
                    numerator * reciprocal(denominator),
                    lambda: peak + jnp.log2(denominator),
                )

    def hand_on():
        for head in range(STEP_HEADS):
            for part in range(PARTS):
                here = slice(part * part_rows, (part + 1) * part_rows)
                emit(head, part, kept_refs[0][head, here, :], lambda: kept_refs[1][head, here, :])

    near = width * cores * tok if lowest == 0 else 0
    levels = sorted(set(range(lowest, highest + 1)))
    if len(levels) > 4:
        levels = sorted({lowest + (len(levels) - 1) * part // 3 for part in range(4)})
    below = lowest - 1
    if kept and lowest > 0:

        @pl.when(zz < lowest)
        def _():
            hand_on()

    for level in levels:
        used = [piece for piece in pieces if piece[0] <= level]
        alone = level == below + 1
        span = near if alone else len(used) * tok
        reached = jnp.logical_and(zz > below, zz <= level)
        if level == levels[-1]:
            reached = zz > below

        @pl.when(reached)
        def _(used=used, span=span):
            attend(used, span)

        below = level


def solution(mesh):
    grid = chip_grid(mesh.shape["tp"])
    depth, width, cores = grid
    assert cores == 2 and depth > 2

    def body(query_rows, key_rows, value_rows):
        tok, columns = query_rows.shape
        dim = key_rows.shape[1] // KV_HEADS
        rows = GROUP * tok
        query_rows, key_rows, value_rows = (
            pltpu.with_memory_space_constraint(array, pltpu.HBM)
            for array in (query_rows, key_rows, value_rows)
        )
        block = stack([key_rows, value_rows], "pack")
        rows_of = []
        for dz in range(depth):
            row = [block, y_swap(block, grid)] if width == 2 else [block]
            if dz + 1 < depth:
                following = z_forward(block, grid)
                block, row = lax.optimization_barrier((following, row))
            rows_of.append(row)

        query_spec = pl.BlockSpec(
            (tok, STEP_HEADS * columns // KV_HEADS), lambda step: (0, step)
        )
        state_spec = pl.BlockSpec((STEP_HEADS, rows, dim), lambda step: (step, 0, 0))
        state_shape = pltpu.HBM((KV_HEADS, rows, dim), jnp.float32)

        def merge(span):
            merged = stack([block for dz in span for block in rows_of[dz]], "merge")
            return [merged, core_swap(merged, grid)]

        def phase(spans, operands, state, last):
            groups = [[dz for dz in span for _ in range(width)] for span in spans]
            count = sum(2 * len(group) for group in groups)
            keys = tok * count
            masked = spans[0][0] == 0 or spans[-1][-1] - spans[0][0] > 3
            return pl.pallas_call(
                functools.partial(attend_kernel, grid, groups, bool(state), last),
                out_shape=query_rows if last else [state_shape] * 2,
                grid=(KV_HEADS // STEP_HEADS,),
                in_specs=[query_spec]
                + [
                    pl.BlockSpec(
                        (operand.shape[0], 2, tok, STEP_HEADS * dim), lambda step: (0, 0, 0, step)
                    )
                    for operand in operands
                ]
                + [state_spec] * len(state),
                out_specs=query_spec if last else [state_spec] * 2,
                scratch_shapes=[pltpu.VMEM((tok, keys), jnp.float32)] if masked else [],
                compiler_params=pltpu.CompilerParams(vmem_limit_bytes=40 * 2**20),
                cost_estimate=pl.CostEstimate(
                    flops=4 * HEADS * tok * keys * dim,
                    bytes_accessed=4 * HEADS * tok * dim,
                    transcendentals=HEADS * tok * keys,
                ),
                name="attend_last" if last else "attend_first",
            )(query_rows, *operands, *state)

        early = [range(0, 2)]
        late = [range(2, depth - 1), range(depth - 1, depth)]
        late = [span for span in late if len(span)]
        operands = merge(early[0])
        operands, rows_of[-1][0] = lax.optimization_barrier((operands, rows_of[-1][0]))
        state = phase(early, operands, [], False)
        rows_of[-1], state = lax.optimization_barrier((rows_of[-1], state))
        state = [pltpu.with_memory_space_constraint(array, pltpu.HBM) for array in state]
        operands = [operand for span in late for operand in merge(span)]
        return phase(late, operands, list(state), True)

    spec = P(("groups", "tp"), None)
    return jax.shard_map(
        body, mesh=mesh, in_specs=(spec, spec, spec), out_specs=spec, check_vma=False
    )
```

time: 60.8 us -> 51.8 us (0.85)
  the two profiles are of different devices: /device:TPU:0 before, /device:TPU:25 now
where the time goes in v5:
time: 51.8 us; the launch traced here: 51.6 us
  Pallas kernels  20.1 us (39%)
  waiting for transfers between devices  17.9 us (35%)
  starting transfers between devices  13.6 us (26%)
    pallas_call x2, Pallas kernels, phase(): pl.pallas_call(functools.partial(attend_kernel, grid, groups, bool(state)...  19 us
    ppermute x4, waiting for transfers between devices, y_swap(): lax.ppermute(block, 'tp', [(at, at ^ cores) for at in range(depth * width...  12.6 us
    ppermute x3, starting transfers between devices, z_forward(): lax.ppermute(block, 'tp', [(at, (at + width * cores) % count) for at in r...  5.69 us
    ppermute x3, starting transfers between devices, core_swap(): lax.ppermute(blocks, 'tp', [(at, at ^ 1) for at in range(depth * width *...  4.61 us
    ppermute x3, waiting for transfers between devices, z_forward(): lax.ppermute(block, 'tp', [(at, (at + width * cores) % count) for at in r...  3.39 us
    ppermute x4, starting transfers between devices, y_swap(): lax.ppermute(block, 'tp', [(at, at ^ cores) for at in range(depth * width...  3.26 us
    ppermute x3, waiting for transfers between devices, core_swap(): lax.ppermute(blocks, 'tp', [(at, at ^ 1) for at in range(depth * width *...  1.88 us
    pallas_call x4, Pallas kernels, stack(): pl.pallas_call(kernel, out_shape=jax.ShapeDtypeStruct((count, *arrays[0]....  1.12 us
  transfers between devices with their start and end apart: 10, of which 7 were waited for; matrix products, arithmetic and copies ran while one was open for 0% of the time, Pallas kernels for 18%

profile of v5, /device:TPU:25, one launch (start us, length us, event | category | flops | bytes accessed | tf_op | source)
XLA Modules:
  0.0 51.6 jit_solution(8946163209658519118)
XLA Ops:
  0.0 1.0 %pack.1.refs_0_ = bf16[2,64,1024]{2,1,0:T(8,128)(2,1)S(1)} custom-call(bf16[64,1024]{1,0:T(8,128)(2,1)} %refs_0_.1, bf16[64,1024]{1,0:T(8,128)(2,1)} %refs_1_.1), custom_call_target="tpu_custom_call" | custom-call | tf_op jit(solution)/shard_map/pack/pallas_call | solution.py:41
  1.0 1.3 %collective-permute-start.1 = (bf16[2,64,1024]{2,1,0:T(8,128)(2,1)S(1)}, bf16[2,64,1024]{2,1,0:T(8,128)(2,1)S(1)}, u32[]{:S(2)}, u32[]{:S(2)}) collective-permute-start(bf16[2,64,1024]{2,1,0:T(8,128)(2,1)S(1)} %pack.1.refs_0_), channel_id=1, source_target_pairs={{0,2},{1,3},{2,0},{3,1},{4,6},{5,7},{6,4},{7,5},{8,10},{9,11},{10,... | collective-permute-start | bytes 786440 | tf_op jit(solution)/shard_map/ppermute | solution.py:61
  2.3 0.0 collective-permute-start
  2.3 5.9 %collective-permute-done.1.refs_1_ = bf16[2,64,1024]{2,1,0:T(8,128)(2,1)S(1)} collective-permute-done((bf16[2,64,1024]{2,1,0:T(8,128)(2,1)S(1)}, bf16[2,64,1024]{2,1,0:T(8,128)(2,1)S(1)}, u32[]{:S(2)}, u32[]{:S(2)}) %collective-permute-start.1) | collective-permute-done | bytes 262176 | tf_op jit(solution)/shard_map/ppermute | solution.py:61
  8.2 0.9 %collective-permute-done.refs_2_ = bf16[2,64,1024]{2,1,0:T(8,128)(2,1)S(1)} collective-permute-done((bf16[2,64,1024]{2,1,0:T(8,128)(2,1)S(1)}, bf16[2,64,1024]{2,1,0:T(8,128)(2,1)S(1)}, u32[]{:S(2)}, u32[]{:S(2)}) %collective-permute-start) | collective-permute-done | bytes 262176 | tf_op jit(solution)/shard_map/ppermute | solution.py:54
  9.2 0.3 collective-permute-start.3
  9.5 2.0 %collective-permute-start.2 = (bf16[2,64,1024]{2,1,0:T(8,128)(2,1)S(1)}, bf16[2,64,1024]{2,1,0:T(8,128)(2,1)S(1)}, u32[]{:S(2)}, u32[]{:S(2)}) collective-permute-start(bf16[2,64,1024]{2,1,0:T(8,128)(2,1)S(1)} %collective-permute-done.refs_2_), channel_id=1, source_target_pairs={{0,4},{1,5},{2,6},{3,7},{4,8},{5,9},{6,10},{7,11},{8,12},{9,13},{1... | collective-permute-start | bytes 786440 | tf_op jit(solution)/shard_map/ppermute | solution.py:54
  11.5 3.6 %collective-permute-done.3.refs_3_ = bf16[2,64,1024]{2,1,0:T(8,128)(2,1)S(1)} collective-permute-done((bf16[2,64,1024]{2,1,0:T(8,128)(2,1)S(1)}, bf16[2,64,1024]{2,1,0:T(8,128)(2,1)S(1)}, u32[]{:S(2)}, u32[]{:S(2)}) %collective-permute-start.3) | collective-permute-done | bytes 262176 | tf_op jit(solution)/shard_map/ppermute | solution.py:61
  15.1 0.2 collective-permute-done.2.refs_0_
  15.3 0.1 merge.4.refs_0_
  15.3 3.0 %collective-permute-start.7 = (bf16[4,2,64,1024]{3,2,1,0:T(8,128)(2,1)S(1)}, bf16[4,2,64,1024]{3,2,1,0:T(8,128)(2,1)S(1)}, u32[]{:S(2)}, u32[]{:S(2)}) collective-permute-start(bf16[4,2,64,1024]{3,2,1,0:T(8,128)(2,1)S(1)} %merge.4.refs_0_), channel_id=1, source_target_pairs={{0,1},{1,0},{2,3},{3,2},{4,5},{5,4},{6,7},{7,6},{8,9},{9,8},{10,11... | collective-permute-start | bytes 3145736 | tf_op jit(solution)/shard_map/ppermute | solution.py:68
  18.3 1.2 %collective-permute-start.5 = (bf16[2,64,1024]{2,1,0:T(8,128)(2,1)S(1)}, bf16[2,64,1024]{2,1,0:T(8,128)(2,1)S(1)}, u32[]{:S(2)}, u32[]{:S(2)}) collective-permute-start(bf16[2,64,1024]{2,1,0:T(8,128)(2,1)S(1)} %collective-permute-done.2.refs_0_), channel_id=1, source_target_pairs={{0,2},{1,3},{2,0},{3,1},{4,6},{5,7},{6,4},{7,5},{8,10},{9,11},{10,... | collective-permute-start | bytes 786440 | tf_op jit(solution)/shard_map/ppermute | solution.py:61
  19.5 3.7 %collective-permute-start.4 = (bf16[2,64,1024]{2,1,0:T(8,128)(2,1)S(1)}, bf16[2,64,1024]{2,1,0:T(8,128)(2,1)S(1)}, u32[]{:S(2)}, u32[]{:S(2)}) collective-permute-start(bf16[2,64,1024]{2,1,0:T(8,128)(2,1)S(1)} %collective-permute-done.2.refs_0_), channel_id=1, source_target_pairs={{0,4},{1,5},{2,6},{3,7},{4,8},{5,9},{6,10},{7,11},{8,12},{9,13},{1... | collective-permute-start | bytes 786440 | tf_op jit(solution)/shard_map/ppermute | solution.py:54
  23.2 3.1 %collective-permute-done.5.refs_1_ = bf16[2,64,1024]{2,1,0:T(8,128)(2,1)S(1)} collective-permute-done((bf16[2,64,1024]{2,1,0:T(8,128)(2,1)S(1)}, bf16[2,64,1024]{2,1,0:T(8,128)(2,1)S(1)}, u32[]{:S(2)}, u32[]{:S(2)}) %collective-permute-start.5) | collective-permute-done | bytes 262176 | tf_op jit(solution)/shard_map/ppermute | solution.py:61
  26.2 2.3 %collective-permute-done.4.refs_0_ = bf16[2,64,1024]{2,1,0:T(8,128)(2,1)S(1)} collective-permute-done((bf16[2,64,1024]{2,1,0:T(8,128)(2,1)S(1)}, bf16[2,64,1024]{2,1,0:T(8,128)(2,1)S(1)}, u32[]{:S(2)}, u32[]{:S(2)}) %collective-permute-start.4) | collective-permute-done | bytes 262176 | tf_op jit(solution)/shard_map/ppermute | solution.py:54
  28.5 0.5 collective-permute-start.8
  29.0 1.5 %collective-permute-start.6 = (bf16[2,2,64,1024]{3,2,1,0:T(8,128)(2,1)S(1)}, bf16[2,2,64,1024]{3,2,1,0:T(8,128)(2,1)S(1)}, u32[]{:S(2)}, u32[]{:S(2)}) collective-permute-start(bf16[2,2,64,1024]{3,2,1,0:T(8,128)(2,1)S(1)} %merge.3.refs_0_), channel_id=1, source_target_pairs={{0,1},{1,0},{2,3},{3,2},{4,5},{5,4},{6,7},{7,6},{8,9},{9,8},{10,11... | collective-permute-start | bytes 1572872 | tf_op jit(solution)/shard_map/ppermute | solution.py:68
  30.5 0.0 collective-permute-done.7.refs_1_
  30.5 9.4 %attend_first.1 = (f32[8,1024,128]{2,1,0:T(8,128)}, f32[8,1024,128]{2,1,0:T(8,128)}) custom-call(bf16[64,16384]{1,0:T(8,128)(2,1)} %query_ref.3, bf16[4,2,64,1024]{3,2,1,0:T(8,128)(2,1)S(1)} %merge.4.refs_0_, bf16[4,2,64,1024]{3,2,1,0:T(8,128)(2,1)S(1)} %collective-permute-done.7.refs_1_), custom_call_target="tpu_custom_call" | custom-call | flops 2147483648 | bytes 4194304 | tf_op jit(solution)/shard_map/attend_first/pallas_call | solution.py:249
  39.9 0.0 collective-permute-done.8.refs_1_
  40.0 0.1 collective-permute-start.9
  40.1 0.0 collective-permute-done.6.refs_1_
  40.1 1.9 %collective-permute-done.9.refs_3_ = bf16[2,2,64,1024]{3,2,1,0:T(8,128)(2,1)S(1)} collective-permute-done((bf16[2,2,64,1024]{3,2,1,0:T(8,128)(2,1)S(1)}, bf16[2,2,64,1024]{3,2,1,0:T(8,128)(2,1)S(1)}, u32[]{:S(2)}, u32[]{:S(2)}) %collective-permute-start.9) | collective-permute-done | bytes 524320 | tf_op jit(solution)/shard_map/ppermute | solution.py:68
  42.0 9.6 %attend_last.1 = bf16[64,16384]{1,0:T(8,128)(2,1)} custom-call(bf16[64,16384]{1,0:T(8,128)(2,1)} %query_ref.3, bf16[2,2,64,1024]{3,2,1,0:T(8,128)(2,1)S(1)} %merge.3.refs_0_, bf16[2,2,64,1024]{3,2,1,0:T(8,128)(2,1)S(1)} %collective-permute-done.6.refs_1_, bf16[2,2,64,1024]{3,2,1,0:T(8,128)(2,1)S(1)} %merge.5.refs_2_, ...), custom_call_target="tpu_custom_call" | custom-call | flops 2147483648 | bytes 4194304 | tf_op jit(solution)/shard_map/attend_last/pallas_call | solution.py:249
  (2 shorter events, 0.1 us)
Async XLA Ops:
  1.0 7.2 %collective-permute-start.1 = (bf16[2,64,1024]{2,1,0:T(8,128)(2,1)S(1)}, bf16[2,64,1024]{2,1,0:T(8,128)(2,1)S(1)}, u32[]{:S(2)}, u32[]{:S(2)}) collective-permute-start(bf16[2,64,1024]{2,1,0:T(8,128)(2,1)S(1)} %pack.1.refs_0_), channel_id=1, source_target_pairs={{0,2},{1,3},{2,0},{3,1},{4,6},{5,7},{6,4},{7,5},{8,10},{9,11},{10,... | collective-permute-start | bytes 786440 | tf_op jit(solution)/shard_map/ppermute | solution.py:61
  2.3 6.9 %collective-permute-start = (bf16[2,64,1024]{2,1,0:T(8,128)(2,1)S(1)}, bf16[2,64,1024]{2,1,0:T(8,128)(2,1)S(1)}, u32[]{:S(2)}, u32[]{:S(2)}) collective-permute-start(bf16[2,64,1024]{2,1,0:T(8,128)(2,1)S(1)} %pack.1.refs_0_), channel_id=1, source_target_pairs={{0,4},{1,5},{2,6},{3,7},{4,8},{5,9},{6,10},{7,11},{8,12},{9,13},{1... | collective-permute-start | bytes 786440 | tf_op jit(solution)/shard_map/ppermute | solution.py:54
  9.2 5.9 %collective-permute-start.3 = (bf16[2,64,1024]{2,1,0:T(8,128)(2,1)S(1)}, bf16[2,64,1024]{2,1,0:T(8,128)(2,1)S(1)}, u32[]{:S(2)}, u32[]{:S(2)}) collective-permute-start(bf16[2,64,1024]{2,1,0:T(8,128)(2,1)S(1)} %collective-permute-done.refs_2_), channel_id=1, source_target_pairs={{0,2},{1,3},{2,0},{3,1},{4,6},{5,7},{6,4},{7,5},{8,10},{9,11},{10,... | collective-permute-start | bytes 786440 | tf_op jit(solution)/shard_map/ppermute | solution.py:61
  9.5 5.8 %collective-permute-start.2 = (bf16[2,64,1024]{2,1,0:T(8,128)(2,1)S(1)}, bf16[2,64,1024]{2,1,0:T(8,128)(2,1)S(1)}, u32[]{:S(2)}, u32[]{:S(2)}) collective-permute-start(bf16[2,64,1024]{2,1,0:T(8,128)(2,1)S(1)} %collective-permute-done.refs_2_), channel_id=1, source_target_pairs={{0,4},{1,5},{2,6},{3,7},{4,8},{5,9},{6,10},{7,11},{8,12},{9,13},{1... | collective-permute-start | bytes 786440 | tf_op jit(solution)/shard_map/ppermute | solution.py:54
  15.3 15.2 %collective-permute-start.7 = (bf16[4,2,64,1024]{3,2,1,0:T(8,128)(2,1)S(1)}, bf16[4,2,64,1024]{3,2,1,0:T(8,128)(2,1)S(1)}, u32[]{:S(2)}, u32[]{:S(2)}) collective-permute-start(bf16[4,2,64,1024]{3,2,1,0:T(8,128)(2,1)S(1)} %merge.4.refs_0_), channel_id=1, source_target_pairs={{0,1},{1,0},{2,3},{3,2},{4,5},{5,4},{6,7},{7,6},{8,9},{9,8},{10,11... | collective-permute-start | bytes 3145736 | tf_op jit(solution)/shard_map/ppermute | solution.py:68
  18.3 7.9 %collective-permute-start.5 = (bf16[2,64,1024]{2,1,0:T(8,128)(2,1)S(1)}, bf16[2,64,1024]{2,1,0:T(8,128)(2,1)S(1)}, u32[]{:S(2)}, u32[]{:S(2)}) collective-permute-start(bf16[2,64,1024]{2,1,0:T(8,128)(2,1)S(1)} %collective-permute-done.2.refs_0_), channel_id=1, source_target_pairs={{0,2},{1,3},{2,0},{3,1},{4,6},{5,7},{6,4},{7,5},{8,10},{9,11},{10,... | collective-permute-start | bytes 786440 | tf_op jit(solution)/shard_map/ppermute | solution.py:61
  19.5 9.0 %collective-permute-start.4 = (bf16[2,64,1024]{2,1,0:T(8,128)(2,1)S(1)}, bf16[2,64,1024]{2,1,0:T(8,128)(2,1)S(1)}, u32[]{:S(2)}, u32[]{:S(2)}) collective-permute-start(bf16[2,64,1024]{2,1,0:T(8,128)(2,1)S(1)} %collective-permute-done.2.refs_0_), channel_id=1, source_target_pairs={{0,4},{1,5},{2,6},{3,7},{4,8},{5,9},{6,10},{7,11},{8,12},{9,13},{1... | collective-permute-start | bytes 786440 | tf_op jit(solution)/shard_map/ppermute | solution.py:54
  28.5 11.4 %collective-permute-start.8 = (bf16[2,64,1024]{2,1,0:T(8,128)(2,1)S(1)}, bf16[2,64,1024]{2,1,0:T(8,128)(2,1)S(1)}, u32[]{:S(2)}, u32[]{:S(2)}) collective-permute-start(bf16[2,64,1024]{2,1,0:T(8,128)(2,1)S(1)} %collective-permute-done.4.refs_0_), channel_id=1, source_target_pairs={{0,2},{1,3},{2,0},{3,1},{4,6},{5,7},{6,4},{7,5},{8,10},{9,11},{10,... | collective-permute-start | bytes 786440 | tf_op jit(solution)/shard_map/ppermute | solution.py:61
  29.0 11.1 %collective-permute-start.6 = (bf16[2,2,64,1024]{3,2,1,0:T(8,128)(2,1)S(1)}, bf16[2,2,64,1024]{3,2,1,0:T(8,128)(2,1)S(1)}, u32[]{:S(2)}, u32[]{:S(2)}) collective-permute-start(bf16[2,2,64,1024]{3,2,1,0:T(8,128)(2,1)S(1)} %merge.3.refs_0_), channel_id=1, source_target_pairs={{0,1},{1,0},{2,3},{3,2},{4,5},{5,4},{6,7},{7,6},{8,9},{9,8},{10,11... | collective-permute-start | bytes 1572872 | tf_op jit(solution)/shard_map/ppermute | solution.py:68
  40.0 2.0 %collective-permute-start.9 = (bf16[2,2,64,1024]{3,2,1,0:T(8,128)(2,1)S(1)}, bf16[2,2,64,1024]{3,2,1,0:T(8,128)(2,1)S(1)}, u32[]{:S(2)}, u32[]{:S(2)}) collective-permute-start(bf16[2,2,64,1024]{3,2,1,0:T(8,128)(2,1)S(1)} %merge.5.refs_2_), channel_id=1, source_target_pairs={{0,1},{1,0},{2,3},{3,2},{4,5},{5,4},{6,7},{7,6},{8,9},{9,8},{10,11... | collective-permute-start | bytes 1572872 | tf_op jit(solution)/shard_map/ppermute | solution.py:68

commit v6 on v5

--- a/solution.py
+++ b/solution.py
@@ -48,6 +48,19 @@
     )(*arrays)
 
 
+def fetch(array):
+    def kernel(array_ref, out_ref):
+        out_ref[...] = array_ref[...]
+
+    return pl.pallas_call(
+        kernel,
+        out_shape=jax.ShapeDtypeStruct(array.shape, array.dtype),
+        in_specs=[pl.BlockSpec(memory_space=pltpu.VMEM)],
+        out_specs=pl.BlockSpec(memory_space=pltpu.VMEM),
+        name="fetch",
+    )(array)
+
+
 def z_forward(block, grid):
     depth, width, cores = grid
     count = depth * width * cores
@@ -77,9 +90,12 @@
     depth, width, cores = grid
     blocks_refs, refs = refs[: 2 * len(groups)], refs[2 * len(groups) :]
     kept_refs, refs = refs[: 2 * kept], refs[2 * kept :]
-    out_refs, scratch = refs[: 2 - last], refs[2 - last :]
+    out_refs, scratch = list(refs[: 2 - last]), list(refs[2 - last :])
+    if last:
+        result_ref = out_refs[0]
+        out_refs[0], sems = scratch.pop(0), scratch.pop(0)
     tok = query_ref.shape[0]
-    dim = blocks_refs[0].shape[-1] // STEP_HEADS
+    dim = blocks_refs[0].shape[-1] // KV_HEADS
     rows = GROUP * tok
     part_rows = rows // PARTS
     heads = part_rows // tok
@@ -97,22 +113,21 @@
     if scratch:
         bias_ref = scratch[0]
 
-        @pl.when(pl.program_id(0) == 0)
-        def _():
-            row = lax.broadcasted_iota(jnp.int32, (tok, tok), 0)
-            key = lax.broadcasted_iota(jnp.int32, (tok, tok), 1)
-            for at, (dz, dc, dy, _, _) in enumerate(pieces):
-                if dz:
-                    limit = jnp.where(zz >= dz, 0, tok) + 0 * key
-                elif dy:
-                    limit = jnp.where(yy == 1, 0, tok) + 0 * key
-                elif dc:
-                    limit = jnp.where(cc == 1, 0, tok) + 0 * key
-                else:
-                    limit = key
-                bias_ref[:, at * tok : (at + 1) * tok] = jnp.where(
-                    limit <= row, 0.0, masked_score
-                )
+        row = lax.broadcasted_iota(jnp.int32, (tok, tok), 0)
+        key = lax.broadcasted_iota(jnp.int32, (tok, tok), 1)
+        for at, (dz, dc, dy, _, _) in enumerate(pieces):
+            if dz:
+                limit = jnp.where(zz >= dz, 0, tok) + 0 * key
+            elif dy:
+                limit = jnp.where(yy == 1, 0, tok) + 0 * key
+            elif dc:
+                limit = jnp.where(cc == 1, 0, tok) + 0 * key
+            else:
+                limit = key
+            bias_ref[:, at * tok : (at + 1) * tok] = jnp.where(limit <= row, 0.0, masked_score)
+
+    def column(index):
+        return pl.ds(pl.multiple_of(index * dim, dim), dim)
 
     def emit(head, part, result, level):
         here = slice(part * part_rows, (part + 1) * part_rows)
@@ -122,22 +137,23 @@
             return
         result = result.astype(out_refs[0].dtype)
         for index in range(heads):
-            at = ((head * PARTS + part) * heads + index) * dim
-            out_refs[0][:, at : at + dim] = result[index * tok : (index + 1) * tok]
+            out_refs[0][:, column((head * PARTS + part) * heads + index)] = result[
+                index * tok : (index + 1) * tok
+            ]
 
     def attend(used, span):
-        for head in range(STEP_HEADS):
-            column = slice(head * dim, (head + 1) * dim)
-            keys = jnp.concatenate([ref[at, 0, :, column] for _, _, _, ref, at in used], axis=0)
-            values = jnp.concatenate([ref[at, 1, :, column] for _, _, _, ref, at in used], axis=0)
+        def one(head):
+            span_of = column(head)
+            keys = jnp.concatenate([ref[at, 0, :, span_of] for _, _, _, ref, at in used], axis=0)
+            values = jnp.concatenate([ref[at, 1, :, span_of] for _, _, _, ref, at in used], axis=0)
             values = jnp.concatenate([values, jnp.ones_like(values)], axis=1)
             first_head = head * GROUP
             for part in range(PARTS):
                 here = slice(part * part_rows, (part + 1) * part_rows)
                 query = jnp.concatenate(
                     [
-                        query_ref[:, at * dim : (at + 1) * dim]
-                        for at in range(first_head + part * heads, first_head + (part + 1) * heads)
+                        query_ref[:, column(first_head + index)]
+                        for index in range(part * heads, (part + 1) * heads)
                     ],
                     axis=0,
                 )
@@ -177,11 +193,28 @@
                     lambda: peak + jnp.log2(denominator),
                 )
 
+        all_heads(one)
+
     def hand_on():
-        for head in range(STEP_HEADS):
+        def one(head):
             for part in range(PARTS):
                 here = slice(part * part_rows, (part + 1) * part_rows)
                 emit(head, part, kept_refs[0][head, here, :], lambda: kept_refs[1][head, here, :])
+
+        all_heads(one)
+
+    def out_copy(step):
+        span = STEP_HEADS * GROUP * dim
+        here = pl.ds(pl.multiple_of(step * span, span), span)
+        return pltpu.make_async_copy(out_refs[0].at[:, here], result_ref.at[:, here], sems.at[step])
+
+    def all_heads(one):
+        @pl.loop(0, KV_HEADS // STEP_HEADS)
+        def _(step):
+            for index in range(STEP_HEADS):
+                one(step * STEP_HEADS + index)
+            if last:
+                out_copy(step).start()
 
     near = width * cores * tok if lowest == 0 else 0
     levels = sorted(set(range(lowest, highest + 1)))
@@ -207,6 +240,12 @@
             attend(used, span)
 
         below = level
+
+    if last:
+
+        @pl.loop(0, KV_HEADS // STEP_HEADS)
+        def _(step):
+            out_copy(step).wait()
 
 
 def solution(mesh):
@@ -223,20 +262,18 @@
             for array in (query_rows, key_rows, value_rows)
         )
         block = stack([key_rows, value_rows], "pack")
+        queries = fetch(query_rows)
         rows_of = []
         for dz in range(depth):
             row = [block, y_swap(block, grid)] if width == 2 else [block]
             if dz + 1 < depth:
                 following = z_forward(block, grid)
-                block, row = lax.optimization_barrier((following, row))
+                block, row, queries = lax.optimization_barrier((following, row, queries))
             rows_of.append(row)
 
-        query_spec = pl.BlockSpec(
-            (tok, STEP_HEADS * columns // KV_HEADS), lambda step: (0, step)
-        )
-        state_spec = pl.BlockSpec((STEP_HEADS, rows, dim), lambda step: (step, 0, 0))
-        state_shape = pltpu.HBM((KV_HEADS, rows, dim), jnp.float32)
-
+        whole = pl.BlockSpec(memory_space=pltpu.VMEM)
+        state_shape = jax.ShapeDtypeStruct((KV_HEADS, rows, dim), jnp.float32)
+        steps = KV_HEADS // STEP_HEADS
         def merge(span):
             merged = stack([block for dz in span for block in rows_of[dz]], "merge")
             return [merged, core_swap(merged, grid)]
@@ -246,28 +283,26 @@
             count = sum(2 * len(group) for group in groups)
             keys = tok * count
             masked = spans[0][0] == 0 or spans[-1][-1] - spans[0][0] > 3
+            scratch = []
+            if last:
+                scratch += [pltpu.VMEM((tok, columns), query_rows.dtype)]
+                scratch += [pltpu.SemaphoreType.DMA((steps,))]
+            if masked:
+                scratch += [pltpu.VMEM((tok, keys), jnp.float32)]
             return pl.pallas_call(
                 functools.partial(attend_kernel, grid, groups, bool(state), last),
                 out_shape=query_rows if last else [state_shape] * 2,
-                grid=(KV_HEADS // STEP_HEADS,),
-                in_specs=[query_spec]
-                + [
-                    pl.BlockSpec(
-                        (operand.shape[0], 2, tok, STEP_HEADS * dim), lambda step: (0, 0, 0, step)
-                    )
-                    for operand in operands
-                ]
-                + [state_spec] * len(state),
-                out_specs=query_spec if last else [state_spec] * 2,
-                scratch_shapes=[pltpu.VMEM((tok, keys), jnp.float32)] if masked else [],
-                compiler_params=pltpu.CompilerParams(vmem_limit_bytes=40 * 2**20),
+                in_specs=[whole] * (1 + len(operands) + len(state)),
+                out_specs=pl.BlockSpec(memory_space=pltpu.HBM) if last else [whole] * 2,
+                scratch_shapes=scratch,
+                compiler_params=pltpu.CompilerParams(vmem_limit_bytes=24 * 2**20),
                 cost_estimate=pl.CostEstimate(
                     flops=4 * HEADS * tok * keys * dim,
                     bytes_accessed=4 * HEADS * tok * dim,
                     transcendentals=HEADS * tok * keys,
                 ),
                 name="attend_last" if last else "attend_first",
-            )(query_rows, *operands, *state)
+            )(queries, *operands, *state)
 
         early = [range(0, 2)]
         late = [range(2, depth - 1), range(depth - 1, depth)]
@@ -276,7 +311,6 @@
         operands, rows_of[-1][0] = lax.optimization_barrier((operands, rows_of[-1][0]))
         state = phase(early, operands, [], False)
         rows_of[-1], state = lax.optimization_barrier((rows_of[-1], state))
-        state = [pltpu.with_memory_space_constraint(array, pltpu.HBM) for array in state]
         operands = [operand for span in late for operand in merge(span)]
         return phase(late, operands, list(state), True)
 

time: 51.8 us -> 47.4 us (0.915)
  waiting for transfers between devices: 17.9 us -> 14.8 us
  Pallas kernels: 20.1 us -> 18.8 us
    pallas_call x2, Pallas kernels: 19 us -> 14.7 us  [phase(): pl.pallas_call(functools.partial(attend_kernel, grid, groups, bool(state)...]
    ppermute x4, waiting for transfers between devices: 12.6 us -> 9.54 us  [y_swap(): lax.ppermute(block, 'tp', [(at, at ^ cores) for at in range(depth * width...]
    pallas_call x0 -> x1, Pallas kernels: none -> 3.04 us  [fetch(): pl.pallas_call(kernel, out_shape=jax.ShapeDtypeStruct(array.shape, array....]
  transfers between devices with their start and end apart: 10 -> 10, of which waited for: 7 -> 7; matrix products, arithmetic and copies ran while one was open for 0% -> 0% of each run, Pallas kernels for 18% -> 21%
where the time goes in v6:
time: 47.4 us; the launch traced here: 47.3 us
  Pallas kernels  18.8 us (40%)
  waiting for transfers between devices  14.8 us (31%)
  starting transfers between devices  13.6 us (29%)
    pallas_call x2, Pallas kernels, phase(): pl.pallas_call(functools.partial(attend_kernel, grid, groups, bool(state)...  14.7 us
    ppermute x4, waiting for transfers between devices, y_swap(): lax.ppermute(block, 'tp', [(at, at ^ cores) for at in range(depth * width...  9.54 us
    ppermute x3, starting transfers between devices, z_forward(): lax.ppermute(block, 'tp', [(at, (at + width * cores) % count) for at in r...  5.69 us
    ppermute x3, starting transfers between devices, core_swap(): lax.ppermute(blocks, 'tp', [(at, at ^ 1) for at in range(depth * width *...  4.61 us
    ppermute x3, waiting for transfers between devices, z_forward(): lax.ppermute(block, 'tp', [(at, (at + width * cores) % count) for at in r...  3.39 us
    ppermute x4, starting transfers between devices, y_swap(): lax.ppermute(block, 'tp', [(at, at ^ cores) for at in range(depth * width...  3.26 us
    pallas_call x1, Pallas kernels, fetch(): pl.pallas_call(kernel, out_shape=jax.ShapeDtypeStruct(array.shape, array....  3.04 us
    ppermute x3, waiting for transfers between devices, core_swap(): lax.ppermute(blocks, 'tp', [(at, at ^ 1) for at in range(depth * width *...  1.88 us
  transfers between devices with their start and end apart: 10, of which 7 were waited for; matrix products, arithmetic and copies ran while one was open for 0% of the time, Pallas kernels for 21%

profile of v6, /device:TPU:25, one launch (start us, length us, event | category | flops | bytes accessed | tf_op | source)
XLA Modules:
  0.0 47.3 jit_solution(13785827209906224890)
XLA Ops:
  0.0 1.0 %pack.1.refs_0_ = bf16[2,64,1024]{2,1,0:T(8,128)(2,1)S(1)} custom-call(bf16[64,1024]{1,0:T(8,128)(2,1)} %refs_0_.1, bf16[64,1024]{1,0:T(8,128)(2,1)} %refs_1_.1), custom_call_target="tpu_custom_call" | custom-call | tf_op jit(solution)/shard_map/pack/pallas_call | solution.py:41
  1.0 1.3 %collective-permute-start.1 = (bf16[2,64,1024]{2,1,0:T(8,128)(2,1)S(1)}, bf16[2,64,1024]{2,1,0:T(8,128)(2,1)S(1)}, u32[]{:S(2)}, u32[]{:S(2)}) collective-permute-start(bf16[2,64,1024]{2,1,0:T(8,128)(2,1)S(1)} %pack.1.refs_0_), channel_id=1, source_target_pairs={{0,2},{1,3},{2,0},{3,1},{4,6},{5,7},{6,4},{7,5},{8,10},{9,11},{10,... | collective-permute-start | bytes 786440 | tf_op jit(solution)/shard_map/ppermute | solution.py:74
  2.3 0.0 collective-permute-start
  2.3 3.0 %fetch.1.query_ref = bf16[64,16384]{1,0:T(8,128)(2,1)} custom-call(bf16[64,16384]{1,0:T(8,128)(2,1)} %array_ref.1), custom_call_target="tpu_custom_call" | custom-call | tf_op jit(solution)/shard_map/fetch/pallas_call | solution.py:55
  5.3 0.0 copy-start
  5.3 2.9 %collective-permute-done.1.refs_1_ = bf16[2,64,1024]{2,1,0:T(8,128)(2,1)S(1)} collective-permute-done((bf16[2,64,1024]{2,1,0:T(8,128)(2,1)S(1)}, bf16[2,64,1024]{2,1,0:T(8,128)(2,1)S(1)}, u32[]{:S(2)}, u32[]{:S(2)}) %collective-permute-start.1) | collective-permute-done | bytes 262176 | tf_op jit(solution)/shard_map/ppermute | solution.py:74
  8.2 0.9 %collective-permute-done.refs_2_ = bf16[2,64,1024]{2,1,0:T(8,128)(2,1)S(1)} collective-permute-done((bf16[2,64,1024]{2,1,0:T(8,128)(2,1)S(1)}, bf16[2,64,1024]{2,1,0:T(8,128)(2,1)S(1)}, u32[]{:S(2)}, u32[]{:S(2)}) %collective-permute-start) | collective-permute-done | bytes 262176 | tf_op jit(solution)/shard_map/ppermute | solution.py:67
  9.2 0.3 collective-permute-start.3
  9.5 2.0 %collective-permute-start.2 = (bf16[2,64,1024]{2,1,0:T(8,128)(2,1)S(1)}, bf16[2,64,1024]{2,1,0:T(8,128)(2,1)S(1)}, u32[]{:S(2)}, u32[]{:S(2)}) collective-permute-start(bf16[2,64,1024]{2,1,0:T(8,128)(2,1)S(1)} %collective-permute-done.refs_2_), channel_id=1, source_target_pairs={{0,4},{1,5},{2,6},{3,7},{4,8},{5,9},{6,10},{7,11},{8,12},{9,13},{1... | collective-permute-start | bytes 786440 | tf_op jit(solution)/shard_map/ppermute | solution.py:67
  11.5 3.6 %collective-permute-done.3.refs_3_ = bf16[2,64,1024]{2,1,0:T(8,128)(2,1)S(1)} collective-permute-done((bf16[2,64,1024]{2,1,0:T(8,128)(2,1)S(1)}, bf16[2,64,1024]{2,1,0:T(8,128)(2,1)S(1)}, u32[]{:S(2)}, u32[]{:S(2)}) %collective-permute-start.3) | collective-permute-done | bytes 262176 | tf_op jit(solution)/shard_map/ppermute | solution.py:74
  15.1 0.2 collective-permute-done.2.refs_0_
  15.3 0.1 merge.4.refs_0_
  15.3 3.0 %collective-permute-start.7 = (bf16[4,2,64,1024]{3,2,1,0:T(8,128)(2,1)S(1)}, bf16[4,2,64,1024]{3,2,1,0:T(8,128)(2,1)S(1)}, u32[]{:S(2)}, u32[]{:S(2)}) collective-permute-start(bf16[4,2,64,1024]{3,2,1,0:T(8,128)(2,1)S(1)} %merge.4.refs_0_), channel_id=1, source_target_pairs={{0,1},{1,0},{2,3},{3,2},{4,5},{5,4},{6,7},{7,6},{8,9},{9,8},{10,11... | collective-permute-start | bytes 3145736 | tf_op jit(solution)/shard_map/ppermute | solution.py:81
  18.3 1.2 %collective-permute-start.5 = (bf16[2,64,1024]{2,1,0:T(8,128)(2,1)S(1)}, bf16[2,64,1024]{2,1,0:T(8,128)(2,1)S(1)}, u32[]{:S(2)}, u32[]{:S(2)}) collective-permute-start(bf16[2,64,1024]{2,1,0:T(8,128)(2,1)S(1)} %collective-permute-done.2.refs_0_), channel_id=1, source_target_pairs={{0,2},{1,3},{2,0},{3,1},{4,6},{5,7},{6,4},{7,5},{8,10},{9,11},{10,... | collective-permute-start | bytes 786440 | tf_op jit(solution)/shard_map/ppermute | solution.py:74
  19.5 3.7 %collective-permute-start.4 = (bf16[2,64,1024]{2,1,0:T(8,128)(2,1)S(1)}, bf16[2,64,1024]{2,1,0:T(8,128)(2,1)S(1)}, u32[]{:S(2)}, u32[]{:S(2)}) collective-permute-start(bf16[2,64,1024]{2,1,0:T(8,128)(2,1)S(1)} %collective-permute-done.2.refs_0_), channel_id=1, source_target_pairs={{0,4},{1,5},{2,6},{3,7},{4,8},{5,9},{6,10},{7,11},{8,12},{9,13},{1... | collective-permute-start | bytes 786440 | tf_op jit(solution)/shard_map/ppermute | solution.py:67
  23.2 3.1 %collective-permute-done.5.refs_1_ = bf16[2,64,1024]{2,1,0:T(8,128)(2,1)S(1)} collective-permute-done((bf16[2,64,1024]{2,1,0:T(8,128)(2,1)S(1)}, bf16[2,64,1024]{2,1,0:T(8,128)(2,1)S(1)}, u32[]{:S(2)}, u32[]{:S(2)}) %collective-permute-start.5) | collective-permute-done | bytes 262176 | tf_op jit(solution)/shard_map/ppermute | solution.py:74
  26.2 2.3 %collective-permute-done.4.refs_0_ = bf16[2,64,1024]{2,1,0:T(8,128)(2,1)S(1)} collective-permute-done((bf16[2,64,1024]{2,1,0:T(8,128)(2,1)S(1)}, bf16[2,64,1024]{2,1,0:T(8,128)(2,1)S(1)}, u32[]{:S(2)}, u32[]{:S(2)}) %collective-permute-start.4) | collective-permute-done | bytes 262176 | tf_op jit(solution)/shard_map/ppermute | solution.py:67
  28.5 0.5 %collective-permute-start.8 = (bf16[2,64,1024]{2,1,0:T(8,128)(2,1)S(1)}, bf16[2,64,1024]{2,1,0:T(8,128)(2,1)S(1)}, u32[]{:S(2)}, u32[]{:S(2)}) collective-permute-start(bf16[2,64,1024]{2,1,0:T(8,128)(2,1)S(1)} %collective-permute-done.4.refs_0_), channel_id=1, source_target_pairs={{0,2},{1,3},{2,0},{3,1},{4,6},{5,7},{6,4},{7,5},{8,10},{9,11},{10,... | collective-permute-start | bytes 786440 | tf_op jit(solution)/shard_map/ppermute | solution.py:74
  29.0 1.5 %collective-permute-start.6 = (bf16[2,2,64,1024]{3,2,1,0:T(8,128)(2,1)S(1)}, bf16[2,2,64,1024]{3,2,1,0:T(8,128)(2,1)S(1)}, u32[]{:S(2)}, u32[]{:S(2)}) collective-permute-start(bf16[2,2,64,1024]{3,2,1,0:T(8,128)(2,1)S(1)} %merge.3.refs_0_), channel_id=1, source_target_pairs={{0,1},{1,0},{2,3},{3,2},{4,5},{5,4},{6,7},{7,6},{8,9},{9,8},{10,11... | collective-permute-start | bytes 1572872 | tf_op jit(solution)/shard_map/ppermute | solution.py:81
  30.5 0.0 collective-permute-done.7.refs_1_
  30.5 0.0 copy-done
  30.5 6.9 %attend_first.1 = (f32[8,1024,128]{2,1,0:T(8,128)S(1)}, f32[8,1024,128]{2,1,0:T(8,128)S(1)}) custom-call(bf16[64,16384]{1,0:T(8,128)(2,1)S(1)} %copy-done, bf16[4,2,64,1024]{3,2,1,0:T(8,128)(2,1)S(1)} %merge.4.refs_0_, bf16[4,2,64,1024]{3,2,1,0:T(8,128)(2,1)S(1)} %collective-permute-done.7.refs_1_), custom_call_target="tpu_custom_call" | custom-call | flops 2147483648 | bytes 4194304 | tf_op jit(solution)/shard_map/attend_first/pallas_call | solution.py:292
  37.4 0.0 collective-permute-done.8.refs_1_
  37.5 0.1 collective-permute-start.9
  37.6 0.0 collective-permute-done.6.refs_1_
  37.6 1.9 %collective-permute-done.9.refs_3_ = bf16[2,2,64,1024]{3,2,1,0:T(8,128)(2,1)S(1)} collective-permute-done((bf16[2,2,64,1024]{3,2,1,0:T(8,128)(2,1)S(1)}, bf16[2,2,64,1024]{3,2,1,0:T(8,128)(2,1)S(1)}, u32[]{:S(2)}, u32[]{:S(2)}) %collective-permute-start.9) | collective-permute-done | bytes 524320 | tf_op jit(solution)/shard_map/ppermute | solution.py:81
  39.5 7.8 %attend_last.1 = bf16[64,16384]{1,0:T(8,128)(2,1)} custom-call(bf16[64,16384]{1,0:T(8,128)(2,1)S(1)} %copy-done, bf16[2,2,64,1024]{3,2,1,0:T(8,128)(2,1)S(1)} %merge.3.refs_0_, bf16[2,2,64,1024]{3,2,1,0:T(8,128)(2,1)S(1)} %collective-permute-done.6.refs_1_, bf16[2,2,64,1024]{3,2,1,0:T(8,128)(2,1)S(1)} %merge.5.refs_2_, ...), custom_call_target="tpu_custom_call" | custom-call | flops 2147483648 | bytes 4194304 | tf_op jit(solution)/shard_map/attend_last/pallas_call | solution.py:292
  (2 shorter events, 0.1 us)
Async XLA Ops:
  1.0 7.2 %collective-permute-start.1 = (bf16[2,64,1024]{2,1,0:T(8,128)(2,1)S(1)}, bf16[2,64,1024]{2,1,0:T(8,128)(2,1)S(1)}, u32[]{:S(2)}, u32[]{:S(2)}) collective-permute-start(bf16[2,64,1024]{2,1,0:T(8,128)(2,1)S(1)} %pack.1.refs_0_), channel_id=1, source_target_pairs={{0,2},{1,3},{2,0},{3,1},{4,6},{5,7},{6,4},{7,5},{8,10},{9,11},{10,... | collective-permute-start | bytes 786440 | tf_op jit(solution)/shard_map/ppermute | solution.py:74
  2.3 6.9 %collective-permute-start = (bf16[2,64,1024]{2,1,0:T(8,128)(2,1)S(1)}, bf16[2,64,1024]{2,1,0:T(8,128)(2,1)S(1)}, u32[]{:S(2)}, u32[]{:S(2)}) collective-permute-start(bf16[2,64,1024]{2,1,0:T(8,128)(2,1)S(1)} %pack.1.refs_0_), channel_id=1, source_target_pairs={{0,4},{1,5},{2,6},{3,7},{4,8},{5,9},{6,10},{7,11},{8,12},{9,13},{1... | collective-permute-start | bytes 786440 | tf_op jit(solution)/shard_map/ppermute | solution.py:67
  5.3 25.2 %copy-start = (bf16[64,16384]{1,0:T(8,128)(2,1)S(1)}, bf16[64,16384]{1,0:T(8,128)(2,1)}, u32[]{:S(2)}) copy-start(bf16[64,16384]{1,0:T(8,128)(2,1)} %fetch.1.query_ref) | copy-start | bytes 6291460
  9.2 5.9 %collective-permute-start.3 = (bf16[2,64,1024]{2,1,0:T(8,128)(2,1)S(1)}, bf16[2,64,1024]{2,1,0:T(8,128)(2,1)S(1)}, u32[]{:S(2)}, u32[]{:S(2)}) collective-permute-start(bf16[2,64,1024]{2,1,0:T(8,128)(2,1)S(1)} %collective-permute-done.refs_2_), channel_id=1, source_target_pairs={{0,2},{1,3},{2,0},{3,1},{4,6},{5,7},{6,4},{7,5},{8,10},{9,11},{10,... | collective-permute-start | bytes 786440 | tf_op jit(solution)/shard_map/ppermute | solution.py:74
  9.5 5.8 %collective-permute-start.2 = (bf16[2,64,1024]{2,1,0:T(8,128)(2,1)S(1)}, bf16[2,64,1024]{2,1,0:T(8,128)(2,1)S(1)}, u32[]{:S(2)}, u32[]{:S(2)}) collective-permute-start(bf16[2,64,1024]{2,1,0:T(8,128)(2,1)S(1)} %collective-permute-done.refs_2_), channel_id=1, source_target_pairs={{0,4},{1,5},{2,6},{3,7},{4,8},{5,9},{6,10},{7,11},{8,12},{9,13},{1... | collective-permute-start | bytes 786440 | tf_op jit(solution)/shard_map/ppermute | solution.py:67
  15.3 15.2 %collective-permute-start.7 = (bf16[4,2,64,1024]{3,2,1,0:T(8,128)(2,1)S(1)}, bf16[4,2,64,1024]{3,2,1,0:T(8,128)(2,1)S(1)}, u32[]{:S(2)}, u32[]{:S(2)}) collective-permute-start(bf16[4,2,64,1024]{3,2,1,0:T(8,128)(2,1)S(1)} %merge.4.refs_0_), channel_id=1, source_target_pairs={{0,1},{1,0},{2,3},{3,2},{4,5},{5,4},{6,7},{7,6},{8,9},{9,8},{10,11... | collective-permute-start | bytes 3145736 | tf_op jit(solution)/shard_map/ppermute | solution.py:81
  18.3 7.9 %collective-permute-start.5 = (bf16[2,64,1024]{2,1,0:T(8,128)(2,1)S(1)}, bf16[2,64,1024]{2,1,0:T(8,128)(2,1)S(1)}, u32[]{:S(2)}, u32[]{:S(2)}) collective-permute-start(bf16[2,64,1024]{2,1,0:T(8,128)(2,1)S(1)} %collective-permute-done.2.refs_0_), channel_id=1, source_target_pairs={{0,2},{1,3},{2,0},{3,1},{4,6},{5,7},{6,4},{7,5},{8,10},{9,11},{10,... | collective-permute-start | bytes 786440 | tf_op jit(solution)/shard_map/ppermute | solution.py:74
  19.5 9.0 %collective-permute-start.4 = (bf16[2,64,1024]{2,1,0:T(8,128)(2,1)S(1)}, bf16[2,64,1024]{2,1,0:T(8,128)(2,1)S(1)}, u32[]{:S(2)}, u32[]{:S(2)}) collective-permute-start(bf16[2,64,1024]{2,1,0:T(8,128)(2,1)S(1)} %collective-permute-done.2.refs_0_), channel_id=1, source_target_pairs={{0,4},{1,5},{2,6},{3,7},{4,8},{5,9},{6,10},{7,11},{8,12},{9,13},{1... | collective-permute-start | bytes 786440 | tf_op jit(solution)/shard_map/ppermute | solution.py:67
  28.5 8.9 %collective-permute-start.8 = (bf16[2,64,1024]{2,1,0:T(8,128)(2,1)S(1)}, bf16[2,64,1024]{2,1,0:T(8,128)(2,1)S(1)}, u32[]{:S(2)}, u32[]{:S(2)}) collective-permute-start(bf16[2,64,1024]{2,1,0:T(8,128)(2,1)S(1)} %collective-permute-done.4.refs_0_), channel_id=1, source_target_pairs={{0,2},{1,3},{2,0},{3,1},{4,6},{5,7},{6,4},{7,5},{8,10},{9,11},{10,... | collective-permute-start | bytes 786440 | tf_op jit(solution)/shard_map/ppermute | solution.py:74
  29.0 8.6 %collective-permute-start.6 = (bf16[2,2,64,1024]{3,2,1,0:T(8,128)(2,1)S(1)}, bf16[2,2,64,1024]{3,2,1,0:T(8,128)(2,1)S(1)}, u32[]{:S(2)}, u32[]{:S(2)}) collective-permute-start(bf16[2,2,64,1024]{3,2,1,0:T(8,128)(2,1)S(1)} %merge.3.refs_0_), channel_id=1, source_target_pairs={{0,1},{1,0},{2,3},{3,2},{4,5},{5,4},{6,7},{7,6},{8,9},{9,8},{10,11... | collective-permute-start | bytes 1572872 | tf_op jit(solution)/shard_map/ppermute | solution.py:81
  37.5 2.0 %collective-permute-start.9 = (bf16[2,2,64,1024]{3,2,1,0:T(8,128)(2,1)S(1)}, bf16[2,2,64,1024]{3,2,1,0:T(8,128)(2,1)S(1)}, u32[]{:S(2)}, u32[]{:S(2)}) collective-permute-start(bf16[2,2,64,1024]{3,2,1,0:T(8,128)(2,1)S(1)} %merge.5.refs_2_), channel_id=1, source_target_pairs={{0,1},{1,0},{2,3},{3,2},{4,5},{5,4},{6,7},{7,6},{8,9},{9,8},{10,11... | collective-permute-start | bytes 1572872 | tf_op jit(solution)/shard_map/ppermute | solution.py:81

commit v7 on v6

--- a/solution.py
+++ b/solution.py
@@ -48,19 +48,6 @@
     )(*arrays)
 
 
-def fetch(array):
-    def kernel(array_ref, out_ref):
-        out_ref[...] = array_ref[...]
-
-    return pl.pallas_call(
-        kernel,
-        out_shape=jax.ShapeDtypeStruct(array.shape, array.dtype),
-        in_specs=[pl.BlockSpec(memory_space=pltpu.VMEM)],
-        out_specs=pl.BlockSpec(memory_space=pltpu.VMEM),
-        name="fetch",
-    )(array)
-
-
 def z_forward(block, grid):
     depth, width, cores = grid
     count = depth * width * cores
@@ -91,6 +78,8 @@
     blocks_refs, refs = refs[: 2 * len(groups)], refs[2 * len(groups) :]
     kept_refs, refs = refs[: 2 * kept], refs[2 * kept :]
     out_refs, scratch = list(refs[: 2 - last]), list(refs[2 - last :])
+    if not kept:
+        source_ref, query_ref, query_sems = query_ref, scratch.pop(0), scratch.pop(0)
     if last:
         result_ref = out_refs[0]
         out_refs[0], sems = scratch.pop(0), scratch.pop(0)
@@ -129,13 +118,13 @@
     def column(index):
         return pl.ds(pl.multiple_of(index * dim, dim), dim)
 
-    def emit(head, part, result, level):
+    def emit(head, part, sums, peak):
         here = slice(part * part_rows, (part + 1) * part_rows)
         if not last:
-            out_refs[0][head, here, :] = result
-            out_refs[1][head, here, :] = level()
+            out_refs[0][head, here, :] = sums
+            out_refs[1][head, here, :] = jnp.broadcast_to(peak, (part_rows, dim))
             return
-        result = result.astype(out_refs[0].dtype)
+        result = (sums[:, :dim] * reciprocal(sums[:, dim:])).astype(out_refs[0].dtype)
         for index in range(heads):
             out_refs[0][:, column((head * PARTS + part) * heads + index)] = result[
                 index * tok : (index + 1) * tok
@@ -181,17 +170,11 @@
                     shifted = scores * factor - peak
                 weights = jnp.exp2(shifted).astype(jnp.bfloat16)
                 sums = jnp.dot(weights, values, preferred_element_type=jnp.float32)
-                numerator, denominator = sums[:, :dim], sums[:, dim:]
                 if kept:
                     carry = jnp.exp2(before - peak)
-                    numerator = numerator + carry * kept_refs[0][head, here, :]
-                    denominator = denominator + carry
-                emit(
-                    head,
-                    part,
-                    numerator * reciprocal(denominator),
-                    lambda: peak + jnp.log2(denominator),
-                )
+                    carry = jnp.concatenate([carry, carry], axis=1)
+                    sums = sums + carry * kept_refs[0][head, here, :]
+                emit(head, part, sums, peak)
 
         all_heads(one)
 
@@ -199,7 +182,7 @@
         def one(head):
             for part in range(PARTS):
                 here = slice(part * part_rows, (part + 1) * part_rows)
-                emit(head, part, kept_refs[0][head, here, :], lambda: kept_refs[1][head, here, :])
+                emit(head, part, kept_refs[0][head, here, :], kept_refs[1][head, here, :])
 
         all_heads(one)
 
@@ -208,9 +191,24 @@
         here = pl.ds(pl.multiple_of(step * span, span), span)
         return pltpu.make_async_copy(out_refs[0].at[:, here], result_ref.at[:, here], sems.at[step])
 
+    def query_copy(step):
+        span = STEP_HEADS * GROUP * dim
+        here = pl.ds(pl.multiple_of(step * span, span), span)
+        return pltpu.make_async_copy(
+            source_ref.at[:, here], query_ref.at[:, here], query_sems.at[step]
+        )
+
+    if not kept:
+
+        @pl.loop(0, KV_HEADS // STEP_HEADS)
+        def _(step):
+            query_copy(step).start()
+
     def all_heads(one):
         @pl.loop(0, KV_HEADS // STEP_HEADS)
         def _(step):
+            if not kept:
+                query_copy(step).wait()
             for index in range(STEP_HEADS):
                 one(step * STEP_HEADS + index)
             if last:
@@ -257,62 +255,71 @@
         tok, columns = query_rows.shape
         dim = key_rows.shape[1] // KV_HEADS
         rows = GROUP * tok
-        query_rows, key_rows, value_rows = (
+        pinned, key_rows, value_rows = (
             pltpu.with_memory_space_constraint(array, pltpu.HBM)
             for array in (query_rows, key_rows, value_rows)
         )
-        block = stack([key_rows, value_rows], "pack")
-        queries = fetch(query_rows)
-        rows_of = []
-        for dz in range(depth):
-            row = [block, y_swap(block, grid)] if width == 2 else [block]
-            if dz + 1 < depth:
-                following = z_forward(block, grid)
-                block, row, queries = lax.optimization_barrier((following, row, queries))
-            rows_of.append(row)
-
         whole = pl.BlockSpec(memory_space=pltpu.VMEM)
-        state_shape = jax.ShapeDtypeStruct((KV_HEADS, rows, dim), jnp.float32)
+        state_shapes = [
+            jax.ShapeDtypeStruct((KV_HEADS, rows, size), jnp.float32) for size in (2 * dim, dim)
+        ]
         steps = KV_HEADS // STEP_HEADS
-        def merge(span):
+
+        def phase(span, state):
+            last = span[-1] == depth - 1
             merged = stack([block for dz in span for block in rows_of[dz]], "merge")
-            return [merged, core_swap(merged, grid)]
-
-        def phase(spans, operands, state, last):
-            groups = [[dz for dz in span for _ in range(width)] for span in spans]
-            count = sum(2 * len(group) for group in groups)
-            keys = tok * count
-            masked = spans[0][0] == 0 or spans[-1][-1] - spans[0][0] > 3
+            operands = [merged, core_swap(merged, grid)]
+            groups = [[dz for dz in span for _ in range(width)]]
+            keys = tok * 2 * len(groups[0])
             scratch = []
+            if not state:
+                scratch += [pltpu.VMEM((tok, columns), query_rows.dtype)]
+                scratch += [pltpu.SemaphoreType.DMA((steps,))]
             if last:
                 scratch += [pltpu.VMEM((tok, columns), query_rows.dtype)]
                 scratch += [pltpu.SemaphoreType.DMA((steps,))]
-            if masked:
+            if span[0] == 0 or len(span) > 4:
                 scratch += [pltpu.VMEM((tok, keys), jnp.float32)]
             return pl.pallas_call(
                 functools.partial(attend_kernel, grid, groups, bool(state), last),
-                out_shape=query_rows if last else [state_shape] * 2,
-                in_specs=[whole] * (1 + len(operands) + len(state)),
+                out_shape=query_rows if last else state_shapes,
+                in_specs=[whole if state else pl.BlockSpec(memory_space=pltpu.HBM)]
+                + [whole] * (len(operands) + len(state)),
                 out_specs=pl.BlockSpec(memory_space=pltpu.HBM) if last else [whole] * 2,
                 scratch_shapes=scratch,
-                compiler_params=pltpu.CompilerParams(vmem_limit_bytes=24 * 2**20),
+                input_output_aliases={} if last or not state else {3: 0, 4: 1},
+                compiler_params=pltpu.CompilerParams(vmem_limit_bytes=16 * 2**20),
                 cost_estimate=pl.CostEstimate(
                     flops=4 * HEADS * tok * keys * dim,
                     bytes_accessed=4 * HEADS * tok * dim,
                     transcendentals=HEADS * tok * keys,
                 ),
-                name="attend_last" if last else "attend_first",
-            )(queries, *operands, *state)
-
-        early = [range(0, 2)]
-        late = [range(2, depth - 1), range(depth - 1, depth)]
-        late = [span for span in late if len(span)]
-        operands = merge(early[0])
-        operands, rows_of[-1][0] = lax.optimization_barrier((operands, rows_of[-1][0]))
-        state = phase(early, operands, [], False)
-        rows_of[-1], state = lax.optimization_barrier((rows_of[-1], state))
-        operands = [operand for span in late for operand in merge(span)]
-        return phase(late, operands, list(state), True)
+                name=f"attend_{span[0]}",
+            )(query_rows if state else pinned, *operands, *state)
+
+        spans = [range(0, 1), range(1, 2)]
+        spans += [range(at, min(at + 4, depth - 1)) for at in range(2, depth - 1, 4)]
+        spans += [range(depth - 1, depth)]
+        block = stack([key_rows, value_rows], "pack")
+        rows_of, state = [], []
+        for dz in range(depth):
+            rows_of.append([block, y_swap(block, grid)] if width == 2 else [block])
+            if dz + 1 == depth:
+                break
+            block = z_forward(block, grid)
+            at = dz - 1
+            if dz and spans[0][-1] <= at:
+                span = spans.pop(0)
+                state = phase(span, state)
+            if dz:
+                block, state, rows_of[dz] = lax.optimization_barrier((block, state, rows_of[dz]))
+            else:
+                block, rows_of[0] = lax.optimization_barrier((block, rows_of[0]))
+        while spans:
+            if len(spans) == 1:
+                rows_of[-1], state = lax.optimization_barrier((rows_of[-1], state))
+            state = phase(spans.pop(0), state)
+        return state
 
     spec = P(("groups", "tp"), None)
     return jax.shard_map(

time: 47.4 us -> 47.2 us (level)
  waiting for transfers between devices: 14.8 us -> 13.4 us
  Pallas kernels: 18.8 us -> 20 us
    ppermute x4, waiting for transfers between devices: 9.54 us -> 5.04 us  [y_swap(): lax.ppermute(block, 'tp', [(at, at ^ cores) for at in range(depth * width...]
    pallas_call x2 -> x4, Pallas kernels: 14.7 us -> 18.7 us  [phase(): pl.pallas_call(functools.partial(attend_kernel, grid, groups, bool(state)...]
    ppermute x3, waiting for transfers between devices: 3.39 us -> 6.54 us  [z_forward(): lax.ppermute(block, 'tp', [(at, (at + width * cores) % count) for at in r...]
    pallas_call x1 -> x0, Pallas kernels: 3.04 us -> none  [fetch(): pl.pallas_call(kernel, out_shape=jax.ShapeDtypeStruct(array.shape, array....]
    ppermute x3, starting transfers between devices: 5.69 us -> 3.59 us  [z_forward(): lax.ppermute(block, 'tp', [(at, (at + width * cores) % count) for at in r...]
    ppermute x4, starting transfers between devices: 3.26 us -> 5.04 us  [y_swap(): lax.ppermute(block, 'tp', [(at, at ^ cores) for at in range(depth * width...]
    ppermute x3 -> x4, starting transfers between devices: 4.61 us -> 5.01 us  [core_swap(): lax.ppermute(blocks, 'tp', [(at, at ^ 1) for at in range(depth * width *...]
    pallas_call x4 -> x5, Pallas kernels: 1.12 us -> 1.27 us  [stack(): pl.pallas_call(kernel, out_shape=jax.ShapeDtypeStruct((count, *arrays[0]....]
  transfers between devices with their start and end apart: 10 -> 11, of which waited for: 7 -> 9; matrix products, arithmetic and copies ran while one was open for 0% -> 0% of each run, Pallas kernels for 21% -> 28%
where the time goes in v7:
time: 47.2 us; the launch traced here: 47.1 us
  Pallas kernels  20 us (42%)
  starting transfers between devices  13.6 us (29%)
  waiting for transfers between devices  13.4 us (28%)
    pallas_call x4, Pallas kernels, phase(): pl.pallas_call(functools.partial(attend_kernel, grid, groups, bool(state)...  18.7 us
    ppermute x3, waiting for transfers between devices, z_forward(): lax.ppermute(block, 'tp', [(at, (at + width * cores) % count) for at in r...  6.54 us
    ppermute x4, waiting for transfers between devices, y_swap(): lax.ppermute(block, 'tp', [(at, at ^ cores) for at in range(depth * width...  5.04 us
    ppermute x4, starting transfers between devices, y_swap(): lax.ppermute(block, 'tp', [(at, at ^ cores) for at in range(depth * width...  5.04 us
    ppermute x4, starting transfers between devices, core_swap(): lax.ppermute(blocks, 'tp', [(at, at ^ 1) for at in range(depth * width *...  5.01 us
    ppermute x3, starting transfers between devices, z_forward(): lax.ppermute(block, 'tp', [(at, (at + width * cores) % count) for at in r...  3.59 us
    ppermute x4, waiting for transfers between devices, core_swap(): lax.ppermute(blocks, 'tp', [(at, at ^ 1) for at in range(depth * width *...  1.82 us
    pallas_call x5, Pallas kernels, stack(): pl.pallas_call(kernel, out_shape=jax.ShapeDtypeStruct((count, *arrays[0]....  1.27 us
  transfers between devices with their start and end apart: 11, of which 9 were waited for; matrix products, arithmetic and copies ran while one was open for 0% of the time, Pallas kernels for 28%

profile of v7, /device:TPU:25, one launch (start us, length us, event | category | flops | bytes accessed | tf_op | source)
XLA Modules:
  0.0 47.1 jit_solution(10194004075698911059)
XLA Ops:
  0.0 0.0 copy-start
  0.0 1.1 %pack.1.refs_0_ = bf16[2,64,1024]{2,1,0:T(8,128)(2,1)S(1)} custom-call(bf16[64,1024]{1,0:T(8,128)(2,1)} %refs_0_.1, bf16[64,1024]{1,0:T(8,128)(2,1)} %refs_1_.1), custom_call_target="tpu_custom_call" | custom-call | tf_op jit(solution)/shard_map/pack/pallas_call | solution.py:41
  1.1 0.1 collective-permute-start
  1.2 1.3 %collective-permute-start.1 = (bf16[2,64,1024]{2,1,0:T(8,128)(2,1)S(1)}, bf16[2,64,1024]{2,1,0:T(8,128)(2,1)S(1)}, u32[]{:S(2)}, u32[]{:S(2)}) collective-permute-start(bf16[2,64,1024]{2,1,0:T(8,128)(2,1)S(1)} %pack.1.refs_0_), channel_id=1, source_target_pairs={{0,2},{1,3},{2,0},{3,1},{4,6},{5,7},{6,4},{7,5},{8,10},{9,11},{10,... | collective-permute-start | bytes 786440 | tf_op jit(solution)/shard_map/ppermute | solution.py:61
  2.5 5.9 %collective-permute-done.refs_0_ = bf16[2,64,1024]{2,1,0:T(8,128)(2,1)S(1)} collective-permute-done((bf16[2,64,1024]{2,1,0:T(8,128)(2,1)S(1)}, bf16[2,64,1024]{2,1,0:T(8,128)(2,1)S(1)}, u32[]{:S(2)}, u32[]{:S(2)}) %collective-permute-start) | collective-permute-done | bytes 262176 | tf_op jit(solution)/shard_map/ppermute | solution.py:54
  8.4 0.1 collective-permute-done.1.refs_1_
  8.5 1.6 %collective-permute-start.3 = (bf16[2,2,64,1024]{3,2,1,0:T(8,128)(2,1)S(1)}, bf16[2,2,64,1024]{3,2,1,0:T(8,128)(2,1)S(1)}, u32[]{:S(2)}, u32[]{:S(2)}) collective-permute-start(bf16[2,2,64,1024]{3,2,1,0:T(8,128)(2,1)S(1)} %merge.4.refs_0_), channel_id=1, source_target_pairs={{0,1},{1,0},{2,3},{3,2},{4,5},{5,4},{6,7},{7,6},{8,9},{9,8},{10,11... | collective-permute-start | bytes 1572872 | tf_op jit(solution)/shard_map/ppermute | solution.py:68
  10.1 1.7 %collective-permute-start.2 = (bf16[2,64,1024]{2,1,0:T(8,128)(2,1)S(1)}, bf16[2,64,1024]{2,1,0:T(8,128)(2,1)S(1)}, u32[]{:S(2)}, u32[]{:S(2)}) collective-permute-start(bf16[2,64,1024]{2,1,0:T(8,128)(2,1)S(1)} %collective-permute-done.refs_0_), channel_id=1, source_target_pairs={{0,4},{1,5},{2,6},{3,7},{4,8},{5,9},{6,10},{7,11},{8,12},{9,13},{1... | collective-permute-start | bytes 786440 | tf_op jit(solution)/shard_map/ppermute | solution.py:54
  11.8 1.2 %collective-permute-start.4 = (bf16[2,64,1024]{2,1,0:T(8,128)(2,1)S(1)}, bf16[2,64,1024]{2,1,0:T(8,128)(2,1)S(1)}, u32[]{:S(2)}, u32[]{:S(2)}) collective-permute-start(bf16[2,64,1024]{2,1,0:T(8,128)(2,1)S(1)} %collective-permute-done.refs_0_), channel_id=1, source_target_pairs={{0,2},{1,3},{2,0},{3,1},{4,6},{5,7},{6,4},{7,5},{8,10},{9,11},{10,... | collective-permute-start | bytes 786440 | tf_op jit(solution)/shard_map/ppermute | solution.py:61
  13.1 0.0 collective-permute-done.3.refs_1_
  13.1 4.7 %attend_0.1 = (f32[8,1024,256]{2,1,0:T(8,128)S(1)}, f32[8,1024,128]{2,1,0:T(8,128)S(1)}) custom-call(bf16[64,16384]{1,0:T(8,128)(2,1)} %query_ref.7, bf16[2,2,64,1024]{3,2,1,0:T(8,128)(2,1)S(1)} %merge.4.refs_0_, bf16[2,2,64,1024]{3,2,1,0:T(8,128)(2,1)S(1)} %collective-permute-done.3.refs_1_), custom_call_target="tpu_custom_call" | custom-call | flops 1073741824 | bytes 4194304 | tf_op jit(solution)/shard_map/attend_0/pallas_call | solution.py:283
  17.8 0.1 collective-permute-done.2.refs_0_
  18.0 1.4 %collective-permute-done.4.refs_1_ = bf16[2,64,1024]{2,1,0:T(8,128)(2,1)S(1)} collective-permute-done((bf16[2,64,1024]{2,1,0:T(8,128)(2,1)S(1)}, bf16[2,64,1024]{2,1,0:T(8,128)(2,1)S(1)}, u32[]{:S(2)}, u32[]{:S(2)}) %collective-permute-start.4) | collective-permute-done | bytes 262176 | tf_op jit(solution)/shard_map/ppermute | solution.py:61
  19.4 1.2 %collective-permute-start.6 = (bf16[2,2,64,1024]{3,2,1,0:T(8,128)(2,1)S(1)}, bf16[2,2,64,1024]{3,2,1,0:T(8,128)(2,1)S(1)}, u32[]{:S(2)}, u32[]{:S(2)}) collective-permute-start(bf16[2,2,64,1024]{3,2,1,0:T(8,128)(2,1)S(1)} %merge.5.refs_0_), channel_id=1, source_target_pairs={{0,1},{1,0},{2,3},{3,2},{4,5},{5,4},{6,7},{7,6},{8,9},{9,8},{10,11... | collective-permute-start | bytes 1572872 | tf_op jit(solution)/shard_map/ppermute | solution.py:68
  20.7 1.8 %collective-permute-start.5 = (bf16[2,64,1024]{2,1,0:T(8,128)(2,1)S(1)}, bf16[2,64,1024]{2,1,0:T(8,128)(2,1)S(1)}, u32[]{:S(2)}, u32[]{:S(2)}) collective-permute-start(bf16[2,64,1024]{2,1,0:T(8,128)(2,1)S(1)} %collective-permute-done.2.refs_0_), channel_id=1, source_target_pairs={{0,4},{1,5},{2,6},{3,7},{4,8},{5,9},{6,10},{7,11},{8,12},{9,13},{1... | collective-permute-start | bytes 786440 | tf_op jit(solution)/shard_map/ppermute | solution.py:54
  22.5 1.2 %collective-permute-start.7 = (bf16[2,64,1024]{2,1,0:T(8,128)(2,1)S(1)}, bf16[2,64,1024]{2,1,0:T(8,128)(2,1)S(1)}, u32[]{:S(2)}, u32[]{:S(2)}) collective-permute-start(bf16[2,64,1024]{2,1,0:T(8,128)(2,1)S(1)} %collective-permute-done.2.refs_0_), channel_id=1, source_target_pairs={{0,2},{1,3},{2,0},{3,1},{4,6},{5,7},{6,4},{7,5},{8,10},{9,11},{10,... | collective-permute-start | bytes 786440 | tf_op jit(solution)/shard_map/ppermute | solution.py:61
  23.7 0.0 collective-permute-done.6.refs_1_
  23.7 0.0 copy-done
  23.7 4.3 %attend_1.1 = (f32[8,1024,256]{2,1,0:T(8,128)S(1)}, f32[8,1024,128]{2,1,0:T(8,128)S(1)}) custom-call(bf16[64,16384]{1,0:T(8,128)(2,1)S(1)} %copy-done, bf16[2,2,64,1024]{3,2,1,0:T(8,128)(2,1)S(1)} %merge.5.refs_0_, bf16[2,2,64,1024]{3,2,1,0:T(8,128)(2,1)S(1)} %collective-permute-done.6.refs_1_, ...), custom_call_target="tpu_custom_call", output_to_operand_aliasing={{0}: (3, {}), {1}: (4, {})} | custom-call | flops 1073741824 | bytes 4194304 | tf_op jit(solution)/shard_map/attend_1/pallas_call | solution.py:283
  28.0 0.5 %collective-permute-done.5.refs_0_ = bf16[2,64,1024]{2,1,0:T(8,128)(2,1)S(1)} collective-permute-done((bf16[2,64,1024]{2,1,0:T(8,128)(2,1)S(1)}, bf16[2,64,1024]{2,1,0:T(8,128)(2,1)S(1)}, u32[]{:S(2)}, u32[]{:S(2)}) %collective-permute-start.5) | collective-permute-done | bytes 262176 | tf_op jit(solution)/shard_map/ppermute | solution.py:54
  28.5 1.5 %collective-permute-done.7.refs_1_ = bf16[2,64,1024]{2,1,0:T(8,128)(2,1)S(1)} collective-permute-done((bf16[2,64,1024]{2,1,0:T(8,128)(2,1)S(1)}, bf16[2,64,1024]{2,1,0:T(8,128)(2,1)S(1)}, u32[]{:S(2)}, u32[]{:S(2)}) %collective-permute-start.7) | collective-permute-done | bytes 262176 | tf_op jit(solution)/shard_map/ppermute | solution.py:61
  30.0 1.2 %collective-permute-start.9 = (bf16[2,2,64,1024]{3,2,1,0:T(8,128)(2,1)S(1)}, bf16[2,2,64,1024]{3,2,1,0:T(8,128)(2,1)S(1)}, u32[]{:S(2)}, u32[]{:S(2)}) collective-permute-start(bf16[2,2,64,1024]{3,2,1,0:T(8,128)(2,1)S(1)} %merge.6.refs_0_), channel_id=1, source_target_pairs={{0,1},{1,0},{2,3},{3,2},{4,5},{5,4},{6,7},{7,6},{8,9},{9,8},{10,11... | collective-permute-start | bytes 1572872 | tf_op jit(solution)/shard_map/ppermute | solution.py:68
  31.3 1.3 %collective-permute-start.8 = (bf16[2,64,1024]{2,1,0:T(8,128)(2,1)S(1)}, bf16[2,64,1024]{2,1,0:T(8,128)(2,1)S(1)}, u32[]{:S(2)}, u32[]{:S(2)}) collective-permute-start(bf16[2,64,1024]{2,1,0:T(8,128)(2,1)S(1)} %collective-permute-done.5.refs_0_), channel_id=1, source_target_pairs={{0,2},{1,3},{2,0},{3,1},{4,6},{5,7},{6,4},{7,5},{8,10},{9,11},{10,... | collective-permute-start | bytes 786440 | tf_op jit(solution)/shard_map/ppermute | solution.py:61
  32.5 0.3 collective-permute-done.9.refs_1_
  32.8 4.3 %attend_2.1 = (f32[8,1024,256]{2,1,0:T(8,128)S(1)}, f32[8,1024,128]{2,1,0:T(8,128)S(1)}) custom-call(bf16[64,16384]{1,0:T(8,128)(2,1)S(1)} %copy-done, bf16[2,2,64,1024]{3,2,1,0:T(8,128)(2,1)S(1)} %merge.6.refs_0_, bf16[2,2,64,1024]{3,2,1,0:T(8,128)(2,1)S(1)} %collective-permute-done.9.refs_1_, ...), custom_call_target="tpu_custom_call", output_to_operand_aliasing={{0}: (3, {}), {1}: (4, {})} | custom-call | flops 1073741824 | bytes 4194304 | tf_op jit(solution)/shard_map/attend_2/pallas_call | solution.py:283
  37.1 2.1 %collective-permute-done.8.refs_1_ = bf16[2,64,1024]{2,1,0:T(8,128)(2,1)S(1)} collective-permute-done((bf16[2,64,1024]{2,1,0:T(8,128)(2,1)S(1)}, bf16[2,64,1024]{2,1,0:T(8,128)(2,1)S(1)}, u32[]{:S(2)}, u32[]{:S(2)}) %collective-permute-start.8) | collective-permute-done | bytes 262176 | tf_op jit(solution)/shard_map/ppermute | solution.py:61
  39.2 0.9 %collective-permute-start.10 = (bf16[2,2,64,1024]{3,2,1,0:T(8,128)(2,1)S(1)}, bf16[2,2,64,1024]{3,2,1,0:T(8,128)(2,1)S(1)}, u32[]{:S(2)}, u32[]{:S(2)}) collective-permute-start(bf16[2,2,64,1024]{3,2,1,0:T(8,128)(2,1)S(1)} %merge.7.refs_0_), channel_id=1, source_target_pairs={{0,1},{1,0},{2,3},{3,2},{4,5},{5,4},{6,7},{7,6},{8,9},{9,8},{10,11... | collective-permute-start | bytes 1572872 | tf_op jit(solution)/shard_map/ppermute | solution.py:68
  40.1 1.5 %collective-permute-done.10.refs_1_ = bf16[2,2,64,1024]{3,2,1,0:T(8,128)(2,1)S(1)} collective-permute-done((bf16[2,2,64,1024]{3,2,1,0:T(8,128)(2,1)S(1)}, bf16[2,2,64,1024]{3,2,1,0:T(8,128)(2,1)S(1)}, u32[]{:S(2)}, u32[]{:S(2)}) %collective-permute-start.10) | collective-permute-done | bytes 524320 | tf_op jit(solution)/shard_map/ppermute | solution.py:68
  41.7 5.4 %attend_3.1 = bf16[64,16384]{1,0:T(8,128)(2,1)} custom-call(bf16[64,16384]{1,0:T(8,128)(2,1)S(1)} %copy-done, bf16[2,2,64,1024]{3,2,1,0:T(8,128)(2,1)S(1)} %merge.7.refs_0_, bf16[2,2,64,1024]{3,2,1,0:T(8,128)(2,1)S(1)} %collective-permute-done.10.refs_1_, f32[8,1024,256]{2,1,0:T(8,128)S(1)} %get-tuple-element.49.refs_2_, ...), custom_call_target="tpu_custom_call" | custom-call | flops 1073741824 | bytes 4194304 | tf_op jit(solution)/shard_map/attend_3/pallas_call | solution.py:283
  (4 shorter events, 0.1 us)
Async XLA Ops:
  0.0 23.7 %copy-start = (bf16[64,16384]{1,0:T(8,128)(2,1)S(1)}, bf16[64,16384]{1,0:T(8,128)(2,1)}, u32[]{:S(2)}) copy-start(bf16[64,16384]{1,0:T(8,128)(2,1)} %query_ref.7) | copy-start | bytes 6291460
  1.1 7.2 %collective-permute-start = (bf16[2,64,1024]{2,1,0:T(8,128)(2,1)S(1)}, bf16[2,64,1024]{2,1,0:T(8,128)(2,1)S(1)}, u32[]{:S(2)}, u32[]{:S(2)}) collective-permute-start(bf16[2,64,1024]{2,1,0:T(8,128)(2,1)S(1)} %pack.1.refs_0_), channel_id=1, source_target_pairs={{0,4},{1,5},{2,6},{3,7},{4,8},{5,9},{6,10},{7,11},{8,12},{9,13},{1... | collective-permute-start | bytes 786440 | tf_op jit(solution)/shard_map/ppermute | solution.py:54
  1.2 7.2 %collective-permute-start.1 = (bf16[2,64,1024]{2,1,0:T(8,128)(2,1)S(1)}, bf16[2,64,1024]{2,1,0:T(8,128)(2,1)S(1)}, u32[]{:S(2)}, u32[]{:S(2)}) collective-permute-start(bf16[2,64,1024]{2,1,0:T(8,128)(2,1)S(1)} %pack.1.refs_0_), channel_id=1, source_target_pairs={{0,2},{1,3},{2,0},{3,1},{4,6},{5,7},{6,4},{7,5},{8,10},{9,11},{10,... | collective-permute-start | bytes 786440 | tf_op jit(solution)/shard_map/ppermute | solution.py:61
  8.5 4.6 %collective-permute-start.3 = (bf16[2,2,64,1024]{3,2,1,0:T(8,128)(2,1)S(1)}, bf16[2,2,64,1024]{3,2,1,0:T(8,128)(2,1)S(1)}, u32[]{:S(2)}, u32[]{:S(2)}) collective-permute-start(bf16[2,2,64,1024]{3,2,1,0:T(8,128)(2,1)S(1)} %merge.4.refs_0_), channel_id=1, source_target_pairs={{0,1},{1,0},{2,3},{3,2},{4,5},{5,4},{6,7},{7,6},{8,9},{9,8},{10,11... | collective-permute-start | bytes 1572872 | tf_op jit(solution)/shard_map/ppermute | solution.py:68
  10.1 7.9 %collective-permute-start.2 = (bf16[2,64,1024]{2,1,0:T(8,128)(2,1)S(1)}, bf16[2,64,1024]{2,1,0:T(8,128)(2,1)S(1)}, u32[]{:S(2)}, u32[]{:S(2)}) collective-permute-start(bf16[2,64,1024]{2,1,0:T(8,128)(2,1)S(1)} %collective-permute-done.refs_0_), channel_id=1, source_target_pairs={{0,4},{1,5},{2,6},{3,7},{4,8},{5,9},{6,10},{7,11},{8,12},{9,13},{1... | collective-permute-start | bytes 786440 | tf_op jit(solution)/shard_map/ppermute | solution.py:54
  11.8 7.5 %collective-permute-start.4 = (bf16[2,64,1024]{2,1,0:T(8,128)(2,1)S(1)}, bf16[2,64,1024]{2,1,0:T(8,128)(2,1)S(1)}, u32[]{:S(2)}, u32[]{:S(2)}) collective-permute-start(bf16[2,64,1024]{2,1,0:T(8,128)(2,1)S(1)} %collective-permute-done.refs_0_), channel_id=1, source_target_pairs={{0,2},{1,3},{2,0},{3,1},{4,6},{5,7},{6,4},{7,5},{8,10},{9,11},{10,... | collective-permute-start | bytes 786440 | tf_op jit(solution)/shard_map/ppermute | solution.py:61
  19.4 4.3 %collective-permute-start.6 = (bf16[2,2,64,1024]{3,2,1,0:T(8,128)(2,1)S(1)}, bf16[2,2,64,1024]{3,2,1,0:T(8,128)(2,1)S(1)}, u32[]{:S(2)}, u32[]{:S(2)}) collective-permute-start(bf16[2,2,64,1024]{3,2,1,0:T(8,128)(2,1)S(1)} %merge.5.refs_0_), channel_id=1, source_target_pairs={{0,1},{1,0},{2,3},{3,2},{4,5},{5,4},{6,7},{7,6},{8,9},{9,8},{10,11... | collective-permute-start | bytes 1572872 | tf_op jit(solution)/shard_map/ppermute | solution.py:68
  20.7 7.9 %collective-permute-start.5 = (bf16[2,64,1024]{2,1,0:T(8,128)(2,1)S(1)}, bf16[2,64,1024]{2,1,0:T(8,128)(2,1)S(1)}, u32[]{:S(2)}, u32[]{:S(2)}) collective-permute-start(bf16[2,64,1024]{2,1,0:T(8,128)(2,1)S(1)} %collective-permute-done.2.refs_0_), channel_id=1, source_target_pairs={{0,4},{1,5},{2,6},{3,7},{4,8},{5,9},{6,10},{7,11},{8,12},{9,13},{1... | collective-permute-start | bytes 786440 | tf_op jit(solution)/shard_map/ppermute | solution.py:54
  22.5 7.5 %collective-permute-start.7 = (bf16[2,64,1024]{2,1,0:T(8,128)(2,1)S(1)}, bf16[2,64,1024]{2,1,0:T(8,128)(2,1)S(1)}, u32[]{:S(2)}, u32[]{:S(2)}) collective-permute-start(bf16[2,64,1024]{2,1,0:T(8,128)(2,1)S(1)} %collective-permute-done.2.refs_0_), channel_id=1, source_target_pairs={{0,2},{1,3},{2,0},{3,1},{4,6},{5,7},{6,4},{7,5},{8,10},{9,11},{10,... | collective-permute-start | bytes 786440 | tf_op jit(solution)/shard_map/ppermute | solution.py:61
  30.0 2.8 %collective-permute-start.9 = (bf16[2,2,64,1024]{3,2,1,0:T(8,128)(2,1)S(1)}, bf16[2,2,64,1024]{3,2,1,0:T(8,128)(2,1)S(1)}, u32[]{:S(2)}, u32[]{:S(2)}) collective-permute-start(bf16[2,2,64,1024]{3,2,1,0:T(8,128)(2,1)S(1)} %merge.6.refs_0_), channel_id=1, source_target_pairs={{0,1},{1,0},{2,3},{3,2},{4,5},{5,4},{6,7},{7,6},{8,9},{9,8},{10,11... | collective-permute-start | bytes 1572872 | tf_op jit(solution)/shard_map/ppermute | solution.py:68
  31.3 7.9 %collective-permute-start.8 = (bf16[2,64,1024]{2,1,0:T(8,128)(2,1)S(1)}, bf16[2,64,1024]{2,1,0:T(8,128)(2,1)S(1)}, u32[]{:S(2)}, u32[]{:S(2)}) collective-permute-start(bf16[2,64,1024]{2,1,0:T(8,128)(2,1)S(1)} %collective-permute-done.5.refs_0_), channel_id=1, source_target_pairs={{0,2},{1,3},{2,0},{3,1},{4,6},{5,7},{6,4},{7,5},{8,10},{9,11},{10,... | collective-permute-start | bytes 786440 | tf_op jit(solution)/shard_map/ppermute | solution.py:61
  39.2 2.5 %collective-permute-start.10 = (bf16[2,2,64,1024]{3,2,1,0:T(8,128)(2,1)S(1)}, bf16[2,2,64,1024]{3,2,1,0:T(8,128)(2,1)S(1)}, u32[]{:S(2)}, u32[]{:S(2)}) collective-permute-start(bf16[2,2,64,1024]{3,2,1,0:T(8,128)(2,1)S(1)} %merge.7.refs_0_), channel_id=1, source_target_pairs={{0,1},{1,0},{2,3},{3,2},{4,5},{5,4},{6,7},{7,6},{8,9},{9,8},{10,11... | collective-permute-start | bytes 1572872 | tf_op jit(solution)/shard_map/ppermute | solution.py:68

commit v8 on v7

--- a/solution.py
+++ b/solution.py
@@ -63,6 +63,43 @@
     )
 
 
+def step(block, grid):
+    depth, width, cores = grid
+    count = depth * width * cores
+    halves = [
+        lax.ppermute(
+            block,
+            "tp",
+            [
+                (at, (at + width * cores) % count if at % cores == along_z else at ^ cores)
+                for at in range(count)
+            ],
+        )
+        for along_z in range(cores)
+    ]
+
+    def kernel(first_ref, second_ref, z_ref, y_ref):
+        _, _, cc = place(grid)
+
+        @pl.when(cc == 0)
+        def _():
+            z_ref[...] = first_ref[...]
+            y_ref[...] = second_ref[...]
+
+        @pl.when(cc != 0)
+        def _():
+            z_ref[...] = second_ref[...]
+            y_ref[...] = first_ref[...]
+
+    return halves, lambda halves: pl.pallas_call(
+        kernel,
+        out_shape=[jax.ShapeDtypeStruct(block.shape, block.dtype)] * 2,
+        in_specs=[pl.BlockSpec(memory_space=pltpu.VMEM)] * 2,
+        out_specs=[pl.BlockSpec(memory_space=pltpu.VMEM)] * 2,
+        name="sort",
+    )(*halves)
+
+
 def core_swap(blocks, grid):
     depth, width, cores = grid
     return lax.ppermute(blocks, "tp", [(at, at ^ 1) for at in range(depth * width * cores)])
@@ -73,9 +110,9 @@
     return guess * (2.0 - x * guess)
 
 
-def attend_kernel(grid, groups, kept, last, query_ref, *refs):
-    depth, width, cores = grid
-    blocks_refs, refs = refs[: 2 * len(groups)], refs[2 * len(groups) :]
+def attend_kernel(grid, entries, kept, last, query_ref, *refs):
+    depth, width, cores = grid
+    blocks_refs, refs = refs[:2], refs[2:]
     kept_refs, refs = refs[: 2 * kept], refs[2 * kept :]
     out_refs, scratch = list(refs[: 2 - last]), list(refs[2 - last :])
     if not kept:
@@ -92,10 +129,9 @@
     zz, yy, cc = place(grid)
 
     pieces = []
-    for below, own_ref, core_ref in zip(groups, blocks_refs[::2], blocks_refs[1::2]):
-        for dc, ref in ((0, own_ref), (1, core_ref)):
-            for at, dz in enumerate(below):
-                pieces.append((dz, dc, below[:at].count(dz), ref, at))
+    for dc, ref in enumerate(blocks_refs):
+        for at, (dz, dy) in enumerate(entries):
+            pieces.append((dz, dc, dy, ref, at))
     pieces.sort(key=lambda piece: piece[:3])
     lowest, highest = pieces[0][0], pieces[-1][0]
 
@@ -265,12 +301,11 @@
         ]
         steps = KV_HEADS // STEP_HEADS
 
-        def phase(span, state):
-            last = span[-1] == depth - 1
-            merged = stack([block for dz in span for block in rows_of[dz]], "merge")
+        def phase(entries, blocks, state, last=False):
+            merged = stack([blocks[entry] for entry in entries], "merge")
             operands = [merged, core_swap(merged, grid)]
-            groups = [[dz for dz in span for _ in range(width)]]
-            keys = tok * 2 * len(groups[0])
+            keys = tok * 2 * len(entries)
+            rows_below = entries[-1][0] - entries[0][0]
             scratch = []
             if not state:
                 scratch += [pltpu.VMEM((tok, columns), query_rows.dtype)]
@@ -278,10 +313,10 @@
             if last:
                 scratch += [pltpu.VMEM((tok, columns), query_rows.dtype)]
                 scratch += [pltpu.SemaphoreType.DMA((steps,))]
-            if span[0] == 0 or len(span) > 4:
+            if entries[0][0] == 0 or rows_below > 3:
                 scratch += [pltpu.VMEM((tok, keys), jnp.float32)]
             return pl.pallas_call(
-                functools.partial(attend_kernel, grid, groups, bool(state), last),
+                functools.partial(attend_kernel, grid, entries, bool(state), last),
                 out_shape=query_rows if last else state_shapes,
                 in_specs=[whole if state else pl.BlockSpec(memory_space=pltpu.HBM)]
                 + [whole] * (len(operands) + len(state)),
@@ -294,32 +329,32 @@
                     bytes_accessed=4 * HEADS * tok * dim,
                     transcendentals=HEADS * tok * keys,
                 ),
-                name=f"attend_{span[0]}",
+                name="attend_last" if last else f"attend_{entries[0][0]}",
             )(query_rows if state else pinned, *operands, *state)
 
-        spans = [range(0, 1), range(1, 2)]
-        spans += [range(at, min(at + 4, depth - 1)) for at in range(2, depth - 1, 4)]
-        spans += [range(depth - 1, depth)]
-        block = stack([key_rows, value_rows], "pack")
-        rows_of, state = [], []
-        for dz in range(depth):
-            rows_of.append([block, y_swap(block, grid)] if width == 2 else [block])
-            if dz + 1 == depth:
-                break
-            block = z_forward(block, grid)
-            at = dz - 1
-            if dz and spans[0][-1] <= at:
-                span = spans.pop(0)
-                state = phase(span, state)
-            if dz:
-                block, state, rows_of[dz] = lax.optimization_barrier((block, state, rows_of[dz]))
+        batches = [[(dz, dy) for dy in range(width)] for dz in range(depth - 1)]
+        while len(batches) > 3 + depth // 4:
+            batches[-2:] = [batches[-2] + batches[-1]]
+        final = (depth - 1, width - 1)
+        if width == 2:
+            batches[-1].append((depth - 1, 0))
+        blocks = {(0, 0): stack([key_rows, value_rows], "pack")}
+        state = []
+        for dz in range(depth - 1):
+            if width == 2:
+                halves, sort = step(blocks[dz, 0], grid)
+                halves, state = lax.optimization_barrier((halves, state))
+                blocks[dz + 1, 0], blocks[dz, 1] = sort(halves)
             else:
-                block, rows_of[0] = lax.optimization_barrier((block, rows_of[0]))
-        while spans:
-            if len(spans) == 1:
-                rows_of[-1], state = lax.optimization_barrier((rows_of[-1], state))
-            state = phase(spans.pop(0), state)
-        return state
+                blocks[dz + 1, 0], state = lax.optimization_barrier(
+                    (z_forward(blocks[dz, 0], grid), state)
+                )
+            if batches and all(entry in blocks for entry in batches[0]):
+                state = phase(batches.pop(0), blocks, state)
+        if width == 2:
+            blocks[final] = y_swap(blocks[depth - 1, 0], grid)
+        blocks[final], state = lax.optimization_barrier((blocks[final], state))
+        return phase([final], blocks, state, last=True)
 
     spec = P(("groups", "tp"), None)
     return jax.shard_map(

time: 47.2 us -> 87.9 us (1.86)
  local copies, waits for them, and re-layouts: 0.01 us -> 38.7 us
  Pallas kernels: 20 us -> 30.4 us
  waiting for transfers between devices: 13.4 us -> 8.07 us
  starting transfers between devices: 13.6 us -> 10.1 us
    unnamed x2 -> x50, local copies, waits for them, and re-layouts: 0.01 us -> 38.7 us
    pallas_call x4 -> x7, Pallas kernels: 18.7 us -> 29.1 us  [the longest x4 23.5 us: phase(): pl.pallas_call(functools.partial(attend_kernel, grid, entries, bool(state...]
    ppermute x4 -> x1, waiting for transfers between devices: 5.04 us -> 0.01 us  [y_swap(): lax.ppermute(block, 'tp', [(at, at ^ cores) for at in range(depth * width...]
    ppermute x4 -> x1, starting transfers between devices: 5.04 us -> 1.24 us  [y_swap(): lax.ppermute(block, 'tp', [(at, at ^ cores) for at in range(depth * width...]
    ppermute x3 -> x6, starting transfers between devices: 3.59 us -> 4.96 us  [step(): lax.ppermute(block, 'tp', [(at, (at + width * cores) % count if at % core...]
    ppermute x4, starting transfers between devices: 5.01 us -> 3.87 us  [core_swap(): lax.ppermute(blocks, 'tp', [(at, at ^ 1) for at in range(depth * width *...]
    ppermute x3 -> x6, waiting for transfers between devices: 6.54 us -> 6.02 us  [step(): lax.ppermute(block, 'tp', [(at, (at + width * cores) % count if at % core...]
  transfers between devices with their start and end apart: 11 -> 11, of which waited for: 9 -> 5; matrix products, arithmetic and copies ran while one was open for 0% -> 0% of each run, Pallas kernels for 28% -> 20%
where the time goes in v8:
time: 87.9 us; the launch traced here: 87.4 us
  local copies, waits for them, and re-layouts  38.7 us (44%)
  Pallas kernels  30.4 us (35%)
  starting transfers between devices  10.1 us (11%)
  waiting for transfers between devices  8.07 us (9%)
    unnamed x50, local copies, waits for them, and re-layouts  38.7 us
    pallas_call x4, Pallas kernels, phase(): pl.pallas_call(functools.partial(attend_kernel, grid, entries, bool(state...  23.5 us
    ppermute x6, waiting for transfers between devices, step(): lax.ppermute(block, 'tp', [(at, (at + width * cores) % count if at % core...  6.02 us
    pallas_call x3, Pallas kernels, step(): pl.pallas_call(kernel, out_shape=[jax.ShapeDtypeStruct(block.shape, block...  5.58 us
    ppermute x6, starting transfers between devices, step(): lax.ppermute(block, 'tp', [(at, (at + width * cores) % count if at % core...  4.96 us
    ppermute x4, starting transfers between devices, core_swap(): lax.ppermute(blocks, 'tp', [(at, at ^ 1) for at in range(depth * width *...  3.87 us
    ppermute x4, waiting for transfers between devices, core_swap(): lax.ppermute(blocks, 'tp', [(at, at ^ 1) for at in range(depth * width *...  2.04 us
  transfers between devices with their start and end apart: 11, of which 5 were waited for; matrix products, arithmetic and copies ran while one was open for 0% of the time, Pallas kernels for 20%

profile of v8, /device:TPU:25, one launch (start us, length us, event | category | flops | bytes accessed | tf_op | source)
XLA Modules:
  0.0 87.4 jit_solution(4498450819286169620)
XLA Ops:
  0.0 1.1 %pack.1.refs_0_ = bf16[2,64,1024]{2,1,0:T(8,128)(2,1)S(1)} custom-call(bf16[64,1024]{1,0:T(8,128)(2,1)} %refs_0_.1, bf16[64,1024]{1,0:T(8,128)(2,1)} %refs_1_.1), custom_call_target="tpu_custom_call" | custom-call | tf_op jit(solution)/shard_map/pack/pallas_call | solution.py:41
  1.2 1.3 %collective-permute-start = (bf16[2,64,1024]{2,1,0:T(8,128)(2,1)S(1)}, bf16[2,64,1024]{2,1,0:T(8,128)(2,1)S(1)}, u32[]{:S(2)}, u32[]{:S(2)}) collective-permute-start(bf16[2,64,1024]{2,1,0:T(8,128)(2,1)S(1)} %pack.1.refs_0_), channel_id=1, source_target_pairs={{0,4},{1,3},{2,6},{3,1},{4,8},{5,7},{6,10},{7,5},{8,12},{9,11},{10... | collective-permute-start | bytes 786440 | tf_op jit(solution)/shard_map/ppermute | solution.py:70
  2.5 4.3 %collective-permute-done.1.second_ref = bf16[2,64,1024]{2,1,0:T(8,128)(2,1)S(1)} collective-permute-done((bf16[2,64,1024]{2,1,0:T(8,128)(2,1)S(1)}, bf16[2,64,1024]{2,1,0:T(8,128)(2,1)S(1)}, u32[]{:S(2)}, u32[]{:S(2)}) %collective-permute-start.1) | collective-permute-done | bytes 262176 | tf_op jit(solution)/shard_map/ppermute | solution.py:70
  6.8 1.7 %collective-permute-done.first_ref = bf16[2,64,1024]{2,1,0:T(8,128)(2,1)S(1)} collective-permute-done((bf16[2,64,1024]{2,1,0:T(8,128)(2,1)S(1)}, bf16[2,64,1024]{2,1,0:T(8,128)(2,1)S(1)}, u32[]{:S(2)}, u32[]{:S(2)}) %collective-permute-start) | collective-permute-done | bytes 262176 | tf_op jit(solution)/shard_map/ppermute | solution.py:70
  9.2 1.8 %sort.3 = (bf16[2,64,1024]{2,1,0:T(8,128)(2,1)}, bf16[2,64,1024]{2,1,0:T(8,128)(2,1)}) custom-call(bf16[2,64,1024]{2,1,0:T(8,128)(2,1)} %copy-done.24, bf16[2,64,1024]{2,1,0:T(8,128)(2,1)} %copy-done.23), custom_call_target="tpu_custom_call" | custom-call | tf_op jit(solution)/shard_map/sort/pallas_call | solution.py:94
  11.1 1.0 %copy-done.16 = bf16[2,64,1024]{2,1,0:T(8,128)(2,1)S(1)} copy-done((bf16[2,64,1024]{2,1,0:T(8,128)(2,1)S(1)}, bf16[2,64,1024]{2,1,0:T(8,128)(2,1)}, u32[]{:S(2)}) %copy-start.16) | copy-done | bytes 262168
  12.1 2.2 %collective-permute-start.4 = (bf16[2,2,64,1024]{3,2,1,0:T(8,128)(2,1)S(1)}, bf16[2,2,64,1024]{3,2,1,0:T(8,128)(2,1)S(1)}, u32[]{:S(2)}, u32[]{:S(2)}) collective-permute-start(bf16[2,2,64,1024]{3,2,1,0:T(8,128)(2,1)S(1)} %merge.4.refs_0_), channel_id=1, source_target_pairs={{0,1},{1,0},{2,3},{3,2},{4,5},{5,4},{6,7},{7,6},{8,9},{9,8},{10,11... | collective-permute-start | bytes 1572872 | tf_op jit(solution)/shard_map/ppermute | solution.py:105
  14.3 1.0 %collective-permute-start.3 = (bf16[2,64,1024]{2,1,0:T(8,128)(2,1)}, bf16[2,64,1024]{2,1,0:T(8,128)(2,1)S(1)}, u32[]{:S(2)}, u32[]{:S(2)}) collective-permute-start(bf16[2,64,1024]{2,1,0:T(8,128)(2,1)} %get-tuple-element.32.refs_0_), channel_id=1, source_target_pairs={{0,2},{1,5},{2,0},{3,7},{4,6},{5,9},{6,4},{7,11},{8,10},{9,13},{10... | collective-permute-start | bytes 786440 | tf_op jit(solution)/shard_map/ppermute | solution.py:70
  15.4 1.2 %collective-permute-start.2 = (bf16[2,64,1024]{2,1,0:T(8,128)(2,1)}, bf16[2,64,1024]{2,1,0:T(8,128)(2,1)S(1)}, u32[]{:S(2)}, u32[]{:S(2)}) collective-permute-start(bf16[2,64,1024]{2,1,0:T(8,128)(2,1)} %get-tuple-element.32.refs_0_), channel_id=1, source_target_pairs={{0,4},{1,3},{2,6},{3,1},{4,8},{5,7},{6,10},{7,5},{8,12},{9,11},{10... | collective-permute-start | bytes 786440 | tf_op jit(solution)/shard_map/ppermute | solution.py:70
  16.6 4.7 %attend_0.1 = (f32[8,1024,256]{2,1,0:T(8,128)S(1)}, f32[8,1024,128]{2,1,0:T(8,128)S(1)}) custom-call(bf16[64,16384]{1,0:T(8,128)(2,1)} %query_ref.7, bf16[2,2,64,1024]{3,2,1,0:T(8,128)(2,1)S(1)} %merge.4.refs_0_, bf16[2,2,64,1024]{3,2,1,0:T(8,128)(2,1)S(1)} %collective-permute-done.4.refs_1_), custom_call_target="tpu_custom_call" | custom-call | flops 1073741824 | bytes 4194304 | tf_op jit(solution)/shard_map/attend_0/pallas_call | solution.py:318
  21.4 3.3 %copy-done = f32[8,1024,256]{2,1,0:T(8,128)} copy-done((f32[8,1024,256]{2,1,0:T(8,128)}, f32[8,1024,256]{2,1,0:T(8,128)S(1)}, u32[]{:S(2)}) %copy-start) | copy-done | bytes 8388632
  24.7 2.0 %copy-done.6 = f32[8,1024,128]{2,1,0:T(8,128)} copy-done((f32[8,1024,128]{2,1,0:T(8,128)}, f32[8,1024,128]{2,1,0:T(8,128)S(1)}, u32[]{:S(2)}) %copy-start.6) | copy-done | bytes 4194328
  27.5 1.9 %sort.4 = (bf16[2,64,1024]{2,1,0:T(8,128)(2,1)}, bf16[2,64,1024]{2,1,0:T(8,128)(2,1)}) custom-call(bf16[2,64,1024]{2,1,0:T(8,128)(2,1)} %copy-done.22, bf16[2,64,1024]{2,1,0:T(8,128)(2,1)} %copy-done.20), custom_call_target="tpu_custom_call" | custom-call | tf_op jit(solution)/shard_map/sort/pallas_call | solution.py:94
  29.4 0.9 %copy-done.17 = bf16[2,64,1024]{2,1,0:T(8,128)(2,1)S(1)} copy-done((bf16[2,64,1024]{2,1,0:T(8,128)(2,1)S(1)}, bf16[2,64,1024]{2,1,0:T(8,128)(2,1)}, u32[]{:S(2)}) %copy-start.17) | copy-done | bytes 262168
  31.0 1.1 %collective-permute-start.6 = (bf16[2,64,1024]{2,1,0:T(8,128)(2,1)}, bf16[2,64,1024]{2,1,0:T(8,128)(2,1)S(1)}, u32[]{:S(2)}, u32[]{:S(2)}) collective-permute-start(bf16[2,64,1024]{2,1,0:T(8,128)(2,1)} %get-tuple-element.38.refs_0_), channel_id=1, source_target_pairs={{0,2},{1,5},{2,0},{3,7},{4,6},{5,9},{6,4},{7,11},{8,10},{9,13},{10... | collective-permute-start | bytes 786440 | tf_op jit(solution)/shard_map/ppermute | solution.py:70
  32.6 3.4 %copy-done.1 = f32[8,1024,256]{2,1,0:T(8,128)S(1)} copy-done((f32[8,1024,256]{2,1,0:T(8,128)S(1)}, f32[8,1024,256]{2,1,0:T(8,128)}, u32[]{:S(2)}) %copy-start.1) | copy-done | bytes 8388632
  36.0 2.2 %copy-done.7 = f32[8,1024,128]{2,1,0:T(8,128)S(1)} copy-done((f32[8,1024,128]{2,1,0:T(8,128)S(1)}, f32[8,1024,128]{2,1,0:T(8,128)}, u32[]{:S(2)}) %copy-start.7) | copy-done | bytes 4194328
  38.1 4.3 %attend_1.1 = (f32[8,1024,256]{2,1,0:T(8,128)S(1)}, f32[8,1024,128]{2,1,0:T(8,128)S(1)}) custom-call(bf16[64,16384]{1,0:T(8,128)(2,1)S(1)} %copy-done.12, bf16[2,2,64,1024]{3,2,1,0:T(8,128)(2,1)S(1)} %merge.5.refs_0_, bf16[2,2,64,1024]{3,2,1,0:T(8,128)(2,1)S(1)} %collective-permute-done.7.refs_1_, ...), custom_call_target="tpu_custom_call", output_to_operand_aliasing={{0}: (3, {}), {1}: (4, {})} | custom-call | flops 1073741824 | bytes 4194304 | tf_op jit(solution)/shard_map/attend_1/pallas_call | solution.py:318
  42.4 3.3 %copy-done.2 = f32[8,1024,256]{2,1,0:T(8,128)} copy-done((f32[8,1024,256]{2,1,0:T(8,128)}, f32[8,1024,256]{2,1,0:T(8,128)S(1)}, u32[]{:S(2)}) %copy-start.2) | copy-done | bytes 8388632
  45.7 2.0 %copy-done.8 = f32[8,1024,128]{2,1,0:T(8,128)} copy-done((f32[8,1024,128]{2,1,0:T(8,128)}, f32[8,1024,128]{2,1,0:T(8,128)S(1)}, u32[]{:S(2)}) %copy-start.8) | copy-done | bytes 4194328
  48.5 1.9 %sort.5 = (bf16[2,64,1024]{2,1,0:T(8,128)(2,1)}, bf16[2,64,1024]{2,1,0:T(8,128)(2,1)}) custom-call(bf16[2,64,1024]{2,1,0:T(8,128)(2,1)} %copy-done.21, bf16[2,64,1024]{2,1,0:T(8,128)(2,1)} %copy-done.19), custom_call_target="tpu_custom_call" | custom-call | tf_op jit(solution)/shard_map/sort/pallas_call | solution.py:94
  50.4 0.9 %copy-done.15 = bf16[2,64,1024]{2,1,0:T(8,128)(2,1)S(1)} copy-done((bf16[2,64,1024]{2,1,0:T(8,128)(2,1)S(1)}, bf16[2,64,1024]{2,1,0:T(8,128)(2,1)}, u32[]{:S(2)}) %copy-start.15) | copy-done | bytes 262168
  52.9 1.2 %collective-permute-start.8 = (bf16[2,64,1024]{2,1,0:T(8,128)(2,1)S(1)}, bf16[2,64,1024]{2,1,0:T(8,128)(2,1)S(1)}, u32[]{:S(2)}, u32[]{:S(2)}) collective-permute-start(bf16[2,64,1024]{2,1,0:T(8,128)(2,1)S(1)} %copy-done.15), channel_id=1, source_target_pairs={{0,2},{1,3},{2,0},{3,1},{4,6},{5,7},{6,4},{7,5},{8,10},{9,11},{10,... | collective-permute-start | bytes 786440 | tf_op jit(solution)/shard_map/ppermute | solution.py:61
  54.8 3.4 %copy-done.3 = f32[8,1024,256]{2,1,0:T(8,128)S(1)} copy-done((f32[8,1024,256]{2,1,0:T(8,128)S(1)}, f32[8,1024,256]{2,1,0:T(8,128)}, u32[]{:S(2)}) %copy-start.3) | copy-done | bytes 8388632
  58.1 2.2 %copy-done.9 = f32[8,1024,128]{2,1,0:T(8,128)S(1)} copy-done((f32[8,1024,128]{2,1,0:T(8,128)S(1)}, f32[8,1024,128]{2,1,0:T(8,128)}, u32[]{:S(2)}) %copy-start.9) | copy-done | bytes 4194328
  60.3 8.3 %attend_2.1 = (f32[8,1024,256]{2,1,0:T(8,128)S(1)}, f32[8,1024,128]{2,1,0:T(8,128)S(1)}) custom-call(bf16[64,16384]{1,0:T(8,128)(2,1)S(1)} %copy-done.12, bf16[3,2,64,1024]{3,2,1,0:T(8,128)(2,1)S(1)} %merge.6.refs_0_, bf16[3,2,64,1024]{3,2,1,0:T(8,128)(2,1)S(1)} %collective-permute-done.9.refs_1_, ...), custom_call_target="tpu_custom_call", output_to_operand_aliasing={{0}: (3, {}), {1}: (4, {})} | custom-call | flops 1610612736 | bytes 4194304 | tf_op jit(solution)/shard_map/attend_2/pallas_call | solution.py:318
  68.6 3.3 %copy-done.4 = f32[8,1024,256]{2,1,0:T(8,128)} copy-done((f32[8,1024,256]{2,1,0:T(8,128)}, f32[8,1024,256]{2,1,0:T(8,128)S(1)}, u32[]{:S(2)}) %copy-start.4) | copy-done | bytes 8388632
  71.9 2.0 %copy-done.10 = f32[8,1024,128]{2,1,0:T(8,128)} copy-done((f32[8,1024,128]{2,1,0:T(8,128)}, f32[8,1024,128]{2,1,0:T(8,128)S(1)}, u32[]{:S(2)}) %copy-start.10) | copy-done | bytes 4194328
  74.4 1.2 %collective-permute-done.10.refs_1_ = bf16[1,2,64,1024]{3,2,1,0:T(8,128)(2,1)S(1)} collective-permute-done((bf16[1,2,64,1024]{3,2,1,0:T(8,128)(2,1)S(1)}, bf16[1,2,64,1024]{3,2,1,0:T(8,128)(2,1)S(1)}, u32[]{:S(2)}, u32[]{:S(2)}) %collective-permute-start.10) | collective-permute-done | bytes 262176 | tf_op jit(solution)/shard_map/ppermute | solution.py:105
  75.5 3.4 %copy-done.5 = f32[8,1024,256]{2,1,0:T(8,128)S(1)} copy-done((f32[8,1024,256]{2,1,0:T(8,128)S(1)}, f32[8,1024,256]{2,1,0:T(8,128)}, u32[]{:S(2)}) %copy-start.5) | copy-done | bytes 8388632
  78.9 2.2 %copy-done.11 = f32[8,1024,128]{2,1,0:T(8,128)S(1)} copy-done((f32[8,1024,128]{2,1,0:T(8,128)S(1)}, f32[8,1024,128]{2,1,0:T(8,128)}, u32[]{:S(2)}) %copy-start.11) | copy-done | bytes 4194328
  81.1 6.2 %attend_last.1 = bf16[64,16384]{1,0:T(8,128)(2,1)} custom-call(bf16[64,16384]{1,0:T(8,128)(2,1)S(1)} %copy-done.12, bf16[1,2,64,1024]{3,2,1,0:T(8,128)(2,1)S(1)} %merge.7.refs_0_, bf16[1,2,64,1024]{3,2,1,0:T(8,128)(2,1)S(1)} %collective-permute-done.10.refs_1_, f32[8,1024,256]{2,1,0:T(8,128)S(1)} %copy-done.5, f32[8,1024,128]{2,1,0:T(8,128)S(1)} %copy-done.11), custom_call_target="tpu_custom_call" | custom-call | flops 536870912 | bytes 4194304 | tf_op jit(solution)/shard_map/attend_last/pallas_call | solution.py:318
  (52 shorter events, 6.2 us)
Async XLA Ops:
  0.0 32.6 %copy-start.12 = (bf16[64,16384]{1,0:T(8,128)(2,1)S(1)}, bf16[64,16384]{1,0:T(8,128)(2,1)}, u32[]{:S(2)}) copy-start(bf16[64,16384]{1,0:T(8,128)(2,1)} %query_ref.7) | copy-start | bytes 6291460
  1.1 5.7 %collective-permute-start.1 = (bf16[2,64,1024]{2,1,0:T(8,128)(2,1)S(1)}, bf16[2,64,1024]{2,1,0:T(8,128)(2,1)S(1)}, u32[]{:S(2)}, u32[]{:S(2)}) collective-permute-start(bf16[2,64,1024]{2,1,0:T(8,128)(2,1)S(1)} %pack.1.refs_0_), channel_id=1, source_target_pairs={{0,2},{1,5},{2,0},{3,7},{4,6},{5,9},{6,4},{7,11},{8,10},{9,13},{10... | collective-permute-start | bytes 786440 | tf_op jit(solution)/shard_map/ppermute | solution.py:70
  1.2 7.3 %collective-permute-start = (bf16[2,64,1024]{2,1,0:T(8,128)(2,1)S(1)}, bf16[2,64,1024]{2,1,0:T(8,128)(2,1)S(1)}, u32[]{:S(2)}, u32[]{:S(2)}) collective-permute-start(bf16[2,64,1024]{2,1,0:T(8,128)(2,1)S(1)} %pack.1.refs_0_), channel_id=1, source_target_pairs={{0,4},{1,3},{2,6},{3,1},{4,8},{5,7},{6,10},{7,5},{8,12},{9,11},{10... | collective-permute-start | bytes 786440 | tf_op jit(solution)/shard_map/ppermute | solution.py:70
  6.8 1.7 %copy-start.23 = (bf16[2,64,1024]{2,1,0:T(8,128)(2,1)}, bf16[2,64,1024]{2,1,0:T(8,128)(2,1)S(1)}, u32[]{:S(2)}) copy-start(bf16[2,64,1024]{2,1,0:T(8,128)(2,1)S(1)} %collective-permute-done.1.second_ref) | copy-start | bytes 786436
  11.1 18.3 %copy-start.14 = (bf16[2,64,1024]{2,1,0:T(8,128)(2,1)S(1)}, bf16[2,64,1024]{2,1,0:T(8,128)(2,1)}, u32[]{:S(2)}) copy-start(bf16[2,64,1024]{2,1,0:T(8,128)(2,1)} %get-tuple-element.32.refs_0_) | copy-start | bytes 786436
  11.1 1.0 %copy-start.16 = (bf16[2,64,1024]{2,1,0:T(8,128)(2,1)S(1)}, bf16[2,64,1024]{2,1,0:T(8,128)(2,1)}, u32[]{:S(2)}) copy-start(bf16[2,64,1024]{2,1,0:T(8,128)(2,1)} %get-tuple-element.33.refs_1_) | copy-start | bytes 786436
  12.1 4.5 %collective-permute-start.4 = (bf16[2,2,64,1024]{3,2,1,0:T(8,128)(2,1)S(1)}, bf16[2,2,64,1024]{3,2,1,0:T(8,128)(2,1)S(1)}, u32[]{:S(2)}, u32[]{:S(2)}) collective-permute-start(bf16[2,2,64,1024]{3,2,1,0:T(8,128)(2,1)S(1)} %merge.4.refs_0_), channel_id=1, source_target_pairs={{0,1},{1,0},{2,3},{3,2},{4,5},{5,4},{6,7},{7,6},{8,9},{9,8},{10,11... | collective-permute-start | bytes 1572872 | tf_op jit(solution)/shard_map/ppermute | solution.py:105
  14.3 12.3 %collective-permute-start.3 = (bf16[2,64,1024]{2,1,0:T(8,128)(2,1)}, bf16[2,64,1024]{2,1,0:T(8,128)(2,1)S(1)}, u32[]{:S(2)}, u32[]{:S(2)}) collective-permute-start(bf16[2,64,1024]{2,1,0:T(8,128)(2,1)} %get-tuple-element.32.refs_0_), channel_id=1, source_target_pairs={{0,2},{1,5},{2,0},{3,7},{4,6},{5,9},{6,4},{7,11},{8,10},{9,13},{10... | collective-permute-start | bytes 786440 | tf_op jit(solution)/shard_map/ppermute | solution.py:70
  15.4 11.3 %collective-permute-start.2 = (bf16[2,64,1024]{2,1,0:T(8,128)(2,1)}, bf16[2,64,1024]{2,1,0:T(8,128)(2,1)S(1)}, u32[]{:S(2)}, u32[]{:S(2)}) collective-permute-start(bf16[2,64,1024]{2,1,0:T(8,128)(2,1)} %get-tuple-element.32.refs_0_), channel_id=1, source_target_pairs={{0,4},{1,3},{2,6},{3,1},{4,8},{5,7},{6,10},{7,5},{8,12},{9,11},{10... | collective-permute-start | bytes 786440 | tf_op jit(solution)/shard_map/ppermute | solution.py:70
  21.4 3.3 %copy-start = (f32[8,1024,256]{2,1,0:T(8,128)}, f32[8,1024,256]{2,1,0:T(8,128)S(1)}, u32[]{:S(2)}) copy-start(f32[8,1024,256]{2,1,0:T(8,128)S(1)} %get-tuple-element.40.refs_2_) | copy-start | bytes 25165828
  24.7 2.0 %copy-start.6 = (f32[8,1024,128]{2,1,0:T(8,128)}, f32[8,1024,128]{2,1,0:T(8,128)S(1)}, u32[]{:S(2)}) copy-start(f32[8,1024,128]{2,1,0:T(8,128)S(1)} %get-tuple-element.41.refs_3_) | copy-start | bytes 12582916
  26.7 0.8 copy-start.22
  29.4 1.0 %copy-start.17 = (bf16[2,64,1024]{2,1,0:T(8,128)(2,1)S(1)}, bf16[2,64,1024]{2,1,0:T(8,128)(2,1)}, u32[]{:S(2)}) copy-start(bf16[2,64,1024]{2,1,0:T(8,128)(2,1)} %get-tuple-element.39.refs_1_) | copy-start | bytes 786436
  30.3 2.2 %collective-permute-start.7 = (bf16[2,2,64,1024]{3,2,1,0:T(8,128)(2,1)S(1)}, bf16[2,2,64,1024]{3,2,1,0:T(8,128)(2,1)S(1)}, u32[]{:S(2)}, u32[]{:S(2)}) collective-permute-start(bf16[2,2,64,1024]{3,2,1,0:T(8,128)(2,1)S(1)} %merge.5.refs_0_), channel_id=1, source_target_pairs={{0,1},{1,0},{2,3},{3,2},{4,5},{5,4},{6,7},{7,6},{8,9},{9,8},{10,11... | collective-permute-start | bytes 1572872 | tf_op jit(solution)/shard_map/ppermute | solution.py:105
  31.0 16.7 %collective-permute-start.6 = (bf16[2,64,1024]{2,1,0:T(8,128)(2,1)}, bf16[2,64,1024]{2,1,0:T(8,128)(2,1)S(1)}, u32[]{:S(2)}, u32[]{:S(2)}) collective-permute-start(bf16[2,64,1024]{2,1,0:T(8,128)(2,1)} %get-tuple-element.38.refs_0_), channel_id=1, source_target_pairs={{0,2},{1,5},{2,0},{3,7},{4,6},{5,9},{6,4},{7,11},{8,10},{9,13},{10... | collective-permute-start | bytes 786440 | tf_op jit(solution)/shard_map/ppermute | solution.py:70
  32.1 15.6 %collective-permute-start.5 = (bf16[2,64,1024]{2,1,0:T(8,128)(2,1)}, bf16[2,64,1024]{2,1,0:T(8,128)(2,1)S(1)}, u32[]{:S(2)}, u32[]{:S(2)}) collective-permute-start(bf16[2,64,1024]{2,1,0:T(8,128)(2,1)} %get-tuple-element.38.refs_0_), channel_id=1, source_target_pairs={{0,4},{1,3},{2,6},{3,1},{4,8},{5,7},{6,10},{7,5},{8,12},{9,11},{10... | collective-permute-start | bytes 786440 | tf_op jit(solution)/shard_map/ppermute | solution.py:70
  32.6 3.4 %copy-start.1 = (f32[8,1024,256]{2,1,0:T(8,128)S(1)}, f32[8,1024,256]{2,1,0:T(8,128)}, u32[]{:S(2)}) copy-start(f32[8,1024,256]{2,1,0:T(8,128)} %copy-done) | copy-start | bytes 25165828
  36.0 2.2 %copy-start.7 = (f32[8,1024,128]{2,1,0:T(8,128)S(1)}, f32[8,1024,128]{2,1,0:T(8,128)}, u32[]{:S(2)}) copy-start(f32[8,1024,128]{2,1,0:T(8,128)} %copy-done.6) | copy-start | bytes 12582916
  38.1 12.2 %copy-start.13 = (bf16[2,64,1024]{2,1,0:T(8,128)(2,1)S(1)}, bf16[2,64,1024]{2,1,0:T(8,128)(2,1)}, u32[]{:S(2)}) copy-start(bf16[2,64,1024]{2,1,0:T(8,128)(2,1)} %get-tuple-element.38.refs_0_) | copy-start | bytes 786436
  42.4 3.3 %copy-start.2 = (f32[8,1024,256]{2,1,0:T(8,128)}, f32[8,1024,256]{2,1,0:T(8,128)S(1)}, u32[]{:S(2)}) copy-start(f32[8,1024,256]{2,1,0:T(8,128)S(1)} %get-tuple-element.48.refs_2_) | copy-start | bytes 25165828
  45.7 2.0 %copy-start.8 = (f32[8,1024,128]{2,1,0:T(8,128)}, f32[8,1024,128]{2,1,0:T(8,128)S(1)}, u32[]{:S(2)}) copy-start(f32[8,1024,128]{2,1,0:T(8,128)S(1)} %get-tuple-element.49.refs_3_) | copy-start | bytes 12582916
  50.4 1.0 %copy-start.15 = (bf16[2,64,1024]{2,1,0:T(8,128)(2,1)S(1)}, bf16[2,64,1024]{2,1,0:T(8,128)(2,1)}, u32[]{:S(2)}) copy-start(bf16[2,64,1024]{2,1,0:T(8,128)(2,1)} %get-tuple-element.46.refs_2_) | copy-start | bytes 786436
  51.3 0.9 %copy-start.18 = (bf16[2,64,1024]{2,1,0:T(8,128)(2,1)S(1)}, bf16[2,64,1024]{2,1,0:T(8,128)(2,1)}, u32[]{:S(2)}) copy-start(bf16[2,64,1024]{2,1,0:T(8,128)(2,1)} %get-tuple-element.47.refs_1_) | copy-start | bytes 786436
  52.3 2.4 %collective-permute-start.9 = (bf16[3,2,64,1024]{3,2,1,0:T(8,128)(2,1)S(1)}, bf16[3,2,64,1024]{3,2,1,0:T(8,128)(2,1)S(1)}, u32[]{:S(2)}, u32[]{:S(2)}) collective-permute-start(bf16[3,2,64,1024]{3,2,1,0:T(8,128)(2,1)S(1)} %merge.6.refs_0_), channel_id=1, source_target_pairs={{0,1},{1,0},{2,3},{3,2},{4,5},{5,4},{6,7},{7,6},{8,9},{9,8},{10,11... | collective-permute-start | bytes 2359304 | tf_op jit(solution)/shard_map/ppermute | solution.py:105
  52.9 21.1 %collective-permute-start.8 = (bf16[2,64,1024]{2,1,0:T(8,128)(2,1)S(1)}, bf16[2,64,1024]{2,1,0:T(8,128)(2,1)S(1)}, u32[]{:S(2)}, u32[]{:S(2)}) collective-permute-start(bf16[2,64,1024]{2,1,0:T(8,128)(2,1)S(1)} %copy-done.15), channel_id=1, source_target_pairs={{0,2},{1,3},{2,0},{3,1},{4,6},{5,7},{6,4},{7,5},{8,10},{9,11},{10,... | collective-permute-start | bytes 786440 | tf_op jit(solution)/shard_map/ppermute | solution.py:61
  54.8 3.4 %copy-start.3 = (f32[8,1024,256]{2,1,0:T(8,128)S(1)}, f32[8,1024,256]{2,1,0:T(8,128)}, u32[]{:S(2)}) copy-start(f32[8,1024,256]{2,1,0:T(8,128)} %copy-done.2) | copy-start | bytes 25165828
  58.1 2.2 %copy-start.9 = (f32[8,1024,128]{2,1,0:T(8,128)S(1)}, f32[8,1024,128]{2,1,0:T(8,128)}, u32[]{:S(2)}) copy-start(f32[8,1024,128]{2,1,0:T(8,128)} %copy-done.8) | copy-start | bytes 12582916
  68.6 3.3 %copy-start.4 = (f32[8,1024,256]{2,1,0:T(8,128)}, f32[8,1024,256]{2,1,0:T(8,128)S(1)}, u32[]{:S(2)}) copy-start(f32[8,1024,256]{2,1,0:T(8,128)S(1)} %get-tuple-element.53.refs_2_) | copy-start | bytes 25165828
  71.9 2.0 %copy-start.10 = (f32[8,1024,128]{2,1,0:T(8,128)}, f32[8,1024,128]{2,1,0:T(8,128)S(1)}, u32[]{:S(2)}) copy-start(f32[8,1024,128]{2,1,0:T(8,128)S(1)} %get-tuple-element.54.refs_3_) | copy-start | bytes 12582916
  73.9 1.6 %collective-permute-start.10 = (bf16[1,2,64,1024]{3,2,1,0:T(8,128)(2,1)S(1)}, bf16[1,2,64,1024]{3,2,1,0:T(8,128)(2,1)S(1)}, u32[]{:S(2)}, u32[]{:S(2)}) collective-permute-start(bf16[1,2,64,1024]{3,2,1,0:T(8,128)(2,1)S(1)} %merge.7.refs_0_), channel_id=1, source_target_pairs={{0,1},{1,0},{2,3},{3,2},{4,5},{5,4},{6,7},{7,6},{8,9},{9,8},{10,11... | collective-permute-start | bytes 786440 | tf_op jit(solution)/shard_map/ppermute | solution.py:105
  75.5 3.4 %copy-start.5 = (f32[8,1024,256]{2,1,0:T(8,128)S(1)}, f32[8,1024,256]{2,1,0:T(8,128)}, u32[]{:S(2)}) copy-start(f32[8,1024,256]{2,1,0:T(8,128)} %copy-done.4) | copy-start | bytes 25165828
  78.9 2.2 %copy-start.11 = (f32[8,1024,128]{2,1,0:T(8,128)S(1)}, f32[8,1024,128]{2,1,0:T(8,128)}, u32[]{:S(2)}) copy-start(f32[8,1024,128]{2,1,0:T(8,128)} %copy-done.10) | copy-start | bytes 12582916
  (4 other events, 2.9 us)

commit v9 on v7

--- a/solution.py
+++ b/solution.py
@@ -43,7 +43,7 @@
         out_shape=jax.ShapeDtypeStruct((count, *arrays[0].shape), arrays[0].dtype),
         in_specs=[pl.BlockSpec(memory_space=pltpu.VMEM)] * count,
         out_specs=pl.BlockSpec(memory_space=pltpu.VMEM),
-        compiler_params=pltpu.CompilerParams(vmem_limit_bytes=32 * 2**20),
+        compiler_params=pltpu.CompilerParams(vmem_limit_bytes=4 * 2**20),
         name=name,
     )(*arrays)
 
@@ -73,9 +73,10 @@
     return guess * (2.0 - x * guess)
 
 
-def attend_kernel(grid, groups, kept, last, query_ref, *refs):
-    depth, width, cores = grid
-    blocks_refs, refs = refs[: 2 * len(groups)], refs[2 * len(groups) :]
+def attend_kernel(grid, entries, kept, last, query_ref, *refs):
+    depth, width, cores = grid
+    count = len(entries)
+    own_refs, core_refs, refs = refs[:count], refs[count : 3 * count], refs[3 * count :]
     kept_refs, refs = refs[: 2 * kept], refs[2 * kept :]
     out_refs, scratch = list(refs[: 2 - last]), list(refs[2 - last :])
     if not kept:
@@ -84,7 +85,7 @@
         result_ref = out_refs[0]
         out_refs[0], sems = scratch.pop(0), scratch.pop(0)
     tok = query_ref.shape[0]
-    dim = blocks_refs[0].shape[-1] // KV_HEADS
+    dim = own_refs[0].shape[-1] // KV_HEADS
     rows = GROUP * tok
     part_rows = rows // PARTS
     heads = part_rows // tok
@@ -92,12 +93,10 @@
     zz, yy, cc = place(grid)
 
     pieces = []
-    for below, own_ref, core_ref in zip(groups, blocks_refs[::2], blocks_refs[1::2]):
-        for dc, ref in ((0, own_ref), (1, core_ref)):
-            for at, dz in enumerate(below):
-                pieces.append((dz, dc, below[:at].count(dz), ref, at))
+    for at, (dz, dy) in enumerate(entries):
+        pieces.append((dz, 0, dy, own_refs[at].at[0], own_refs[at].at[1]))
+        pieces.append((dz, 1, dy, *core_refs[2 * at : 2 * at + 2]))
     pieces.sort(key=lambda piece: piece[:3])
-    lowest, highest = pieces[0][0], pieces[-1][0]
 
     if scratch:
         bias_ref = scratch[0]
@@ -133,8 +132,8 @@
     def attend(used, span):
         def one(head):
             span_of = column(head)
-            keys = jnp.concatenate([ref[at, 0, :, span_of] for _, _, _, ref, at in used], axis=0)
-            values = jnp.concatenate([ref[at, 1, :, span_of] for _, _, _, ref, at in used], axis=0)
+            keys = jnp.concatenate([piece[3][:, span_of] for piece in used], axis=0)
+            values = jnp.concatenate([piece[4][:, span_of] for piece in used], axis=0)
             values = jnp.concatenate([values, jnp.ones_like(values)], axis=1)
             first_head = head * GROUP
             for part in range(PARTS):
@@ -214,30 +213,24 @@
             if last:
                 out_copy(step).start()
 
-    near = width * cores * tok if lowest == 0 else 0
-    levels = sorted(set(range(lowest, highest + 1)))
-    if len(levels) > 4:
-        levels = sorted({lowest + (len(levels) - 1) * part // 3 for part in range(4)})
-    below = lowest - 1
-    if kept and lowest > 0:
-
-        @pl.when(zz < lowest)
+    near = tok * sum(piece[0] == 0 for piece in pieces)
+    levels = sorted({piece[0] for piece in pieces})
+    masked = len(levels) > 4
+    if masked:
+        levels = levels[:1]
+    if levels[0] > 0:
+
+        @pl.when(zz < levels[0])
         def _():
             hand_on()
 
-    for level in levels:
-        used = [piece for piece in pieces if piece[0] <= level]
-        alone = level == below + 1
-        span = near if alone else len(used) * tok
-        reached = jnp.logical_and(zz > below, zz <= level)
-        if level == levels[-1]:
-            reached = zz > below
-
-        @pl.when(reached)
+    for level, above in zip(levels, levels[1:] + [depth]):
+        used = pieces if masked else [piece for piece in pieces if piece[0] <= level]
+        span = len(used) * tok if masked else near
+
+        @pl.when(jnp.logical_and(zz >= level, zz < above))
         def _(used=used, span=span):
             attend(used, span)
-
-        below = level
 
     if last:
 
@@ -265,12 +258,13 @@
         ]
         steps = KV_HEADS // STEP_HEADS
 
-        def phase(span, state):
-            last = span[-1] == depth - 1
-            merged = stack([block for dz in span for block in rows_of[dz]], "merge")
-            operands = [merged, core_swap(merged, grid)]
-            groups = [[dz for dz in span for _ in range(width)]]
-            keys = tok * 2 * len(groups[0])
+        def phase(entries, blocks, state, last=False, after=None):
+            operands = [blocks[entry] for entry in entries]
+            operands += [core_swap(blocks[entry][half], grid) for entry in entries for half in range(2)]
+            if after in blocks:
+                operands, blocks[after] = lax.optimization_barrier((operands, blocks[after]))
+            keys = tok * 2 * len(entries)
+            levels = {dz for dz, _ in entries}
             scratch = []
             if not state:
                 scratch += [pltpu.VMEM((tok, columns), query_rows.dtype)]
@@ -278,48 +272,44 @@
             if last:
                 scratch += [pltpu.VMEM((tok, columns), query_rows.dtype)]
                 scratch += [pltpu.SemaphoreType.DMA((steps,))]
-            if span[0] == 0 or len(span) > 4:
+            if 0 in levels or len(levels) > 4:
                 scratch += [pltpu.VMEM((tok, keys), jnp.float32)]
             return pl.pallas_call(
-                functools.partial(attend_kernel, grid, groups, bool(state), last),
+                functools.partial(attend_kernel, grid, entries, bool(state), last),
                 out_shape=query_rows if last else state_shapes,
                 in_specs=[whole if state else pl.BlockSpec(memory_space=pltpu.HBM)]
                 + [whole] * (len(operands) + len(state)),
                 out_specs=pl.BlockSpec(memory_space=pltpu.HBM) if last else [whole] * 2,
                 scratch_shapes=scratch,
-                input_output_aliases={} if last or not state else {3: 0, 4: 1},
+                input_output_aliases={} if last or not state else {1 + len(operands) + at: at for at in range(2)},
                 compiler_params=pltpu.CompilerParams(vmem_limit_bytes=16 * 2**20),
-                cost_estimate=pl.CostEstimate(
-                    flops=4 * HEADS * tok * keys * dim,
-                    bytes_accessed=4 * HEADS * tok * dim,
-                    transcendentals=HEADS * tok * keys,
-                ),
-                name=f"attend_{span[0]}",
+                cost_estimate=pl.CostEstimate(flops=1000, bytes_accessed=1000, transcendentals=0),
+                name="attend_last" if last else f"attend_{entries[0][0]}",
             )(query_rows if state else pinned, *operands, *state)
 
-        spans = [range(0, 1), range(1, 2)]
-        spans += [range(at, min(at + 4, depth - 1)) for at in range(2, depth - 1, 4)]
-        spans += [range(depth - 1, depth)]
-        block = stack([key_rows, value_rows], "pack")
-        rows_of, state = [], []
+        batches = [[(0, 0), (1, 0)]] + [[(dz, 0)] for dz in range(2, depth)]
+        if width == 2:
+            for dz in range(depth - 2):
+                batches[dz + 1].append((dz, 1))
+            batches.append([(depth - 2, 1), (depth - 1, 1)])
+        while len(batches) > 8:
+            batches = [sum(batches[at : at + 2], []) for at in range(0, len(batches), 2)]
+        blocks = {(0, 0): stack([key_rows, value_rows], "pack")}
+        state = []
         for dz in range(depth):
-            rows_of.append([block, y_swap(block, grid)] if width == 2 else [block])
-            if dz + 1 == depth:
-                break
-            block = z_forward(block, grid)
-            at = dz - 1
-            if dz and spans[0][-1] <= at:
-                span = spans.pop(0)
-                state = phase(span, state)
-            if dz:
-                block, state, rows_of[dz] = lax.optimization_barrier((block, state, rows_of[dz]))
-            else:
-                block, rows_of[0] = lax.optimization_barrier((block, rows_of[0]))
-        while spans:
-            if len(spans) == 1:
-                rows_of[-1], state = lax.optimization_barrier((rows_of[-1], state))
-            state = phase(spans.pop(0), state)
-        return state
+            block = blocks[dz, 0]
+            if dz + 1 < depth:
+                blocks[dz + 1, 0] = z_forward(block, grid)
+            if width == 2:
+                blocks[dz, 1] = y_swap(block, grid)
+            while len(batches) > 1 and all(entry[0] + 2 * entry[1] <= dz for entry in batches[0]):
+                state = phase(batches.pop(0), blocks, state, after=(dz - 1, 1))
+            if dz + 1 < depth:
+                blocks[dz + 1, 0], state = lax.optimization_barrier((blocks[dz + 1, 0], state))
+        tied = batches[0]
+        values, state = lax.optimization_barrier(([blocks[entry] for entry in tied], state))
+        blocks.update(zip(tied, values))
+        return phase(tied, blocks, state, last=True)
 
     spec = P(("groups", "tp"), None)
     return jax.shard_map(

time: 47.2 us -> 45.8 us (0.970)
  waiting for transfers between devices: 13.4 us -> 7.24 us
  starting transfers between devices: 13.6 us -> 18.2 us
    ppermute x4, waiting for transfers between devices: 5.04 us -> 0.37 us  [y_swap(): lax.ppermute(block, 'tp', [(at, at ^ cores) for at in range(depth * width...]
    ppermute x4 -> x16, starting transfers between devices: 5.01 us -> 9.33 us  [core_swap(): lax.ppermute(blocks, 'tp', [(at, at ^ 1) for at in range(depth * width *...]
    ppermute x3, waiting for transfers between devices: 6.54 us -> 4.6 us  [z_forward(): lax.ppermute(block, 'tp', [(at, (at + width * cores) % count) for at in r...]
    ppermute x3, starting transfers between devices: 3.59 us -> 4.8 us  [z_forward(): lax.ppermute(block, 'tp', [(at, (at + width * cores) % count) for at in r...]
    ppermute x4, starting transfers between devices: 5.04 us -> 4.07 us  [y_swap(): lax.ppermute(block, 'tp', [(at, at ^ cores) for at in range(depth * width...]
    ppermute x4 -> x16, waiting for transfers between devices: 1.82 us -> 2.27 us  [core_swap(): lax.ppermute(blocks, 'tp', [(at, at ^ 1) for at in range(depth * width *...]
    pallas_call x5 -> x1, Pallas kernels: 1.27 us -> 1.13 us  [stack(): pl.pallas_call(kernel, out_shape=jax.ShapeDtypeStruct((count, *arrays[0]....]
  transfers between devices with their start and end apart: 11 -> 23, of which waited for: 9 -> 8; matrix products, arithmetic and copies ran while one was open for 0% -> 0% of each run, Pallas kernels for 28% -> 29%
where the time goes in v9:
time: 45.8 us; the launch traced here: 45.6 us
  Pallas kernels  19.9 us (43%)
  starting transfers between devices  18.2 us (40%)
  waiting for transfers between devices  7.24 us (16%)
    pallas_call x4, Pallas kernels, phase(): pl.pallas_call(functools.partial(attend_kernel, grid, entries, bool(state...  18.8 us
    ppermute x16, starting transfers between devices, core_swap(): lax.ppermute(blocks, 'tp', [(at, at ^ 1) for at in range(depth * width *...  9.33 us
    ppermute x3, starting transfers between devices, z_forward(): lax.ppermute(block, 'tp', [(at, (at + width * cores) % count) for at in r...  4.8 us
    ppermute x3, waiting for transfers between devices, z_forward(): lax.ppermute(block, 'tp', [(at, (at + width * cores) % count) for at in r...  4.6 us
    ppermute x4, starting transfers between devices, y_swap(): lax.ppermute(block, 'tp', [(at, at ^ cores) for at in range(depth * width...  4.07 us
    ppermute x16, waiting for transfers between devices, core_swap(): lax.ppermute(blocks, 'tp', [(at, at ^ 1) for at in range(depth * width *...  2.27 us
    pallas_call x1, Pallas kernels, stack(): pl.pallas_call(kernel, out_shape=jax.ShapeDtypeStruct((count, *arrays[0]....  1.13 us
  transfers between devices with their start and end apart: 23, of which 8 were waited for; matrix products, arithmetic and copies ran while one was open for 0% of the time, Pallas kernels for 29%

profile of v9, /device:TPU:25, one launch (start us, length us, event | category | flops | bytes accessed | tf_op | source)
XLA Modules:
  0.0 45.6 jit_solution(3747143565028781386)
XLA Ops:
  0.0 1.1 %pack.1.refs_0_ = bf16[2,64,1024]{2,1,0:T(8,128)(2,1)S(1)} custom-call(bf16[64,1024]{1,0:T(8,128)(2,1)} %refs_0_.1, bf16[64,1024]{1,0:T(8,128)(2,1)} %refs_1_.1), custom_call_target="tpu_custom_call" | custom-call | tf_op jit(solution)/shard_map/pack/pallas_call | solution.py:41
  1.2 1.3 %collective-permute-start.6 = (bf16[2,64,1024]{2,1,0:T(8,128)(2,1)S(1)}, bf16[2,64,1024]{2,1,0:T(8,128)(2,1)S(1)}, u32[]{:S(2)}, u32[]{:S(2)}) collective-permute-start(bf16[2,64,1024]{2,1,0:T(8,128)(2,1)S(1)} %pack.1.refs_0_), channel_id=1, source_target_pairs={{0,2},{1,3},{2,0},{3,1},{4,6},{5,7},{6,4},{7,5},{8,10},{9,11},{10,... | collective-permute-start | bytes 786440 | tf_op jit(solution)/shard_map/ppermute | solution.py:61
  2.5 1.2 %collective-permute-start.3 = (bf16[64,1024]{1,0:T(8,128)(2,1)S(1)}, bf16[64,1024]{1,0:T(8,128)(2,1)S(1)}, u32[]{:S(2)}, u32[]{:S(2)}) collective-permute-start(bf16[64,1024]{1,0:T(8,128)(2,1)S(1)} %get-tuple-element.93), channel_id=1, source_target_pairs={{0,1},{1,0},{2,3},{3,2},{4,5},{5,4},{6,7},{7,6},{8,9},{9,8},{10,11... | collective-permute-start | bytes 393224 | tf_op jit(solution)/shard_map/ppermute | solution.py:68
  3.7 0.1 collective-permute-start.2
  3.8 4.6 %collective-permute-done.refs_1_ = bf16[2,64,1024]{2,1,0:T(8,128)(2,1)S(1)} collective-permute-done((bf16[2,64,1024]{2,1,0:T(8,128)(2,1)S(1)}, bf16[2,64,1024]{2,1,0:T(8,128)(2,1)S(1)}, u32[]{:S(2)}, u32[]{:S(2)}) %collective-permute-start) | collective-permute-done | bytes 262176 | tf_op jit(solution)/shard_map/ppermute | solution.py:54
  8.4 1.6 %collective-permute-start.5 = (bf16[64,1024]{1,0:T(8,128)(2,1)S(1)}, bf16[64,1024]{1,0:T(8,128)(2,1)S(1)}, u32[]{:S(2)}, u32[]{:S(2)}) collective-permute-start(bf16[64,1024]{1,0:T(8,128)(2,1)S(1)} %get-tuple-element.91), channel_id=1, source_target_pairs={{0,1},{1,0},{2,3},{3,2},{4,5},{5,4},{6,7},{7,6},{8,9},{9,8},{10,11... | collective-permute-start | bytes 393224 | tf_op jit(solution)/shard_map/ppermute | solution.py:68
  10.0 0.1 collective-permute-start.4
  10.1 1.8 %collective-permute-start.1 = (bf16[2,64,1024]{2,1,0:T(8,128)(2,1)S(1)}, bf16[2,64,1024]{2,1,0:T(8,128)(2,1)S(1)}, u32[]{:S(2)}, u32[]{:S(2)}) collective-permute-start(bf16[2,64,1024]{2,1,0:T(8,128)(2,1)S(1)} %collective-permute-done.refs_1_), channel_id=1, source_target_pairs={{0,4},{1,5},{2,6},{3,7},{4,8},{5,9},{6,10},{7,11},{8,12},{9,13},{1... | collective-permute-start | bytes 786440 | tf_op jit(solution)/shard_map/ppermute | solution.py:54
  11.9 1.2 %collective-permute-start.12 = (bf16[2,64,1024]{2,1,0:T(8,128)(2,1)S(1)}, bf16[2,64,1024]{2,1,0:T(8,128)(2,1)S(1)}, u32[]{:S(2)}, u32[]{:S(2)}) collective-permute-start(bf16[2,64,1024]{2,1,0:T(8,128)(2,1)S(1)} %collective-permute-done.refs_1_), channel_id=1, source_target_pairs={{0,2},{1,3},{2,0},{3,1},{4,6},{5,7},{6,4},{7,5},{8,10},{9,11},{10,... | collective-permute-start | bytes 786440 | tf_op jit(solution)/shard_map/ppermute | solution.py:61
  13.2 1.1 %collective-permute-start.11 = (bf16[64,1024]{1,0:T(8,128)(2,1)S(1)}, bf16[64,1024]{1,0:T(8,128)(2,1)S(1)}, u32[]{:S(2)}, u32[]{:S(2)}) collective-permute-start(bf16[64,1024]{1,0:T(8,128)(2,1)S(1)} %get-tuple-element.87), channel_id=1, source_target_pairs={{0,1},{1,0},{2,3},{3,2},{4,5},{5,4},{6,7},{7,6},{8,9},{9,8},{10,11... | collective-permute-start | bytes 393224 | tf_op jit(solution)/shard_map/ppermute | solution.py:68
  14.2 0.1 collective-permute-start.10
  14.3 4.7 %attend_0.1 = (f32[8,1024,256]{2,1,0:T(8,128)S(1)}, f32[8,1024,128]{2,1,0:T(8,128)S(1)}) custom-call(bf16[64,16384]{1,0:T(8,128)(2,1)} %query_ref.7, bf16[2,64,1024]{2,1,0:T(8,128)(2,1)S(1)} %pack.1.refs_0_, bf16[2,64,1024]{2,1,0:T(8,128)(2,1)S(1)} %collective-permute-done.refs_1_, bf16[64,1024]{1,0:T(8,128)(2,1)S(1)} %collective-permute-done.2.refs_2_, ...), custom_call_target="tpu_custom_call" | custom-call | flops 1000 | bytes 1000 | tf_op jit(solution)/shard_map/attend_0/pallas_call | solution.py:277
  19.1 0.5 %collective-permute-start.9 = (bf16[64,1024]{1,0:T(8,128)(2,1)S(1)}, bf16[64,1024]{1,0:T(8,128)(2,1)S(1)}, u32[]{:S(2)}, u32[]{:S(2)}) collective-permute-start(bf16[64,1024]{1,0:T(8,128)(2,1)S(1)} %get-tuple-element.89), channel_id=1, source_target_pairs={{0,1},{1,0},{2,3},{3,2},{4,5},{5,4},{6,7},{7,6},{8,9},{9,8},{10,11... | collective-permute-start | bytes 393224 | tf_op jit(solution)/shard_map/ppermute | solution.py:68
  19.6 0.1 collective-permute-start.8
  19.6 2.9 %collective-permute-start.7 = (bf16[2,64,1024]{2,1,0:T(8,128)(2,1)S(1)}, bf16[2,64,1024]{2,1,0:T(8,128)(2,1)S(1)}, u32[]{:S(2)}, u32[]{:S(2)}) collective-permute-start(bf16[2,64,1024]{2,1,0:T(8,128)(2,1)S(1)} %collective-permute-done.1.refs_0_), channel_id=1, source_target_pairs={{0,4},{1,5},{2,6},{3,7},{4,8},{5,9},{6,10},{7,11},{8,12},{9,13},{1... | collective-permute-start | bytes 786440 | tf_op jit(solution)/shard_map/ppermute | solution.py:54
  22.6 1.2 %collective-permute-start.17 = (bf16[2,64,1024]{2,1,0:T(8,128)(2,1)S(1)}, bf16[2,64,1024]{2,1,0:T(8,128)(2,1)S(1)}, u32[]{:S(2)}, u32[]{:S(2)}) collective-permute-start(bf16[2,64,1024]{2,1,0:T(8,128)(2,1)S(1)} %collective-permute-done.1.refs_0_), channel_id=1, source_target_pairs={{0,2},{1,3},{2,0},{3,1},{4,6},{5,7},{6,4},{7,5},{8,10},{9,11},{10,... | collective-permute-start | bytes 786440 | tf_op jit(solution)/shard_map/ppermute | solution.py:61
  23.9 1.1 %collective-permute-start.16 = (bf16[64,1024]{1,0:T(8,128)(2,1)S(1)}, bf16[64,1024]{1,0:T(8,128)(2,1)S(1)}, u32[]{:S(2)}, u32[]{:S(2)}) collective-permute-start(bf16[64,1024]{1,0:T(8,128)(2,1)S(1)} %get-tuple-element.83), channel_id=1, source_target_pairs={{0,1},{1,0},{2,3},{3,2},{4,5},{5,4},{6,7},{7,6},{8,9},{9,8},{10,11... | collective-permute-start | bytes 393224 | tf_op jit(solution)/shard_map/ppermute | solution.py:68
  25.0 4.4 %attend_2.1 = (f32[8,1024,256]{2,1,0:T(8,128)S(1)}, f32[8,1024,128]{2,1,0:T(8,128)S(1)}) custom-call(bf16[64,16384]{1,0:T(8,128)(2,1)S(1)} %copy-done, bf16[2,64,1024]{2,1,0:T(8,128)(2,1)S(1)} %collective-permute-done.1.refs_0_, bf16[2,64,1024]{2,1,0:T(8,128)(2,1)S(1)} %collective-permute-done.6.refs_1_, ...), custom_call_target="tpu_custom_call", output_to_operand_aliasing={{0}: (7, {}), {1}: (8, {})} | custom-call | flops 1000 | bytes 1000 | tf_op jit(solution)/shard_map/attend_2/pallas_call | solution.py:277
  29.4 0.3 collective-permute-start.18
  29.7 1.0 %collective-permute-start.14 = (bf16[64,1024]{1,0:T(8,128)(2,1)S(1)}, bf16[64,1024]{1,0:T(8,128)(2,1)S(1)}, u32[]{:S(2)}, u32[]{:S(2)}) collective-permute-start(bf16[64,1024]{1,0:T(8,128)(2,1)S(1)} %get-tuple-element.85), channel_id=1, source_target_pairs={{0,1},{1,0},{2,3},{3,2},{4,5},{5,4},{6,7},{7,6},{8,9},{9,8},{10,11... | collective-permute-start | bytes 393224 | tf_op jit(solution)/shard_map/ppermute | solution.py:68
  30.7 0.6 %collective-permute-start.13 = (bf16[64,1024]{1,0:T(8,128)(2,1)S(1)}, bf16[64,1024]{1,0:T(8,128)(2,1)S(1)}, u32[]{:S(2)}, u32[]{:S(2)}) collective-permute-start(bf16[64,1024]{1,0:T(8,128)(2,1)S(1)} %get-tuple-element.86), channel_id=1, source_target_pairs={{0,1},{1,0},{2,3},{3,2},{4,5},{5,4},{6,7},{7,6},{8,9},{9,8},{10,11... | collective-permute-start | bytes 393224 | tf_op jit(solution)/shard_map/ppermute | solution.py:68
  31.3 0.4 collective-permute-done.14.refs_3_
  31.7 0.6 %collective-permute-done.13.refs_2_ = bf16[64,1024]{1,0:T(8,128)(2,1)S(1)} collective-permute-done((bf16[64,1024]{1,0:T(8,128)(2,1)S(1)}, bf16[64,1024]{1,0:T(8,128)(2,1)S(1)}, u32[]{:S(2)}, u32[]{:S(2)}) %collective-permute-start.13) | collective-permute-done | bytes 131104 | tf_op jit(solution)/shard_map/ppermute | solution.py:68
  32.3 4.3 %attend_3.1 = (f32[8,1024,256]{2,1,0:T(8,128)S(1)}, f32[8,1024,128]{2,1,0:T(8,128)S(1)}) custom-call(bf16[64,16384]{1,0:T(8,128)(2,1)S(1)} %copy-done, bf16[2,64,1024]{2,1,0:T(8,128)(2,1)S(1)} %collective-permute-done.7.refs_0_, bf16[2,64,1024]{2,1,0:T(8,128)(2,1)S(1)} %collective-permute-done.12.refs_1_, ...), custom_call_target="tpu_custom_call", output_to_operand_aliasing={{0}: (7, {}), {1}: (8, {})} | custom-call | flops 1000 | bytes 1000 | tf_op jit(solution)/shard_map/attend_3/pallas_call | solution.py:277
  36.6 0.4 collective-permute-done.18.refs_1_
  37.0 1.3 %collective-permute-start.20 = (bf16[64,1024]{1,0:T(8,128)(2,1)S(1)}, bf16[64,1024]{1,0:T(8,128)(2,1)S(1)}, u32[]{:S(2)}, u32[]{:S(2)}) collective-permute-start(bf16[64,1024]{1,0:T(8,128)(2,1)S(1)} %get-tuple-element.81), channel_id=1, source_target_pairs={{0,1},{1,0},{2,3},{3,2},{4,5},{5,4},{6,7},{7,6},{8,9},{9,8},{10,11... | collective-permute-start | bytes 393224 | tf_op jit(solution)/shard_map/ppermute | solution.py:68
  38.4 0.5 %collective-permute-start.22 = (bf16[64,1024]{1,0:T(8,128)(2,1)S(1)}, bf16[64,1024]{1,0:T(8,128)(2,1)S(1)}, u32[]{:S(2)}, u32[]{:S(2)}) collective-permute-start(bf16[64,1024]{1,0:T(8,128)(2,1)S(1)} %get-tuple-element.79), channel_id=1, source_target_pairs={{0,1},{1,0},{2,3},{3,2},{4,5},{5,4},{6,7},{7,6},{8,9},{9,8},{10,11... | collective-permute-start | bytes 393224 | tf_op jit(solution)/shard_map/ppermute | solution.py:68
  39.0 0.3 collective-permute-done.20.refs_3_
  39.3 0.4 collective-permute-done.19.refs_2_
  39.7 0.2 collective-permute-done.22.refs_5_
  39.9 0.4 collective-permute-done.21.refs_4_
  40.3 5.4 %attend_last.1 = bf16[64,16384]{1,0:T(8,128)(2,1)} custom-call(bf16[64,16384]{1,0:T(8,128)(2,1)S(1)} %copy-done, bf16[2,64,1024]{2,1,0:T(8,128)(2,1)S(1)} %collective-permute-done.17.refs_0_, bf16[2,64,1024]{2,1,0:T(8,128)(2,1)S(1)} %collective-permute-done.18.refs_1_, bf16[64,1024]{1,0:T(8,128)(2,1)S(1)} %collective-permute-done.19.refs_2_, ...), custom_call_target="tpu_custom_call" | custom-call | flops 1000 | bytes 1000 | tf_op jit(solution)/shard_map/attend_last/pallas_call | solution.py:277
  (29 shorter events, 0.5 us)
Async XLA Ops:
  0.0 25.0 %copy-start = (bf16[64,16384]{1,0:T(8,128)(2,1)S(1)}, bf16[64,16384]{1,0:T(8,128)(2,1)}, u32[]{:S(2)}) copy-start(bf16[64,16384]{1,0:T(8,128)(2,1)} %query_ref.7) | copy-start | bytes 6291460
  1.1 7.2 %collective-permute-start = (bf16[2,64,1024]{2,1,0:T(8,128)(2,1)S(1)}, bf16[2,64,1024]{2,1,0:T(8,128)(2,1)S(1)}, u32[]{:S(2)}, u32[]{:S(2)}) collective-permute-start(bf16[2,64,1024]{2,1,0:T(8,128)(2,1)S(1)} %pack.1.refs_0_), channel_id=1, source_target_pairs={{0,4},{1,5},{2,6},{3,7},{4,8},{5,9},{6,10},{7,11},{8,12},{9,13},{1... | collective-permute-start | bytes 786440 | tf_op jit(solution)/shard_map/ppermute | solution.py:54
  1.2 11.9 %collective-permute-start.6 = (bf16[2,64,1024]{2,1,0:T(8,128)(2,1)S(1)}, bf16[2,64,1024]{2,1,0:T(8,128)(2,1)S(1)}, u32[]{:S(2)}, u32[]{:S(2)}) collective-permute-start(bf16[2,64,1024]{2,1,0:T(8,128)(2,1)S(1)} %pack.1.refs_0_), channel_id=1, source_target_pairs={{0,2},{1,3},{2,0},{3,1},{4,6},{5,7},{6,4},{7,5},{8,10},{9,11},{10,... | collective-permute-start | bytes 786440 | tf_op jit(solution)/shard_map/ppermute | solution.py:61
  2.5 7.6 %collective-permute-start.3 = (bf16[64,1024]{1,0:T(8,128)(2,1)S(1)}, bf16[64,1024]{1,0:T(8,128)(2,1)S(1)}, u32[]{:S(2)}, u32[]{:S(2)}) collective-permute-start(bf16[64,1024]{1,0:T(8,128)(2,1)S(1)} %get-tuple-element.93), channel_id=1, source_target_pairs={{0,1},{1,0},{2,3},{3,2},{4,5},{5,4},{6,7},{7,6},{8,9},{9,8},{10,11... | collective-permute-start | bytes 393224 | tf_op jit(solution)/shard_map/ppermute | solution.py:68
  3.7 8.2 %collective-permute-start.2 = (bf16[64,1024]{1,0:T(8,128)(2,1)S(1)}, bf16[64,1024]{1,0:T(8,128)(2,1)S(1)}, u32[]{:S(2)}, u32[]{:S(2)}) collective-permute-start(bf16[64,1024]{1,0:T(8,128)(2,1)S(1)} %get-tuple-element.94), channel_id=1, source_target_pairs={{0,1},{1,0},{2,3},{3,2},{4,5},{5,4},{6,7},{7,6},{8,9},{9,8},{10,11... | collective-permute-start | bytes 393224 | tf_op jit(solution)/shard_map/ppermute | solution.py:68
  8.4 4.7 %collective-permute-start.5 = (bf16[64,1024]{1,0:T(8,128)(2,1)S(1)}, bf16[64,1024]{1,0:T(8,128)(2,1)S(1)}, u32[]{:S(2)}, u32[]{:S(2)}) collective-permute-start(bf16[64,1024]{1,0:T(8,128)(2,1)S(1)} %get-tuple-element.91), channel_id=1, source_target_pairs={{0,1},{1,0},{2,3},{3,2},{4,5},{5,4},{6,7},{7,6},{8,9},{9,8},{10,11... | collective-permute-start | bytes 393224 | tf_op jit(solution)/shard_map/ppermute | solution.py:68
  10.0 3.1 %collective-permute-start.4 = (bf16[64,1024]{1,0:T(8,128)(2,1)S(1)}, bf16[64,1024]{1,0:T(8,128)(2,1)S(1)}, u32[]{:S(2)}, u32[]{:S(2)}) collective-permute-start(bf16[64,1024]{1,0:T(8,128)(2,1)S(1)} %get-tuple-element.92), channel_id=1, source_target_pairs={{0,1},{1,0},{2,3},{3,2},{4,5},{5,4},{6,7},{7,6},{8,9},{9,8},{10,11... | collective-permute-start | bytes 393224 | tf_op jit(solution)/shard_map/ppermute | solution.py:68
  10.1 8.9 %collective-permute-start.1 = (bf16[2,64,1024]{2,1,0:T(8,128)(2,1)S(1)}, bf16[2,64,1024]{2,1,0:T(8,128)(2,1)S(1)}, u32[]{:S(2)}, u32[]{:S(2)}) collective-permute-start(bf16[2,64,1024]{2,1,0:T(8,128)(2,1)S(1)} %collective-permute-done.refs_1_), channel_id=1, source_target_pairs={{0,4},{1,5},{2,6},{3,7},{4,8},{5,9},{6,10},{7,11},{8,12},{9,13},{1... | collective-permute-start | bytes 786440 | tf_op jit(solution)/shard_map/ppermute | solution.py:54
  11.9 11.9 %collective-permute-start.12 = (bf16[2,64,1024]{2,1,0:T(8,128)(2,1)S(1)}, bf16[2,64,1024]{2,1,0:T(8,128)(2,1)S(1)}, u32[]{:S(2)}, u32[]{:S(2)}) collective-permute-start(bf16[2,64,1024]{2,1,0:T(8,128)(2,1)S(1)} %collective-permute-done.refs_1_), channel_id=1, source_target_pairs={{0,2},{1,3},{2,0},{3,1},{4,6},{5,7},{6,4},{7,5},{8,10},{9,11},{10,... | collective-permute-start | bytes 786440 | tf_op jit(solution)/shard_map/ppermute | solution.py:61
  13.2 6.5 %collective-permute-start.11 = (bf16[64,1024]{1,0:T(8,128)(2,1)S(1)}, bf16[64,1024]{1,0:T(8,128)(2,1)S(1)}, u32[]{:S(2)}, u32[]{:S(2)}) collective-permute-start(bf16[64,1024]{1,0:T(8,128)(2,1)S(1)} %get-tuple-element.87), channel_id=1, source_target_pairs={{0,1},{1,0},{2,3},{3,2},{4,5},{5,4},{6,7},{7,6},{8,9},{9,8},{10,11... | collective-permute-start | bytes 393224 | tf_op jit(solution)/shard_map/ppermute | solution.py:68
  14.2 8.4 %collective-permute-start.10 = (bf16[64,1024]{1,0:T(8,128)(2,1)S(1)}, bf16[64,1024]{1,0:T(8,128)(2,1)S(1)}, u32[]{:S(2)}, u32[]{:S(2)}) collective-permute-start(bf16[64,1024]{1,0:T(8,128)(2,1)S(1)} %get-tuple-element.88), channel_id=1, source_target_pairs={{0,1},{1,0},{2,3},{3,2},{4,5},{5,4},{6,7},{7,6},{8,9},{9,8},{10,11... | collective-permute-start | bytes 393224 | tf_op jit(solution)/shard_map/ppermute | solution.py:68
  19.1 4.8 %collective-permute-start.9 = (bf16[64,1024]{1,0:T(8,128)(2,1)S(1)}, bf16[64,1024]{1,0:T(8,128)(2,1)S(1)}, u32[]{:S(2)}, u32[]{:S(2)}) collective-permute-start(bf16[64,1024]{1,0:T(8,128)(2,1)S(1)} %get-tuple-element.89), channel_id=1, source_target_pairs={{0,1},{1,0},{2,3},{3,2},{4,5},{5,4},{6,7},{7,6},{8,9},{9,8},{10,11... | collective-permute-start | bytes 393224 | tf_op jit(solution)/shard_map/ppermute | solution.py:68
  19.6 4.3 %collective-permute-start.8 = (bf16[64,1024]{1,0:T(8,128)(2,1)S(1)}, bf16[64,1024]{1,0:T(8,128)(2,1)S(1)}, u32[]{:S(2)}, u32[]{:S(2)}) collective-permute-start(bf16[64,1024]{1,0:T(8,128)(2,1)S(1)} %get-tuple-element.90), channel_id=1, source_target_pairs={{0,1},{1,0},{2,3},{3,2},{4,5},{5,4},{6,7},{7,6},{8,9},{9,8},{10,11... | collective-permute-start | bytes 393224 | tf_op jit(solution)/shard_map/ppermute | solution.py:68
  19.6 9.8 %collective-permute-start.7 = (bf16[2,64,1024]{2,1,0:T(8,128)(2,1)S(1)}, bf16[2,64,1024]{2,1,0:T(8,128)(2,1)S(1)}, u32[]{:S(2)}, u32[]{:S(2)}) collective-permute-start(bf16[2,64,1024]{2,1,0:T(8,128)(2,1)S(1)} %collective-permute-done.1.refs_0_), channel_id=1, source_target_pairs={{0,4},{1,5},{2,6},{3,7},{4,8},{5,9},{6,10},{7,11},{8,12},{9,13},{1... | collective-permute-start | bytes 786440 | tf_op jit(solution)/shard_map/ppermute | solution.py:54
  22.6 8.1 %collective-permute-start.17 = (bf16[2,64,1024]{2,1,0:T(8,128)(2,1)S(1)}, bf16[2,64,1024]{2,1,0:T(8,128)(2,1)S(1)}, u32[]{:S(2)}, u32[]{:S(2)}) collective-permute-start(bf16[2,64,1024]{2,1,0:T(8,128)(2,1)S(1)} %collective-permute-done.1.refs_0_), channel_id=1, source_target_pairs={{0,2},{1,3},{2,0},{3,1},{4,6},{5,7},{6,4},{7,5},{8,10},{9,11},{10,... | collective-permute-start | bytes 786440 | tf_op jit(solution)/shard_map/ppermute | solution.py:61
  23.9 7.4 %collective-permute-start.16 = (bf16[64,1024]{1,0:T(8,128)(2,1)S(1)}, bf16[64,1024]{1,0:T(8,128)(2,1)S(1)}, u32[]{:S(2)}, u32[]{:S(2)}) collective-permute-start(bf16[64,1024]{1,0:T(8,128)(2,1)S(1)} %get-tuple-element.83), channel_id=1, source_target_pairs={{0,1},{1,0},{2,3},{3,2},{4,5},{5,4},{6,7},{7,6},{8,9},{9,8},{10,11... | collective-permute-start | bytes 393224 | tf_op jit(solution)/shard_map/ppermute | solution.py:68
  24.9 6.4 %collective-permute-start.15 = (bf16[64,1024]{1,0:T(8,128)(2,1)S(1)}, bf16[64,1024]{1,0:T(8,128)(2,1)S(1)}, u32[]{:S(2)}, u32[]{:S(2)}) collective-permute-start(bf16[64,1024]{1,0:T(8,128)(2,1)S(1)} %get-tuple-element.84), channel_id=1, source_target_pairs={{0,1},{1,0},{2,3},{3,2},{4,5},{5,4},{6,7},{7,6},{8,9},{9,8},{10,11... | collective-permute-start | bytes 393224 | tf_op jit(solution)/shard_map/ppermute | solution.py:68
  29.4 7.5 %collective-permute-start.18 = (bf16[2,64,1024]{2,1,0:T(8,128)(2,1)S(1)}, bf16[2,64,1024]{2,1,0:T(8,128)(2,1)S(1)}, u32[]{:S(2)}, u32[]{:S(2)}) collective-permute-start(bf16[2,64,1024]{2,1,0:T(8,128)(2,1)S(1)} %collective-permute-done.7.refs_0_), channel_id=1, source_target_pairs={{0,2},{1,3},{2,0},{3,1},{4,6},{5,7},{6,4},{7,5},{8,10},{9,11},{10,... | collective-permute-start | bytes 786440 | tf_op jit(solution)/shard_map/ppermute | solution.py:61
  29.7 2.0 %collective-permute-start.14 = (bf16[64,1024]{1,0:T(8,128)(2,1)S(1)}, bf16[64,1024]{1,0:T(8,128)(2,1)S(1)}, u32[]{:S(2)}, u32[]{:S(2)}) collective-permute-start(bf16[64,1024]{1,0:T(8,128)(2,1)S(1)} %get-tuple-element.85), channel_id=1, source_target_pairs={{0,1},{1,0},{2,3},{3,2},{4,5},{5,4},{6,7},{7,6},{8,9},{9,8},{10,11... | collective-permute-start | bytes 393224 | tf_op jit(solution)/shard_map/ppermute | solution.py:68
  30.7 1.6 %collective-permute-start.13 = (bf16[64,1024]{1,0:T(8,128)(2,1)S(1)}, bf16[64,1024]{1,0:T(8,128)(2,1)S(1)}, u32[]{:S(2)}, u32[]{:S(2)}) collective-permute-start(bf16[64,1024]{1,0:T(8,128)(2,1)S(1)} %get-tuple-element.86), channel_id=1, source_target_pairs={{0,1},{1,0},{2,3},{3,2},{4,5},{5,4},{6,7},{7,6},{8,9},{9,8},{10,11... | collective-permute-start | bytes 393224 | tf_op jit(solution)/shard_map/ppermute | solution.py:68
  37.0 2.3 %collective-permute-start.20 = (bf16[64,1024]{1,0:T(8,128)(2,1)S(1)}, bf16[64,1024]{1,0:T(8,128)(2,1)S(1)}, u32[]{:S(2)}, u32[]{:S(2)}) collective-permute-start(bf16[64,1024]{1,0:T(8,128)(2,1)S(1)} %get-tuple-element.81), channel_id=1, source_target_pairs={{0,1},{1,0},{2,3},{3,2},{4,5},{5,4},{6,7},{7,6},{8,9},{9,8},{10,11... | collective-permute-start | bytes 393224 | tf_op jit(solution)/shard_map/ppermute | solution.py:68
  38.3 1.3 %collective-permute-start.19 = (bf16[64,1024]{1,0:T(8,128)(2,1)S(1)}, bf16[64,1024]{1,0:T(8,128)(2,1)S(1)}, u32[]{:S(2)}, u32[]{:S(2)}) collective-permute-start(bf16[64,1024]{1,0:T(8,128)(2,1)S(1)} %get-tuple-element.82), channel_id=1, source_target_pairs={{0,1},{1,0},{2,3},{3,2},{4,5},{5,4},{6,7},{7,6},{8,9},{9,8},{10,11... | collective-permute-start | bytes 393224 | tf_op jit(solution)/shard_map/ppermute | solution.py:68
  38.4 1.5 %collective-permute-start.22 = (bf16[64,1024]{1,0:T(8,128)(2,1)S(1)}, bf16[64,1024]{1,0:T(8,128)(2,1)S(1)}, u32[]{:S(2)}, u32[]{:S(2)}) collective-permute-start(bf16[64,1024]{1,0:T(8,128)(2,1)S(1)} %get-tuple-element.79), channel_id=1, source_target_pairs={{0,1},{1,0},{2,3},{3,2},{4,5},{5,4},{6,7},{7,6},{8,9},{9,8},{10,11... | collective-permute-start | bytes 393224 | tf_op jit(solution)/shard_map/ppermute | solution.py:68
  38.9 1.3 %collective-permute-start.21 = (bf16[64,1024]{1,0:T(8,128)(2,1)S(1)}, bf16[64,1024]{1,0:T(8,128)(2,1)S(1)}, u32[]{:S(2)}, u32[]{:S(2)}) collective-permute-start(bf16[64,1024]{1,0:T(8,128)(2,1)S(1)} %get-tuple-element.80), channel_id=1, source_target_pairs={{0,1},{1,0},{2,3},{3,2},{4,5},{5,4},{6,7},{7,6},{8,9},{9,8},{10,11... | collective-permute-start | bytes 393224 | tf_op jit(solution)/shard_map/ppermute | solution.py:68

commit v10 on v9

--- a/solution.py
+++ b/solution.py
@@ -11,7 +11,7 @@
 HEADS = 128
 KV_HEADS = 8
 GROUP = HEADS // KV_HEADS
-PARTS = 4
+PARTS = 1
 STEP_HEADS = 2
 
 masked_score = -1e30

time: 45.8 us -> 46 us (level)
  transfers between devices with their start and end apart: 23 -> 23, of which waited for: 8 -> 8; matrix products, arithmetic and copies ran while one was open for 0% -> 0% of each run, Pallas kernels for 29% -> 30%
where the time goes in v10:
time: 46 us; the launch traced here: 45.8 us
  Pallas kernels  20.3 us (44%)
  starting transfers between devices  18 us (39%)
  waiting for transfers between devices  7.21 us (16%)
    pallas_call x4, Pallas kernels, phase(): pl.pallas_call(functools.partial(attend_kernel, grid, entries, bool(state...  19.2 us
    ppermute x16, starting transfers between devices, core_swap(): lax.ppermute(blocks, 'tp', [(at, at ^ 1) for at in range(depth * width *...  9.14 us
    ppermute x3, starting transfers between devices, z_forward(): lax.ppermute(block, 'tp', [(at, (at + width * cores) % count) for at in r...  4.8 us
    ppermute x3, waiting for transfers between devices, z_forward(): lax.ppermute(block, 'tp', [(at, (at + width * cores) % count) for at in r...  4.6 us
    ppermute x4, starting transfers between devices, y_swap(): lax.ppermute(block, 'tp', [(at, at ^ cores) for at in range(depth * width...  4.07 us
    ppermute x16, waiting for transfers between devices, core_swap(): lax.ppermute(blocks, 'tp', [(at, at ^ 1) for at in range(depth * width *...  2.27 us
    pallas_call x1, Pallas kernels, stack(): pl.pallas_call(kernel, out_shape=jax.ShapeDtypeStruct((count, *arrays[0]....  1.13 us
  transfers between devices with their start and end apart: 23, of which 8 were waited for; matrix products, arithmetic and copies ran while one was open for 0% of the time, Pallas kernels for 30%

profile of v10, /device:TPU:25, one launch (start us, length us, event | category | flops | bytes accessed | tf_op | source)
XLA Modules:
  0.0 45.8 jit_solution(13352014205858924083)
XLA Ops:
  0.0 1.1 %pack.1.refs_0_ = bf16[2,64,1024]{2,1,0:T(8,128)(2,1)S(1)} custom-call(bf16[64,1024]{1,0:T(8,128)(2,1)} %refs_0_.1, bf16[64,1024]{1,0:T(8,128)(2,1)} %refs_1_.1), custom_call_target="tpu_custom_call" | custom-call | tf_op jit(solution)/shard_map/pack/pallas_call | solution.py:41
  1.2 1.3 %collective-permute-start.6 = (bf16[2,64,1024]{2,1,0:T(8,128)(2,1)S(1)}, bf16[2,64,1024]{2,1,0:T(8,128)(2,1)S(1)}, u32[]{:S(2)}, u32[]{:S(2)}) collective-permute-start(bf16[2,64,1024]{2,1,0:T(8,128)(2,1)S(1)} %pack.1.refs_0_), channel_id=1, source_target_pairs={{0,2},{1,3},{2,0},{3,1},{4,6},{5,7},{6,4},{7,5},{8,10},{9,11},{10,... | collective-permute-start | bytes 786440 | tf_op jit(solution)/shard_map/ppermute | solution.py:61
  2.5 1.2 %collective-permute-start.3 = (bf16[64,1024]{1,0:T(8,128)(2,1)S(1)}, bf16[64,1024]{1,0:T(8,128)(2,1)S(1)}, u32[]{:S(2)}, u32[]{:S(2)}) collective-permute-start(bf16[64,1024]{1,0:T(8,128)(2,1)S(1)} %get-tuple-element.93), channel_id=1, source_target_pairs={{0,1},{1,0},{2,3},{3,2},{4,5},{5,4},{6,7},{7,6},{8,9},{9,8},{10,11... | collective-permute-start | bytes 393224 | tf_op jit(solution)/shard_map/ppermute | solution.py:68
  3.7 0.1 collective-permute-start.2
  3.8 4.6 %collective-permute-done.refs_1_ = bf16[2,64,1024]{2,1,0:T(8,128)(2,1)S(1)} collective-permute-done((bf16[2,64,1024]{2,1,0:T(8,128)(2,1)S(1)}, bf16[2,64,1024]{2,1,0:T(8,128)(2,1)S(1)}, u32[]{:S(2)}, u32[]{:S(2)}) %collective-permute-start) | collective-permute-done | bytes 262176 | tf_op jit(solution)/shard_map/ppermute | solution.py:54
  8.4 1.6 %collective-permute-start.5 = (bf16[64,1024]{1,0:T(8,128)(2,1)S(1)}, bf16[64,1024]{1,0:T(8,128)(2,1)S(1)}, u32[]{:S(2)}, u32[]{:S(2)}) collective-permute-start(bf16[64,1024]{1,0:T(8,128)(2,1)S(1)} %get-tuple-element.91), channel_id=1, source_target_pairs={{0,1},{1,0},{2,3},{3,2},{4,5},{5,4},{6,7},{7,6},{8,9},{9,8},{10,11... | collective-permute-start | bytes 393224 | tf_op jit(solution)/shard_map/ppermute | solution.py:68
  10.0 0.1 collective-permute-start.4
  10.1 1.8 %collective-permute-start.1 = (bf16[2,64,1024]{2,1,0:T(8,128)(2,1)S(1)}, bf16[2,64,1024]{2,1,0:T(8,128)(2,1)S(1)}, u32[]{:S(2)}, u32[]{:S(2)}) collective-permute-start(bf16[2,64,1024]{2,1,0:T(8,128)(2,1)S(1)} %collective-permute-done.refs_1_), channel_id=1, source_target_pairs={{0,4},{1,5},{2,6},{3,7},{4,8},{5,9},{6,10},{7,11},{8,12},{9,13},{1... | collective-permute-start | bytes 786440 | tf_op jit(solution)/shard_map/ppermute | solution.py:54
  11.9 1.2 %collective-permute-start.12 = (bf16[2,64,1024]{2,1,0:T(8,128)(2,1)S(1)}, bf16[2,64,1024]{2,1,0:T(8,128)(2,1)S(1)}, u32[]{:S(2)}, u32[]{:S(2)}) collective-permute-start(bf16[2,64,1024]{2,1,0:T(8,128)(2,1)S(1)} %collective-permute-done.refs_1_), channel_id=1, source_target_pairs={{0,2},{1,3},{2,0},{3,1},{4,6},{5,7},{6,4},{7,5},{8,10},{9,11},{10,... | collective-permute-start | bytes 786440 | tf_op jit(solution)/shard_map/ppermute | solution.py:61
  13.2 1.1 %collective-permute-start.11 = (bf16[64,1024]{1,0:T(8,128)(2,1)S(1)}, bf16[64,1024]{1,0:T(8,128)(2,1)S(1)}, u32[]{:S(2)}, u32[]{:S(2)}) collective-permute-start(bf16[64,1024]{1,0:T(8,128)(2,1)S(1)} %get-tuple-element.87), channel_id=1, source_target_pairs={{0,1},{1,0},{2,3},{3,2},{4,5},{5,4},{6,7},{7,6},{8,9},{9,8},{10,11... | collective-permute-start | bytes 393224 | tf_op jit(solution)/shard_map/ppermute | solution.py:68
  14.2 0.1 collective-permute-start.10
  14.3 4.7 %attend_0.1 = (f32[8,1024,256]{2,1,0:T(8,128)S(1)}, f32[8,1024,128]{2,1,0:T(8,128)S(1)}) custom-call(bf16[64,16384]{1,0:T(8,128)(2,1)} %query_ref.7, bf16[2,64,1024]{2,1,0:T(8,128)(2,1)S(1)} %pack.1.refs_0_, bf16[2,64,1024]{2,1,0:T(8,128)(2,1)S(1)} %collective-permute-done.refs_1_, bf16[64,1024]{1,0:T(8,128)(2,1)S(1)} %collective-permute-done.2.refs_2_, ...), custom_call_target="tpu_custom_call" | custom-call | flops 1000 | bytes 1000 | tf_op jit(solution)/shard_map/attend_0/pallas_call | solution.py:277
  19.1 0.5 %collective-permute-start.9 = (bf16[64,1024]{1,0:T(8,128)(2,1)S(1)}, bf16[64,1024]{1,0:T(8,128)(2,1)S(1)}, u32[]{:S(2)}, u32[]{:S(2)}) collective-permute-start(bf16[64,1024]{1,0:T(8,128)(2,1)S(1)} %get-tuple-element.89), channel_id=1, source_target_pairs={{0,1},{1,0},{2,3},{3,2},{4,5},{5,4},{6,7},{7,6},{8,9},{9,8},{10,11... | collective-permute-start | bytes 393224 | tf_op jit(solution)/shard_map/ppermute | solution.py:68
  19.6 0.1 collective-permute-start.8
  19.6 2.9 %collective-permute-start.7 = (bf16[2,64,1024]{2,1,0:T(8,128)(2,1)S(1)}, bf16[2,64,1024]{2,1,0:T(8,128)(2,1)S(1)}, u32[]{:S(2)}, u32[]{:S(2)}) collective-permute-start(bf16[2,64,1024]{2,1,0:T(8,128)(2,1)S(1)} %collective-permute-done.1.refs_0_), channel_id=1, source_target_pairs={{0,4},{1,5},{2,6},{3,7},{4,8},{5,9},{6,10},{7,11},{8,12},{9,13},{1... | collective-permute-start | bytes 786440 | tf_op jit(solution)/shard_map/ppermute | solution.py:54
  22.6 1.2 %collective-permute-start.17 = (bf16[2,64,1024]{2,1,0:T(8,128)(2,1)S(1)}, bf16[2,64,1024]{2,1,0:T(8,128)(2,1)S(1)}, u32[]{:S(2)}, u32[]{:S(2)}) collective-permute-start(bf16[2,64,1024]{2,1,0:T(8,128)(2,1)S(1)} %collective-permute-done.1.refs_0_), channel_id=1, source_target_pairs={{0,2},{1,3},{2,0},{3,1},{4,6},{5,7},{6,4},{7,5},{8,10},{9,11},{10,... | collective-permute-start | bytes 786440 | tf_op jit(solution)/shard_map/ppermute | solution.py:61
  23.9 1.1 %collective-permute-start.16 = (bf16[64,1024]{1,0:T(8,128)(2,1)S(1)}, bf16[64,1024]{1,0:T(8,128)(2,1)S(1)}, u32[]{:S(2)}, u32[]{:S(2)}) collective-permute-start(bf16[64,1024]{1,0:T(8,128)(2,1)S(1)} %get-tuple-element.83), channel_id=1, source_target_pairs={{0,1},{1,0},{2,3},{3,2},{4,5},{5,4},{6,7},{7,6},{8,9},{9,8},{10,11... | collective-permute-start | bytes 393224 | tf_op jit(solution)/shard_map/ppermute | solution.py:68
  25.0 4.6 %attend_2.1 = (f32[8,1024,256]{2,1,0:T(8,128)S(1)}, f32[8,1024,128]{2,1,0:T(8,128)S(1)}) custom-call(bf16[64,16384]{1,0:T(8,128)(2,1)S(1)} %copy-done, bf16[2,64,1024]{2,1,0:T(8,128)(2,1)S(1)} %collective-permute-done.1.refs_0_, bf16[2,64,1024]{2,1,0:T(8,128)(2,1)S(1)} %collective-permute-done.6.refs_1_, ...), custom_call_target="tpu_custom_call", output_to_operand_aliasing={{0}: (7, {}), {1}: (8, {})} | custom-call | flops 1000 | bytes 1000 | tf_op jit(solution)/shard_map/attend_2/pallas_call | solution.py:277
  29.6 0.3 collective-permute-start.18
  29.9 0.8 %collective-permute-start.14 = (bf16[64,1024]{1,0:T(8,128)(2,1)S(1)}, bf16[64,1024]{1,0:T(8,128)(2,1)S(1)}, u32[]{:S(2)}, u32[]{:S(2)}) collective-permute-start(bf16[64,1024]{1,0:T(8,128)(2,1)S(1)} %get-tuple-element.85), channel_id=1, source_target_pairs={{0,1},{1,0},{2,3},{3,2},{4,5},{5,4},{6,7},{7,6},{8,9},{9,8},{10,11... | collective-permute-start | bytes 393224 | tf_op jit(solution)/shard_map/ppermute | solution.py:68
  30.7 0.6 %collective-permute-start.13 = (bf16[64,1024]{1,0:T(8,128)(2,1)S(1)}, bf16[64,1024]{1,0:T(8,128)(2,1)S(1)}, u32[]{:S(2)}, u32[]{:S(2)}) collective-permute-start(bf16[64,1024]{1,0:T(8,128)(2,1)S(1)} %get-tuple-element.86), channel_id=1, source_target_pairs={{0,1},{1,0},{2,3},{3,2},{4,5},{5,4},{6,7},{7,6},{8,9},{9,8},{10,11... | collective-permute-start | bytes 393224 | tf_op jit(solution)/shard_map/ppermute | solution.py:68
  31.3 0.4 collective-permute-done.14.refs_3_
  31.7 0.6 %collective-permute-done.13.refs_2_ = bf16[64,1024]{1,0:T(8,128)(2,1)S(1)} collective-permute-done((bf16[64,1024]{1,0:T(8,128)(2,1)S(1)}, bf16[64,1024]{1,0:T(8,128)(2,1)S(1)}, u32[]{:S(2)}, u32[]{:S(2)}) %collective-permute-start.13) | collective-permute-done | bytes 131104 | tf_op jit(solution)/shard_map/ppermute | solution.py:68
  32.3 4.5 %attend_3.1 = (f32[8,1024,256]{2,1,0:T(8,128)S(1)}, f32[8,1024,128]{2,1,0:T(8,128)S(1)}) custom-call(bf16[64,16384]{1,0:T(8,128)(2,1)S(1)} %copy-done, bf16[2,64,1024]{2,1,0:T(8,128)(2,1)S(1)} %collective-permute-done.7.refs_0_, bf16[2,64,1024]{2,1,0:T(8,128)(2,1)S(1)} %collective-permute-done.12.refs_1_, ...), custom_call_target="tpu_custom_call", output_to_operand_aliasing={{0}: (7, {}), {1}: (8, {})} | custom-call | flops 1000 | bytes 1000 | tf_op jit(solution)/shard_map/attend_3/pallas_call | solution.py:277
  36.8 0.3 collective-permute-done.18.refs_1_
  37.2 1.3 %collective-permute-start.20 = (bf16[64,1024]{1,0:T(8,128)(2,1)S(1)}, bf16[64,1024]{1,0:T(8,128)(2,1)S(1)}, u32[]{:S(2)}, u32[]{:S(2)}) collective-permute-start(bf16[64,1024]{1,0:T(8,128)(2,1)S(1)} %get-tuple-element.81), channel_id=1, source_target_pairs={{0,1},{1,0},{2,3},{3,2},{4,5},{5,4},{6,7},{7,6},{8,9},{9,8},{10,11... | collective-permute-start | bytes 393224 | tf_op jit(solution)/shard_map/ppermute | solution.py:68
  38.6 0.5 %collective-permute-start.22 = (bf16[64,1024]{1,0:T(8,128)(2,1)S(1)}, bf16[64,1024]{1,0:T(8,128)(2,1)S(1)}, u32[]{:S(2)}, u32[]{:S(2)}) collective-permute-start(bf16[64,1024]{1,0:T(8,128)(2,1)S(1)} %get-tuple-element.79), channel_id=1, source_target_pairs={{0,1},{1,0},{2,3},{3,2},{4,5},{5,4},{6,7},{7,6},{8,9},{9,8},{10,11... | collective-permute-start | bytes 393224 | tf_op jit(solution)/shard_map/ppermute | solution.py:68
  39.2 0.3 collective-permute-done.20.refs_3_
  39.5 0.4 collective-permute-done.19.refs_2_
  39.8 0.2 collective-permute-done.22.refs_5_
  40.1 0.4 collective-permute-done.21.refs_4_
  40.4 5.4 %attend_last.1 = bf16[64,16384]{1,0:T(8,128)(2,1)} custom-call(bf16[64,16384]{1,0:T(8,128)(2,1)S(1)} %copy-done, bf16[2,64,1024]{2,1,0:T(8,128)(2,1)S(1)} %collective-permute-done.17.refs_0_, bf16[2,64,1024]{2,1,0:T(8,128)(2,1)S(1)} %collective-permute-done.18.refs_1_, bf16[64,1024]{1,0:T(8,128)(2,1)S(1)} %collective-permute-done.19.refs_2_, ...), custom_call_target="tpu_custom_call" | custom-call | flops 1000 | bytes 1000 | tf_op jit(solution)/shard_map/attend_last/pallas_call | solution.py:277
  (29 shorter events, 0.5 us)
Async XLA Ops:
  0.0 25.0 %copy-start = (bf16[64,16384]{1,0:T(8,128)(2,1)S(1)}, bf16[64,16384]{1,0:T(8,128)(2,1)}, u32[]{:S(2)}) copy-start(bf16[64,16384]{1,0:T(8,128)(2,1)} %query_ref.7) | copy-start | bytes 6291460
  1.1 7.2 %collective-permute-start = (bf16[2,64,1024]{2,1,0:T(8,128)(2,1)S(1)}, bf16[2,64,1024]{2,1,0:T(8,128)(2,1)S(1)}, u32[]{:S(2)}, u32[]{:S(2)}) collective-permute-start(bf16[2,64,1024]{2,1,0:T(8,128)(2,1)S(1)} %pack.1.refs_0_), channel_id=1, source_target_pairs={{0,4},{1,5},{2,6},{3,7},{4,8},{5,9},{6,10},{7,11},{8,12},{9,13},{1... | collective-permute-start | bytes 786440 | tf_op jit(solution)/shard_map/ppermute | solution.py:54
  1.2 11.9 %collective-permute-start.6 = (bf16[2,64,1024]{2,1,0:T(8,128)(2,1)S(1)}, bf16[2,64,1024]{2,1,0:T(8,128)(2,1)S(1)}, u32[]{:S(2)}, u32[]{:S(2)}) collective-permute-start(bf16[2,64,1024]{2,1,0:T(8,128)(2,1)S(1)} %pack.1.refs_0_), channel_id=1, source_target_pairs={{0,2},{1,3},{2,0},{3,1},{4,6},{5,7},{6,4},{7,5},{8,10},{9,11},{10,... | collective-permute-start | bytes 786440 | tf_op jit(solution)/shard_map/ppermute | solution.py:61
  2.5 7.6 %collective-permute-start.3 = (bf16[64,1024]{1,0:T(8,128)(2,1)S(1)}, bf16[64,1024]{1,0:T(8,128)(2,1)S(1)}, u32[]{:S(2)}, u32[]{:S(2)}) collective-permute-start(bf16[64,1024]{1,0:T(8,128)(2,1)S(1)} %get-tuple-element.93), channel_id=1, source_target_pairs={{0,1},{1,0},{2,3},{3,2},{4,5},{5,4},{6,7},{7,6},{8,9},{9,8},{10,11... | collective-permute-start | bytes 393224 | tf_op jit(solution)/shard_map/ppermute | solution.py:68
  3.7 8.2 %collective-permute-start.2 = (bf16[64,1024]{1,0:T(8,128)(2,1)S(1)}, bf16[64,1024]{1,0:T(8,128)(2,1)S(1)}, u32[]{:S(2)}, u32[]{:S(2)}) collective-permute-start(bf16[64,1024]{1,0:T(8,128)(2,1)S(1)} %get-tuple-element.94), channel_id=1, source_target_pairs={{0,1},{1,0},{2,3},{3,2},{4,5},{5,4},{6,7},{7,6},{8,9},{9,8},{10,11... | collective-permute-start | bytes 393224 | tf_op jit(solution)/shard_map/ppermute | solution.py:68
  8.4 4.7 %collective-permute-start.5 = (bf16[64,1024]{1,0:T(8,128)(2,1)S(1)}, bf16[64,1024]{1,0:T(8,128)(2,1)S(1)}, u32[]{:S(2)}, u32[]{:S(2)}) collective-permute-start(bf16[64,1024]{1,0:T(8,128)(2,1)S(1)} %get-tuple-element.91), channel_id=1, source_target_pairs={{0,1},{1,0},{2,3},{3,2},{4,5},{5,4},{6,7},{7,6},{8,9},{9,8},{10,11... | collective-permute-start | bytes 393224 | tf_op jit(solution)/shard_map/ppermute | solution.py:68
  10.0 3.1 %collective-permute-start.4 = (bf16[64,1024]{1,0:T(8,128)(2,1)S(1)}, bf16[64,1024]{1,0:T(8,128)(2,1)S(1)}, u32[]{:S(2)}, u32[]{:S(2)}) collective-permute-start(bf16[64,1024]{1,0:T(8,128)(2,1)S(1)} %get-tuple-element.92), channel_id=1, source_target_pairs={{0,1},{1,0},{2,3},{3,2},{4,5},{5,4},{6,7},{7,6},{8,9},{9,8},{10,11... | collective-permute-start | bytes 393224 | tf_op jit(solution)/shard_map/ppermute | solution.py:68
  10.1 8.9 %collective-permute-start.1 = (bf16[2,64,1024]{2,1,0:T(8,128)(2,1)S(1)}, bf16[2,64,1024]{2,1,0:T(8,128)(2,1)S(1)}, u32[]{:S(2)}, u32[]{:S(2)}) collective-permute-start(bf16[2,64,1024]{2,1,0:T(8,128)(2,1)S(1)} %collective-permute-done.refs_1_), channel_id=1, source_target_pairs={{0,4},{1,5},{2,6},{3,7},{4,8},{5,9},{6,10},{7,11},{8,12},{9,13},{1... | collective-permute-start | bytes 786440 | tf_op jit(solution)/shard_map/ppermute | solution.py:54
  11.9 11.9 %collective-permute-start.12 = (bf16[2,64,1024]{2,1,0:T(8,128)(2,1)S(1)}, bf16[2,64,1024]{2,1,0:T(8,128)(2,1)S(1)}, u32[]{:S(2)}, u32[]{:S(2)}) collective-permute-start(bf16[2,64,1024]{2,1,0:T(8,128)(2,1)S(1)} %collective-permute-done.refs_1_), channel_id=1, source_target_pairs={{0,2},{1,3},{2,0},{3,1},{4,6},{5,7},{6,4},{7,5},{8,10},{9,11},{10,... | collective-permute-start | bytes 786440 | tf_op jit(solution)/shard_map/ppermute | solution.py:61
  13.2 6.5 %collective-permute-start.11 = (bf16[64,1024]{1,0:T(8,128)(2,1)S(1)}, bf16[64,1024]{1,0:T(8,128)(2,1)S(1)}, u32[]{:S(2)}, u32[]{:S(2)}) collective-permute-start(bf16[64,1024]{1,0:T(8,128)(2,1)S(1)} %get-tuple-element.87), channel_id=1, source_target_pairs={{0,1},{1,0},{2,3},{3,2},{4,5},{5,4},{6,7},{7,6},{8,9},{9,8},{10,11... | collective-permute-start | bytes 393224 | tf_op jit(solution)/shard_map/ppermute | solution.py:68
  14.2 8.4 %collective-permute-start.10 = (bf16[64,1024]{1,0:T(8,128)(2,1)S(1)}, bf16[64,1024]{1,0:T(8,128)(2,1)S(1)}, u32[]{:S(2)}, u32[]{:S(2)}) collective-permute-start(bf16[64,1024]{1,0:T(8,128)(2,1)S(1)} %get-tuple-element.88), channel_id=1, source_target_pairs={{0,1},{1,0},{2,3},{3,2},{4,5},{5,4},{6,7},{7,6},{8,9},{9,8},{10,11... | collective-permute-start | bytes 393224 | tf_op jit(solution)/shard_map/ppermute | solution.py:68
  19.1 4.8 %collective-permute-start.9 = (bf16[64,1024]{1,0:T(8,128)(2,1)S(1)}, bf16[64,1024]{1,0:T(8,128)(2,1)S(1)}, u32[]{:S(2)}, u32[]{:S(2)}) collective-permute-start(bf16[64,1024]{1,0:T(8,128)(2,1)S(1)} %get-tuple-element.89), channel_id=1, source_target_pairs={{0,1},{1,0},{2,3},{3,2},{4,5},{5,4},{6,7},{7,6},{8,9},{9,8},{10,11... | collective-permute-start | bytes 393224 | tf_op jit(solution)/shard_map/ppermute | solution.py:68
  19.6 4.3 %collective-permute-start.8 = (bf16[64,1024]{1,0:T(8,128)(2,1)S(1)}, bf16[64,1024]{1,0:T(8,128)(2,1)S(1)}, u32[]{:S(2)}, u32[]{:S(2)}) collective-permute-start(bf16[64,1024]{1,0:T(8,128)(2,1)S(1)} %get-tuple-element.90), channel_id=1, source_target_pairs={{0,1},{1,0},{2,3},{3,2},{4,5},{5,4},{6,7},{7,6},{8,9},{9,8},{10,11... | collective-permute-start | bytes 393224 | tf_op jit(solution)/shard_map/ppermute | solution.py:68
  19.6 10.0 %collective-permute-start.7 = (bf16[2,64,1024]{2,1,0:T(8,128)(2,1)S(1)}, bf16[2,64,1024]{2,1,0:T(8,128)(2,1)S(1)}, u32[]{:S(2)}, u32[]{:S(2)}) collective-permute-start(bf16[2,64,1024]{2,1,0:T(8,128)(2,1)S(1)} %collective-permute-done.1.refs_0_), channel_id=1, source_target_pairs={{0,4},{1,5},{2,6},{3,7},{4,8},{5,9},{6,10},{7,11},{8,12},{9,13},{1... | collective-permute-start | bytes 786440 | tf_op jit(solution)/shard_map/ppermute | solution.py:54
  22.6 8.1 %collective-permute-start.17 = (bf16[2,64,1024]{2,1,0:T(8,128)(2,1)S(1)}, bf16[2,64,1024]{2,1,0:T(8,128)(2,1)S(1)}, u32[]{:S(2)}, u32[]{:S(2)}) collective-permute-start(bf16[2,64,1024]{2,1,0:T(8,128)(2,1)S(1)} %collective-permute-done.1.refs_0_), channel_id=1, source_target_pairs={{0,2},{1,3},{2,0},{3,1},{4,6},{5,7},{6,4},{7,5},{8,10},{9,11},{10,... | collective-permute-start | bytes 786440 | tf_op jit(solution)/shard_map/ppermute | solution.py:61
  23.9 7.4 %collective-permute-start.16 = (bf16[64,1024]{1,0:T(8,128)(2,1)S(1)}, bf16[64,1024]{1,0:T(8,128)(2,1)S(1)}, u32[]{:S(2)}, u32[]{:S(2)}) collective-permute-start(bf16[64,1024]{1,0:T(8,128)(2,1)S(1)} %get-tuple-element.83), channel_id=1, source_target_pairs={{0,1},{1,0},{2,3},{3,2},{4,5},{5,4},{6,7},{7,6},{8,9},{9,8},{10,11... | collective-permute-start | bytes 393224 | tf_op jit(solution)/shard_map/ppermute | solution.py:68
  24.9 6.4 %collective-permute-start.15 = (bf16[64,1024]{1,0:T(8,128)(2,1)S(1)}, bf16[64,1024]{1,0:T(8,128)(2,1)S(1)}, u32[]{:S(2)}, u32[]{:S(2)}) collective-permute-start(bf16[64,1024]{1,0:T(8,128)(2,1)S(1)} %get-tuple-element.84), channel_id=1, source_target_pairs={{0,1},{1,0},{2,3},{3,2},{4,5},{5,4},{6,7},{7,6},{8,9},{9,8},{10,11... | collective-permute-start | bytes 393224 | tf_op jit(solution)/shard_map/ppermute | solution.py:68
  29.6 7.5 %collective-permute-start.18 = (bf16[2,64,1024]{2,1,0:T(8,128)(2,1)S(1)}, bf16[2,64,1024]{2,1,0:T(8,128)(2,1)S(1)}, u32[]{:S(2)}, u32[]{:S(2)}) collective-permute-start(bf16[2,64,1024]{2,1,0:T(8,128)(2,1)S(1)} %collective-permute-done.7.refs_0_), channel_id=1, source_target_pairs={{0,2},{1,3},{2,0},{3,1},{4,6},{5,7},{6,4},{7,5},{8,10},{9,11},{10,... | collective-permute-start | bytes 786440 | tf_op jit(solution)/shard_map/ppermute | solution.py:61
  29.9 1.8 %collective-permute-start.14 = (bf16[64,1024]{1,0:T(8,128)(2,1)S(1)}, bf16[64,1024]{1,0:T(8,128)(2,1)S(1)}, u32[]{:S(2)}, u32[]{:S(2)}) collective-permute-start(bf16[64,1024]{1,0:T(8,128)(2,1)S(1)} %get-tuple-element.85), channel_id=1, source_target_pairs={{0,1},{1,0},{2,3},{3,2},{4,5},{5,4},{6,7},{7,6},{8,9},{9,8},{10,11... | collective-permute-start | bytes 393224 | tf_op jit(solution)/shard_map/ppermute | solution.py:68
  30.7 1.6 %collective-permute-start.13 = (bf16[64,1024]{1,0:T(8,128)(2,1)S(1)}, bf16[64,1024]{1,0:T(8,128)(2,1)S(1)}, u32[]{:S(2)}, u32[]{:S(2)}) collective-permute-start(bf16[64,1024]{1,0:T(8,128)(2,1)S(1)} %get-tuple-element.86), channel_id=1, source_target_pairs={{0,1},{1,0},{2,3},{3,2},{4,5},{5,4},{6,7},{7,6},{8,9},{9,8},{10,11... | collective-permute-start | bytes 393224 | tf_op jit(solution)/shard_map/ppermute | solution.py:68
  37.2 2.3 %collective-permute-start.20 = (bf16[64,1024]{1,0:T(8,128)(2,1)S(1)}, bf16[64,1024]{1,0:T(8,128)(2,1)S(1)}, u32[]{:S(2)}, u32[]{:S(2)}) collective-permute-start(bf16[64,1024]{1,0:T(8,128)(2,1)S(1)} %get-tuple-element.81), channel_id=1, source_target_pairs={{0,1},{1,0},{2,3},{3,2},{4,5},{5,4},{6,7},{7,6},{8,9},{9,8},{10,11... | collective-permute-start | bytes 393224 | tf_op jit(solution)/shard_map/ppermute | solution.py:68
  38.5 1.3 %collective-permute-start.19 = (bf16[64,1024]{1,0:T(8,128)(2,1)S(1)}, bf16[64,1024]{1,0:T(8,128)(2,1)S(1)}, u32[]{:S(2)}, u32[]{:S(2)}) collective-permute-start(bf16[64,1024]{1,0:T(8,128)(2,1)S(1)} %get-tuple-element.82), channel_id=1, source_target_pairs={{0,1},{1,0},{2,3},{3,2},{4,5},{5,4},{6,7},{7,6},{8,9},{9,8},{10,11... | collective-permute-start | bytes 393224 | tf_op jit(solution)/shard_map/ppermute | solution.py:68
  38.6 1.5 %collective-permute-start.22 = (bf16[64,1024]{1,0:T(8,128)(2,1)S(1)}, bf16[64,1024]{1,0:T(8,128)(2,1)S(1)}, u32[]{:S(2)}, u32[]{:S(2)}) collective-permute-start(bf16[64,1024]{1,0:T(8,128)(2,1)S(1)} %get-tuple-element.79), channel_id=1, source_target_pairs={{0,1},{1,0},{2,3},{3,2},{4,5},{5,4},{6,7},{7,6},{8,9},{9,8},{10,11... | collective-permute-start | bytes 393224 | tf_op jit(solution)/shard_map/ppermute | solution.py:68
  39.1 1.3 %collective-permute-start.21 = (bf16[64,1024]{1,0:T(8,128)(2,1)S(1)}, bf16[64,1024]{1,0:T(8,128)(2,1)S(1)}, u32[]{:S(2)}, u32[]{:S(2)}) collective-permute-start(bf16[64,1024]{1,0:T(8,128)(2,1)S(1)} %get-tuple-element.80), channel_id=1, source_target_pairs={{0,1},{1,0},{2,3},{3,2},{4,5},{5,4},{6,7},{7,6},{8,9},{9,8},{10,11... | collective-permute-start | bytes 393224 | tf_op jit(solution)/shard_map/ppermute | solution.py:68

commit v11 on v10

--- a/solution.py
+++ b/solution.py
@@ -11,7 +11,7 @@
 HEADS = 128
 KV_HEADS = 8
 GROUP = HEADS // KV_HEADS
-PARTS = 1
+PARTS = 2
 STEP_HEADS = 2
 
 masked_score = -1e30
@@ -48,12 +48,31 @@
     )(*arrays)
 
 
-def z_forward(block, grid):
-    depth, width, cores = grid
-    count = depth * width * cores
-    return lax.ppermute(
-        block, "tp", [(at, (at + width * cores) % count) for at in range(count)]
-    )
+def fetch(array):
+    def kernel(array_ref, out_ref, sem):
+        copy = pltpu.make_async_copy(array_ref, out_ref, sem)
+        copy.start()
+        copy.wait()
+
+    return pl.pallas_call(
+        kernel,
+        out_shape=jax.ShapeDtypeStruct(array.shape, array.dtype),
+        in_specs=[pl.BlockSpec(memory_space=pltpu.HBM)],
+        out_specs=pl.BlockSpec(memory_space=pltpu.VMEM),
+        scratch_shapes=[pltpu.SemaphoreType.DMA],
+        compiler_params=pltpu.CompilerParams(vmem_limit_bytes=4 * 2**20),
+        name="fetch",
+    )(array)
+
+
+def z_forward(block, grid, dz):
+    depth, width, cores = grid
+    side = width * cores
+    pairs = []
+    for z in range(depth):
+        target = z if z < dz - 1 else dz - 1 if z == depth - 1 else z + 1
+        pairs += [(z * side + at, target * side + at) for at in range(side)]
+    return lax.ppermute(block, "tp", pairs)
 
 
 def y_swap(block, grid):
@@ -79,8 +98,6 @@
     own_refs, core_refs, refs = refs[:count], refs[count : 3 * count], refs[3 * count :]
     kept_refs, refs = refs[: 2 * kept], refs[2 * kept :]
     out_refs, scratch = list(refs[: 2 - last]), list(refs[2 - last :])
-    if not kept:
-        source_ref, query_ref, query_sems = query_ref, scratch.pop(0), scratch.pop(0)
     if last:
         result_ref = out_refs[0]
         out_refs[0], sems = scratch.pop(0), scratch.pop(0)
@@ -190,24 +207,9 @@
         here = pl.ds(pl.multiple_of(step * span, span), span)
         return pltpu.make_async_copy(out_refs[0].at[:, here], result_ref.at[:, here], sems.at[step])
 
-    def query_copy(step):
-        span = STEP_HEADS * GROUP * dim
-        here = pl.ds(pl.multiple_of(step * span, span), span)
-        return pltpu.make_async_copy(
-            source_ref.at[:, here], query_ref.at[:, here], query_sems.at[step]
-        )
-
-    if not kept:
-
-        @pl.loop(0, KV_HEADS // STEP_HEADS)
-        def _(step):
-            query_copy(step).start()
-
     def all_heads(one):
         @pl.loop(0, KV_HEADS // STEP_HEADS)
         def _(step):
-            if not kept:
-                query_copy(step).wait()
             for index in range(STEP_HEADS):
                 one(step * STEP_HEADS + index)
             if last:
@@ -248,7 +250,7 @@
         tok, columns = query_rows.shape
         dim = key_rows.shape[1] // KV_HEADS
         rows = GROUP * tok
-        pinned, key_rows, value_rows = (
+        query_rows, key_rows, value_rows = (
             pltpu.with_memory_space_constraint(array, pltpu.HBM)
             for array in (query_rows, key_rows, value_rows)
         )
@@ -258,17 +260,21 @@
         ]
         steps = KV_HEADS // STEP_HEADS
 
+        swaps = {}
+
+        def swapped(entry):
+            if entry not in swaps:
+                swaps[entry] = [core_swap(blocks[entry][half], grid) for half in range(2)]
+            return swaps[entry]
+
         def phase(entries, blocks, state, last=False, after=None):
             operands = [blocks[entry] for entry in entries]
-            operands += [core_swap(blocks[entry][half], grid) for entry in entries for half in range(2)]
-            if after in blocks:
+            operands += [half for entry in entries for half in swapped(entry)]
+            if after:
                 operands, blocks[after] = lax.optimization_barrier((operands, blocks[after]))
             keys = tok * 2 * len(entries)
             levels = {dz for dz, _ in entries}
             scratch = []
-            if not state:
-                scratch += [pltpu.VMEM((tok, columns), query_rows.dtype)]
-                scratch += [pltpu.SemaphoreType.DMA((steps,))]
             if last:
                 scratch += [pltpu.VMEM((tok, columns), query_rows.dtype)]
                 scratch += [pltpu.SemaphoreType.DMA((steps,))]
@@ -277,15 +283,14 @@
             return pl.pallas_call(
                 functools.partial(attend_kernel, grid, entries, bool(state), last),
                 out_shape=query_rows if last else state_shapes,
-                in_specs=[whole if state else pl.BlockSpec(memory_space=pltpu.HBM)]
-                + [whole] * (len(operands) + len(state)),
+                in_specs=[whole] * (1 + len(operands) + len(state)),
                 out_specs=pl.BlockSpec(memory_space=pltpu.HBM) if last else [whole] * 2,
                 scratch_shapes=scratch,
                 input_output_aliases={} if last or not state else {1 + len(operands) + at: at for at in range(2)},
                 compiler_params=pltpu.CompilerParams(vmem_limit_bytes=16 * 2**20),
                 cost_estimate=pl.CostEstimate(flops=1000, bytes_accessed=1000, transcendentals=0),
                 name="attend_last" if last else f"attend_{entries[0][0]}",
-            )(query_rows if state else pinned, *operands, *state)
+            )(queries, *operands, *state)
 
         batches = [[(0, 0), (1, 0)]] + [[(dz, 0)] for dz in range(2, depth)]
         if width == 2:
@@ -295,17 +300,20 @@
         while len(batches) > 8:
             batches = [sum(batches[at : at + 2], []) for at in range(0, len(batches), 2)]
         blocks = {(0, 0): stack([key_rows, value_rows], "pack")}
+        queries = fetch(query_rows)
         state = []
         for dz in range(depth):
             block = blocks[dz, 0]
             if dz + 1 < depth:
-                blocks[dz + 1, 0] = z_forward(block, grid)
+                blocks[dz + 1, 0] = z_forward(block, grid, dz + 1)
             if width == 2:
                 blocks[dz, 1] = y_swap(block, grid)
             while len(batches) > 1 and all(entry[0] + 2 * entry[1] <= dz for entry in batches[0]):
-                state = phase(batches.pop(0), blocks, state, after=(dz - 1, 1))
+                state = phase(batches.pop(0), blocks, state, after=(dz - 1, 1) if width == 2 else None)
             if dz + 1 < depth:
-                blocks[dz + 1, 0], state = lax.optimization_barrier((blocks[dz + 1, 0], state))
+                blocks[dz + 1, 0], state, queries = lax.optimization_barrier(
+                    (blocks[dz + 1, 0], state, queries)
+                )
         tied = batches[0]
         values, state = lax.optimization_barrier(([blocks[entry] for entry in tied], state))
         blocks.update(zip(tied, values))

time: 46 us -> 47.6 us (1.035)
  the two profiles are of different devices: /device:TPU:25 before, /device:TPU:19 now
where the time goes in v11:
time: 47.6 us; the launch traced here: 47.4 us
  starting transfers between devices  21.7 us (46%)
  Pallas kernels  21.2 us (45%)
  waiting for transfers between devices  4.22 us (9%)
    pallas_call x4, Pallas kernels, phase(): pl.pallas_call(functools.partial(attend_kernel, grid, entries, bool(state...  18.7 us
    ppermute x16, starting transfers between devices, core_swap(): lax.ppermute(blocks, 'tp', [(at, at ^ 1) for at in range(depth * width *...  9.77 us
    ppermute x3, starting transfers between devices, z_forward(): return lax.ppermute(block, 'tp', pairs)  7.74 us
    ppermute x4, starting transfers between devices, y_swap(): lax.ppermute(block, 'tp', [(at, at ^ cores) for at in range(depth * width...  4.16 us
    ppermute x16, waiting for transfers between devices, core_swap(): lax.ppermute(blocks, 'tp', [(at, at ^ 1) for at in range(depth * width *...  2.55 us
    ppermute x3, waiting for transfers between devices, z_forward(): return lax.ppermute(block, 'tp', pairs)  1.65 us
    pallas_call x1, Pallas kernels, fetch(): pl.pallas_call(kernel, out_shape=jax.ShapeDtypeStruct(array.shape, array....  1.6 us
    pallas_call x1, Pallas kernels, stack(): pl.pallas_call(kernel, out_shape=jax.ShapeDtypeStruct((count, *arrays[0]....  0.98 us
  transfers between devices with their start and end apart: 23, of which 7 were waited for; matrix products, arithmetic and copies ran while one was open for 0% of the time, Pallas kernels for 31%

profile of v11, /device:TPU:19, one launch (start us, length us, event | category | flops | bytes accessed | tf_op | source)
XLA Modules:
  0.0 47.4 jit_solution(8967411373892188144)
XLA Ops:
  0.0 1.0 %pack.1.refs_0_ = bf16[2,64,1024]{2,1,0:T(8,128)(2,1)S(1)} custom-call(bf16[64,1024]{1,0:T(8,128)(2,1)} %refs_0_.1, bf16[64,1024]{1,0:T(8,128)(2,1)} %refs_1_.1), custom_call_target="tpu_custom_call" | custom-call | tf_op jit(solution)/shard_map/pack/pallas_call | solution.py:41
  1.0 1.3 %collective-permute-start = (bf16[2,64,1024]{2,1,0:T(8,128)(2,1)S(1)}, bf16[2,64,1024]{2,1,0:T(8,128)(2,1)S(1)}, u32[]{:S(2)}, u32[]{:S(2)}) collective-permute-start(bf16[2,64,1024]{2,1,0:T(8,128)(2,1)S(1)} %pack.1.refs_0_), channel_id=1, source_target_pairs={{0,4},{1,5},{2,6},{3,7},{4,8},{5,9},{6,10},{7,11},{8,12},{9,13},{1... | collective-permute-start | bytes 786440 | tf_op jit(solution)/shard_map/ppermute | solution.py:75
  2.3 1.2 %collective-permute-start.6 = (bf16[2,64,1024]{2,1,0:T(8,128)(2,1)S(1)}, bf16[2,64,1024]{2,1,0:T(8,128)(2,1)S(1)}, u32[]{:S(2)}, u32[]{:S(2)}) collective-permute-start(bf16[2,64,1024]{2,1,0:T(8,128)(2,1)S(1)} %pack.1.refs_0_), channel_id=1, source_target_pairs={{0,2},{1,3},{2,0},{3,1},{4,6},{5,7},{6,4},{7,5},{8,10},{9,11},{10,... | collective-permute-start | bytes 786440 | tf_op jit(solution)/shard_map/ppermute | solution.py:80
  3.6 1.3 %collective-permute-start.3 = (bf16[64,1024]{1,0:T(8,128)(2,1)S(1)}, bf16[64,1024]{1,0:T(8,128)(2,1)S(1)}, u32[]{:S(2)}, u32[]{:S(2)}) collective-permute-start(bf16[64,1024]{1,0:T(8,128)(2,1)S(1)} %get-tuple-element.101), channel_id=1, source_target_pairs={{0,1},{1,0},{2,3},{3,2},{4,5},{5,4},{6,7},{7,6},{8,9},{9,8},{10,11... | collective-permute-start | bytes 393224 | tf_op jit(solution)/shard_map/ppermute | solution.py:87
  4.9 0.1 collective-permute-start.2
  5.0 1.6 %fetch.1.query_ref = bf16[64,16384]{1,0:T(8,128)(2,1)S(1)} custom-call(bf16[64,16384]{1,0:T(8,128)(2,1)} %array_ref.1), custom_call_target="tpu_custom_call" | custom-call | tf_op jit(solution)/shard_map/fetch/pallas_call | solution.py:57
  6.6 1.6 %collective-permute-done.refs_1_ = bf16[2,64,1024]{2,1,0:T(8,128)(2,1)S(1)} collective-permute-done((bf16[2,64,1024]{2,1,0:T(8,128)(2,1)S(1)}, bf16[2,64,1024]{2,1,0:T(8,128)(2,1)S(1)}, u32[]{:S(2)}, u32[]{:S(2)}) %collective-permute-start) | collective-permute-done | bytes 262176 | tf_op jit(solution)/shard_map/ppermute | solution.py:75
  8.2 1.6 %collective-permute-start.5 = (bf16[64,1024]{1,0:T(8,128)(2,1)S(1)}, bf16[64,1024]{1,0:T(8,128)(2,1)S(1)}, u32[]{:S(2)}, u32[]{:S(2)}) collective-permute-start(bf16[64,1024]{1,0:T(8,128)(2,1)S(1)} %get-tuple-element.99), channel_id=1, source_target_pairs={{0,1},{1,0},{2,3},{3,2},{4,5},{5,4},{6,7},{7,6},{8,9},{9,8},{10,11... | collective-permute-start | bytes 393224 | tf_op jit(solution)/shard_map/ppermute | solution.py:87
  9.8 0.1 collective-permute-start.4
  9.9 3.2 %collective-permute-start.1 = (bf16[2,64,1024]{2,1,0:T(8,128)(2,1)S(1)}, bf16[2,64,1024]{2,1,0:T(8,128)(2,1)S(1)}, u32[]{:S(2)}, u32[]{:S(2)}) collective-permute-start(bf16[2,64,1024]{2,1,0:T(8,128)(2,1)S(1)} %collective-permute-done.refs_1_), channel_id=1, source_target_pairs={{0,0},{1,1},{2,2},{3,3},{4,8},{5,9},{6,10},{7,11},{8,12},{9,13},{1... | collective-permute-start | bytes 786440 | tf_op jit(solution)/shard_map/ppermute | solution.py:75
  13.1 1.3 %collective-permute-start.12 = (bf16[2,64,1024]{2,1,0:T(8,128)(2,1)S(1)}, bf16[2,64,1024]{2,1,0:T(8,128)(2,1)S(1)}, u32[]{:S(2)}, u32[]{:S(2)}) collective-permute-start(bf16[2,64,1024]{2,1,0:T(8,128)(2,1)S(1)} %collective-permute-done.refs_1_), channel_id=1, source_target_pairs={{0,2},{1,3},{2,0},{3,1},{4,6},{5,7},{6,4},{7,5},{8,10},{9,11},{10,... | collective-permute-start | bytes 786440 | tf_op jit(solution)/shard_map/ppermute | solution.py:80
  14.5 1.1 %collective-permute-start.11 = (bf16[64,1024]{1,0:T(8,128)(2,1)S(1)}, bf16[64,1024]{1,0:T(8,128)(2,1)S(1)}, u32[]{:S(2)}, u32[]{:S(2)}) collective-permute-start(bf16[64,1024]{1,0:T(8,128)(2,1)S(1)} %get-tuple-element.95), channel_id=1, source_target_pairs={{0,1},{1,0},{2,3},{3,2},{4,5},{5,4},{6,7},{7,6},{8,9},{9,8},{10,11... | collective-permute-start | bytes 393224 | tf_op jit(solution)/shard_map/ppermute | solution.py:87
  15.6 3.6 %attend_0.1 = (f32[8,1024,256]{2,1,0:T(8,128)S(1)}, f32[8,1024,128]{2,1,0:T(8,128)S(1)}) custom-call(bf16[64,16384]{1,0:T(8,128)(2,1)S(1)} %fetch.1.query_ref, bf16[2,64,1024]{2,1,0:T(8,128)(2,1)S(1)} %pack.1.refs_0_, bf16[2,64,1024]{2,1,0:T(8,128)(2,1)S(1)} %collective-permute-done.refs_1_, bf16[64,1024]{1,0:T(8,128)(2,1)S(1)} %collective-permute-done.2.refs_2_, ...), custom_call_target="tpu_custom_call" | custom-call | flops 1000 | bytes 1000 | tf_op jit(solution)/shard_map/attend_0/pallas_call | solution.py:283
  19.3 1.3 %collective-permute-start.9 = (bf16[64,1024]{1,0:T(8,128)(2,1)S(1)}, bf16[64,1024]{1,0:T(8,128)(2,1)S(1)}, u32[]{:S(2)}, u32[]{:S(2)}) collective-permute-start(bf16[64,1024]{1,0:T(8,128)(2,1)S(1)} %get-tuple-element.97), channel_id=1, source_target_pairs={{0,1},{1,0},{2,3},{3,2},{4,5},{5,4},{6,7},{7,6},{8,9},{9,8},{10,11... | collective-permute-start | bytes 393224 | tf_op jit(solution)/shard_map/ppermute | solution.py:87
  20.7 3.2 %collective-permute-start.7 = (bf16[2,64,1024]{2,1,0:T(8,128)(2,1)S(1)}, bf16[2,64,1024]{2,1,0:T(8,128)(2,1)S(1)}, u32[]{:S(2)}, u32[]{:S(2)}) collective-permute-start(bf16[2,64,1024]{2,1,0:T(8,128)(2,1)S(1)} %collective-permute-done.1.refs_0_), channel_id=1, source_target_pairs={{0,0},{1,1},{2,2},{3,3},{4,4},{5,5},{6,6},{7,7},{8,12},{9,13},{10,... | collective-permute-start | bytes 786440 | tf_op jit(solution)/shard_map/ppermute | solution.py:75
  23.9 1.3 %collective-permute-start.17 = (bf16[2,64,1024]{2,1,0:T(8,128)(2,1)S(1)}, bf16[2,64,1024]{2,1,0:T(8,128)(2,1)S(1)}, u32[]{:S(2)}, u32[]{:S(2)}) collective-permute-start(bf16[2,64,1024]{2,1,0:T(8,128)(2,1)S(1)} %collective-permute-done.1.refs_0_), channel_id=1, source_target_pairs={{0,2},{1,3},{2,0},{3,1},{4,6},{5,7},{6,4},{7,5},{8,10},{9,11},{10,... | collective-permute-start | bytes 786440 | tf_op jit(solution)/shard_map/ppermute | solution.py:80
  25.3 1.1 %collective-permute-start.16 = (bf16[64,1024]{1,0:T(8,128)(2,1)S(1)}, bf16[64,1024]{1,0:T(8,128)(2,1)S(1)}, u32[]{:S(2)}, u32[]{:S(2)}) collective-permute-start(bf16[64,1024]{1,0:T(8,128)(2,1)S(1)} %get-tuple-element.91), channel_id=1, source_target_pairs={{0,1},{1,0},{2,3},{3,2},{4,5},{5,4},{6,7},{7,6},{8,9},{9,8},{10,11... | collective-permute-start | bytes 393224 | tf_op jit(solution)/shard_map/ppermute | solution.py:87
  26.3 0.1 collective-permute-start.15
  26.4 4.6 %attend_2.1 = (f32[8,1024,256]{2,1,0:T(8,128)S(1)}, f32[8,1024,128]{2,1,0:T(8,128)S(1)}) custom-call(bf16[64,16384]{1,0:T(8,128)(2,1)S(1)} %fetch.1.query_ref, bf16[2,64,1024]{2,1,0:T(8,128)(2,1)S(1)} %collective-permute-done.1.refs_0_, bf16[2,64,1024]{2,1,0:T(8,128)(2,1)S(1)} %collective-permute-done.6.refs_1_, ...), custom_call_target="tpu_custom_call", output_to_operand_aliasing={{0}: (7, {}), {1}: (8, {})} | custom-call | flops 1000 | bytes 1000 | tf_op jit(solution)/shard_map/attend_2/pallas_call | solution.py:283
  31.0 0.3 collective-permute-start.18
  31.3 1.6 %collective-permute-start.14 = (bf16[64,1024]{1,0:T(8,128)(2,1)S(1)}, bf16[64,1024]{1,0:T(8,128)(2,1)S(1)}, u32[]{:S(2)}, u32[]{:S(2)}) collective-permute-start(bf16[64,1024]{1,0:T(8,128)(2,1)S(1)} %get-tuple-element.93), channel_id=1, source_target_pairs={{0,1},{1,0},{2,3},{3,2},{4,5},{5,4},{6,7},{7,6},{8,9},{9,8},{10,11... | collective-permute-start | bytes 393224 | tf_op jit(solution)/shard_map/ppermute | solution.py:87
  32.9 0.1 collective-permute-start.13
  33.0 0.9 %collective-permute-done.14.refs_3_ = bf16[64,1024]{1,0:T(8,128)(2,1)S(1)} collective-permute-done((bf16[64,1024]{1,0:T(8,128)(2,1)S(1)}, bf16[64,1024]{1,0:T(8,128)(2,1)S(1)}, u32[]{:S(2)}, u32[]{:S(2)}) %collective-permute-start.14) | collective-permute-done | bytes 131104 | tf_op jit(solution)/shard_map/ppermute | solution.py:87
  33.9 0.4 collective-permute-done.13.refs_2_
  34.3 4.9 %attend_3.1 = (f32[8,1024,256]{2,1,0:T(8,128)S(1)}, f32[8,1024,128]{2,1,0:T(8,128)S(1)}) custom-call(bf16[64,16384]{1,0:T(8,128)(2,1)S(1)} %fetch.1.query_ref, bf16[2,64,1024]{2,1,0:T(8,128)(2,1)S(1)} %collective-permute-done.7.refs_0_, bf16[2,64,1024]{2,1,0:T(8,128)(2,1)S(1)} %collective-permute-done.12.refs_1_, ...), custom_call_target="tpu_custom_call", output_to_operand_aliasing={{0}: (7, {}), {1}: (8, {})} | custom-call | flops 1000 | bytes 1000 | tf_op jit(solution)/shard_map/attend_3/pallas_call | solution.py:283
  39.2 0.7 %collective-permute-start.20 = (bf16[64,1024]{1,0:T(8,128)(2,1)S(1)}, bf16[64,1024]{1,0:T(8,128)(2,1)S(1)}, u32[]{:S(2)}, u32[]{:S(2)}) collective-permute-start(bf16[64,1024]{1,0:T(8,128)(2,1)S(1)} %get-tuple-element.89), channel_id=1, source_target_pairs={{0,1},{1,0},{2,3},{3,2},{4,5},{5,4},{6,7},{7,6},{8,9},{9,8},{10,11... | collective-permute-start | bytes 393224 | tf_op jit(solution)/shard_map/ppermute | solution.py:87
  39.9 0.5 %collective-permute-start.22 = (bf16[64,1024]{1,0:T(8,128)(2,1)S(1)}, bf16[64,1024]{1,0:T(8,128)(2,1)S(1)}, u32[]{:S(2)}, u32[]{:S(2)}) collective-permute-start(bf16[64,1024]{1,0:T(8,128)(2,1)S(1)} %get-tuple-element.87), channel_id=1, source_target_pairs={{0,1},{1,0},{2,3},{3,2},{4,5},{5,4},{6,7},{7,6},{8,9},{9,8},{10,11... | collective-permute-start | bytes 393224 | tf_op jit(solution)/shard_map/ppermute | solution.py:87
  40.5 0.3 collective-permute-done.20.refs_3_
  40.8 0.4 collective-permute-done.19.refs_2_
  41.2 0.2 collective-permute-done.22.refs_5_
  41.4 0.4 collective-permute-done.21.refs_4_
  41.8 5.6 %attend_last.1 = bf16[64,16384]{1,0:T(8,128)(2,1)} custom-call(bf16[64,16384]{1,0:T(8,128)(2,1)S(1)} %fetch.1.query_ref, bf16[2,64,1024]{2,1,0:T(8,128)(2,1)S(1)} %collective-permute-done.17.refs_0_, bf16[2,64,1024]{2,1,0:T(8,128)(2,1)S(1)} %collective-permute-done.18.refs_1_, bf16[64,1024]{1,0:T(8,128)(2,1)S(1)} %collective-permute-done.19.refs_2_, ...), custom_call_target="tpu_custom_call" | custom-call | flops 1000 | bytes 1000 | tf_op jit(solution)/shard_map/attend_last/pallas_call | solution.py:283
  (28 shorter events, 0.5 us)
Async XLA Ops:
  1.0 7.2 %collective-permute-start = (bf16[2,64,1024]{2,1,0:T(8,128)(2,1)S(1)}, bf16[2,64,1024]{2,1,0:T(8,128)(2,1)S(1)}, u32[]{:S(2)}, u32[]{:S(2)}) collective-permute-start(bf16[2,64,1024]{2,1,0:T(8,128)(2,1)S(1)} %pack.1.refs_0_), channel_id=1, source_target_pairs={{0,4},{1,5},{2,6},{3,7},{4,8},{5,9},{6,10},{7,11},{8,12},{9,13},{1... | collective-permute-start | bytes 786440 | tf_op jit(solution)/shard_map/ppermute | solution.py:75
  2.3 12.1 %collective-permute-start.6 = (bf16[2,64,1024]{2,1,0:T(8,128)(2,1)S(1)}, bf16[2,64,1024]{2,1,0:T(8,128)(2,1)S(1)}, u32[]{:S(2)}, u32[]{:S(2)}) collective-permute-start(bf16[2,64,1024]{2,1,0:T(8,128)(2,1)S(1)} %pack.1.refs_0_), channel_id=1, source_target_pairs={{0,2},{1,3},{2,0},{3,1},{4,6},{5,7},{6,4},{7,5},{8,10},{9,11},{10,... | collective-permute-start | bytes 786440 | tf_op jit(solution)/shard_map/ppermute | solution.py:80
  3.6 6.3 %collective-permute-start.3 = (bf16[64,1024]{1,0:T(8,128)(2,1)S(1)}, bf16[64,1024]{1,0:T(8,128)(2,1)S(1)}, u32[]{:S(2)}, u32[]{:S(2)}) collective-permute-start(bf16[64,1024]{1,0:T(8,128)(2,1)S(1)} %get-tuple-element.101), channel_id=1, source_target_pairs={{0,1},{1,0},{2,3},{3,2},{4,5},{5,4},{6,7},{7,6},{8,9},{9,8},{10,11... | collective-permute-start | bytes 393224 | tf_op jit(solution)/shard_map/ppermute | solution.py:87
  4.9 8.2 %collective-permute-start.2 = (bf16[64,1024]{1,0:T(8,128)(2,1)S(1)}, bf16[64,1024]{1,0:T(8,128)(2,1)S(1)}, u32[]{:S(2)}, u32[]{:S(2)}) collective-permute-start(bf16[64,1024]{1,0:T(8,128)(2,1)S(1)} %get-tuple-element.102), channel_id=1, source_target_pairs={{0,1},{1,0},{2,3},{3,2},{4,5},{5,4},{6,7},{7,6},{8,9},{9,8},{10,11... | collective-permute-start | bytes 393224 | tf_op jit(solution)/shard_map/ppermute | solution.py:87
  8.2 6.2 %collective-permute-start.5 = (bf16[64,1024]{1,0:T(8,128)(2,1)S(1)}, bf16[64,1024]{1,0:T(8,128)(2,1)S(1)}, u32[]{:S(2)}, u32[]{:S(2)}) collective-permute-start(bf16[64,1024]{1,0:T(8,128)(2,1)S(1)} %get-tuple-element.99), channel_id=1, source_target_pairs={{0,1},{1,0},{2,3},{3,2},{4,5},{5,4},{6,7},{7,6},{8,9},{9,8},{10,11... | collective-permute-start | bytes 393224 | tf_op jit(solution)/shard_map/ppermute | solution.py:87
  9.8 4.6 %collective-permute-start.4 = (bf16[64,1024]{1,0:T(8,128)(2,1)S(1)}, bf16[64,1024]{1,0:T(8,128)(2,1)S(1)}, u32[]{:S(2)}, u32[]{:S(2)}) collective-permute-start(bf16[64,1024]{1,0:T(8,128)(2,1)S(1)} %get-tuple-element.100), channel_id=1, source_target_pairs={{0,1},{1,0},{2,3},{3,2},{4,5},{5,4},{6,7},{7,6},{8,9},{9,8},{10,11... | collective-permute-start | bytes 393224 | tf_op jit(solution)/shard_map/ppermute | solution.py:87
  9.9 9.3 %collective-permute-start.1 = (bf16[2,64,1024]{2,1,0:T(8,128)(2,1)S(1)}, bf16[2,64,1024]{2,1,0:T(8,128)(2,1)S(1)}, u32[]{:S(2)}, u32[]{:S(2)}) collective-permute-start(bf16[2,64,1024]{2,1,0:T(8,128)(2,1)S(1)} %collective-permute-done.refs_1_), channel_id=1, source_target_pairs={{0,0},{1,1},{2,2},{3,3},{4,8},{5,9},{6,10},{7,11},{8,12},{9,13},{1... | collective-permute-start | bytes 786440 | tf_op jit(solution)/shard_map/ppermute | solution.py:75
  13.1 12.1 %collective-permute-start.12 = (bf16[2,64,1024]{2,1,0:T(8,128)(2,1)S(1)}, bf16[2,64,1024]{2,1,0:T(8,128)(2,1)S(1)}, u32[]{:S(2)}, u32[]{:S(2)}) collective-permute-start(bf16[2,64,1024]{2,1,0:T(8,128)(2,1)S(1)} %collective-permute-done.refs_1_), channel_id=1, source_target_pairs={{0,2},{1,3},{2,0},{3,1},{4,6},{5,7},{6,4},{7,5},{8,10},{9,11},{10,... | collective-permute-start | bytes 786440 | tf_op jit(solution)/shard_map/ppermute | solution.py:80
  14.5 6.2 %collective-permute-start.11 = (bf16[64,1024]{1,0:T(8,128)(2,1)S(1)}, bf16[64,1024]{1,0:T(8,128)(2,1)S(1)}, u32[]{:S(2)}, u32[]{:S(2)}) collective-permute-start(bf16[64,1024]{1,0:T(8,128)(2,1)S(1)} %get-tuple-element.95), channel_id=1, source_target_pairs={{0,1},{1,0},{2,3},{3,2},{4,5},{5,4},{6,7},{7,6},{8,9},{9,8},{10,11... | collective-permute-start | bytes 393224 | tf_op jit(solution)/shard_map/ppermute | solution.py:87
  15.5 8.4 %collective-permute-start.10 = (bf16[64,1024]{1,0:T(8,128)(2,1)S(1)}, bf16[64,1024]{1,0:T(8,128)(2,1)S(1)}, u32[]{:S(2)}, u32[]{:S(2)}) collective-permute-start(bf16[64,1024]{1,0:T(8,128)(2,1)S(1)} %get-tuple-element.96), channel_id=1, source_target_pairs={{0,1},{1,0},{2,3},{3,2},{4,5},{5,4},{6,7},{7,6},{8,9},{9,8},{10,11... | collective-permute-start | bytes 393224 | tf_op jit(solution)/shard_map/ppermute | solution.py:87
  19.3 5.9 %collective-permute-start.9 = (bf16[64,1024]{1,0:T(8,128)(2,1)S(1)}, bf16[64,1024]{1,0:T(8,128)(2,1)S(1)}, u32[]{:S(2)}, u32[]{:S(2)}) collective-permute-start(bf16[64,1024]{1,0:T(8,128)(2,1)S(1)} %get-tuple-element.97), channel_id=1, source_target_pairs={{0,1},{1,0},{2,3},{3,2},{4,5},{5,4},{6,7},{7,6},{8,9},{9,8},{10,11... | collective-permute-start | bytes 393224 | tf_op jit(solution)/shard_map/ppermute | solution.py:87
  20.6 4.6 %collective-permute-start.8 = (bf16[64,1024]{1,0:T(8,128)(2,1)S(1)}, bf16[64,1024]{1,0:T(8,128)(2,1)S(1)}, u32[]{:S(2)}, u32[]{:S(2)}) collective-permute-start(bf16[64,1024]{1,0:T(8,128)(2,1)S(1)} %get-tuple-element.98), channel_id=1, source_target_pairs={{0,1},{1,0},{2,3},{3,2},{4,5},{5,4},{6,7},{7,6},{8,9},{9,8},{10,11... | collective-permute-start | bytes 393224 | tf_op jit(solution)/shard_map/ppermute | solution.py:87
  20.7 10.3 %collective-permute-start.7 = (bf16[2,64,1024]{2,1,0:T(8,128)(2,1)S(1)}, bf16[2,64,1024]{2,1,0:T(8,128)(2,1)S(1)}, u32[]{:S(2)}, u32[]{:S(2)}) collective-permute-start(bf16[2,64,1024]{2,1,0:T(8,128)(2,1)S(1)} %collective-permute-done.1.refs_0_), channel_id=1, source_target_pairs={{0,0},{1,1},{2,2},{3,3},{4,4},{5,5},{6,6},{7,7},{8,12},{9,13},{10,... | collective-permute-start | bytes 786440 | tf_op jit(solution)/shard_map/ppermute | solution.py:75
  23.9 9.0 %collective-permute-start.17 = (bf16[2,64,1024]{2,1,0:T(8,128)(2,1)S(1)}, bf16[2,64,1024]{2,1,0:T(8,128)(2,1)S(1)}, u32[]{:S(2)}, u32[]{:S(2)}) collective-permute-start(bf16[2,64,1024]{2,1,0:T(8,128)(2,1)S(1)} %collective-permute-done.1.refs_0_), channel_id=1, source_target_pairs={{0,2},{1,3},{2,0},{3,1},{4,6},{5,7},{6,4},{7,5},{8,10},{9,11},{10,... | collective-permute-start | bytes 786440 | tf_op jit(solution)/shard_map/ppermute | solution.py:80
  25.3 7.7 %collective-permute-start.16 = (bf16[64,1024]{1,0:T(8,128)(2,1)S(1)}, bf16[64,1024]{1,0:T(8,128)(2,1)S(1)}, u32[]{:S(2)}, u32[]{:S(2)}) collective-permute-start(bf16[64,1024]{1,0:T(8,128)(2,1)S(1)} %get-tuple-element.91), channel_id=1, source_target_pairs={{0,1},{1,0},{2,3},{3,2},{4,5},{5,4},{6,7},{7,6},{8,9},{9,8},{10,11... | collective-permute-start | bytes 393224 | tf_op jit(solution)/shard_map/ppermute | solution.py:87
  26.3 6.7 %collective-permute-start.15 = (bf16[64,1024]{1,0:T(8,128)(2,1)S(1)}, bf16[64,1024]{1,0:T(8,128)(2,1)S(1)}, u32[]{:S(2)}, u32[]{:S(2)}) collective-permute-start(bf16[64,1024]{1,0:T(8,128)(2,1)S(1)} %get-tuple-element.92), channel_id=1, source_target_pairs={{0,1},{1,0},{2,3},{3,2},{4,5},{5,4},{6,7},{7,6},{8,9},{9,8},{10,11... | collective-permute-start | bytes 393224 | tf_op jit(solution)/shard_map/ppermute | solution.py:87
  31.0 8.2 %collective-permute-start.18 = (bf16[2,64,1024]{2,1,0:T(8,128)(2,1)S(1)}, bf16[2,64,1024]{2,1,0:T(8,128)(2,1)S(1)}, u32[]{:S(2)}, u32[]{:S(2)}) collective-permute-start(bf16[2,64,1024]{2,1,0:T(8,128)(2,1)S(1)} %collective-permute-done.7.refs_0_), channel_id=1, source_target_pairs={{0,2},{1,3},{2,0},{3,1},{4,6},{5,7},{6,4},{7,5},{8,10},{9,11},{10,... | collective-permute-start | bytes 786440 | tf_op jit(solution)/shard_map/ppermute | solution.py:80
  31.3 2.6 %collective-permute-start.14 = (bf16[64,1024]{1,0:T(8,128)(2,1)S(1)}, bf16[64,1024]{1,0:T(8,128)(2,1)S(1)}, u32[]{:S(2)}, u32[]{:S(2)}) collective-permute-start(bf16[64,1024]{1,0:T(8,128)(2,1)S(1)} %get-tuple-element.93), channel_id=1, source_target_pairs={{0,1},{1,0},{2,3},{3,2},{4,5},{5,4},{6,7},{7,6},{8,9},{9,8},{10,11... | collective-permute-start | bytes 393224 | tf_op jit(solution)/shard_map/ppermute | solution.py:87
  32.9 1.3 %collective-permute-start.13 = (bf16[64,1024]{1,0:T(8,128)(2,1)S(1)}, bf16[64,1024]{1,0:T(8,128)(2,1)S(1)}, u32[]{:S(2)}, u32[]{:S(2)}) collective-permute-start(bf16[64,1024]{1,0:T(8,128)(2,1)S(1)} %get-tuple-element.94), channel_id=1, source_target_pairs={{0,1},{1,0},{2,3},{3,2},{4,5},{5,4},{6,7},{7,6},{8,9},{9,8},{10,11... | collective-permute-start | bytes 393224 | tf_op jit(solution)/shard_map/ppermute | solution.py:87
  39.2 1.6 %collective-permute-start.20 = (bf16[64,1024]{1,0:T(8,128)(2,1)S(1)}, bf16[64,1024]{1,0:T(8,128)(2,1)S(1)}, u32[]{:S(2)}, u32[]{:S(2)}) collective-permute-start(bf16[64,1024]{1,0:T(8,128)(2,1)S(1)} %get-tuple-element.89), channel_id=1, source_target_pairs={{0,1},{1,0},{2,3},{3,2},{4,5},{5,4},{6,7},{7,6},{8,9},{9,8},{10,11... | collective-permute-start | bytes 393224 | tf_op jit(solution)/shard_map/ppermute | solution.py:87
  39.8 1.3 %collective-permute-start.19 = (bf16[64,1024]{1,0:T(8,128)(2,1)S(1)}, bf16[64,1024]{1,0:T(8,128)(2,1)S(1)}, u32[]{:S(2)}, u32[]{:S(2)}) collective-permute-start(bf16[64,1024]{1,0:T(8,128)(2,1)S(1)} %get-tuple-element.90), channel_id=1, source_target_pairs={{0,1},{1,0},{2,3},{3,2},{4,5},{5,4},{6,7},{7,6},{8,9},{9,8},{10,11... | collective-permute-start | bytes 393224 | tf_op jit(solution)/shard_map/ppermute | solution.py:87
  39.9 1.5 %collective-permute-start.22 = (bf16[64,1024]{1,0:T(8,128)(2,1)S(1)}, bf16[64,1024]{1,0:T(8,128)(2,1)S(1)}, u32[]{:S(2)}, u32[]{:S(2)}) collective-permute-start(bf16[64,1024]{1,0:T(8,128)(2,1)S(1)} %get-tuple-element.87), channel_id=1, source_target_pairs={{0,1},{1,0},{2,3},{3,2},{4,5},{5,4},{6,7},{7,6},{8,9},{9,8},{10,11... | collective-permute-start | bytes 393224 | tf_op jit(solution)/shard_map/ppermute | solution.py:87
  40.4 1.3 %collective-permute-start.21 = (bf16[64,1024]{1,0:T(8,128)(2,1)S(1)}, bf16[64,1024]{1,0:T(8,128)(2,1)S(1)}, u32[]{:S(2)}, u32[]{:S(2)}) collective-permute-start(bf16[64,1024]{1,0:T(8,128)(2,1)S(1)} %get-tuple-element.88), channel_id=1, source_target_pairs={{0,1},{1,0},{2,3},{3,2},{4,5},{5,4},{6,7},{7,6},{8,9},{9,8},{10,11... | collective-permute-start | bytes 393224 | tf_op jit(solution)/shard_map/ppermute | solution.py:87

commit v12 on v11

--- a/solution.py
+++ b/solution.py
@@ -70,7 +70,7 @@
     side = width * cores
     pairs = []
     for z in range(depth):
-        target = z if z < dz - 1 else dz - 1 if z == depth - 1 else z + 1
+        target = z ^ 1 if dz == depth - 1 and depth % 2 == 0 else (z + 1) % depth
         pairs += [(z * side + at, target * side + at) for at in range(side)]
     return lax.ppermute(block, "tp", pairs)
 
@@ -95,7 +95,9 @@
 def attend_kernel(grid, entries, kept, last, query_ref, *refs):
     depth, width, cores = grid
     count = len(entries)
-    own_refs, core_refs, refs = refs[:count], refs[count : 3 * count], refs[3 * count :]
+    halves = 1 if last else 2
+    own_refs, refs = refs[:count], refs[count:]
+    core_refs, refs = refs[: halves * count], refs[halves * count :]
     kept_refs, refs = refs[: 2 * kept], refs[2 * kept :]
     out_refs, scratch = list(refs[: 2 - last]), list(refs[2 - last :])
     if last:
@@ -112,7 +114,10 @@
     pieces = []
     for at, (dz, dy) in enumerate(entries):
         pieces.append((dz, 0, dy, own_refs[at].at[0], own_refs[at].at[1]))
-        pieces.append((dz, 1, dy, *core_refs[2 * at : 2 * at + 2]))
+        if last:
+            pieces.append((dz, 1, dy, core_refs[at].at[0], core_refs[at].at[1]))
+        else:
+            pieces.append((dz, 1, dy, *core_refs[2 * at : 2 * at + 2]))
     pieces.sort(key=lambda piece: piece[:3])
 
     if scratch:
@@ -269,7 +274,10 @@
 
         def phase(entries, blocks, state, last=False, after=None):
             operands = [blocks[entry] for entry in entries]
-            operands += [half for entry in entries for half in swapped(entry)]
+            if last:
+                operands += [core_swap(block, grid) for block in operands]
+            else:
+                operands += [half for entry in entries for half in swapped(entry)]
             if after:
                 operands, blocks[after] = lax.optimization_barrier((operands, blocks[after]))
             keys = tok * 2 * len(entries)

time: 47.6 us -> 43.4 us (0.912)
  the two profiles are of different devices: /device:TPU:19 before, /device:TPU:0 now
where the time goes in v12:
time: 43.4 us; the launch traced here: 43.2 us
  Pallas kernels  15.1 us (35%)
  waiting for transfers between devices  14.7 us (34%)
  starting transfers between devices  13.2 us (30%)
    pallas_call x4, Pallas kernels, phase(): pl.pallas_call(functools.partial(attend_kernel, grid, entries, bool(state...  12.5 us
    ppermute x3, waiting for transfers between devices, z_forward(): return lax.ppermute(block, 'tp', pairs)  9.07 us
    ppermute x4, starting transfers between devices, y_swap(): lax.ppermute(block, 'tp', [(at, at ^ cores) for at in range(depth * width...  6.21 us
    ppermute x14, starting transfers between devices, core_swap(): lax.ppermute(blocks, 'tp', [(at, at ^ 1) for at in range(depth * width *...  3.91 us
    ppermute x4, waiting for transfers between devices, y_swap(): lax.ppermute(block, 'tp', [(at, at ^ cores) for at in range(depth * width...  3.14 us
    ppermute x3, starting transfers between devices, z_forward(): return lax.ppermute(block, 'tp', pairs)  3.08 us
    ppermute x14, waiting for transfers between devices, core_swap(): lax.ppermute(blocks, 'tp', [(at, at ^ 1) for at in range(depth * width *...  2.44 us
    pallas_call x1, Pallas kernels, fetch(): pl.pallas_call(kernel, out_shape=jax.ShapeDtypeStruct(array.shape, array....  1.6 us
  transfers between devices with their start and end apart: 21, of which 8 were waited for; matrix products, arithmetic and copies ran while one was open for 0% of the time, Pallas kernels for 28%

profile of v12, /device:TPU:0, one launch (start us, length us, event | category | flops | bytes accessed | tf_op | source)
XLA Modules:
  0.0 43.2 jit_solution(4878571214223837298)
XLA Ops:
  0.0 1.0 %pack.1.refs_0_ = bf16[2,64,1024]{2,1,0:T(8,128)(2,1)S(1)} custom-call(bf16[64,1024]{1,0:T(8,128)(2,1)} %refs_0_.1, bf16[64,1024]{1,0:T(8,128)(2,1)} %refs_1_.1), custom_call_target="tpu_custom_call" | custom-call | tf_op jit(solution)/shard_map/pack/pallas_call | solution.py:41
  1.0 3.1 %collective-permute-start = (bf16[2,64,1024]{2,1,0:T(8,128)(2,1)S(1)}, bf16[2,64,1024]{2,1,0:T(8,128)(2,1)S(1)}, u32[]{:S(2)}, u32[]{:S(2)}) collective-permute-start(bf16[2,64,1024]{2,1,0:T(8,128)(2,1)S(1)} %pack.1.refs_0_), channel_id=1, source_target_pairs={{0,4},{1,5},{2,6},{3,7},{4,8},{5,9},{6,10},{7,11},{8,12},{9,13},{1... | collective-permute-start | bytes 786440 | tf_op jit(solution)/shard_map/ppermute | solution.py:75
  4.1 1.5 %collective-permute-start.6 = (bf16[2,64,1024]{2,1,0:T(8,128)(2,1)S(1)}, bf16[2,64,1024]{2,1,0:T(8,128)(2,1)S(1)}, u32[]{:S(2)}, u32[]{:S(2)}) collective-permute-start(bf16[2,64,1024]{2,1,0:T(8,128)(2,1)S(1)} %pack.1.refs_0_), channel_id=1, source_target_pairs={{0,2},{1,3},{2,0},{3,1},{4,6},{5,7},{6,4},{7,5},{8,10},{9,11},{10,... | collective-permute-start | bytes 786440 | tf_op jit(solution)/shard_map/ppermute | solution.py:80
  5.6 0.1 collective-permute-start.3
  5.7 0.5 %collective-permute-start.2 = (bf16[64,1024]{1,0:T(8,128)(2,1)S(1)}, bf16[64,1024]{1,0:T(8,128)(2,1)S(1)}, u32[]{:S(2)}, u32[]{:S(2)}) collective-permute-start(bf16[64,1024]{1,0:T(8,128)(2,1)S(1)} %get-tuple-element.98), channel_id=1, source_target_pairs={{0,1},{1,0},{2,3},{3,2},{4,5},{5,4},{6,7},{7,6},{8,9},{9,8},{10,11... | collective-permute-start | bytes 393224 | tf_op jit(solution)/shard_map/ppermute | solution.py:87
  6.2 1.6 %fetch.1.query_ref = bf16[64,16384]{1,0:T(8,128)(2,1)S(1)} custom-call(bf16[64,16384]{1,0:T(8,128)(2,1)} %array_ref.1), custom_call_target="tpu_custom_call" | custom-call | tf_op jit(solution)/shard_map/fetch/pallas_call | solution.py:57
  7.8 4.6 %collective-permute-done.refs_1_ = bf16[2,64,1024]{2,1,0:T(8,128)(2,1)S(1)} collective-permute-done((bf16[2,64,1024]{2,1,0:T(8,128)(2,1)S(1)}, bf16[2,64,1024]{2,1,0:T(8,128)(2,1)S(1)}, u32[]{:S(2)}, u32[]{:S(2)}) %collective-permute-start) | collective-permute-done | bytes 262176 | tf_op jit(solution)/shard_map/ppermute | solution.py:75
  12.4 0.1 collective-permute-start.5
  12.5 0.5 %collective-permute-start.4 = (bf16[64,1024]{1,0:T(8,128)(2,1)S(1)}, bf16[64,1024]{1,0:T(8,128)(2,1)S(1)}, u32[]{:S(2)}, u32[]{:S(2)}) collective-permute-start(bf16[64,1024]{1,0:T(8,128)(2,1)S(1)} %get-tuple-element.96), channel_id=1, source_target_pairs={{0,1},{1,0},{2,3},{3,2},{4,5},{5,4},{6,7},{7,6},{8,9},{9,8},{10,11... | collective-permute-start | bytes 393224 | tf_op jit(solution)/shard_map/ppermute | solution.py:87
  13.0 1.6 %collective-permute-start.12 = (bf16[2,64,1024]{2,1,0:T(8,128)(2,1)S(1)}, bf16[2,64,1024]{2,1,0:T(8,128)(2,1)S(1)}, u32[]{:S(2)}, u32[]{:S(2)}) collective-permute-start(bf16[2,64,1024]{2,1,0:T(8,128)(2,1)S(1)} %collective-permute-done.refs_1_), channel_id=1, source_target_pairs={{0,2},{1,3},{2,0},{3,1},{4,6},{5,7},{6,4},{7,5},{8,10},{9,11},{10,... | collective-permute-start | bytes 786440 | tf_op jit(solution)/shard_map/ppermute | solution.py:80
  14.6 0.1 collective-permute-start.11
  14.7 0.5 %collective-permute-start.10 = (bf16[64,1024]{1,0:T(8,128)(2,1)S(1)}, bf16[64,1024]{1,0:T(8,128)(2,1)S(1)}, u32[]{:S(2)}, u32[]{:S(2)}) collective-permute-start(bf16[64,1024]{1,0:T(8,128)(2,1)S(1)} %get-tuple-element.92), channel_id=1, source_target_pairs={{0,1},{1,0},{2,3},{3,2},{4,5},{5,4},{6,7},{7,6},{8,9},{9,8},{10,11... | collective-permute-start | bytes 393224 | tf_op jit(solution)/shard_map/ppermute | solution.py:87
  15.2 4.5 %attend_0.1 = (f32[8,1024,256]{2,1,0:T(8,128)S(1)}, f32[8,1024,128]{2,1,0:T(8,128)S(1)}) custom-call(bf16[64,16384]{1,0:T(8,128)(2,1)S(1)} %fetch.1.query_ref, bf16[2,64,1024]{2,1,0:T(8,128)(2,1)S(1)} %pack.1.refs_0_, bf16[2,64,1024]{2,1,0:T(8,128)(2,1)S(1)} %collective-permute-done.refs_1_, bf16[64,1024]{1,0:T(8,128)(2,1)S(1)} %collective-permute-done.2.refs_2_, ...), custom_call_target="tpu_custom_call" | custom-call | flops 1000 | bytes 1000 | tf_op jit(solution)/shard_map/attend_0/pallas_call | solution.py:291
  19.7 3.3 %collective-permute-done.1.refs_0_ = bf16[2,64,1024]{2,1,0:T(8,128)(2,1)S(1)} collective-permute-done((bf16[2,64,1024]{2,1,0:T(8,128)(2,1)S(1)}, bf16[2,64,1024]{2,1,0:T(8,128)(2,1)S(1)}, u32[]{:S(2)}, u32[]{:S(2)}) %collective-permute-start.1) | collective-permute-done | bytes 262176 | tf_op jit(solution)/shard_map/ppermute | solution.py:75
  23.1 0.1 collective-permute-start.9
  23.2 0.5 %collective-permute-start.8 = (bf16[64,1024]{1,0:T(8,128)(2,1)S(1)}, bf16[64,1024]{1,0:T(8,128)(2,1)S(1)}, u32[]{:S(2)}, u32[]{:S(2)}) collective-permute-start(bf16[64,1024]{1,0:T(8,128)(2,1)S(1)} %get-tuple-element.94), channel_id=1, source_target_pairs={{0,1},{1,0},{2,3},{3,2},{4,5},{5,4},{6,7},{7,6},{8,9},{9,8},{10,11... | collective-permute-start | bytes 393224 | tf_op jit(solution)/shard_map/ppermute | solution.py:87
  23.7 1.6 %collective-permute-start.17 = (bf16[2,64,1024]{2,1,0:T(8,128)(2,1)S(1)}, bf16[2,64,1024]{2,1,0:T(8,128)(2,1)S(1)}, u32[]{:S(2)}, u32[]{:S(2)}) collective-permute-start(bf16[2,64,1024]{2,1,0:T(8,128)(2,1)S(1)} %collective-permute-done.1.refs_0_), channel_id=1, source_target_pairs={{0,2},{1,3},{2,0},{3,1},{4,6},{5,7},{6,4},{7,5},{8,10},{9,11},{10,... | collective-permute-start | bytes 786440 | tf_op jit(solution)/shard_map/ppermute | solution.py:80
  25.3 0.1 collective-permute-start.16
  25.4 0.5 %collective-permute-start.15 = (bf16[64,1024]{1,0:T(8,128)(2,1)S(1)}, bf16[64,1024]{1,0:T(8,128)(2,1)S(1)}, u32[]{:S(2)}, u32[]{:S(2)}) collective-permute-start(bf16[64,1024]{1,0:T(8,128)(2,1)S(1)} %get-tuple-element.88), channel_id=1, source_target_pairs={{0,1},{1,0},{2,3},{3,2},{4,5},{5,4},{6,7},{7,6},{8,9},{9,8},{10,11... | collective-permute-start | bytes 393224 | tf_op jit(solution)/shard_map/ppermute | solution.py:87
  25.9 5.0 %attend_2.1 = (f32[8,1024,256]{2,1,0:T(8,128)S(1)}, f32[8,1024,128]{2,1,0:T(8,128)S(1)}) custom-call(bf16[64,16384]{1,0:T(8,128)(2,1)S(1)} %fetch.1.query_ref, bf16[2,64,1024]{2,1,0:T(8,128)(2,1)S(1)} %collective-permute-done.1.refs_0_, bf16[2,64,1024]{2,1,0:T(8,128)(2,1)S(1)} %collective-permute-done.6.refs_1_, ...), custom_call_target="tpu_custom_call", output_to_operand_aliasing={{0}: (7, {}), {1}: (8, {})} | custom-call | flops 1000 | bytes 1000 | tf_op jit(solution)/shard_map/attend_2/pallas_call | solution.py:291
  30.9 1.1 %collective-permute-done.7.refs_0_ = bf16[2,64,1024]{2,1,0:T(8,128)(2,1)S(1)} collective-permute-done((bf16[2,64,1024]{2,1,0:T(8,128)(2,1)S(1)}, bf16[2,64,1024]{2,1,0:T(8,128)(2,1)S(1)}, u32[]{:S(2)}, u32[]{:S(2)}) %collective-permute-start.7) | collective-permute-done | bytes 262176 | tf_op jit(solution)/shard_map/ppermute | solution.py:75
  32.0 1.5 %collective-permute-start.18 = (bf16[2,64,1024]{2,1,0:T(8,128)(2,1)S(1)}, bf16[2,64,1024]{2,1,0:T(8,128)(2,1)S(1)}, u32[]{:S(2)}, u32[]{:S(2)}) collective-permute-start(bf16[2,64,1024]{2,1,0:T(8,128)(2,1)S(1)} %collective-permute-done.7.refs_0_), channel_id=1, source_target_pairs={{0,2},{1,3},{2,0},{3,1},{4,6},{5,7},{6,4},{7,5},{8,10},{9,11},{10,... | collective-permute-start | bytes 786440 | tf_op jit(solution)/shard_map/ppermute | solution.py:80
  33.5 0.1 collective-permute-start.14
  33.6 0.5 %collective-permute-start.13 = (bf16[64,1024]{1,0:T(8,128)(2,1)S(1)}, bf16[64,1024]{1,0:T(8,128)(2,1)S(1)}, u32[]{:S(2)}, u32[]{:S(2)}) collective-permute-start(bf16[64,1024]{1,0:T(8,128)(2,1)S(1)} %get-tuple-element.90), channel_id=1, source_target_pairs={{0,1},{1,0},{2,3},{3,2},{4,5},{5,4},{6,7},{7,6},{8,9},{9,8},{10,11... | collective-permute-start | bytes 393224 | tf_op jit(solution)/shard_map/ppermute | solution.py:87
  34.1 0.8 %collective-permute-done.14.refs_3_ = bf16[64,1024]{1,0:T(8,128)(2,1)S(1)} collective-permute-done((bf16[64,1024]{1,0:T(8,128)(2,1)S(1)}, bf16[64,1024]{1,0:T(8,128)(2,1)S(1)}, u32[]{:S(2)}, u32[]{:S(2)}) %collective-permute-start.14) | collective-permute-done | bytes 131104 | tf_op jit(solution)/shard_map/ppermute | solution.py:87
  34.9 0.2 collective-permute-done.13.refs_2_
  35.1 1.2 %attend_3.1 = (f32[8,1024,256]{2,1,0:T(8,128)S(1)}, f32[8,1024,128]{2,1,0:T(8,128)S(1)}) custom-call(bf16[64,16384]{1,0:T(8,128)(2,1)S(1)} %fetch.1.query_ref, bf16[2,64,1024]{2,1,0:T(8,128)(2,1)S(1)} %collective-permute-done.7.refs_0_, bf16[2,64,1024]{2,1,0:T(8,128)(2,1)S(1)} %collective-permute-done.12.refs_1_, ...), custom_call_target="tpu_custom_call", output_to_operand_aliasing={{0}: (7, {}), {1}: (8, {})} | custom-call | flops 1000 | bytes 1000 | tf_op jit(solution)/shard_map/attend_3/pallas_call | solution.py:291
  36.3 3.1 %collective-permute-done.18.refs_1_ = bf16[2,64,1024]{2,1,0:T(8,128)(2,1)S(1)} collective-permute-done((bf16[2,64,1024]{2,1,0:T(8,128)(2,1)S(1)}, bf16[2,64,1024]{2,1,0:T(8,128)(2,1)S(1)}, u32[]{:S(2)}, u32[]{:S(2)}) %collective-permute-start.18) | collective-permute-done | bytes 262176 | tf_op jit(solution)/shard_map/ppermute | solution.py:80
  39.4 0.5 %collective-permute-start.20 = (bf16[2,64,1024]{2,1,0:T(8,128)(2,1)S(1)}, bf16[2,64,1024]{2,1,0:T(8,128)(2,1)S(1)}, u32[]{:S(2)}, u32[]{:S(2)}) collective-permute-start(bf16[2,64,1024]{2,1,0:T(8,128)(2,1)S(1)} %collective-permute-done.18.refs_1_), channel_id=1, source_target_pairs={{0,1},{1,0},{2,3},{3,2},{4,5},{5,4},{6,7},{7,6},{8,9},{9,8},{10,11... | collective-permute-start | bytes 786440 | tf_op jit(solution)/shard_map/ppermute | solution.py:87
  39.9 1.0 %collective-permute-done.19.refs_2_ = bf16[2,64,1024]{2,1,0:T(8,128)(2,1)S(1)} collective-permute-done((bf16[2,64,1024]{2,1,0:T(8,128)(2,1)S(1)}, bf16[2,64,1024]{2,1,0:T(8,128)(2,1)S(1)}, u32[]{:S(2)}, u32[]{:S(2)}) %collective-permute-start.19) | collective-permute-done | bytes 262176 | tf_op jit(solution)/shard_map/ppermute | solution.py:87
  41.0 0.4 collective-permute-done.20.refs_3_
  41.3 1.9 %attend_last.1 = bf16[64,16384]{1,0:T(8,128)(2,1)} custom-call(bf16[64,16384]{1,0:T(8,128)(2,1)S(1)} %fetch.1.query_ref, bf16[2,64,1024]{2,1,0:T(8,128)(2,1)S(1)} %collective-permute-done.17.refs_0_, bf16[2,64,1024]{2,1,0:T(8,128)(2,1)S(1)} %collective-permute-done.18.refs_1_, bf16[2,64,1024]{2,1,0:T(8,128)(2,1)S(1)} %collective-permute-done.19.refs_2_, ...), custom_call_target="tpu_custom_call" | custom-call | flops 1000 | bytes 1000 | tf_op jit(solution)/shard_map/attend_last/pallas_call | solution.py:291
  (22 shorter events, 0.2 us)
Async XLA Ops:
  1.0 11.4 %collective-permute-start = (bf16[2,64,1024]{2,1,0:T(8,128)(2,1)S(1)}, bf16[2,64,1024]{2,1,0:T(8,128)(2,1)S(1)}, u32[]{:S(2)}, u32[]{:S(2)}) collective-permute-start(bf16[2,64,1024]{2,1,0:T(8,128)(2,1)S(1)} %pack.1.refs_0_), channel_id=1, source_target_pairs={{0,4},{1,5},{2,6},{3,7},{4,8},{5,9},{6,10},{7,11},{8,12},{9,13},{1... | collective-permute-start | bytes 786440 | tf_op jit(solution)/shard_map/ppermute | solution.py:75
  4.1 10.5 %collective-permute-start.6 = (bf16[2,64,1024]{2,1,0:T(8,128)(2,1)S(1)}, bf16[2,64,1024]{2,1,0:T(8,128)(2,1)S(1)}, u32[]{:S(2)}, u32[]{:S(2)}) collective-permute-start(bf16[2,64,1024]{2,1,0:T(8,128)(2,1)S(1)} %pack.1.refs_0_), channel_id=1, source_target_pairs={{0,2},{1,3},{2,0},{3,1},{4,6},{5,7},{6,4},{7,5},{8,10},{9,11},{10,... | collective-permute-start | bytes 786440 | tf_op jit(solution)/shard_map/ppermute | solution.py:80
  5.6 7.4 %collective-permute-start.3 = (bf16[64,1024]{1,0:T(8,128)(2,1)S(1)}, bf16[64,1024]{1,0:T(8,128)(2,1)S(1)}, u32[]{:S(2)}, u32[]{:S(2)}) collective-permute-start(bf16[64,1024]{1,0:T(8,128)(2,1)S(1)} %get-tuple-element.97), channel_id=1, source_target_pairs={{0,1},{1,0},{2,3},{3,2},{4,5},{5,4},{6,7},{7,6},{8,9},{9,8},{10,11... | collective-permute-start | bytes 393224 | tf_op jit(solution)/shard_map/ppermute | solution.py:87
  5.7 7.3 %collective-permute-start.2 = (bf16[64,1024]{1,0:T(8,128)(2,1)S(1)}, bf16[64,1024]{1,0:T(8,128)(2,1)S(1)}, u32[]{:S(2)}, u32[]{:S(2)}) collective-permute-start(bf16[64,1024]{1,0:T(8,128)(2,1)S(1)} %get-tuple-element.98), channel_id=1, source_target_pairs={{0,1},{1,0},{2,3},{3,2},{4,5},{5,4},{6,7},{7,6},{8,9},{9,8},{10,11... | collective-permute-start | bytes 393224 | tf_op jit(solution)/shard_map/ppermute | solution.py:87
  12.4 2.2 %collective-permute-start.5 = (bf16[64,1024]{1,0:T(8,128)(2,1)S(1)}, bf16[64,1024]{1,0:T(8,128)(2,1)S(1)}, u32[]{:S(2)}, u32[]{:S(2)}) collective-permute-start(bf16[64,1024]{1,0:T(8,128)(2,1)S(1)} %get-tuple-element.95), channel_id=1, source_target_pairs={{0,1},{1,0},{2,3},{3,2},{4,5},{5,4},{6,7},{7,6},{8,9},{9,8},{10,11... | collective-permute-start | bytes 393224 | tf_op jit(solution)/shard_map/ppermute | solution.py:87
  12.5 2.1 %collective-permute-start.4 = (bf16[64,1024]{1,0:T(8,128)(2,1)S(1)}, bf16[64,1024]{1,0:T(8,128)(2,1)S(1)}, u32[]{:S(2)}, u32[]{:S(2)}) collective-permute-start(bf16[64,1024]{1,0:T(8,128)(2,1)S(1)} %get-tuple-element.96), channel_id=1, source_target_pairs={{0,1},{1,0},{2,3},{3,2},{4,5},{5,4},{6,7},{7,6},{8,9},{9,8},{10,11... | collective-permute-start | bytes 393224 | tf_op jit(solution)/shard_map/ppermute | solution.py:87
  13.0 10.1 %collective-permute-start.1 = (bf16[2,64,1024]{2,1,0:T(8,128)(2,1)S(1)}, bf16[2,64,1024]{2,1,0:T(8,128)(2,1)S(1)}, u32[]{:S(2)}, u32[]{:S(2)}) collective-permute-start(bf16[2,64,1024]{2,1,0:T(8,128)(2,1)S(1)} %collective-permute-done.refs_1_), channel_id=1, source_target_pairs={{0,4},{1,5},{2,6},{3,7},{4,8},{5,9},{6,10},{7,11},{8,12},{9,13},{1... | collective-permute-start | bytes 786440 | tf_op jit(solution)/shard_map/ppermute | solution.py:75
  13.0 12.3 %collective-permute-start.12 = (bf16[2,64,1024]{2,1,0:T(8,128)(2,1)S(1)}, bf16[2,64,1024]{2,1,0:T(8,128)(2,1)S(1)}, u32[]{:S(2)}, u32[]{:S(2)}) collective-permute-start(bf16[2,64,1024]{2,1,0:T(8,128)(2,1)S(1)} %collective-permute-done.refs_1_), channel_id=1, source_target_pairs={{0,2},{1,3},{2,0},{3,1},{4,6},{5,7},{6,4},{7,5},{8,10},{9,11},{10,... | collective-permute-start | bytes 786440 | tf_op jit(solution)/shard_map/ppermute | solution.py:80
  14.6 9.1 %collective-permute-start.11 = (bf16[64,1024]{1,0:T(8,128)(2,1)S(1)}, bf16[64,1024]{1,0:T(8,128)(2,1)S(1)}, u32[]{:S(2)}, u32[]{:S(2)}) collective-permute-start(bf16[64,1024]{1,0:T(8,128)(2,1)S(1)} %get-tuple-element.91), channel_id=1, source_target_pairs={{0,1},{1,0},{2,3},{3,2},{4,5},{5,4},{6,7},{7,6},{8,9},{9,8},{10,11... | collective-permute-start | bytes 393224 | tf_op jit(solution)/shard_map/ppermute | solution.py:87
  14.7 9.0 %collective-permute-start.10 = (bf16[64,1024]{1,0:T(8,128)(2,1)S(1)}, bf16[64,1024]{1,0:T(8,128)(2,1)S(1)}, u32[]{:S(2)}, u32[]{:S(2)}) collective-permute-start(bf16[64,1024]{1,0:T(8,128)(2,1)S(1)} %get-tuple-element.92), channel_id=1, source_target_pairs={{0,1},{1,0},{2,3},{3,2},{4,5},{5,4},{6,7},{7,6},{8,9},{9,8},{10,11... | collective-permute-start | bytes 393224 | tf_op jit(solution)/shard_map/ppermute | solution.py:87
  23.1 2.2 %collective-permute-start.9 = (bf16[64,1024]{1,0:T(8,128)(2,1)S(1)}, bf16[64,1024]{1,0:T(8,128)(2,1)S(1)}, u32[]{:S(2)}, u32[]{:S(2)}) collective-permute-start(bf16[64,1024]{1,0:T(8,128)(2,1)S(1)} %get-tuple-element.93), channel_id=1, source_target_pairs={{0,1},{1,0},{2,3},{3,2},{4,5},{5,4},{6,7},{7,6},{8,9},{9,8},{10,11... | collective-permute-start | bytes 393224 | tf_op jit(solution)/shard_map/ppermute | solution.py:87
  23.2 2.1 %collective-permute-start.8 = (bf16[64,1024]{1,0:T(8,128)(2,1)S(1)}, bf16[64,1024]{1,0:T(8,128)(2,1)S(1)}, u32[]{:S(2)}, u32[]{:S(2)}) collective-permute-start(bf16[64,1024]{1,0:T(8,128)(2,1)S(1)} %get-tuple-element.94), channel_id=1, source_target_pairs={{0,1},{1,0},{2,3},{3,2},{4,5},{5,4},{6,7},{7,6},{8,9},{9,8},{10,11... | collective-permute-start | bytes 393224 | tf_op jit(solution)/shard_map/ppermute | solution.py:87
  23.7 8.3 %collective-permute-start.7 = (bf16[2,64,1024]{2,1,0:T(8,128)(2,1)S(1)}, bf16[2,64,1024]{2,1,0:T(8,128)(2,1)S(1)}, u32[]{:S(2)}, u32[]{:S(2)}) collective-permute-start(bf16[2,64,1024]{2,1,0:T(8,128)(2,1)S(1)} %collective-permute-done.1.refs_0_), channel_id=1, source_target_pairs={{0,4},{1,5},{2,6},{3,7},{4,0},{5,1},{6,2},{7,3},{8,12},{9,13},{10,... | collective-permute-start | bytes 786440 | tf_op jit(solution)/shard_map/ppermute | solution.py:75
  23.7 9.9 %collective-permute-start.17 = (bf16[2,64,1024]{2,1,0:T(8,128)(2,1)S(1)}, bf16[2,64,1024]{2,1,0:T(8,128)(2,1)S(1)}, u32[]{:S(2)}, u32[]{:S(2)}) collective-permute-start(bf16[2,64,1024]{2,1,0:T(8,128)(2,1)S(1)} %collective-permute-done.1.refs_0_), channel_id=1, source_target_pairs={{0,2},{1,3},{2,0},{3,1},{4,6},{5,7},{6,4},{7,5},{8,10},{9,11},{10,... | collective-permute-start | bytes 786440 | tf_op jit(solution)/shard_map/ppermute | solution.py:80
  25.3 8.8 %collective-permute-start.16 = (bf16[64,1024]{1,0:T(8,128)(2,1)S(1)}, bf16[64,1024]{1,0:T(8,128)(2,1)S(1)}, u32[]{:S(2)}, u32[]{:S(2)}) collective-permute-start(bf16[64,1024]{1,0:T(8,128)(2,1)S(1)} %get-tuple-element.87), channel_id=1, source_target_pairs={{0,1},{1,0},{2,3},{3,2},{4,5},{5,4},{6,7},{7,6},{8,9},{9,8},{10,11... | collective-permute-start | bytes 393224 | tf_op jit(solution)/shard_map/ppermute | solution.py:87
  25.4 8.7 %collective-permute-start.15 = (bf16[64,1024]{1,0:T(8,128)(2,1)S(1)}, bf16[64,1024]{1,0:T(8,128)(2,1)S(1)}, u32[]{:S(2)}, u32[]{:S(2)}) collective-permute-start(bf16[64,1024]{1,0:T(8,128)(2,1)S(1)} %get-tuple-element.88), channel_id=1, source_target_pairs={{0,1},{1,0},{2,3},{3,2},{4,5},{5,4},{6,7},{7,6},{8,9},{9,8},{10,11... | collective-permute-start | bytes 393224 | tf_op jit(solution)/shard_map/ppermute | solution.py:87
  32.0 7.4 %collective-permute-start.18 = (bf16[2,64,1024]{2,1,0:T(8,128)(2,1)S(1)}, bf16[2,64,1024]{2,1,0:T(8,128)(2,1)S(1)}, u32[]{:S(2)}, u32[]{:S(2)}) collective-permute-start(bf16[2,64,1024]{2,1,0:T(8,128)(2,1)S(1)} %collective-permute-done.7.refs_0_), channel_id=1, source_target_pairs={{0,2},{1,3},{2,0},{3,1},{4,6},{5,7},{6,4},{7,5},{8,10},{9,11},{10,... | collective-permute-start | bytes 786440 | tf_op jit(solution)/shard_map/ppermute | solution.py:80
  33.5 1.4 %collective-permute-start.14 = (bf16[64,1024]{1,0:T(8,128)(2,1)S(1)}, bf16[64,1024]{1,0:T(8,128)(2,1)S(1)}, u32[]{:S(2)}, u32[]{:S(2)}) collective-permute-start(bf16[64,1024]{1,0:T(8,128)(2,1)S(1)} %get-tuple-element.89), channel_id=1, source_target_pairs={{0,1},{1,0},{2,3},{3,2},{4,5},{5,4},{6,7},{7,6},{8,9},{9,8},{10,11... | collective-permute-start | bytes 393224 | tf_op jit(solution)/shard_map/ppermute | solution.py:87
  33.6 1.5 %collective-permute-start.13 = (bf16[64,1024]{1,0:T(8,128)(2,1)S(1)}, bf16[64,1024]{1,0:T(8,128)(2,1)S(1)}, u32[]{:S(2)}, u32[]{:S(2)}) collective-permute-start(bf16[64,1024]{1,0:T(8,128)(2,1)S(1)} %get-tuple-element.90), channel_id=1, source_target_pairs={{0,1},{1,0},{2,3},{3,2},{4,5},{5,4},{6,7},{7,6},{8,9},{9,8},{10,11... | collective-permute-start | bytes 393224 | tf_op jit(solution)/shard_map/ppermute | solution.py:87
  39.4 1.5 %collective-permute-start.19 = (bf16[2,64,1024]{2,1,0:T(8,128)(2,1)S(1)}, bf16[2,64,1024]{2,1,0:T(8,128)(2,1)S(1)}, u32[]{:S(2)}, u32[]{:S(2)}) collective-permute-start(bf16[2,64,1024]{2,1,0:T(8,128)(2,1)S(1)} %collective-permute-done.17.refs_0_), channel_id=1, source_target_pairs={{0,1},{1,0},{2,3},{3,2},{4,5},{5,4},{6,7},{7,6},{8,9},{9,8},{10,11... | collective-permute-start | bytes 786440 | tf_op jit(solution)/shard_map/ppermute | solution.py:87
  39.4 1.9 %collective-permute-start.20 = (bf16[2,64,1024]{2,1,0:T(8,128)(2,1)S(1)}, bf16[2,64,1024]{2,1,0:T(8,128)(2,1)S(1)}, u32[]{:S(2)}, u32[]{:S(2)}) collective-permute-start(bf16[2,64,1024]{2,1,0:T(8,128)(2,1)S(1)} %collective-permute-done.18.refs_1_), channel_id=1, source_target_pairs={{0,1},{1,0},{2,3},{3,2},{4,5},{5,4},{6,7},{7,6},{8,9},{9,8},{10,11... | collective-permute-start | bytes 786440 | tf_op jit(solution)/shard_map/ppermute | solution.py:87

commit v13 on v12

--- a/solution.py
+++ b/solution.py
@@ -11,7 +11,7 @@
 HEADS = 128
 KV_HEADS = 8
 GROUP = HEADS // KV_HEADS
-PARTS = 2
+PARTS = 8
 STEP_HEADS = 2
 
 masked_score = -1e30
@@ -221,23 +221,23 @@
                 out_copy(step).start()
 
     near = tok * sum(piece[0] == 0 for piece in pieces)
-    levels = sorted({piece[0] for piece in pieces})
-    masked = len(levels) > 4
-    if masked:
-        levels = levels[:1]
-    if levels[0] > 0:
-
-        @pl.when(zz < levels[0])
+    lowest, highest = pieces[0][0], pieces[-1][0]
+
+    @pl.when(zz >= highest)
+    def _():
+        attend(pieces, near)
+
+    if lowest < highest:
+
+        @pl.when(jnp.logical_and(zz >= lowest, zz < highest))
+        def _():
+            attend(pieces, len(pieces) * tok)
+
+    if lowest > 0:
+
+        @pl.when(zz < lowest)
         def _():
             hand_on()
-
-    for level, above in zip(levels, levels[1:] + [depth]):
-        used = pieces if masked else [piece for piece in pieces if piece[0] <= level]
-        span = len(used) * tok if masked else near
-
-        @pl.when(jnp.logical_and(zz >= level, zz < above))
-        def _(used=used, span=span):
-            attend(used, span)
 
     if last:
 
@@ -267,26 +267,29 @@
 
         swaps = {}
 
-        def swapped(entry):
-            if entry not in swaps:
-                swaps[entry] = [core_swap(blocks[entry][half], grid) for half in range(2)]
-            return swaps[entry]
-
         def phase(entries, blocks, state, last=False, after=None):
             operands = [blocks[entry] for entry in entries]
             if last:
-                operands += [core_swap(block, grid) for block in operands]
+                operands += [
+                    swaps[entry] if entry in swaps else core_swap(blocks[entry], grid) for entry in entries
+                ]
             else:
-                operands += [half for entry in entries for half in swapped(entry)]
+                operands += [
+                    core_swap(blocks[entry][half], grid) for entry in entries for half in range(2)
+                ]
             if after:
-                operands, blocks[after] = lax.optimization_barrier((operands, blocks[after]))
+                if dz + 1 == depth:
+                    swaps[after] = core_swap(blocks[after], grid)
+                    operands, swaps[after] = lax.optimization_barrier((operands, swaps[after]))
+                else:
+                    operands, blocks[after] = lax.optimization_barrier((operands, blocks[after]))
             keys = tok * 2 * len(entries)
             levels = {dz for dz, _ in entries}
             scratch = []
             if last:
                 scratch += [pltpu.VMEM((tok, columns), query_rows.dtype)]
                 scratch += [pltpu.SemaphoreType.DMA((steps,))]
-            if 0 in levels or len(levels) > 4:
+            if 0 in levels or len(levels) > 1:
                 scratch += [pltpu.VMEM((tok, keys), jnp.float32)]
             return pl.pallas_call(
                 functools.partial(attend_kernel, grid, entries, bool(state), last),

time: 43.4 us -> 43 us (level)
  waiting for transfers between devices: 14.7 us -> 15.8 us
  Pallas kernels: 15.1 us -> 14 us
    ppermute x3, waiting for transfers between devices: 9.07 us -> 10.2 us  [z_forward(): return lax.ppermute(block, 'tp', pairs)]
    pallas_call x4, Pallas kernels: 12.5 us -> 11.4 us  [phase(): pl.pallas_call(functools.partial(attend_kernel, grid, entries, bool(state...]
  transfers between devices with their start and end apart: 21 -> 21, of which waited for: 8 -> 7; matrix products, arithmetic and copies ran while one was open for 0% -> 0% of each run, Pallas kernels for 28% -> 26%
where the time goes in v13:
time: 43 us; the launch traced here: 42.9 us
  waiting for transfers between devices  15.8 us (37%)
  Pallas kernels  14 us (33%)
  starting transfers between devices  12.8 us (30%)
    pallas_call x4, Pallas kernels, phase(): pl.pallas_call(functools.partial(attend_kernel, grid, entries, bool(state...  11.4 us
    ppermute x3, waiting for transfers between devices, z_forward(): return lax.ppermute(block, 'tp', pairs)  10.2 us
    ppermute x4, starting transfers between devices, y_swap(): lax.ppermute(block, 'tp', [(at, at ^ cores) for at in range(depth * width...  6.21 us
    ppermute x14, starting transfers between devices, core_swap(): lax.ppermute(blocks, 'tp', [(at, at ^ 1) for at in range(depth * width *...  3.5 us
    ppermute x3, starting transfers between devices, z_forward(): return lax.ppermute(block, 'tp', pairs)  3.08 us
    ppermute x14, waiting for transfers between devices, core_swap(): lax.ppermute(blocks, 'tp', [(at, at ^ 1) for at in range(depth * width *...  2.82 us
    ppermute x4, waiting for transfers between devices, y_swap(): lax.ppermute(block, 'tp', [(at, at ^ cores) for at in range(depth * width...  2.8 us
    pallas_call x1, Pallas kernels, fetch(): pl.pallas_call(kernel, out_shape=jax.ShapeDtypeStruct(array.shape, array....  1.6 us
  transfers between devices with their start and end apart: 21, of which 7 were waited for; matrix products, arithmetic and copies ran while one was open for 0% of the time, Pallas kernels for 26%

profile of v13, /device:TPU:0, one launch (start us, length us, event | category | flops | bytes accessed | tf_op | source)
XLA Modules:
  0.0 42.9 jit_solution(14270894246977954088)
XLA Ops:
  0.0 1.0 %pack.1.refs_0_ = bf16[2,64,1024]{2,1,0:T(8,128)(2,1)S(1)} custom-call(bf16[64,1024]{1,0:T(8,128)(2,1)} %refs_0_.1, bf16[64,1024]{1,0:T(8,128)(2,1)} %refs_1_.1), custom_call_target="tpu_custom_call" | custom-call | tf_op jit(solution)/shard_map/pack/pallas_call | solution.py:41
  1.0 3.1 %collective-permute-start = (bf16[2,64,1024]{2,1,0:T(8,128)(2,1)S(1)}, bf16[2,64,1024]{2,1,0:T(8,128)(2,1)S(1)}, u32[]{:S(2)}, u32[]{:S(2)}) collective-permute-start(bf16[2,64,1024]{2,1,0:T(8,128)(2,1)S(1)} %pack.1.refs_0_), channel_id=1, source_target_pairs={{0,4},{1,5},{2,6},{3,7},{4,8},{5,9},{6,10},{7,11},{8,12},{9,13},{1... | collective-permute-start | bytes 786440 | tf_op jit(solution)/shard_map/ppermute | solution.py:75
  4.1 1.5 %collective-permute-start.6 = (bf16[2,64,1024]{2,1,0:T(8,128)(2,1)S(1)}, bf16[2,64,1024]{2,1,0:T(8,128)(2,1)S(1)}, u32[]{:S(2)}, u32[]{:S(2)}) collective-permute-start(bf16[2,64,1024]{2,1,0:T(8,128)(2,1)S(1)} %pack.1.refs_0_), channel_id=1, source_target_pairs={{0,2},{1,3},{2,0},{3,1},{4,6},{5,7},{6,4},{7,5},{8,10},{9,11},{10,... | collective-permute-start | bytes 786440 | tf_op jit(solution)/shard_map/ppermute | solution.py:80
  5.6 0.1 collective-permute-start.3
  5.7 0.5 %collective-permute-start.2 = (bf16[64,1024]{1,0:T(8,128)(2,1)S(1)}, bf16[64,1024]{1,0:T(8,128)(2,1)S(1)}, u32[]{:S(2)}, u32[]{:S(2)}) collective-permute-start(bf16[64,1024]{1,0:T(8,128)(2,1)S(1)} %get-tuple-element.98), channel_id=1, source_target_pairs={{0,1},{1,0},{2,3},{3,2},{4,5},{5,4},{6,7},{7,6},{8,9},{9,8},{10,11... | collective-permute-start | bytes 393224 | tf_op jit(solution)/shard_map/ppermute | solution.py:87
  6.2 1.6 %fetch.1.query_ref = bf16[64,16384]{1,0:T(8,128)(2,1)S(1)} custom-call(bf16[64,16384]{1,0:T(8,128)(2,1)} %array_ref.1), custom_call_target="tpu_custom_call" | custom-call | tf_op jit(solution)/shard_map/fetch/pallas_call | solution.py:57
  7.8 4.6 %collective-permute-done.refs_1_ = bf16[2,64,1024]{2,1,0:T(8,128)(2,1)S(1)} collective-permute-done((bf16[2,64,1024]{2,1,0:T(8,128)(2,1)S(1)}, bf16[2,64,1024]{2,1,0:T(8,128)(2,1)S(1)}, u32[]{:S(2)}, u32[]{:S(2)}) %collective-permute-start) | collective-permute-done | bytes 262176 | tf_op jit(solution)/shard_map/ppermute | solution.py:75
  12.4 0.1 collective-permute-start.5
  12.5 0.5 %collective-permute-start.4 = (bf16[64,1024]{1,0:T(8,128)(2,1)S(1)}, bf16[64,1024]{1,0:T(8,128)(2,1)S(1)}, u32[]{:S(2)}, u32[]{:S(2)}) collective-permute-start(bf16[64,1024]{1,0:T(8,128)(2,1)S(1)} %get-tuple-element.96), channel_id=1, source_target_pairs={{0,1},{1,0},{2,3},{3,2},{4,5},{5,4},{6,7},{7,6},{8,9},{9,8},{10,11... | collective-permute-start | bytes 393224 | tf_op jit(solution)/shard_map/ppermute | solution.py:87
  13.0 0.0 collective-permute-start.1
  13.0 0.0 collective-permute-done.2.refs_2_
  13.0 1.6 %collective-permute-start.12 = (bf16[2,64,1024]{2,1,0:T(8,128)(2,1)S(1)}, bf16[2,64,1024]{2,1,0:T(8,128)(2,1)S(1)}, u32[]{:S(2)}, u32[]{:S(2)}) collective-permute-start(bf16[2,64,1024]{2,1,0:T(8,128)(2,1)S(1)} %collective-permute-done.refs_1_), channel_id=1, source_target_pairs={{0,2},{1,3},{2,0},{3,1},{4,6},{5,7},{6,4},{7,5},{8,10},{9,11},{10,... | collective-permute-start | bytes 786440 | tf_op jit(solution)/shard_map/ppermute | solution.py:80
  14.6 0.1 collective-permute-start.11
  14.7 0.5 %collective-permute-start.10 = (bf16[64,1024]{1,0:T(8,128)(2,1)S(1)}, bf16[64,1024]{1,0:T(8,128)(2,1)S(1)}, u32[]{:S(2)}, u32[]{:S(2)}) collective-permute-start(bf16[64,1024]{1,0:T(8,128)(2,1)S(1)} %get-tuple-element.92), channel_id=1, source_target_pairs={{0,1},{1,0},{2,3},{3,2},{4,5},{5,4},{6,7},{7,6},{8,9},{9,8},{10,11... | collective-permute-start | bytes 393224 | tf_op jit(solution)/shard_map/ppermute | solution.py:87
  15.2 3.7 %attend_0.1 = (f32[8,1024,256]{2,1,0:T(8,128)S(1)}, f32[8,1024,128]{2,1,0:T(8,128)S(1)}) custom-call(bf16[64,16384]{1,0:T(8,128)(2,1)S(1)} %fetch.1.query_ref, bf16[2,64,1024]{2,1,0:T(8,128)(2,1)S(1)} %pack.1.refs_0_, bf16[2,64,1024]{2,1,0:T(8,128)(2,1)S(1)} %collective-permute-done.refs_1_, bf16[64,1024]{1,0:T(8,128)(2,1)S(1)} %collective-permute-done.2.refs_2_, ...), custom_call_target="tpu_custom_call" | custom-call | flops 1000 | bytes 1000 | tf_op jit(solution)/shard_map/attend_0/pallas_call | solution.py:294
  18.9 4.2 %collective-permute-done.1.refs_0_ = bf16[2,64,1024]{2,1,0:T(8,128)(2,1)S(1)} collective-permute-done((bf16[2,64,1024]{2,1,0:T(8,128)(2,1)S(1)}, bf16[2,64,1024]{2,1,0:T(8,128)(2,1)S(1)}, u32[]{:S(2)}, u32[]{:S(2)}) %collective-permute-start.1) | collective-permute-done | bytes 262176 | tf_op jit(solution)/shard_map/ppermute | solution.py:75
  23.1 0.1 collective-permute-start.9
  23.2 0.5 %collective-permute-start.8 = (bf16[64,1024]{1,0:T(8,128)(2,1)S(1)}, bf16[64,1024]{1,0:T(8,128)(2,1)S(1)}, u32[]{:S(2)}, u32[]{:S(2)}) collective-permute-start(bf16[64,1024]{1,0:T(8,128)(2,1)S(1)} %get-tuple-element.94), channel_id=1, source_target_pairs={{0,1},{1,0},{2,3},{3,2},{4,5},{5,4},{6,7},{7,6},{8,9},{9,8},{10,11... | collective-permute-start | bytes 393224 | tf_op jit(solution)/shard_map/ppermute | solution.py:87
  23.7 1.6 %collective-permute-start.13 = (bf16[2,64,1024]{2,1,0:T(8,128)(2,1)S(1)}, bf16[2,64,1024]{2,1,0:T(8,128)(2,1)S(1)}, u32[]{:S(2)}, u32[]{:S(2)}) collective-permute-start(bf16[2,64,1024]{2,1,0:T(8,128)(2,1)S(1)} %collective-permute-done.1.refs_0_), channel_id=1, source_target_pairs={{0,2},{1,3},{2,0},{3,1},{4,6},{5,7},{6,4},{7,5},{8,10},{9,11},{10,... | collective-permute-start | bytes 786440 | tf_op jit(solution)/shard_map/ppermute | solution.py:80
  25.3 0.1 collective-permute-start.18
  25.4 0.5 %collective-permute-start.17 = (bf16[64,1024]{1,0:T(8,128)(2,1)S(1)}, bf16[64,1024]{1,0:T(8,128)(2,1)S(1)}, u32[]{:S(2)}, u32[]{:S(2)}) collective-permute-start(bf16[64,1024]{1,0:T(8,128)(2,1)S(1)} %get-tuple-element.88), channel_id=1, source_target_pairs={{0,1},{1,0},{2,3},{3,2},{4,5},{5,4},{6,7},{7,6},{8,9},{9,8},{10,11... | collective-permute-start | bytes 393224 | tf_op jit(solution)/shard_map/ppermute | solution.py:87
  25.9 4.7 %attend_2.1 = (f32[8,1024,256]{2,1,0:T(8,128)S(1)}, f32[8,1024,128]{2,1,0:T(8,128)S(1)}) custom-call(bf16[64,16384]{1,0:T(8,128)(2,1)S(1)} %fetch.1.query_ref, bf16[2,64,1024]{2,1,0:T(8,128)(2,1)S(1)} %collective-permute-done.1.refs_0_, bf16[2,64,1024]{2,1,0:T(8,128)(2,1)S(1)} %collective-permute-done.6.refs_1_, ...), custom_call_target="tpu_custom_call", output_to_operand_aliasing={{0}: (7, {}), {1}: (8, {})} | custom-call | flops 1000 | bytes 1000 | tf_op jit(solution)/shard_map/attend_2/pallas_call | solution.py:294
  30.6 1.4 %collective-permute-done.7.refs_0_ = bf16[2,64,1024]{2,1,0:T(8,128)(2,1)S(1)} collective-permute-done((bf16[2,64,1024]{2,1,0:T(8,128)(2,1)S(1)}, bf16[2,64,1024]{2,1,0:T(8,128)(2,1)S(1)}, u32[]{:S(2)}, u32[]{:S(2)}) %collective-permute-start.7) | collective-permute-done | bytes 262176 | tf_op jit(solution)/shard_map/ppermute | solution.py:75
  32.0 1.5 %collective-permute-start.14 = (bf16[2,64,1024]{2,1,0:T(8,128)(2,1)S(1)}, bf16[2,64,1024]{2,1,0:T(8,128)(2,1)S(1)}, u32[]{:S(2)}, u32[]{:S(2)}) collective-permute-start(bf16[2,64,1024]{2,1,0:T(8,128)(2,1)S(1)} %collective-permute-done.7.refs_0_), channel_id=1, source_target_pairs={{0,2},{1,3},{2,0},{3,1},{4,6},{5,7},{6,4},{7,5},{8,10},{9,11},{10,... | collective-permute-start | bytes 786440 | tf_op jit(solution)/shard_map/ppermute | solution.py:80
  33.5 0.6 %collective-permute-start.16 = (bf16[64,1024]{1,0:T(8,128)(2,1)S(1)}, bf16[64,1024]{1,0:T(8,128)(2,1)S(1)}, u32[]{:S(2)}, u32[]{:S(2)}) collective-permute-start(bf16[64,1024]{1,0:T(8,128)(2,1)S(1)} %get-tuple-element.89), channel_id=1, source_target_pairs={{0,1},{1,0},{2,3},{3,2},{4,5},{5,4},{6,7},{7,6},{8,9},{9,8},{10,11... | collective-permute-start | bytes 393224 | tf_op jit(solution)/shard_map/ppermute | solution.py:87
  34.1 0.1 collective-permute-start.15
  34.2 1.0 %collective-permute-done.16.refs_3_ = bf16[64,1024]{1,0:T(8,128)(2,1)S(1)} collective-permute-done((bf16[64,1024]{1,0:T(8,128)(2,1)S(1)}, bf16[64,1024]{1,0:T(8,128)(2,1)S(1)}, u32[]{:S(2)}, u32[]{:S(2)}) %collective-permute-start.16) | collective-permute-done | bytes 131104 | tf_op jit(solution)/shard_map/ppermute | solution.py:87
  35.2 0.2 collective-permute-done.15.refs_2_
  35.5 1.2 %attend_3.1 = (f32[8,1024,256]{2,1,0:T(8,128)S(1)}, f32[8,1024,128]{2,1,0:T(8,128)S(1)}) custom-call(bf16[64,16384]{1,0:T(8,128)(2,1)S(1)} %fetch.1.query_ref, bf16[2,64,1024]{2,1,0:T(8,128)(2,1)S(1)} %collective-permute-done.7.refs_0_, bf16[2,64,1024]{2,1,0:T(8,128)(2,1)S(1)} %collective-permute-done.12.refs_1_, ...), custom_call_target="tpu_custom_call", output_to_operand_aliasing={{0}: (7, {}), {1}: (8, {})} | custom-call | flops 1000 | bytes 1000 | tf_op jit(solution)/shard_map/attend_3/pallas_call | solution.py:294
  36.6 2.8 %collective-permute-done.14.refs_1_ = bf16[2,64,1024]{2,1,0:T(8,128)(2,1)S(1)} collective-permute-done((bf16[2,64,1024]{2,1,0:T(8,128)(2,1)S(1)}, bf16[2,64,1024]{2,1,0:T(8,128)(2,1)S(1)}, u32[]{:S(2)}, u32[]{:S(2)}) %collective-permute-start.14) | collective-permute-done | bytes 262176 | tf_op jit(solution)/shard_map/ppermute | solution.py:80
  39.4 1.5 %collective-permute-done.20.refs_3_ = bf16[2,64,1024]{2,1,0:T(8,128)(2,1)S(1)} collective-permute-done((bf16[2,64,1024]{2,1,0:T(8,128)(2,1)S(1)}, bf16[2,64,1024]{2,1,0:T(8,128)(2,1)S(1)}, u32[]{:S(2)}, u32[]{:S(2)}) %collective-permute-start.20) | collective-permute-done | bytes 262176 | tf_op jit(solution)/shard_map/ppermute | solution.py:87
  41.0 1.9 %attend_last.1 = bf16[64,16384]{1,0:T(8,128)(2,1)} custom-call(bf16[64,16384]{1,0:T(8,128)(2,1)S(1)} %fetch.1.query_ref, bf16[2,64,1024]{2,1,0:T(8,128)(2,1)S(1)} %collective-permute-done.13.refs_0_, bf16[2,64,1024]{2,1,0:T(8,128)(2,1)S(1)} %collective-permute-done.14.refs_1_, bf16[2,64,1024]{2,1,0:T(8,128)(2,1)S(1)} %collective-permute-done.19.refs_2_, ...), custom_call_target="tpu_custom_call" | custom-call | flops 1000 | bytes 1000 | tf_op jit(solution)/shard_map/attend_last/pallas_call | solution.py:294
  (22 shorter events, 0.2 us)
Async XLA Ops:
  1.0 11.4 %collective-permute-start = (bf16[2,64,1024]{2,1,0:T(8,128)(2,1)S(1)}, bf16[2,64,1024]{2,1,0:T(8,128)(2,1)S(1)}, u32[]{:S(2)}, u32[]{:S(2)}) collective-permute-start(bf16[2,64,1024]{2,1,0:T(8,128)(2,1)S(1)} %pack.1.refs_0_), channel_id=1, source_target_pairs={{0,4},{1,5},{2,6},{3,7},{4,8},{5,9},{6,10},{7,11},{8,12},{9,13},{1... | collective-permute-start | bytes 786440 | tf_op jit(solution)/shard_map/ppermute | solution.py:75
  4.1 10.5 %collective-permute-start.6 = (bf16[2,64,1024]{2,1,0:T(8,128)(2,1)S(1)}, bf16[2,64,1024]{2,1,0:T(8,128)(2,1)S(1)}, u32[]{:S(2)}, u32[]{:S(2)}) collective-permute-start(bf16[2,64,1024]{2,1,0:T(8,128)(2,1)S(1)} %pack.1.refs_0_), channel_id=1, source_target_pairs={{0,2},{1,3},{2,0},{3,1},{4,6},{5,7},{6,4},{7,5},{8,10},{9,11},{10,... | collective-permute-start | bytes 786440 | tf_op jit(solution)/shard_map/ppermute | solution.py:80
  5.6 7.4 %collective-permute-start.3 = (bf16[64,1024]{1,0:T(8,128)(2,1)S(1)}, bf16[64,1024]{1,0:T(8,128)(2,1)S(1)}, u32[]{:S(2)}, u32[]{:S(2)}) collective-permute-start(bf16[64,1024]{1,0:T(8,128)(2,1)S(1)} %get-tuple-element.97), channel_id=1, source_target_pairs={{0,1},{1,0},{2,3},{3,2},{4,5},{5,4},{6,7},{7,6},{8,9},{9,8},{10,11... | collective-permute-start | bytes 393224 | tf_op jit(solution)/shard_map/ppermute | solution.py:87
  5.7 7.3 %collective-permute-start.2 = (bf16[64,1024]{1,0:T(8,128)(2,1)S(1)}, bf16[64,1024]{1,0:T(8,128)(2,1)S(1)}, u32[]{:S(2)}, u32[]{:S(2)}) collective-permute-start(bf16[64,1024]{1,0:T(8,128)(2,1)S(1)} %get-tuple-element.98), channel_id=1, source_target_pairs={{0,1},{1,0},{2,3},{3,2},{4,5},{5,4},{6,7},{7,6},{8,9},{9,8},{10,11... | collective-permute-start | bytes 393224 | tf_op jit(solution)/shard_map/ppermute | solution.py:87
  12.4 2.2 %collective-permute-start.5 = (bf16[64,1024]{1,0:T(8,128)(2,1)S(1)}, bf16[64,1024]{1,0:T(8,128)(2,1)S(1)}, u32[]{:S(2)}, u32[]{:S(2)}) collective-permute-start(bf16[64,1024]{1,0:T(8,128)(2,1)S(1)} %get-tuple-element.95), channel_id=1, source_target_pairs={{0,1},{1,0},{2,3},{3,2},{4,5},{5,4},{6,7},{7,6},{8,9},{9,8},{10,11... | collective-permute-start | bytes 393224 | tf_op jit(solution)/shard_map/ppermute | solution.py:87
  12.5 2.1 %collective-permute-start.4 = (bf16[64,1024]{1,0:T(8,128)(2,1)S(1)}, bf16[64,1024]{1,0:T(8,128)(2,1)S(1)}, u32[]{:S(2)}, u32[]{:S(2)}) collective-permute-start(bf16[64,1024]{1,0:T(8,128)(2,1)S(1)} %get-tuple-element.96), channel_id=1, source_target_pairs={{0,1},{1,0},{2,3},{3,2},{4,5},{5,4},{6,7},{7,6},{8,9},{9,8},{10,11... | collective-permute-start | bytes 393224 | tf_op jit(solution)/shard_map/ppermute | solution.py:87
  13.0 10.1 %collective-permute-start.1 = (bf16[2,64,1024]{2,1,0:T(8,128)(2,1)S(1)}, bf16[2,64,1024]{2,1,0:T(8,128)(2,1)S(1)}, u32[]{:S(2)}, u32[]{:S(2)}) collective-permute-start(bf16[2,64,1024]{2,1,0:T(8,128)(2,1)S(1)} %collective-permute-done.refs_1_), channel_id=1, source_target_pairs={{0,4},{1,5},{2,6},{3,7},{4,8},{5,9},{6,10},{7,11},{8,12},{9,13},{1... | collective-permute-start | bytes 786440 | tf_op jit(solution)/shard_map/ppermute | solution.py:75
  13.0 12.3 %collective-permute-start.12 = (bf16[2,64,1024]{2,1,0:T(8,128)(2,1)S(1)}, bf16[2,64,1024]{2,1,0:T(8,128)(2,1)S(1)}, u32[]{:S(2)}, u32[]{:S(2)}) collective-permute-start(bf16[2,64,1024]{2,1,0:T(8,128)(2,1)S(1)} %collective-permute-done.refs_1_), channel_id=1, source_target_pairs={{0,2},{1,3},{2,0},{3,1},{4,6},{5,7},{6,4},{7,5},{8,10},{9,11},{10,... | collective-permute-start | bytes 786440 | tf_op jit(solution)/shard_map/ppermute | solution.py:80
  14.6 9.1 %collective-permute-start.11 = (bf16[64,1024]{1,0:T(8,128)(2,1)S(1)}, bf16[64,1024]{1,0:T(8,128)(2,1)S(1)}, u32[]{:S(2)}, u32[]{:S(2)}) collective-permute-start(bf16[64,1024]{1,0:T(8,128)(2,1)S(1)} %get-tuple-element.91), channel_id=1, source_target_pairs={{0,1},{1,0},{2,3},{3,2},{4,5},{5,4},{6,7},{7,6},{8,9},{9,8},{10,11... | collective-permute-start | bytes 393224 | tf_op jit(solution)/shard_map/ppermute | solution.py:87
  14.7 9.0 %collective-permute-start.10 = (bf16[64,1024]{1,0:T(8,128)(2,1)S(1)}, bf16[64,1024]{1,0:T(8,128)(2,1)S(1)}, u32[]{:S(2)}, u32[]{:S(2)}) collective-permute-start(bf16[64,1024]{1,0:T(8,128)(2,1)S(1)} %get-tuple-element.92), channel_id=1, source_target_pairs={{0,1},{1,0},{2,3},{3,2},{4,5},{5,4},{6,7},{7,6},{8,9},{9,8},{10,11... | collective-permute-start | bytes 393224 | tf_op jit(solution)/shard_map/ppermute | solution.py:87
  23.1 2.2 %collective-permute-start.9 = (bf16[64,1024]{1,0:T(8,128)(2,1)S(1)}, bf16[64,1024]{1,0:T(8,128)(2,1)S(1)}, u32[]{:S(2)}, u32[]{:S(2)}) collective-permute-start(bf16[64,1024]{1,0:T(8,128)(2,1)S(1)} %get-tuple-element.93), channel_id=1, source_target_pairs={{0,1},{1,0},{2,3},{3,2},{4,5},{5,4},{6,7},{7,6},{8,9},{9,8},{10,11... | collective-permute-start | bytes 393224 | tf_op jit(solution)/shard_map/ppermute | solution.py:87
  23.2 2.1 %collective-permute-start.8 = (bf16[64,1024]{1,0:T(8,128)(2,1)S(1)}, bf16[64,1024]{1,0:T(8,128)(2,1)S(1)}, u32[]{:S(2)}, u32[]{:S(2)}) collective-permute-start(bf16[64,1024]{1,0:T(8,128)(2,1)S(1)} %get-tuple-element.94), channel_id=1, source_target_pairs={{0,1},{1,0},{2,3},{3,2},{4,5},{5,4},{6,7},{7,6},{8,9},{9,8},{10,11... | collective-permute-start | bytes 393224 | tf_op jit(solution)/shard_map/ppermute | solution.py:87
  23.7 8.3 %collective-permute-start.7 = (bf16[2,64,1024]{2,1,0:T(8,128)(2,1)S(1)}, bf16[2,64,1024]{2,1,0:T(8,128)(2,1)S(1)}, u32[]{:S(2)}, u32[]{:S(2)}) collective-permute-start(bf16[2,64,1024]{2,1,0:T(8,128)(2,1)S(1)} %collective-permute-done.1.refs_0_), channel_id=1, source_target_pairs={{0,4},{1,5},{2,6},{3,7},{4,0},{5,1},{6,2},{7,3},{8,12},{9,13},{10,... | collective-permute-start | bytes 786440 | tf_op jit(solution)/shard_map/ppermute | solution.py:75
  23.7 9.8 %collective-permute-start.13 = (bf16[2,64,1024]{2,1,0:T(8,128)(2,1)S(1)}, bf16[2,64,1024]{2,1,0:T(8,128)(2,1)S(1)}, u32[]{:S(2)}, u32[]{:S(2)}) collective-permute-start(bf16[2,64,1024]{2,1,0:T(8,128)(2,1)S(1)} %collective-permute-done.1.refs_0_), channel_id=1, source_target_pairs={{0,2},{1,3},{2,0},{3,1},{4,6},{5,7},{6,4},{7,5},{8,10},{9,11},{10,... | collective-permute-start | bytes 786440 | tf_op jit(solution)/shard_map/ppermute | solution.py:80
  25.3 8.8 %collective-permute-start.18 = (bf16[64,1024]{1,0:T(8,128)(2,1)S(1)}, bf16[64,1024]{1,0:T(8,128)(2,1)S(1)}, u32[]{:S(2)}, u32[]{:S(2)}) collective-permute-start(bf16[64,1024]{1,0:T(8,128)(2,1)S(1)} %get-tuple-element.87), channel_id=1, source_target_pairs={{0,1},{1,0},{2,3},{3,2},{4,5},{5,4},{6,7},{7,6},{8,9},{9,8},{10,11... | collective-permute-start | bytes 393224 | tf_op jit(solution)/shard_map/ppermute | solution.py:87
  25.4 8.8 %collective-permute-start.17 = (bf16[64,1024]{1,0:T(8,128)(2,1)S(1)}, bf16[64,1024]{1,0:T(8,128)(2,1)S(1)}, u32[]{:S(2)}, u32[]{:S(2)}) collective-permute-start(bf16[64,1024]{1,0:T(8,128)(2,1)S(1)} %get-tuple-element.88), channel_id=1, source_target_pairs={{0,1},{1,0},{2,3},{3,2},{4,5},{5,4},{6,7},{7,6},{8,9},{9,8},{10,11... | collective-permute-start | bytes 393224 | tf_op jit(solution)/shard_map/ppermute | solution.py:87
  32.0 7.4 %collective-permute-start.14 = (bf16[2,64,1024]{2,1,0:T(8,128)(2,1)S(1)}, bf16[2,64,1024]{2,1,0:T(8,128)(2,1)S(1)}, u32[]{:S(2)}, u32[]{:S(2)}) collective-permute-start(bf16[2,64,1024]{2,1,0:T(8,128)(2,1)S(1)} %collective-permute-done.7.refs_0_), channel_id=1, source_target_pairs={{0,2},{1,3},{2,0},{3,1},{4,6},{5,7},{6,4},{7,5},{8,10},{9,11},{10,... | collective-permute-start | bytes 786440 | tf_op jit(solution)/shard_map/ppermute | solution.py:80
  33.5 2.0 %collective-permute-start.19 = (bf16[2,64,1024]{2,1,0:T(8,128)(2,1)S(1)}, bf16[2,64,1024]{2,1,0:T(8,128)(2,1)S(1)}, u32[]{:S(2)}, u32[]{:S(2)}) collective-permute-start(bf16[2,64,1024]{2,1,0:T(8,128)(2,1)S(1)} %collective-permute-done.13.refs_0_), channel_id=1, source_target_pairs={{0,1},{1,0},{2,3},{3,2},{4,5},{5,4},{6,7},{7,6},{8,9},{9,8},{10,11... | collective-permute-start | bytes 786440 | tf_op jit(solution)/shard_map/ppermute | solution.py:87
  33.5 1.7 %collective-permute-start.16 = (bf16[64,1024]{1,0:T(8,128)(2,1)S(1)}, bf16[64,1024]{1,0:T(8,128)(2,1)S(1)}, u32[]{:S(2)}, u32[]{:S(2)}) collective-permute-start(bf16[64,1024]{1,0:T(8,128)(2,1)S(1)} %get-tuple-element.89), channel_id=1, source_target_pairs={{0,1},{1,0},{2,3},{3,2},{4,5},{5,4},{6,7},{7,6},{8,9},{9,8},{10,11... | collective-permute-start | bytes 393224 | tf_op jit(solution)/shard_map/ppermute | solution.py:87
  34.1 1.3 %collective-permute-start.15 = (bf16[64,1024]{1,0:T(8,128)(2,1)S(1)}, bf16[64,1024]{1,0:T(8,128)(2,1)S(1)}, u32[]{:S(2)}, u32[]{:S(2)}) collective-permute-start(bf16[64,1024]{1,0:T(8,128)(2,1)S(1)} %get-tuple-element.90), channel_id=1, source_target_pairs={{0,1},{1,0},{2,3},{3,2},{4,5},{5,4},{6,7},{7,6},{8,9},{9,8},{10,11... | collective-permute-start | bytes 393224 | tf_op jit(solution)/shard_map/ppermute | solution.py:87
  39.4 1.5 %collective-permute-start.20 = (bf16[2,64,1024]{2,1,0:T(8,128)(2,1)S(1)}, bf16[2,64,1024]{2,1,0:T(8,128)(2,1)S(1)}, u32[]{:S(2)}, u32[]{:S(2)}) collective-permute-start(bf16[2,64,1024]{2,1,0:T(8,128)(2,1)S(1)} %collective-permute-done.14.refs_1_), channel_id=1, source_target_pairs={{0,1},{1,0},{2,3},{3,2},{4,5},{5,4},{6,7},{7,6},{8,9},{9,8},{10,11... | collective-permute-start | bytes 786440 | tf_op jit(solution)/shard_map/ppermute | solution.py:87

commit v14 on v13

--- a/solution.py
+++ b/solution.py
@@ -92,19 +92,16 @@
     return guess * (2.0 - x * guess)
 
 
-def attend_kernel(grid, entries, kept, last, query_ref, *refs):
-    depth, width, cores = grid
-    count = len(entries)
-    halves = 1 if last else 2
-    own_refs, refs = refs[:count], refs[count:]
-    core_refs, refs = refs[: halves * count], refs[halves * count :]
+def attend_kernel(grid, sources, kept, last, query_ref, *refs):
+    depth, width, cores = grid
+    blocks_refs, refs = refs[: len(sources)], refs[len(sources) :]
     kept_refs, refs = refs[: 2 * kept], refs[2 * kept :]
     out_refs, scratch = list(refs[: 2 - last]), list(refs[2 - last :])
     if last:
         result_ref = out_refs[0]
         out_refs[0], sems = scratch.pop(0), scratch.pop(0)
     tok = query_ref.shape[0]
-    dim = own_refs[0].shape[-1] // KV_HEADS
+    dim = blocks_refs[0].shape[-1] // KV_HEADS
     rows = GROUP * tok
     part_rows = rows // PARTS
     heads = part_rows // tok
@@ -112,12 +109,9 @@
     zz, yy, cc = place(grid)
 
     pieces = []
-    for at, (dz, dy) in enumerate(entries):
-        pieces.append((dz, 0, dy, own_refs[at].at[0], own_refs[at].at[1]))
-        if last:
-            pieces.append((dz, 1, dy, core_refs[at].at[0], core_refs[at].at[1]))
-        else:
-            pieces.append((dz, 1, dy, *core_refs[2 * at : 2 * at + 2]))
+    for places, ref in zip(sources, blocks_refs):
+        for (dz, dy, dc), at in places:
+            pieces.append((dz, dc, dy, ref.at[0], ref.at[1]))
     pieces.sort(key=lambda piece: piece[:3])
 
     if scratch:
@@ -182,7 +176,7 @@
                     peak = jnp.maximum(jnp.broadcast_to(peak, before.shape), before)
                     shifted = jnp.concatenate(
                         [
-                            scores[:, at : at + dim] * factor - peak
+                            scores[:, at : at + dim] * factor - peak[:, : scores.shape[1] - at]
                             for at in range(0, scores.shape[1], dim)
                         ],
                         axis=1,
@@ -221,6 +215,7 @@
                 out_copy(step).start()
 
     near = tok * sum(piece[0] == 0 for piece in pieces)
+    near = min(-(-near // dim) * dim, len(pieces) * tok)
     lowest, highest = pieces[0][0], pieces[-1][0]
 
     @pl.when(zz >= highest)
@@ -265,26 +260,21 @@
         ]
         steps = KV_HEADS // STEP_HEADS
 
-        swaps = {}
-
-        def phase(entries, blocks, state, last=False, after=None):
-            operands = [blocks[entry] for entry in entries]
-            if last:
-                operands += [
-                    swaps[entry] if entry in swaps else core_swap(blocks[entry], grid) for entry in entries
-                ]
-            else:
-                operands += [
-                    core_swap(blocks[entry][half], grid) for entry in entries for half in range(2)
-                ]
-            if after:
-                if dz + 1 == depth:
-                    swaps[after] = core_swap(blocks[after], grid)
-                    operands, swaps[after] = lax.optimization_barrier((operands, swaps[after]))
-                else:
-                    operands, blocks[after] = lax.optimization_barrier((operands, blocks[after]))
-            keys = tok * 2 * len(entries)
-            levels = {dz for dz, _ in entries}
+        arrays, found = {}, {}
+
+        def keep(name, array, places):
+            arrays[name] = array
+            found.update({place: (name, at) for at, place in enumerate(places)})
+
+        def phase(places, state, last=False):
+            names = list(dict.fromkeys(found[place][0] for place in places))
+            sources = [
+                [(place, found[place][1]) for place in places if found[place][0] == name]
+                for name in names
+            ]
+            operands = [arrays[name] for name in names]
+            keys = tok * len(places)
+            levels = {dz for dz, _, _ in places}
             scratch = []
             if last:
                 scratch += [pltpu.VMEM((tok, columns), query_rows.dtype)]
@@ -292,43 +282,56 @@
             if 0 in levels or len(levels) > 1:
                 scratch += [pltpu.VMEM((tok, keys), jnp.float32)]
             return pl.pallas_call(
-                functools.partial(attend_kernel, grid, entries, bool(state), last),
+                functools.partial(attend_kernel, grid, sources, bool(state), last),
                 out_shape=query_rows if last else state_shapes,
                 in_specs=[whole] * (1 + len(operands) + len(state)),
                 out_specs=pl.BlockSpec(memory_space=pltpu.HBM) if last else [whole] * 2,
                 scratch_shapes=scratch,
-                input_output_aliases={} if last or not state else {1 + len(operands) + at: at for at in range(2)},
+                input_output_aliases={}
+                if last or not state
+                else {1 + len(operands) + at: at for at in range(2)},
                 compiler_params=pltpu.CompilerParams(vmem_limit_bytes=16 * 2**20),
                 cost_estimate=pl.CostEstimate(flops=1000, bytes_accessed=1000, transcendentals=0),
-                name="attend_last" if last else f"attend_{entries[0][0]}",
+                name="attend_last" if last else "attend",
             )(queries, *operands, *state)
 
-        batches = [[(0, 0), (1, 0)]] + [[(dz, 0)] for dz in range(2, depth)]
+        batches = []
+        for dz in range(1, depth):
+            batches.append([(dz, 0, 0), (dz - 1, 0, 1)])
+            if width == 2:
+                batches[-1] += [(dz - 1, 1, 0)] + [(dz - 2, 1, 1)] * (dz > 1)
+        batches[0].append((0, 0, 0))
+        final = [(depth - 1, 0, 1)]
         if width == 2:
-            for dz in range(depth - 2):
-                batches[dz + 1].append((dz, 1))
-            batches.append([(depth - 2, 1), (depth - 1, 1)])
+            final += [(depth - 1, 1, 0), (depth - 2, 1, 1), (depth - 1, 1, 1)]
         while len(batches) > 8:
             batches = [sum(batches[at : at + 2], []) for at in range(0, len(batches), 2)]
-        blocks = {(0, 0): stack([key_rows, value_rows], "pack")}
+
+        keep("z0", stack([key_rows, value_rows], "pack"), [(0, 0, 0)])
         queries = fetch(query_rows)
         state = []
         for dz in range(depth):
-            block = blocks[dz, 0]
+            block = arrays[f"z{dz}"]
             if dz + 1 < depth:
-                blocks[dz + 1, 0] = z_forward(block, grid, dz + 1)
+                keep(f"z{dz + 1}", z_forward(block, grid, dz + 1), [(dz + 1, 0, 0)])
             if width == 2:
-                blocks[dz, 1] = y_swap(block, grid)
-            while len(batches) > 1 and all(entry[0] + 2 * entry[1] <= dz for entry in batches[0]):
-                state = phase(batches.pop(0), blocks, state, after=(dz - 1, 1) if width == 2 else None)
+                keep(f"y{dz}", y_swap(block, grid), [(dz, 1, 0)])
+            if dz and all(place in found for place in batches[0]):
+                state = phase(batches.pop(0), state)
+            keep(f"c{dz}", core_swap(block, grid), [(dz, 0, 1)])
+            if dz and width == 2:
+                keep(f"d{dz}", core_swap(arrays[f"y{dz - 1}"], grid), [(dz - 1, 1, 1)])
             if dz + 1 < depth:
-                blocks[dz + 1, 0], state, queries = lax.optimization_barrier(
-                    (blocks[dz + 1, 0], state, queries)
+                tied = [f"z{dz + 1}"]
+                values, state, queries = lax.optimization_barrier(
+                    ([arrays[name] for name in tied], state, queries)
                 )
-        tied = batches[0]
-        values, state = lax.optimization_barrier(([blocks[entry] for entry in tied], state))
-        blocks.update(zip(tied, values))
-        return phase(tied, blocks, state, last=True)
+                arrays.update(zip(tied, values))
+        if width == 2:
+            block, state = lax.optimization_barrier((arrays[f"y{depth - 1}"], state))
+            arrays[f"y{depth - 1}"] = block
+            keep("c", core_swap(block, grid), [(depth - 1, 1, 1)])
+        return phase(final, state, last=True)
 
     spec = P(("groups", "tp"), None)
     return jax.shard_map(

time: 43 us -> 40.5 us (0.942)
  the two profiles are of different devices: /device:TPU:0 before, /device:TPU:25 now
where the time goes in v14:
time: 40.5 us; the launch traced here: 39.9 us
  Pallas kernels  20.4 us (50%)
  starting transfers between devices  13.7 us (34%)
  waiting for transfers between devices  5.74 us (14%)
    pallas_call x4, Pallas kernels, phase(): pl.pallas_call(functools.partial(attend_kernel, grid, sources, bool(state...  17.8 us
    ppermute x8, starting transfers between devices, core_swap(): lax.ppermute(blocks, 'tp', [(at, at ^ 1) for at in range(depth * width *...  8.83 us
    ppermute x3, waiting for transfers between devices, z_forward(): return lax.ppermute(block, 'tp', pairs)  4.19 us
    ppermute x4, starting transfers between devices, y_swap(): lax.ppermute(block, 'tp', [(at, at ^ cores) for at in range(depth * width...  2.62 us
    ppermute x3, starting transfers between devices, z_forward(): return lax.ppermute(block, 'tp', pairs)  2.25 us
    pallas_call x1, Pallas kernels, fetch(): pl.pallas_call(kernel, out_shape=jax.ShapeDtypeStruct(array.shape, array....  1.6 us
    ppermute x8, waiting for transfers between devices, core_swap(): lax.ppermute(blocks, 'tp', [(at, at ^ 1) for at in range(depth * width *...  1.17 us
    pallas_call x1, Pallas kernels, stack(): pl.pallas_call(kernel, out_shape=jax.ShapeDtypeStruct((count, *arrays[0]....  0.98 us
  transfers between devices with their start and end apart: 15, of which 4 were waited for; matrix products, arithmetic and copies ran while one was open for 0% of the time, Pallas kernels for 35%

profile of v14, /device:TPU:25, one launch (start us, length us, event | category | flops | bytes accessed | tf_op | source)
XLA Modules:
  0.0 39.9 jit_solution(17656125434936151323)
XLA Ops:
  0.0 1.0 %pack.1.refs_3_ = bf16[2,64,1024]{2,1,0:T(8,128)(2,1)S(1)} custom-call(bf16[64,1024]{1,0:T(8,128)(2,1)} %refs_0_.1, bf16[64,1024]{1,0:T(8,128)(2,1)} %refs_1_.1), custom_call_target="tpu_custom_call" | custom-call | tf_op jit(solution)/shard_map/pack/pallas_call | solution.py:41
  1.0 0.1 collective-permute-start
  1.1 1.3 %collective-permute-start.3 = (bf16[2,64,1024]{2,1,0:T(8,128)(2,1)S(1)}, bf16[2,64,1024]{2,1,0:T(8,128)(2,1)S(1)}, u32[]{:S(2)}, u32[]{:S(2)}) collective-permute-start(bf16[2,64,1024]{2,1,0:T(8,128)(2,1)S(1)} %pack.1.refs_3_), channel_id=1, source_target_pairs={{0,2},{1,3},{2,0},{3,1},{4,6},{5,7},{6,4},{7,5},{8,10},{9,11},{10,... | collective-permute-start | bytes 786440 | tf_op jit(solution)/shard_map/ppermute | solution.py:80
  2.4 1.1 %collective-permute-start.2 = (bf16[2,64,1024]{2,1,0:T(8,128)(2,1)S(1)}, bf16[2,64,1024]{2,1,0:T(8,128)(2,1)S(1)}, u32[]{:S(2)}, u32[]{:S(2)}) collective-permute-start(bf16[2,64,1024]{2,1,0:T(8,128)(2,1)S(1)} %pack.1.refs_3_), channel_id=1, source_target_pairs={{0,1},{1,0},{2,3},{3,2},{4,5},{5,4},{6,7},{7,6},{8,9},{9,8},{10,11... | collective-permute-start | bytes 786440 | tf_op jit(solution)/shard_map/ppermute | solution.py:87
  3.5 1.6 %fetch.1.query_ref = bf16[64,16384]{1,0:T(8,128)(2,1)S(1)} custom-call(bf16[64,16384]{1,0:T(8,128)(2,1)} %array_ref.1), custom_call_target="tpu_custom_call" | custom-call | tf_op jit(solution)/shard_map/fetch/pallas_call | solution.py:57
  5.1 3.1 %collective-permute-done.refs_0_ = bf16[2,64,1024]{2,1,0:T(8,128)(2,1)S(1)} collective-permute-done((bf16[2,64,1024]{2,1,0:T(8,128)(2,1)S(1)}, bf16[2,64,1024]{2,1,0:T(8,128)(2,1)S(1)}, u32[]{:S(2)}, u32[]{:S(2)}) %collective-permute-start) | collective-permute-done | bytes 262176 | tf_op jit(solution)/shard_map/ppermute | solution.py:75
  8.2 2.1 %collective-permute-start.1 = (bf16[2,64,1024]{2,1,0:T(8,128)(2,1)S(1)}, bf16[2,64,1024]{2,1,0:T(8,128)(2,1)S(1)}, u32[]{:S(2)}, u32[]{:S(2)}) collective-permute-start(bf16[2,64,1024]{2,1,0:T(8,128)(2,1)S(1)} %collective-permute-done.refs_0_), channel_id=1, source_target_pairs={{0,4},{1,5},{2,6},{3,7},{4,8},{5,9},{6,10},{7,11},{8,12},{9,13},{1... | collective-permute-start | bytes 786440 | tf_op jit(solution)/shard_map/ppermute | solution.py:75
  10.3 1.0 %collective-permute-start.6 = (bf16[2,64,1024]{2,1,0:T(8,128)(2,1)S(1)}, bf16[2,64,1024]{2,1,0:T(8,128)(2,1)S(1)}, u32[]{:S(2)}, u32[]{:S(2)}) collective-permute-start(bf16[2,64,1024]{2,1,0:T(8,128)(2,1)S(1)} %collective-permute-done.refs_0_), channel_id=1, source_target_pairs={{0,2},{1,3},{2,0},{3,1},{4,6},{5,7},{6,4},{7,5},{8,10},{9,11},{10,... | collective-permute-start | bytes 786440 | tf_op jit(solution)/shard_map/ppermute | solution.py:80
  11.3 2.0 %collective-permute-start.5 = (bf16[2,64,1024]{2,1,0:T(8,128)(2,1)S(1)}, bf16[2,64,1024]{2,1,0:T(8,128)(2,1)S(1)}, u32[]{:S(2)}, u32[]{:S(2)}) collective-permute-start(bf16[2,64,1024]{2,1,0:T(8,128)(2,1)S(1)} %collective-permute-done.refs_0_), channel_id=1, source_target_pairs={{0,1},{1,0},{2,3},{3,2},{4,5},{5,4},{6,7},{7,6},{8,9},{9,8},{10,11... | collective-permute-start | bytes 786440 | tf_op jit(solution)/shard_map/ppermute | solution.py:87
  13.4 0.0 collective-permute-start.7
  13.4 0.0 collective-permute-done.2.refs_1_
  13.4 3.7 %attend.3 = (f32[8,1024,256]{2,1,0:T(8,128)S(1)}, f32[8,1024,128]{2,1,0:T(8,128)S(1)}) custom-call(bf16[64,16384]{1,0:T(8,128)(2,1)S(1)} %fetch.1.query_ref, bf16[2,64,1024]{2,1,0:T(8,128)(2,1)S(1)} %collective-permute-done.refs_0_, bf16[2,64,1024]{2,1,0:T(8,128)(2,1)S(1)} %collective-permute-done.2.refs_1_, ...), custom_call_target="tpu_custom_call" | custom-call | flops 1000 | bytes 1000 | tf_op jit(solution)/shard_map/attend/pallas_call | solution.py:284
  17.1 0.1 collective-permute-start.4
  17.2 0.3 collective-permute-start.11
  17.5 0.0 collective-permute-done.6.refs_2_
  17.5 1.6 %collective-permute-start.10 = (bf16[2,64,1024]{2,1,0:T(8,128)(2,1)S(1)}, bf16[2,64,1024]{2,1,0:T(8,128)(2,1)S(1)}, u32[]{:S(2)}, u32[]{:S(2)}) collective-permute-start(bf16[2,64,1024]{2,1,0:T(8,128)(2,1)S(1)} %collective-permute-done.1.refs_0_), channel_id=1, source_target_pairs={{0,1},{1,0},{2,3},{3,2},{4,5},{5,4},{6,7},{7,6},{8,9},{9,8},{10,11... | collective-permute-start | bytes 786440 | tf_op jit(solution)/shard_map/ppermute | solution.py:87
  19.1 0.0 collective-permute-start.12
  19.1 0.0 collective-permute-done.7.refs_3_
  19.1 4.4 %attend.4 = (f32[8,1024,256]{2,1,0:T(8,128)S(1)}, f32[8,1024,128]{2,1,0:T(8,128)S(1)}) custom-call(bf16[64,16384]{1,0:T(8,128)(2,1)S(1)} %fetch.1.query_ref, bf16[2,64,1024]{2,1,0:T(8,128)(2,1)S(1)} %collective-permute-done.1.refs_0_, bf16[2,64,1024]{2,1,0:T(8,128)(2,1)S(1)} %collective-permute-done.5.refs_1_, ...), custom_call_target="tpu_custom_call", output_to_operand_aliasing={{0}: (5, {}), {1}: (6, {})} | custom-call | flops 1000 | bytes 1000 | tf_op jit(solution)/shard_map/attend/pallas_call | solution.py:284
  23.5 1.0 %collective-permute-done.4.refs_0_ = bf16[2,64,1024]{2,1,0:T(8,128)(2,1)S(1)} collective-permute-done((bf16[2,64,1024]{2,1,0:T(8,128)(2,1)S(1)}, bf16[2,64,1024]{2,1,0:T(8,128)(2,1)S(1)}, u32[]{:S(2)}, u32[]{:S(2)}) %collective-permute-start.4) | collective-permute-done | bytes 262176 | tf_op jit(solution)/shard_map/ppermute | solution.py:75
  24.5 0.0 collective-permute-start.9
  24.6 1.8 %collective-permute-start.8 = (bf16[2,64,1024]{2,1,0:T(8,128)(2,1)S(1)}, bf16[2,64,1024]{2,1,0:T(8,128)(2,1)S(1)}, u32[]{:S(2)}, u32[]{:S(2)}) collective-permute-start(bf16[2,64,1024]{2,1,0:T(8,128)(2,1)S(1)} %collective-permute-done.4.refs_0_), channel_id=1, source_target_pairs={{0,1},{1,0},{2,3},{3,2},{4,5},{5,4},{6,7},{7,6},{8,9},{9,8},{10,11... | collective-permute-start | bytes 786440 | tf_op jit(solution)/shard_map/ppermute | solution.py:87
  26.4 0.0 collective-permute-done.11.refs_2_
  26.4 0.0 collective-permute-start.13
  26.4 0.0 collective-permute-done.12.refs_3_
  26.4 4.2 %attend.5 = (f32[8,1024,256]{2,1,0:T(8,128)S(1)}, f32[8,1024,128]{2,1,0:T(8,128)S(1)}) custom-call(bf16[64,16384]{1,0:T(8,128)(2,1)S(1)} %fetch.1.query_ref, bf16[2,64,1024]{2,1,0:T(8,128)(2,1)S(1)} %collective-permute-done.4.refs_0_, bf16[2,64,1024]{2,1,0:T(8,128)(2,1)S(1)} %collective-permute-done.10.refs_1_, ...), custom_call_target="tpu_custom_call", output_to_operand_aliasing={{0}: (5, {}), {1}: (6, {})} | custom-call | flops 1000 | bytes 1000 | tf_op jit(solution)/shard_map/attend/pallas_call | solution.py:284
  30.6 0.4 collective-permute-done.9.refs_1_
  31.0 2.3 %collective-permute-start.14 = (bf16[2,64,1024]{2,1,0:T(8,128)(2,1)S(1)}, bf16[2,64,1024]{2,1,0:T(8,128)(2,1)S(1)}, u32[]{:S(2)}, u32[]{:S(2)}) collective-permute-start(bf16[2,64,1024]{2,1,0:T(8,128)(2,1)S(1)} %collective-permute-done.9.refs_1_), channel_id=1, source_target_pairs={{0,1},{1,0},{2,3},{3,2},{4,5},{5,4},{6,7},{7,6},{8,9},{9,8},{10,11... | collective-permute-start | bytes 786440 | tf_op jit(solution)/shard_map/ppermute | solution.py:87
  33.2 0.0 collective-permute-done.8.refs_0_
  33.3 0.0 collective-permute-done.13.refs_2_
  33.3 1.2 %collective-permute-done.14.refs_3_ = bf16[2,64,1024]{2,1,0:T(8,128)(2,1)S(1)} collective-permute-done((bf16[2,64,1024]{2,1,0:T(8,128)(2,1)S(1)}, bf16[2,64,1024]{2,1,0:T(8,128)(2,1)S(1)}, u32[]{:S(2)}, u32[]{:S(2)}) %collective-permute-start.14) | collective-permute-done | bytes 262176 | tf_op jit(solution)/shard_map/ppermute | solution.py:87
  34.4 5.5 %attend_last.1 = bf16[64,16384]{1,0:T(8,128)(2,1)} custom-call(bf16[64,16384]{1,0:T(8,128)(2,1)S(1)} %fetch.1.query_ref, bf16[2,64,1024]{2,1,0:T(8,128)(2,1)S(1)} %collective-permute-done.8.refs_0_, bf16[2,64,1024]{2,1,0:T(8,128)(2,1)S(1)} %collective-permute-done.9.refs_1_, bf16[2,64,1024]{2,1,0:T(8,128)(2,1)S(1)} %collective-permute-done.13.refs_2_, ...), custom_call_target="tpu_custom_call" | custom-call | flops 1000 | bytes 1000 | tf_op jit(solution)/shard_map/attend_last/pallas_call | solution.py:284
  (4 shorter events, 0.0 us)
Async XLA Ops:
  1.0 7.2 %collective-permute-start = (bf16[2,64,1024]{2,1,0:T(8,128)(2,1)S(1)}, bf16[2,64,1024]{2,1,0:T(8,128)(2,1)S(1)}, u32[]{:S(2)}, u32[]{:S(2)}) collective-permute-start(bf16[2,64,1024]{2,1,0:T(8,128)(2,1)S(1)} %pack.1.refs_3_), channel_id=1, source_target_pairs={{0,4},{1,5},{2,6},{3,7},{4,8},{5,9},{6,10},{7,11},{8,12},{9,13},{1... | collective-permute-start | bytes 786440 | tf_op jit(solution)/shard_map/ppermute | solution.py:75
  1.1 12.3 %collective-permute-start.3 = (bf16[2,64,1024]{2,1,0:T(8,128)(2,1)S(1)}, bf16[2,64,1024]{2,1,0:T(8,128)(2,1)S(1)}, u32[]{:S(2)}, u32[]{:S(2)}) collective-permute-start(bf16[2,64,1024]{2,1,0:T(8,128)(2,1)S(1)} %pack.1.refs_3_), channel_id=1, source_target_pairs={{0,2},{1,3},{2,0},{3,1},{4,6},{5,7},{6,4},{7,5},{8,10},{9,11},{10,... | collective-permute-start | bytes 786440 | tf_op jit(solution)/shard_map/ppermute | solution.py:80
  2.4 11.0 %collective-permute-start.2 = (bf16[2,64,1024]{2,1,0:T(8,128)(2,1)S(1)}, bf16[2,64,1024]{2,1,0:T(8,128)(2,1)S(1)}, u32[]{:S(2)}, u32[]{:S(2)}) collective-permute-start(bf16[2,64,1024]{2,1,0:T(8,128)(2,1)S(1)} %pack.1.refs_3_), channel_id=1, source_target_pairs={{0,1},{1,0},{2,3},{3,2},{4,5},{5,4},{6,7},{7,6},{8,9},{9,8},{10,11... | collective-permute-start | bytes 786440 | tf_op jit(solution)/shard_map/ppermute | solution.py:87
  8.2 8.9 %collective-permute-start.1 = (bf16[2,64,1024]{2,1,0:T(8,128)(2,1)S(1)}, bf16[2,64,1024]{2,1,0:T(8,128)(2,1)S(1)}, u32[]{:S(2)}, u32[]{:S(2)}) collective-permute-start(bf16[2,64,1024]{2,1,0:T(8,128)(2,1)S(1)} %collective-permute-done.refs_0_), channel_id=1, source_target_pairs={{0,4},{1,5},{2,6},{3,7},{4,8},{5,9},{6,10},{7,11},{8,12},{9,13},{1... | collective-permute-start | bytes 786440 | tf_op jit(solution)/shard_map/ppermute | solution.py:75
  10.3 7.1 %collective-permute-start.6 = (bf16[2,64,1024]{2,1,0:T(8,128)(2,1)S(1)}, bf16[2,64,1024]{2,1,0:T(8,128)(2,1)S(1)}, u32[]{:S(2)}, u32[]{:S(2)}) collective-permute-start(bf16[2,64,1024]{2,1,0:T(8,128)(2,1)S(1)} %collective-permute-done.refs_0_), channel_id=1, source_target_pairs={{0,2},{1,3},{2,0},{3,1},{4,6},{5,7},{6,4},{7,5},{8,10},{9,11},{10,... | collective-permute-start | bytes 786440 | tf_op jit(solution)/shard_map/ppermute | solution.py:80
  11.3 7.7 %collective-permute-start.5 = (bf16[2,64,1024]{2,1,0:T(8,128)(2,1)S(1)}, bf16[2,64,1024]{2,1,0:T(8,128)(2,1)S(1)}, u32[]{:S(2)}, u32[]{:S(2)}) collective-permute-start(bf16[2,64,1024]{2,1,0:T(8,128)(2,1)S(1)} %collective-permute-done.refs_0_), channel_id=1, source_target_pairs={{0,1},{1,0},{2,3},{3,2},{4,5},{5,4},{6,7},{7,6},{8,9},{9,8},{10,11... | collective-permute-start | bytes 786440 | tf_op jit(solution)/shard_map/ppermute | solution.py:87
  13.4 5.7 %collective-permute-start.7 = (bf16[2,64,1024]{2,1,0:T(8,128)(2,1)S(1)}, bf16[2,64,1024]{2,1,0:T(8,128)(2,1)S(1)}, u32[]{:S(2)}, u32[]{:S(2)}) collective-permute-start(bf16[2,64,1024]{2,1,0:T(8,128)(2,1)S(1)} %collective-permute-done.3.refs_2_), channel_id=1, source_target_pairs={{0,1},{1,0},{2,3},{3,2},{4,5},{5,4},{6,7},{7,6},{8,9},{9,8},{10,11... | collective-permute-start | bytes 786440 | tf_op jit(solution)/shard_map/ppermute | solution.py:87
  17.1 7.4 %collective-permute-start.4 = (bf16[2,64,1024]{2,1,0:T(8,128)(2,1)S(1)}, bf16[2,64,1024]{2,1,0:T(8,128)(2,1)S(1)}, u32[]{:S(2)}, u32[]{:S(2)}) collective-permute-start(bf16[2,64,1024]{2,1,0:T(8,128)(2,1)S(1)} %collective-permute-done.1.refs_0_), channel_id=1, source_target_pairs={{0,4},{1,5},{2,6},{3,7},{4,0},{5,1},{6,2},{7,3},{8,12},{9,13},{10,... | collective-permute-start | bytes 786440 | tf_op jit(solution)/shard_map/ppermute | solution.py:75
  17.2 9.2 %collective-permute-start.11 = (bf16[2,64,1024]{2,1,0:T(8,128)(2,1)S(1)}, bf16[2,64,1024]{2,1,0:T(8,128)(2,1)S(1)}, u32[]{:S(2)}, u32[]{:S(2)}) collective-permute-start(bf16[2,64,1024]{2,1,0:T(8,128)(2,1)S(1)} %collective-permute-done.1.refs_0_), channel_id=1, source_target_pairs={{0,2},{1,3},{2,0},{3,1},{4,6},{5,7},{6,4},{7,5},{8,10},{9,11},{10,... | collective-permute-start | bytes 786440 | tf_op jit(solution)/shard_map/ppermute | solution.py:80
  17.5 8.9 %collective-permute-start.10 = (bf16[2,64,1024]{2,1,0:T(8,128)(2,1)S(1)}, bf16[2,64,1024]{2,1,0:T(8,128)(2,1)S(1)}, u32[]{:S(2)}, u32[]{:S(2)}) collective-permute-start(bf16[2,64,1024]{2,1,0:T(8,128)(2,1)S(1)} %collective-permute-done.1.refs_0_), channel_id=1, source_target_pairs={{0,1},{1,0},{2,3},{3,2},{4,5},{5,4},{6,7},{7,6},{8,9},{9,8},{10,11... | collective-permute-start | bytes 786440 | tf_op jit(solution)/shard_map/ppermute | solution.py:87
  19.1 7.3 %collective-permute-start.12 = (bf16[2,64,1024]{2,1,0:T(8,128)(2,1)S(1)}, bf16[2,64,1024]{2,1,0:T(8,128)(2,1)S(1)}, u32[]{:S(2)}, u32[]{:S(2)}) collective-permute-start(bf16[2,64,1024]{2,1,0:T(8,128)(2,1)S(1)} %collective-permute-done.6.refs_2_), channel_id=1, source_target_pairs={{0,1},{1,0},{2,3},{3,2},{4,5},{5,4},{6,7},{7,6},{8,9},{9,8},{10,11... | collective-permute-start | bytes 786440 | tf_op jit(solution)/shard_map/ppermute | solution.py:87
  24.5 6.5 %collective-permute-start.9 = (bf16[2,64,1024]{2,1,0:T(8,128)(2,1)S(1)}, bf16[2,64,1024]{2,1,0:T(8,128)(2,1)S(1)}, u32[]{:S(2)}, u32[]{:S(2)}) collective-permute-start(bf16[2,64,1024]{2,1,0:T(8,128)(2,1)S(1)} %collective-permute-done.4.refs_0_), channel_id=1, source_target_pairs={{0,2},{1,3},{2,0},{3,1},{4,6},{5,7},{6,4},{7,5},{8,10},{9,11},{10,... | collective-permute-start | bytes 786440 | tf_op jit(solution)/shard_map/ppermute | solution.py:80
  24.6 8.7 %collective-permute-start.8 = (bf16[2,64,1024]{2,1,0:T(8,128)(2,1)S(1)}, bf16[2,64,1024]{2,1,0:T(8,128)(2,1)S(1)}, u32[]{:S(2)}, u32[]{:S(2)}) collective-permute-start(bf16[2,64,1024]{2,1,0:T(8,128)(2,1)S(1)} %collective-permute-done.4.refs_0_), channel_id=1, source_target_pairs={{0,1},{1,0},{2,3},{3,2},{4,5},{5,4},{6,7},{7,6},{8,9},{9,8},{10,11... | collective-permute-start | bytes 786440 | tf_op jit(solution)/shard_map/ppermute | solution.py:87
  26.4 6.9 %collective-permute-start.13 = (bf16[2,64,1024]{2,1,0:T(8,128)(2,1)S(1)}, bf16[2,64,1024]{2,1,0:T(8,128)(2,1)S(1)}, u32[]{:S(2)}, u32[]{:S(2)}) collective-permute-start(bf16[2,64,1024]{2,1,0:T(8,128)(2,1)S(1)} %collective-permute-done.11.refs_2_), channel_id=1, source_target_pairs={{0,1},{1,0},{2,3},{3,2},{4,5},{5,4},{6,7},{7,6},{8,9},{9,8},{10,11... | collective-permute-start | bytes 786440 | tf_op jit(solution)/shard_map/ppermute | solution.py:87
  31.0 3.4 %collective-permute-start.14 = (bf16[2,64,1024]{2,1,0:T(8,128)(2,1)S(1)}, bf16[2,64,1024]{2,1,0:T(8,128)(2,1)S(1)}, u32[]{:S(2)}, u32[]{:S(2)}) collective-permute-start(bf16[2,64,1024]{2,1,0:T(8,128)(2,1)S(1)} %collective-permute-done.9.refs_1_), channel_id=1, source_target_pairs={{0,1},{1,0},{2,3},{3,2},{4,5},{5,4},{6,7},{7,6},{8,9},{9,8},{10,11... | collective-permute-start | bytes 786440 | tf_op jit(solution)/shard_map/ppermute | solution.py:87

commit v15 on v14

--- a/solution.py
+++ b/solution.py
@@ -80,6 +80,21 @@
     return lax.ppermute(
         block, "tp", [(at, at ^ cores) for at in range(depth * width * cores)]
     )
+
+
+def far_swap(block, grid, groups):
+    depth, width, cores = grid
+    count = depth * width * cores
+    pairs = []
+    for group in range(groups):
+        for at in range(count):
+            z, side = divmod(at, width * cores)
+            if z in (0, depth - 1):
+                target = group * count + (depth - 1 - z) * width * cores + (side ^ cores)
+            else:
+                target = (group ^ 1) * count + at
+            pairs.append((group * count + at, target))
+    return lax.ppermute(block, ("groups", "tp"), pairs)
 
 
 def core_swap(blocks, grid):
@@ -244,7 +259,10 @@
 def solution(mesh):
     grid = chip_grid(mesh.shape["tp"])
     depth, width, cores = grid
+    groups = mesh.shape["groups"]
     assert cores == 2 and depth > 2
+    straight = width == 2 and groups % 2 == 0
+    assert straight or width == 1
 
     def body(query_rows, key_rows, value_rows):
         tok, columns = query_rows.shape
@@ -302,8 +320,9 @@
                 batches[-1] += [(dz - 1, 1, 0)] + [(dz - 2, 1, 1)] * (dz > 1)
         batches[0].append((0, 0, 0))
         final = [(depth - 1, 0, 1)]
-        if width == 2:
-            final += [(depth - 1, 1, 0), (depth - 2, 1, 1), (depth - 1, 1, 1)]
+        if straight:
+            final += [(depth - 1, 0, 0), (depth - 2, 1, 0), (depth - 2, 1, 1)]
+            batches[-1] = [(depth - 1, 1, 0), (depth - 1, 1, 1), (depth - 2, 0, 1), (depth - 3, 1, 1)]
         while len(batches) > 8:
             batches = [sum(batches[at : at + 2], []) for at in range(0, len(batches), 2)]
 
@@ -314,12 +333,16 @@
             block = arrays[f"z{dz}"]
             if dz + 1 < depth:
                 keep(f"z{dz + 1}", z_forward(block, grid, dz + 1), [(dz + 1, 0, 0)])
-            if width == 2:
+            if straight and dz + 1 < depth:
                 keep(f"y{dz}", y_swap(block, grid), [(dz, 1, 0)])
+            if straight and dz == 0:
+                keep("w", far_swap(block, grid, groups), [(depth - 1, 1, 0)])
+            if straight and dz == 1:
+                keep("cw", core_swap(arrays["w"], grid), [(depth - 1, 1, 1)])
             if dz and all(place in found for place in batches[0]):
                 state = phase(batches.pop(0), state)
             keep(f"c{dz}", core_swap(block, grid), [(dz, 0, 1)])
-            if dz and width == 2:
+            if dz and straight:
                 keep(f"d{dz}", core_swap(arrays[f"y{dz - 1}"], grid), [(dz - 1, 1, 1)])
             if dz + 1 < depth:
                 tied = [f"z{dz + 1}"]
@@ -327,10 +350,6 @@
                     ([arrays[name] for name in tied], state, queries)
                 )
                 arrays.update(zip(tied, values))
-        if width == 2:
-            block, state = lax.optimization_barrier((arrays[f"y{depth - 1}"], state))
-            arrays[f"y{depth - 1}"] = block
-            keep("c", core_swap(block, grid), [(depth - 1, 1, 1)])
         return phase(final, state, last=True)
 
     spec = P(("groups", "tp"), None)

time: 40.5 us -> 41.3 us (1.020)
  waiting for transfers between devices: 5.74 us -> 6.64 us
    ppermute x0 -> x1, waiting for transfers between devices: none -> 3.45 us  [far_swap(): return lax.ppermute(block, ('groups', 'tp'), pairs)]
    ppermute x8, starting transfers between devices: 8.83 us -> 7.36 us  [core_swap(): lax.ppermute(blocks, 'tp', [(at, at ^ 1) for at in range(depth * width *...]
    ppermute x8, waiting for transfers between devices: 1.17 us -> 0.02 us  [core_swap(): lax.ppermute(blocks, 'tp', [(at, at ^ 1) for at in range(depth * width *...]
    ppermute x3, starting transfers between devices: 2.25 us -> 3.4 us  [z_forward(): return lax.ppermute(block, 'tp', pairs)]
    ppermute x3, waiting for transfers between devices: 4.19 us -> 3.15 us  [z_forward(): return lax.ppermute(block, 'tp', pairs)]
    ppermute x0 -> x1, starting transfers between devices: none -> 0.71 us  [far_swap(): return lax.ppermute(block, ('groups', 'tp'), pairs)]
    ppermute x4 -> x3, starting transfers between devices: 2.62 us -> 2.51 us  [y_swap(): lax.ppermute(block, 'tp', [(at, at ^ cores) for at in range(depth * width...]
  transfers between devices with their start and end apart: 15 -> 15, of which waited for: 4 -> 2; matrix products, arithmetic and copies ran while one was open for 0% -> 0% of each run, Pallas kernels for 35% -> 34%
where the time goes in v15:
time: 41.3 us; the launch traced here: 41.1 us
  Pallas kernels  20.4 us (49%)
  starting transfers between devices  14 us (34%)
  waiting for transfers between devices  6.64 us (16%)
    pallas_call x4, Pallas kernels, phase(): pl.pallas_call(functools.partial(attend_kernel, grid, sources, bool(state...  17.8 us
    ppermute x8, starting transfers between devices, core_swap(): lax.ppermute(blocks, 'tp', [(at, at ^ 1) for at in range(depth * width *...  7.36 us
    ppermute x1, waiting for transfers between devices, far_swap(): return lax.ppermute(block, ('groups', 'tp'), pairs)  3.45 us
    ppermute x3, starting transfers between devices, z_forward(): return lax.ppermute(block, 'tp', pairs)  3.4 us
    ppermute x3, waiting for transfers between devices, z_forward(): return lax.ppermute(block, 'tp', pairs)  3.15 us
    ppermute x3, starting transfers between devices, y_swap(): lax.ppermute(block, 'tp', [(at, at ^ cores) for at in range(depth * width...  2.51 us
    pallas_call x1, Pallas kernels, fetch(): pl.pallas_call(kernel, out_shape=jax.ShapeDtypeStruct(array.shape, array....  1.6 us
    pallas_call x1, Pallas kernels, stack(): pl.pallas_call(kernel, out_shape=jax.ShapeDtypeStruct((count, *arrays[0]....  0.98 us
  transfers between devices with their start and end apart: 15, of which 2 were waited for; matrix products, arithmetic and copies ran while one was open for 0% of the time, Pallas kernels for 34%

profile of v15, /device:TPU:25, one launch (start us, length us, event | category | flops | bytes accessed | tf_op | source)
XLA Modules:
  0.0 41.1 jit_solution(2051960631766023117)
XLA Ops:
  0.0 1.0 %pack.1.refs_3_ = bf16[2,64,1024]{2,1,0:T(8,128)(2,1)S(1)} custom-call(bf16[64,1024]{1,0:T(8,128)(2,1)} %refs_0_.1, bf16[64,1024]{1,0:T(8,128)(2,1)} %refs_1_.1), custom_call_target="tpu_custom_call" | custom-call | tf_op jit(solution)/shard_map/pack/pallas_call | solution.py:41
  1.0 0.1 collective-permute-start
  1.1 1.3 %collective-permute-start.3 = (bf16[2,64,1024]{2,1,0:T(8,128)(2,1)S(1)}, bf16[2,64,1024]{2,1,0:T(8,128)(2,1)S(1)}, u32[]{:S(2)}, u32[]{:S(2)}) collective-permute-start(bf16[2,64,1024]{2,1,0:T(8,128)(2,1)S(1)} %pack.1.refs_3_), channel_id=1, source_target_pairs={{0,2},{1,3},{2,0},{3,1},{4,6},{5,7},{6,4},{7,5},{8,10},{9,11},{10,... | collective-permute-start | bytes 786440 | tf_op jit(solution)/shard_map/ppermute | solution.py:80
  2.4 1.1 %collective-permute-start.2 = (bf16[2,64,1024]{2,1,0:T(8,128)(2,1)S(1)}, bf16[2,64,1024]{2,1,0:T(8,128)(2,1)S(1)}, u32[]{:S(2)}, u32[]{:S(2)}) collective-permute-start(bf16[2,64,1024]{2,1,0:T(8,128)(2,1)S(1)} %pack.1.refs_3_), channel_id=1, source_target_pairs={{0,1},{1,0},{2,3},{3,2},{4,5},{5,4},{6,7},{7,6},{8,9},{9,8},{10,11... | collective-permute-start | bytes 786440 | tf_op jit(solution)/shard_map/ppermute | solution.py:102
  3.5 1.6 %fetch.1.query_ref = bf16[64,16384]{1,0:T(8,128)(2,1)S(1)} custom-call(bf16[64,16384]{1,0:T(8,128)(2,1)} %array_ref.1), custom_call_target="tpu_custom_call" | custom-call | tf_op jit(solution)/shard_map/fetch/pallas_call | solution.py:57
  5.1 3.1 %collective-permute-done.refs_0_ = bf16[2,64,1024]{2,1,0:T(8,128)(2,1)S(1)} collective-permute-done((bf16[2,64,1024]{2,1,0:T(8,128)(2,1)S(1)}, bf16[2,64,1024]{2,1,0:T(8,128)(2,1)S(1)}, u32[]{:S(2)}, u32[]{:S(2)}) %collective-permute-start) | collective-permute-done | bytes 262176 | tf_op jit(solution)/shard_map/ppermute | solution.py:75
  8.2 2.1 %collective-permute-start.1 = (bf16[2,64,1024]{2,1,0:T(8,128)(2,1)S(1)}, bf16[2,64,1024]{2,1,0:T(8,128)(2,1)S(1)}, u32[]{:S(2)}, u32[]{:S(2)}) collective-permute-start(bf16[2,64,1024]{2,1,0:T(8,128)(2,1)S(1)} %collective-permute-done.refs_0_), channel_id=1, source_target_pairs={{0,4},{1,5},{2,6},{3,7},{4,8},{5,9},{6,10},{7,11},{8,12},{9,13},{1... | collective-permute-start | bytes 786440 | tf_op jit(solution)/shard_map/ppermute | solution.py:75
  10.3 0.7 %collective-permute-start.11 = (bf16[2,64,1024]{2,1,0:T(8,128)(2,1)S(1)}, bf16[2,64,1024]{2,1,0:T(8,128)(2,1)S(1)}, u32[]{:S(2)}, u32[]{:S(2)}) collective-permute-start(bf16[2,64,1024]{2,1,0:T(8,128)(2,1)S(1)} %pack.1.refs_3_), channel_id=1, source_target_pairs={{0,14},{1,15},{2,12},{3,13},{4,20},{5,21},{6,22},{7,23},{8,24},{9,... | collective-permute-start | bytes 786440 | tf_op jit(solution)/shard_map/ppermute | solution.py:97
  11.1 0.5 %collective-permute-start.6 = (bf16[2,64,1024]{2,1,0:T(8,128)(2,1)S(1)}, bf16[2,64,1024]{2,1,0:T(8,128)(2,1)S(1)}, u32[]{:S(2)}, u32[]{:S(2)}) collective-permute-start(bf16[2,64,1024]{2,1,0:T(8,128)(2,1)S(1)} %collective-permute-done.refs_0_), channel_id=1, source_target_pairs={{0,2},{1,3},{2,0},{3,1},{4,6},{5,7},{6,4},{7,5},{8,10},{9,11},{10,... | collective-permute-start | bytes 786440 | tf_op jit(solution)/shard_map/ppermute | solution.py:80
  11.5 0.0 collective-permute-done.3.refs_2_
  11.5 1.8 %collective-permute-start.5 = (bf16[2,64,1024]{2,1,0:T(8,128)(2,1)S(1)}, bf16[2,64,1024]{2,1,0:T(8,128)(2,1)S(1)}, u32[]{:S(2)}, u32[]{:S(2)}) collective-permute-start(bf16[2,64,1024]{2,1,0:T(8,128)(2,1)S(1)} %collective-permute-done.refs_0_), channel_id=1, source_target_pairs={{0,1},{1,0},{2,3},{3,2},{4,5},{5,4},{6,7},{7,6},{8,9},{9,8},{10,11... | collective-permute-start | bytes 786440 | tf_op jit(solution)/shard_map/ppermute | solution.py:102
  13.4 0.0 collective-permute-done.2.refs_1_
  13.4 0.1 collective-permute-start.7
  13.4 3.7 %attend.3 = (f32[8,1024,256]{2,1,0:T(8,128)S(1)}, f32[8,1024,128]{2,1,0:T(8,128)S(1)}) custom-call(bf16[64,16384]{1,0:T(8,128)(2,1)S(1)} %fetch.1.query_ref, bf16[2,64,1024]{2,1,0:T(8,128)(2,1)S(1)} %collective-permute-done.refs_0_, bf16[2,64,1024]{2,1,0:T(8,128)(2,1)S(1)} %collective-permute-done.2.refs_1_, ...), custom_call_target="tpu_custom_call" | custom-call | flops 1000 | bytes 1000 | tf_op jit(solution)/shard_map/attend/pallas_call | solution.py:302
  17.1 0.0 collective-permute-done.1.refs_0_
  17.1 1.2 %collective-permute-start.4 = (bf16[2,64,1024]{2,1,0:T(8,128)(2,1)S(1)}, bf16[2,64,1024]{2,1,0:T(8,128)(2,1)S(1)}, u32[]{:S(2)}, u32[]{:S(2)}) collective-permute-start(bf16[2,64,1024]{2,1,0:T(8,128)(2,1)S(1)} %collective-permute-done.1.refs_0_), channel_id=1, source_target_pairs={{0,4},{1,5},{2,6},{3,7},{4,0},{5,1},{6,2},{7,3},{8,12},{9,13},{10,... | collective-permute-start | bytes 786440 | tf_op jit(solution)/shard_map/ppermute | solution.py:75
  18.4 3.5 %collective-permute-done.11.refs_0_ = bf16[2,64,1024]{2,1,0:T(8,128)(2,1)S(1)} collective-permute-done((bf16[2,64,1024]{2,1,0:T(8,128)(2,1)S(1)}, bf16[2,64,1024]{2,1,0:T(8,128)(2,1)S(1)}, u32[]{:S(2)}, u32[]{:S(2)}) %collective-permute-start.11) | collective-permute-done | bytes 262176 | tf_op jit(solution)/shard_map/ppermute | solution.py:97
  21.8 0.7 %collective-permute-start.9 = (bf16[2,64,1024]{2,1,0:T(8,128)(2,1)S(1)}, bf16[2,64,1024]{2,1,0:T(8,128)(2,1)S(1)}, u32[]{:S(2)}, u32[]{:S(2)}) collective-permute-start(bf16[2,64,1024]{2,1,0:T(8,128)(2,1)S(1)} %collective-permute-done.1.refs_0_), channel_id=1, source_target_pairs={{0,2},{1,3},{2,0},{3,1},{4,6},{5,7},{6,4},{7,5},{8,10},{9,11},{10,... | collective-permute-start | bytes 786440 | tf_op jit(solution)/shard_map/ppermute | solution.py:80
  22.5 0.0 collective-permute-done.6.refs_2_
  22.5 3.3 %collective-permute-start.12 = (bf16[2,64,1024]{2,1,0:T(8,128)(2,1)S(1)}, bf16[2,64,1024]{2,1,0:T(8,128)(2,1)S(1)}, u32[]{:S(2)}, u32[]{:S(2)}) collective-permute-start(bf16[2,64,1024]{2,1,0:T(8,128)(2,1)S(1)} %collective-permute-done.11.refs_0_), channel_id=1, source_target_pairs={{0,1},{1,0},{2,3},{3,2},{4,5},{5,4},{6,7},{7,6},{8,9},{9,8},{10,11... | collective-permute-start | bytes 786440 | tf_op jit(solution)/shard_map/ppermute | solution.py:102
  25.8 0.0 collective-permute-done.5.refs_1_
  25.8 0.0 collective-permute-start.13
  25.8 0.5 %collective-permute-start.14 = (bf16[2,64,1024]{2,1,0:T(8,128)(2,1)S(1)}, bf16[2,64,1024]{2,1,0:T(8,128)(2,1)S(1)}, u32[]{:S(2)}, u32[]{:S(2)}) collective-permute-start(bf16[2,64,1024]{2,1,0:T(8,128)(2,1)S(1)} %collective-permute-done.6.refs_2_), channel_id=1, source_target_pairs={{0,1},{1,0},{2,3},{3,2},{4,5},{5,4},{6,7},{7,6},{8,9},{9,8},{10,11... | collective-permute-start | bytes 786440 | tf_op jit(solution)/shard_map/ppermute | solution.py:102
  26.3 4.4 %attend.4 = (f32[8,1024,256]{2,1,0:T(8,128)S(1)}, f32[8,1024,128]{2,1,0:T(8,128)S(1)}) custom-call(bf16[64,16384]{1,0:T(8,128)(2,1)S(1)} %fetch.1.query_ref, bf16[2,64,1024]{2,1,0:T(8,128)(2,1)S(1)} %collective-permute-done.1.refs_0_, bf16[2,64,1024]{2,1,0:T(8,128)(2,1)S(1)} %collective-permute-done.5.refs_1_, ...), custom_call_target="tpu_custom_call", output_to_operand_aliasing={{0}: (5, {}), {1}: (6, {})} | custom-call | flops 1000 | bytes 1000 | tf_op jit(solution)/shard_map/attend/pallas_call | solution.py:302
  30.7 0.0 collective-permute-done.4.refs_1_
  30.7 0.1 collective-permute-start.8
  30.9 0.4 %collective-permute-start.10 = (bf16[2,64,1024]{2,1,0:T(8,128)(2,1)S(1)}, bf16[2,64,1024]{2,1,0:T(8,128)(2,1)S(1)}, u32[]{:S(2)}, u32[]{:S(2)}) collective-permute-start(bf16[2,64,1024]{2,1,0:T(8,128)(2,1)S(1)} %collective-permute-done.9.refs_2_), channel_id=1, source_target_pairs={{0,1},{1,0},{2,3},{3,2},{4,5},{5,4},{6,7},{7,6},{8,9},{9,8},{10,11... | collective-permute-start | bytes 786440 | tf_op jit(solution)/shard_map/ppermute | solution.py:102
  31.3 0.0 collective-permute-done.12.refs_1_
  31.3 0.0 collective-permute-done.13.refs_2_
  31.3 0.0 collective-permute-done.14.refs_3_
  31.3 4.2 %attend.5 = (f32[8,1024,256]{2,1,0:T(8,128)S(1)}, f32[8,1024,128]{2,1,0:T(8,128)S(1)}) custom-call(bf16[64,16384]{1,0:T(8,128)(2,1)S(1)} %fetch.1.query_ref, bf16[2,64,1024]{2,1,0:T(8,128)(2,1)S(1)} %collective-permute-done.11.refs_0_, bf16[2,64,1024]{2,1,0:T(8,128)(2,1)S(1)} %collective-permute-done.12.refs_1_, ...), custom_call_target="tpu_custom_call", output_to_operand_aliasing={{0}: (5, {}), {1}: (6, {})} | custom-call | flops 1000 | bytes 1000 | tf_op jit(solution)/shard_map/attend/pallas_call | solution.py:302
  35.6 5.6 %attend_last.1 = bf16[64,16384]{1,0:T(8,128)(2,1)} custom-call(bf16[64,16384]{1,0:T(8,128)(2,1)S(1)} %fetch.1.query_ref, bf16[2,64,1024]{2,1,0:T(8,128)(2,1)S(1)} %collective-permute-done.8.refs_0_, bf16[2,64,1024]{2,1,0:T(8,128)(2,1)S(1)} %collective-permute-done.4.refs_1_, bf16[2,64,1024]{2,1,0:T(8,128)(2,1)S(1)} %collective-permute-done.9.refs_2_, ...), custom_call_target="tpu_custom_call" | custom-call | flops 1000 | bytes 1000 | tf_op jit(solution)/shard_map/attend_last/pallas_call | solution.py:302
  (4 shorter events, 0.0 us)
Async XLA Ops:
  1.0 7.2 %collective-permute-start = (bf16[2,64,1024]{2,1,0:T(8,128)(2,1)S(1)}, bf16[2,64,1024]{2,1,0:T(8,128)(2,1)S(1)}, u32[]{:S(2)}, u32[]{:S(2)}) collective-permute-start(bf16[2,64,1024]{2,1,0:T(8,128)(2,1)S(1)} %pack.1.refs_3_), channel_id=1, source_target_pairs={{0,4},{1,5},{2,6},{3,7},{4,8},{5,9},{6,10},{7,11},{8,12},{9,13},{1... | collective-permute-start | bytes 786440 | tf_op jit(solution)/shard_map/ppermute | solution.py:75
  1.1 10.5 %collective-permute-start.3 = (bf16[2,64,1024]{2,1,0:T(8,128)(2,1)S(1)}, bf16[2,64,1024]{2,1,0:T(8,128)(2,1)S(1)}, u32[]{:S(2)}, u32[]{:S(2)}) collective-permute-start(bf16[2,64,1024]{2,1,0:T(8,128)(2,1)S(1)} %pack.1.refs_3_), channel_id=1, source_target_pairs={{0,2},{1,3},{2,0},{3,1},{4,6},{5,7},{6,4},{7,5},{8,10},{9,11},{10,... | collective-permute-start | bytes 786440 | tf_op jit(solution)/shard_map/ppermute | solution.py:80
  2.4 11.0 %collective-permute-start.2 = (bf16[2,64,1024]{2,1,0:T(8,128)(2,1)S(1)}, bf16[2,64,1024]{2,1,0:T(8,128)(2,1)S(1)}, u32[]{:S(2)}, u32[]{:S(2)}) collective-permute-start(bf16[2,64,1024]{2,1,0:T(8,128)(2,1)S(1)} %pack.1.refs_3_), channel_id=1, source_target_pairs={{0,1},{1,0},{2,3},{3,2},{4,5},{5,4},{6,7},{7,6},{8,9},{9,8},{10,11... | collective-permute-start | bytes 786440 | tf_op jit(solution)/shard_map/ppermute | solution.py:102
  8.2 8.9 %collective-permute-start.1 = (bf16[2,64,1024]{2,1,0:T(8,128)(2,1)S(1)}, bf16[2,64,1024]{2,1,0:T(8,128)(2,1)S(1)}, u32[]{:S(2)}, u32[]{:S(2)}) collective-permute-start(bf16[2,64,1024]{2,1,0:T(8,128)(2,1)S(1)} %collective-permute-done.refs_0_), channel_id=1, source_target_pairs={{0,4},{1,5},{2,6},{3,7},{4,8},{5,9},{6,10},{7,11},{8,12},{9,13},{1... | collective-permute-start | bytes 786440 | tf_op jit(solution)/shard_map/ppermute | solution.py:75
  10.3 11.5 %collective-permute-start.11 = (bf16[2,64,1024]{2,1,0:T(8,128)(2,1)S(1)}, bf16[2,64,1024]{2,1,0:T(8,128)(2,1)S(1)}, u32[]{:S(2)}, u32[]{:S(2)}) collective-permute-start(bf16[2,64,1024]{2,1,0:T(8,128)(2,1)S(1)} %pack.1.refs_3_), channel_id=1, source_target_pairs={{0,14},{1,15},{2,12},{3,13},{4,20},{5,21},{6,22},{7,23},{8,24},{9,... | collective-permute-start | bytes 786440 | tf_op jit(solution)/shard_map/ppermute | solution.py:97
  11.1 11.5 %collective-permute-start.6 = (bf16[2,64,1024]{2,1,0:T(8,128)(2,1)S(1)}, bf16[2,64,1024]{2,1,0:T(8,128)(2,1)S(1)}, u32[]{:S(2)}, u32[]{:S(2)}) collective-permute-start(bf16[2,64,1024]{2,1,0:T(8,128)(2,1)S(1)} %collective-permute-done.refs_0_), channel_id=1, source_target_pairs={{0,2},{1,3},{2,0},{3,1},{4,6},{5,7},{6,4},{7,5},{8,10},{9,11},{10,... | collective-permute-start | bytes 786440 | tf_op jit(solution)/shard_map/ppermute | solution.py:80
  11.5 14.3 %collective-permute-start.5 = (bf16[2,64,1024]{2,1,0:T(8,128)(2,1)S(1)}, bf16[2,64,1024]{2,1,0:T(8,128)(2,1)S(1)}, u32[]{:S(2)}, u32[]{:S(2)}) collective-permute-start(bf16[2,64,1024]{2,1,0:T(8,128)(2,1)S(1)} %collective-permute-done.refs_0_), channel_id=1, source_target_pairs={{0,1},{1,0},{2,3},{3,2},{4,5},{5,4},{6,7},{7,6},{8,9},{9,8},{10,11... | collective-permute-start | bytes 786440 | tf_op jit(solution)/shard_map/ppermute | solution.py:102
  13.4 12.5 %collective-permute-start.7 = (bf16[2,64,1024]{2,1,0:T(8,128)(2,1)S(1)}, bf16[2,64,1024]{2,1,0:T(8,128)(2,1)S(1)}, u32[]{:S(2)}, u32[]{:S(2)}) collective-permute-start(bf16[2,64,1024]{2,1,0:T(8,128)(2,1)S(1)} %collective-permute-done.3.refs_2_), channel_id=1, source_target_pairs={{0,1},{1,0},{2,3},{3,2},{4,5},{5,4},{6,7},{7,6},{8,9},{9,8},{10,11... | collective-permute-start | bytes 786440 | tf_op jit(solution)/shard_map/ppermute | solution.py:102
  17.1 13.6 %collective-permute-start.4 = (bf16[2,64,1024]{2,1,0:T(8,128)(2,1)S(1)}, bf16[2,64,1024]{2,1,0:T(8,128)(2,1)S(1)}, u32[]{:S(2)}, u32[]{:S(2)}) collective-permute-start(bf16[2,64,1024]{2,1,0:T(8,128)(2,1)S(1)} %collective-permute-done.1.refs_0_), channel_id=1, source_target_pairs={{0,4},{1,5},{2,6},{3,7},{4,0},{5,1},{6,2},{7,3},{8,12},{9,13},{10,... | collective-permute-start | bytes 786440 | tf_op jit(solution)/shard_map/ppermute | solution.py:75
  21.8 9.1 %collective-permute-start.9 = (bf16[2,64,1024]{2,1,0:T(8,128)(2,1)S(1)}, bf16[2,64,1024]{2,1,0:T(8,128)(2,1)S(1)}, u32[]{:S(2)}, u32[]{:S(2)}) collective-permute-start(bf16[2,64,1024]{2,1,0:T(8,128)(2,1)S(1)} %collective-permute-done.1.refs_0_), channel_id=1, source_target_pairs={{0,2},{1,3},{2,0},{3,1},{4,6},{5,7},{6,4},{7,5},{8,10},{9,11},{10,... | collective-permute-start | bytes 786440 | tf_op jit(solution)/shard_map/ppermute | solution.py:80
  22.5 8.8 %collective-permute-start.12 = (bf16[2,64,1024]{2,1,0:T(8,128)(2,1)S(1)}, bf16[2,64,1024]{2,1,0:T(8,128)(2,1)S(1)}, u32[]{:S(2)}, u32[]{:S(2)}) collective-permute-start(bf16[2,64,1024]{2,1,0:T(8,128)(2,1)S(1)} %collective-permute-done.11.refs_0_), channel_id=1, source_target_pairs={{0,1},{1,0},{2,3},{3,2},{4,5},{5,4},{6,7},{7,6},{8,9},{9,8},{10,11... | collective-permute-start | bytes 786440 | tf_op jit(solution)/shard_map/ppermute | solution.py:102
  25.8 5.5 %collective-permute-start.13 = (bf16[2,64,1024]{2,1,0:T(8,128)(2,1)S(1)}, bf16[2,64,1024]{2,1,0:T(8,128)(2,1)S(1)}, u32[]{:S(2)}, u32[]{:S(2)}) collective-permute-start(bf16[2,64,1024]{2,1,0:T(8,128)(2,1)S(1)} %collective-permute-done.1.refs_0_), channel_id=1, source_target_pairs={{0,1},{1,0},{2,3},{3,2},{4,5},{5,4},{6,7},{7,6},{8,9},{9,8},{10,11... | collective-permute-start | bytes 786440 | tf_op jit(solution)/shard_map/ppermute | solution.py:102
  25.8 5.5 %collective-permute-start.14 = (bf16[2,64,1024]{2,1,0:T(8,128)(2,1)S(1)}, bf16[2,64,1024]{2,1,0:T(8,128)(2,1)S(1)}, u32[]{:S(2)}, u32[]{:S(2)}) collective-permute-start(bf16[2,64,1024]{2,1,0:T(8,128)(2,1)S(1)} %collective-permute-done.6.refs_2_), channel_id=1, source_target_pairs={{0,1},{1,0},{2,3},{3,2},{4,5},{5,4},{6,7},{7,6},{8,9},{9,8},{10,11... | collective-permute-start | bytes 786440 | tf_op jit(solution)/shard_map/ppermute | solution.py:102
  30.7 4.8 %collective-permute-start.8 = (bf16[2,64,1024]{2,1,0:T(8,128)(2,1)S(1)}, bf16[2,64,1024]{2,1,0:T(8,128)(2,1)S(1)}, u32[]{:S(2)}, u32[]{:S(2)}) collective-permute-start(bf16[2,64,1024]{2,1,0:T(8,128)(2,1)S(1)} %collective-permute-done.4.refs_1_), channel_id=1, source_target_pairs={{0,1},{1,0},{2,3},{3,2},{4,5},{5,4},{6,7},{7,6},{8,9},{9,8},{10,11... | collective-permute-start | bytes 786440 | tf_op jit(solution)/shard_map/ppermute | solution.py:102
  30.9 4.7 %collective-permute-start.10 = (bf16[2,64,1024]{2,1,0:T(8,128)(2,1)S(1)}, bf16[2,64,1024]{2,1,0:T(8,128)(2,1)S(1)}, u32[]{:S(2)}, u32[]{:S(2)}) collective-permute-start(bf16[2,64,1024]{2,1,0:T(8,128)(2,1)S(1)} %collective-permute-done.9.refs_2_), channel_id=1, source_target_pairs={{0,1},{1,0},{2,3},{3,2},{4,5},{5,4},{6,7},{7,6},{8,9},{9,8},{10,11... | collective-permute-start | bytes 786440 | tf_op jit(solution)/shard_map/ppermute | solution.py:102

commit v16 on v15

--- a/solution.py
+++ b/solution.py
@@ -284,13 +284,15 @@
             arrays[name] = array
             found.update({place: (name, at) for at, place in enumerate(places)})
 
-        def phase(places, state, last=False):
+        def phase(places, state, last=False, after=None):
             names = list(dict.fromkeys(found[place][0] for place in places))
             sources = [
                 [(place, found[place][1]) for place in places if found[place][0] == name]
                 for name in names
             ]
             operands = [arrays[name] for name in names]
+            if after:
+                operands, arrays[after] = lax.optimization_barrier((operands, arrays[after]))
             keys = tok * len(places)
             levels = {dz for dz, _, _ in places}
             scratch = []
@@ -321,8 +323,8 @@
         batches[0].append((0, 0, 0))
         final = [(depth - 1, 0, 1)]
         if straight:
-            final += [(depth - 1, 0, 0), (depth - 2, 1, 0), (depth - 2, 1, 1)]
-            batches[-1] = [(depth - 1, 1, 0), (depth - 1, 1, 1), (depth - 2, 0, 1), (depth - 3, 1, 1)]
+            final += [(depth - 2, 1, 0), (depth - 2, 1, 1), (depth - 1, 1, 1)]
+            batches[-1] = [(depth - 1, 1, 0), (depth - 1, 0, 0), (depth - 2, 0, 1), (depth - 3, 1, 1)]
         while len(batches) > 8:
             batches = [sum(batches[at : at + 2], []) for at in range(0, len(batches), 2)]
 
@@ -337,10 +339,10 @@
                 keep(f"y{dz}", y_swap(block, grid), [(dz, 1, 0)])
             if straight and dz == 0:
                 keep("w", far_swap(block, grid, groups), [(depth - 1, 1, 0)])
-            if straight and dz == 1:
+            if straight and dz == depth - 1:
                 keep("cw", core_swap(arrays["w"], grid), [(depth - 1, 1, 1)])
             if dz and all(place in found for place in batches[0]):
-                state = phase(batches.pop(0), state)
+                state = phase(batches.pop(0), state, after="w" if straight and dz == 1 else None)
             keep(f"c{dz}", core_swap(block, grid), [(dz, 0, 1)])
             if dz and straight:
                 keep(f"d{dz}", core_swap(arrays[f"y{dz - 1}"], grid), [(dz - 1, 1, 1)])

time: 41.3 us -> 41.8 us (1.012)
  the two profiles are of different devices: /device:TPU:25 before, /device:TPU:17 now
where the time goes in v16:
time: 41.8 us; the launch traced here: 41.6 us
  Pallas kernels  21.2 us (51%)
  starting transfers between devices  19.7 us (47%)
  waiting for transfers between devices  0.72 us (2%)
    pallas_call x4, Pallas kernels, phase(): pl.pallas_call(functools.partial(attend_kernel, grid, sources, bool(state...  18.6 us
    ppermute x8, starting transfers between devices, core_swap(): lax.ppermute(blocks, 'tp', [(at, at ^ 1) for at in range(depth * width *...  11.9 us
    ppermute x3, starting transfers between devices, z_forward(): return lax.ppermute(block, 'tp', pairs)  3.82 us
    ppermute x3, starting transfers between devices, y_swap(): lax.ppermute(block, 'tp', [(at, at ^ cores) for at in range(depth * width...  2.7 us
    pallas_call x1, Pallas kernels, fetch(): pl.pallas_call(kernel, out_shape=jax.ShapeDtypeStruct(array.shape, array....  1.6 us
    ppermute x1, starting transfers between devices, far_swap(): return lax.ppermute(block, ('groups', 'tp'), pairs)  1.21 us
    pallas_call x1, Pallas kernels, stack(): pl.pallas_call(kernel, out_shape=jax.ShapeDtypeStruct((count, *arrays[0]....  0.98 us
  transfers between devices with their start and end apart: 15, of which 1 were waited for; matrix products, arithmetic and copies ran while one was open for 0% of the time, Pallas kernels for 34%

profile of v16, /device:TPU:17, one launch (start us, length us, event | category | flops | bytes accessed | tf_op | source)
XLA Modules:
  0.0 41.6 jit_solution(13401011961116891677)
XLA Ops:
  0.0 1.0 %pack.1.refs_3_ = bf16[2,64,1024]{2,1,0:T(8,128)(2,1)S(1)} custom-call(bf16[64,1024]{1,0:T(8,128)(2,1)} %refs_0_.1, bf16[64,1024]{1,0:T(8,128)(2,1)} %refs_1_.1), custom_call_target="tpu_custom_call" | custom-call | tf_op jit(solution)/shard_map/pack/pallas_call | solution.py:41
  1.0 1.3 %collective-permute-start = (bf16[2,64,1024]{2,1,0:T(8,128)(2,1)S(1)}, bf16[2,64,1024]{2,1,0:T(8,128)(2,1)S(1)}, u32[]{:S(2)}, u32[]{:S(2)}) collective-permute-start(bf16[2,64,1024]{2,1,0:T(8,128)(2,1)S(1)} %pack.1.refs_3_), channel_id=1, source_target_pairs={{0,4},{1,5},{2,6},{3,7},{4,8},{5,9},{6,10},{7,11},{8,12},{9,13},{1... | collective-permute-start | bytes 786440 | tf_op jit(solution)/shard_map/ppermute | solution.py:75
  2.3 1.2 %collective-permute-start.3 = (bf16[2,64,1024]{2,1,0:T(8,128)(2,1)S(1)}, bf16[2,64,1024]{2,1,0:T(8,128)(2,1)S(1)}, u32[]{:S(2)}, u32[]{:S(2)}) collective-permute-start(bf16[2,64,1024]{2,1,0:T(8,128)(2,1)S(1)} %pack.1.refs_3_), channel_id=1, source_target_pairs={{0,2},{1,3},{2,0},{3,1},{4,6},{5,7},{6,4},{7,5},{8,10},{9,11},{10,... | collective-permute-start | bytes 786440 | tf_op jit(solution)/shard_map/ppermute | solution.py:80
  3.6 1.2 %collective-permute-start.2 = (bf16[2,64,1024]{2,1,0:T(8,128)(2,1)S(1)}, bf16[2,64,1024]{2,1,0:T(8,128)(2,1)S(1)}, u32[]{:S(2)}, u32[]{:S(2)}) collective-permute-start(bf16[2,64,1024]{2,1,0:T(8,128)(2,1)S(1)} %pack.1.refs_3_), channel_id=1, source_target_pairs={{0,1},{1,0},{2,3},{3,2},{4,5},{5,4},{6,7},{7,6},{8,9},{9,8},{10,11... | collective-permute-start | bytes 786440 | tf_op jit(solution)/shard_map/ppermute | solution.py:102
  4.8 1.2 %collective-permute-start.4 = (bf16[2,64,1024]{2,1,0:T(8,128)(2,1)S(1)}, bf16[2,64,1024]{2,1,0:T(8,128)(2,1)S(1)}, u32[]{:S(2)}, u32[]{:S(2)}) collective-permute-start(bf16[2,64,1024]{2,1,0:T(8,128)(2,1)S(1)} %pack.1.refs_3_), channel_id=1, source_target_pairs={{0,14},{1,15},{2,12},{3,13},{4,20},{5,21},{6,22},{7,23},{8,24},{9,... | collective-permute-start | bytes 786440 | tf_op jit(solution)/shard_map/ppermute | solution.py:97
  6.0 1.6 %fetch.1.query_ref = bf16[64,16384]{1,0:T(8,128)(2,1)S(1)} custom-call(bf16[64,16384]{1,0:T(8,128)(2,1)} %array_ref.1), custom_call_target="tpu_custom_call" | custom-call | tf_op jit(solution)/shard_map/fetch/pallas_call | solution.py:57
  7.6 0.7 %collective-permute-done.refs_0_ = bf16[2,64,1024]{2,1,0:T(8,128)(2,1)S(1)} collective-permute-done((bf16[2,64,1024]{2,1,0:T(8,128)(2,1)S(1)}, bf16[2,64,1024]{2,1,0:T(8,128)(2,1)S(1)}, u32[]{:S(2)}, u32[]{:S(2)}) %collective-permute-start) | collective-permute-done | bytes 262176 | tf_op jit(solution)/shard_map/ppermute | solution.py:75
  8.3 1.4 %collective-permute-start.1 = (bf16[2,64,1024]{2,1,0:T(8,128)(2,1)S(1)}, bf16[2,64,1024]{2,1,0:T(8,128)(2,1)S(1)}, u32[]{:S(2)}, u32[]{:S(2)}) collective-permute-start(bf16[2,64,1024]{2,1,0:T(8,128)(2,1)S(1)} %collective-permute-done.refs_0_), channel_id=1, source_target_pairs={{0,4},{1,5},{2,6},{3,7},{4,8},{5,9},{6,10},{7,11},{8,12},{9,13},{1... | collective-permute-start | bytes 786440 | tf_op jit(solution)/shard_map/ppermute | solution.py:75
  9.7 1.2 %collective-permute-start.7 = (bf16[2,64,1024]{2,1,0:T(8,128)(2,1)S(1)}, bf16[2,64,1024]{2,1,0:T(8,128)(2,1)S(1)}, u32[]{:S(2)}, u32[]{:S(2)}) collective-permute-start(bf16[2,64,1024]{2,1,0:T(8,128)(2,1)S(1)} %collective-permute-done.refs_0_), channel_id=1, source_target_pairs={{0,2},{1,3},{2,0},{3,1},{4,6},{5,7},{6,4},{7,5},{8,10},{9,11},{10,... | collective-permute-start | bytes 786440 | tf_op jit(solution)/shard_map/ppermute | solution.py:80
  11.0 0.0 collective-permute-done.3.refs_2_
  11.0 6.5 %collective-permute-start.6 = (bf16[2,64,1024]{2,1,0:T(8,128)(2,1)S(1)}, bf16[2,64,1024]{2,1,0:T(8,128)(2,1)S(1)}, u32[]{:S(2)}, u32[]{:S(2)}) collective-permute-start(bf16[2,64,1024]{2,1,0:T(8,128)(2,1)S(1)} %collective-permute-done.refs_0_), channel_id=1, source_target_pairs={{0,1},{1,0},{2,3},{3,2},{4,5},{5,4},{6,7},{7,6},{8,9},{9,8},{10,11... | collective-permute-start | bytes 786440 | tf_op jit(solution)/shard_map/ppermute | solution.py:102
  17.5 0.0 collective-permute-done.2.refs_1_
  17.5 0.0 collective-permute-done.4.refs_0_
  17.5 3.7 %attend.3 = (f32[8,1024,256]{2,1,0:T(8,128)S(1)}, f32[8,1024,128]{2,1,0:T(8,128)S(1)}) custom-call(bf16[64,16384]{1,0:T(8,128)(2,1)S(1)} %fetch.1.query_ref, bf16[2,64,1024]{2,1,0:T(8,128)(2,1)S(1)} %collective-permute-done.refs_0_, bf16[2,64,1024]{2,1,0:T(8,128)(2,1)S(1)} %collective-permute-done.2.refs_1_, ...), custom_call_target="tpu_custom_call" | custom-call | flops 1000 | bytes 1000 | tf_op jit(solution)/shard_map/attend/pallas_call | solution.py:304
  21.2 0.1 collective-permute-start.8
  21.3 0.0 collective-permute-done.1.refs_0_
  21.3 1.1 %collective-permute-start.5 = (bf16[2,64,1024]{2,1,0:T(8,128)(2,1)S(1)}, bf16[2,64,1024]{2,1,0:T(8,128)(2,1)S(1)}, u32[]{:S(2)}, u32[]{:S(2)}) collective-permute-start(bf16[2,64,1024]{2,1,0:T(8,128)(2,1)S(1)} %collective-permute-done.1.refs_0_), channel_id=1, source_target_pairs={{0,4},{1,5},{2,6},{3,7},{4,0},{5,1},{6,2},{7,3},{8,12},{9,13},{10,... | collective-permute-start | bytes 786440 | tf_op jit(solution)/shard_map/ppermute | solution.py:75
  22.4 0.2 collective-permute-start.10
  22.6 0.0 collective-permute-done.7.refs_2_
  22.6 1.5 %collective-permute-start.12 = (bf16[2,64,1024]{2,1,0:T(8,128)(2,1)S(1)}, bf16[2,64,1024]{2,1,0:T(8,128)(2,1)S(1)}, u32[]{:S(2)}, u32[]{:S(2)}) collective-permute-start(bf16[2,64,1024]{2,1,0:T(8,128)(2,1)S(1)} %collective-permute-done.4.refs_0_), channel_id=1, source_target_pairs={{0,1},{1,0},{2,3},{3,2},{4,5},{5,4},{6,7},{7,6},{8,9},{9,8},{10,11... | collective-permute-start | bytes 786440 | tf_op jit(solution)/shard_map/ppermute | solution.py:102
  24.1 0.0 collective-permute-done.6.refs_1_
  24.1 0.1 collective-permute-start.13
  24.2 0.4 %collective-permute-start.14 = (bf16[2,64,1024]{2,1,0:T(8,128)(2,1)S(1)}, bf16[2,64,1024]{2,1,0:T(8,128)(2,1)S(1)}, u32[]{:S(2)}, u32[]{:S(2)}) collective-permute-start(bf16[2,64,1024]{2,1,0:T(8,128)(2,1)S(1)} %collective-permute-done.7.refs_2_), channel_id=1, source_target_pairs={{0,1},{1,0},{2,3},{3,2},{4,5},{5,4},{6,7},{7,6},{8,9},{9,8},{10,11... | collective-permute-start | bytes 786440 | tf_op jit(solution)/shard_map/ppermute | solution.py:102
  24.6 4.4 %attend.4 = (f32[8,1024,256]{2,1,0:T(8,128)S(1)}, f32[8,1024,128]{2,1,0:T(8,128)S(1)}) custom-call(bf16[64,16384]{1,0:T(8,128)(2,1)S(1)} %fetch.1.query_ref, bf16[2,64,1024]{2,1,0:T(8,128)(2,1)S(1)} %collective-permute-done.1.refs_0_, bf16[2,64,1024]{2,1,0:T(8,128)(2,1)S(1)} %collective-permute-done.6.refs_1_, ...), custom_call_target="tpu_custom_call", output_to_operand_aliasing={{0}: (5, {}), {1}: (6, {})} | custom-call | flops 1000 | bytes 1000 | tf_op jit(solution)/shard_map/attend/pallas_call | solution.py:304
  29.0 1.1 %collective-permute-start.9 = (bf16[2,64,1024]{2,1,0:T(8,128)(2,1)S(1)}, bf16[2,64,1024]{2,1,0:T(8,128)(2,1)S(1)}, u32[]{:S(2)}, u32[]{:S(2)}) collective-permute-start(bf16[2,64,1024]{2,1,0:T(8,128)(2,1)S(1)} %collective-permute-done.5.refs_1_), channel_id=1, source_target_pairs={{0,1},{1,0},{2,3},{3,2},{4,5},{5,4},{6,7},{7,6},{8,9},{9,8},{10,11... | collective-permute-start | bytes 786440 | tf_op jit(solution)/shard_map/ppermute | solution.py:102
  30.1 1.0 %collective-permute-start.11 = (bf16[2,64,1024]{2,1,0:T(8,128)(2,1)S(1)}, bf16[2,64,1024]{2,1,0:T(8,128)(2,1)S(1)}, u32[]{:S(2)}, u32[]{:S(2)}) collective-permute-start(bf16[2,64,1024]{2,1,0:T(8,128)(2,1)S(1)} %collective-permute-done.10.refs_1_), channel_id=1, source_target_pairs={{0,1},{1,0},{2,3},{3,2},{4,5},{5,4},{6,7},{7,6},{8,9},{9,8},{10,11... | collective-permute-start | bytes 786440 | tf_op jit(solution)/shard_map/ppermute | solution.py:102
  31.1 0.0 collective-permute-done.13.refs_2_
  31.1 0.0 collective-permute-done.14.refs_3_
  31.1 4.7 %attend.5 = (f32[8,1024,256]{2,1,0:T(8,128)S(1)}, f32[8,1024,128]{2,1,0:T(8,128)S(1)}) custom-call(bf16[64,16384]{1,0:T(8,128)(2,1)S(1)} %fetch.1.query_ref, bf16[2,64,1024]{2,1,0:T(8,128)(2,1)S(1)} %collective-permute-done.4.refs_0_, bf16[2,64,1024]{2,1,0:T(8,128)(2,1)S(1)} %collective-permute-done.5.refs_1_, ...), custom_call_target="tpu_custom_call", output_to_operand_aliasing={{0}: (5, {}), {1}: (6, {})} | custom-call | flops 1000 | bytes 1000 | tf_op jit(solution)/shard_map/attend/pallas_call | solution.py:304
  35.8 0.0 collective-permute-done.9.refs_0_
  35.8 0.0 collective-permute-done.11.refs_2_
  35.8 5.8 %attend_last.1 = bf16[64,16384]{1,0:T(8,128)(2,1)} custom-call(bf16[64,16384]{1,0:T(8,128)(2,1)S(1)} %fetch.1.query_ref, bf16[2,64,1024]{2,1,0:T(8,128)(2,1)S(1)} %collective-permute-done.9.refs_0_, bf16[2,64,1024]{2,1,0:T(8,128)(2,1)S(1)} %collective-permute-done.10.refs_1_, bf16[2,64,1024]{2,1,0:T(8,128)(2,1)S(1)} %collective-permute-done.11.refs_2_, ...), custom_call_target="tpu_custom_call" | custom-call | flops 1000 | bytes 1000 | tf_op jit(solution)/shard_map/attend_last/pallas_call | solution.py:304
  (4 shorter events, 0.0 us)
Async XLA Ops:
  1.0 7.3 %collective-permute-start = (bf16[2,64,1024]{2,1,0:T(8,128)(2,1)S(1)}, bf16[2,64,1024]{2,1,0:T(8,128)(2,1)S(1)}, u32[]{:S(2)}, u32[]{:S(2)}) collective-permute-start(bf16[2,64,1024]{2,1,0:T(8,128)(2,1)S(1)} %pack.1.refs_3_), channel_id=1, source_target_pairs={{0,4},{1,5},{2,6},{3,7},{4,8},{5,9},{6,10},{7,11},{8,12},{9,13},{1... | collective-permute-start | bytes 786440 | tf_op jit(solution)/shard_map/ppermute | solution.py:75
  2.3 8.6 %collective-permute-start.3 = (bf16[2,64,1024]{2,1,0:T(8,128)(2,1)S(1)}, bf16[2,64,1024]{2,1,0:T(8,128)(2,1)S(1)}, u32[]{:S(2)}, u32[]{:S(2)}) collective-permute-start(bf16[2,64,1024]{2,1,0:T(8,128)(2,1)S(1)} %pack.1.refs_3_), channel_id=1, source_target_pairs={{0,2},{1,3},{2,0},{3,1},{4,6},{5,7},{6,4},{7,5},{8,10},{9,11},{10,... | collective-permute-start | bytes 786440 | tf_op jit(solution)/shard_map/ppermute | solution.py:80
  3.6 13.9 %collective-permute-start.2 = (bf16[2,64,1024]{2,1,0:T(8,128)(2,1)S(1)}, bf16[2,64,1024]{2,1,0:T(8,128)(2,1)S(1)}, u32[]{:S(2)}, u32[]{:S(2)}) collective-permute-start(bf16[2,64,1024]{2,1,0:T(8,128)(2,1)S(1)} %pack.1.refs_3_), channel_id=1, source_target_pairs={{0,1},{1,0},{2,3},{3,2},{4,5},{5,4},{6,7},{7,6},{8,9},{9,8},{10,11... | collective-permute-start | bytes 786440 | tf_op jit(solution)/shard_map/ppermute | solution.py:102
  4.8 12.7 %collective-permute-start.4 = (bf16[2,64,1024]{2,1,0:T(8,128)(2,1)S(1)}, bf16[2,64,1024]{2,1,0:T(8,128)(2,1)S(1)}, u32[]{:S(2)}, u32[]{:S(2)}) collective-permute-start(bf16[2,64,1024]{2,1,0:T(8,128)(2,1)S(1)} %pack.1.refs_3_), channel_id=1, source_target_pairs={{0,14},{1,15},{2,12},{3,13},{4,20},{5,21},{6,22},{7,23},{8,24},{9,... | collective-permute-start | bytes 786440 | tf_op jit(solution)/shard_map/ppermute | solution.py:97
  8.3 13.0 %collective-permute-start.1 = (bf16[2,64,1024]{2,1,0:T(8,128)(2,1)S(1)}, bf16[2,64,1024]{2,1,0:T(8,128)(2,1)S(1)}, u32[]{:S(2)}, u32[]{:S(2)}) collective-permute-start(bf16[2,64,1024]{2,1,0:T(8,128)(2,1)S(1)} %collective-permute-done.refs_0_), channel_id=1, source_target_pairs={{0,4},{1,5},{2,6},{3,7},{4,8},{5,9},{6,10},{7,11},{8,12},{9,13},{1... | collective-permute-start | bytes 786440 | tf_op jit(solution)/shard_map/ppermute | solution.py:75
  9.7 12.9 %collective-permute-start.7 = (bf16[2,64,1024]{2,1,0:T(8,128)(2,1)S(1)}, bf16[2,64,1024]{2,1,0:T(8,128)(2,1)S(1)}, u32[]{:S(2)}, u32[]{:S(2)}) collective-permute-start(bf16[2,64,1024]{2,1,0:T(8,128)(2,1)S(1)} %collective-permute-done.refs_0_), channel_id=1, source_target_pairs={{0,2},{1,3},{2,0},{3,1},{4,6},{5,7},{6,4},{7,5},{8,10},{9,11},{10,... | collective-permute-start | bytes 786440 | tf_op jit(solution)/shard_map/ppermute | solution.py:80
  11.0 13.1 %collective-permute-start.6 = (bf16[2,64,1024]{2,1,0:T(8,128)(2,1)S(1)}, bf16[2,64,1024]{2,1,0:T(8,128)(2,1)S(1)}, u32[]{:S(2)}, u32[]{:S(2)}) collective-permute-start(bf16[2,64,1024]{2,1,0:T(8,128)(2,1)S(1)} %collective-permute-done.refs_0_), channel_id=1, source_target_pairs={{0,1},{1,0},{2,3},{3,2},{4,5},{5,4},{6,7},{7,6},{8,9},{9,8},{10,11... | collective-permute-start | bytes 786440 | tf_op jit(solution)/shard_map/ppermute | solution.py:102
  21.2 3.0 %collective-permute-start.8 = (bf16[2,64,1024]{2,1,0:T(8,128)(2,1)S(1)}, bf16[2,64,1024]{2,1,0:T(8,128)(2,1)S(1)}, u32[]{:S(2)}, u32[]{:S(2)}) collective-permute-start(bf16[2,64,1024]{2,1,0:T(8,128)(2,1)S(1)} %collective-permute-done.3.refs_2_), channel_id=1, source_target_pairs={{0,1},{1,0},{2,3},{3,2},{4,5},{5,4},{6,7},{7,6},{8,9},{9,8},{10,11... | collective-permute-start | bytes 786440 | tf_op jit(solution)/shard_map/ppermute | solution.py:102
  21.3 7.7 %collective-permute-start.5 = (bf16[2,64,1024]{2,1,0:T(8,128)(2,1)S(1)}, bf16[2,64,1024]{2,1,0:T(8,128)(2,1)S(1)}, u32[]{:S(2)}, u32[]{:S(2)}) collective-permute-start(bf16[2,64,1024]{2,1,0:T(8,128)(2,1)S(1)} %collective-permute-done.1.refs_0_), channel_id=1, source_target_pairs={{0,4},{1,5},{2,6},{3,7},{4,0},{5,1},{6,2},{7,3},{8,12},{9,13},{10,... | collective-permute-start | bytes 786440 | tf_op jit(solution)/shard_map/ppermute | solution.py:75
  22.4 7.7 %collective-permute-start.10 = (bf16[2,64,1024]{2,1,0:T(8,128)(2,1)S(1)}, bf16[2,64,1024]{2,1,0:T(8,128)(2,1)S(1)}, u32[]{:S(2)}, u32[]{:S(2)}) collective-permute-start(bf16[2,64,1024]{2,1,0:T(8,128)(2,1)S(1)} %collective-permute-done.1.refs_0_), channel_id=1, source_target_pairs={{0,2},{1,3},{2,0},{3,1},{4,6},{5,7},{6,4},{7,5},{8,10},{9,11},{10,... | collective-permute-start | bytes 786440 | tf_op jit(solution)/shard_map/ppermute | solution.py:80
  22.6 13.2 %collective-permute-start.12 = (bf16[2,64,1024]{2,1,0:T(8,128)(2,1)S(1)}, bf16[2,64,1024]{2,1,0:T(8,128)(2,1)S(1)}, u32[]{:S(2)}, u32[]{:S(2)}) collective-permute-start(bf16[2,64,1024]{2,1,0:T(8,128)(2,1)S(1)} %collective-permute-done.4.refs_0_), channel_id=1, source_target_pairs={{0,1},{1,0},{2,3},{3,2},{4,5},{5,4},{6,7},{7,6},{8,9},{9,8},{10,11... | collective-permute-start | bytes 786440 | tf_op jit(solution)/shard_map/ppermute | solution.py:102
  24.1 7.0 %collective-permute-start.13 = (bf16[2,64,1024]{2,1,0:T(8,128)(2,1)S(1)}, bf16[2,64,1024]{2,1,0:T(8,128)(2,1)S(1)}, u32[]{:S(2)}, u32[]{:S(2)}) collective-permute-start(bf16[2,64,1024]{2,1,0:T(8,128)(2,1)S(1)} %collective-permute-done.1.refs_0_), channel_id=1, source_target_pairs={{0,1},{1,0},{2,3},{3,2},{4,5},{5,4},{6,7},{7,6},{8,9},{9,8},{10,11... | collective-permute-start | bytes 786440 | tf_op jit(solution)/shard_map/ppermute | solution.py:102
  24.2 6.9 %collective-permute-start.14 = (bf16[2,64,1024]{2,1,0:T(8,128)(2,1)S(1)}, bf16[2,64,1024]{2,1,0:T(8,128)(2,1)S(1)}, u32[]{:S(2)}, u32[]{:S(2)}) collective-permute-start(bf16[2,64,1024]{2,1,0:T(8,128)(2,1)S(1)} %collective-permute-done.7.refs_2_), channel_id=1, source_target_pairs={{0,1},{1,0},{2,3},{3,2},{4,5},{5,4},{6,7},{7,6},{8,9},{9,8},{10,11... | collective-permute-start | bytes 786440 | tf_op jit(solution)/shard_map/ppermute | solution.py:102
  29.0 6.8 %collective-permute-start.9 = (bf16[2,64,1024]{2,1,0:T(8,128)(2,1)S(1)}, bf16[2,64,1024]{2,1,0:T(8,128)(2,1)S(1)}, u32[]{:S(2)}, u32[]{:S(2)}) collective-permute-start(bf16[2,64,1024]{2,1,0:T(8,128)(2,1)S(1)} %collective-permute-done.5.refs_1_), channel_id=1, source_target_pairs={{0,1},{1,0},{2,3},{3,2},{4,5},{5,4},{6,7},{7,6},{8,9},{9,8},{10,11... | collective-permute-start | bytes 786440 | tf_op jit(solution)/shard_map/ppermute | solution.py:102
  30.1 5.7 %collective-permute-start.11 = (bf16[2,64,1024]{2,1,0:T(8,128)(2,1)S(1)}, bf16[2,64,1024]{2,1,0:T(8,128)(2,1)S(1)}, u32[]{:S(2)}, u32[]{:S(2)}) collective-permute-start(bf16[2,64,1024]{2,1,0:T(8,128)(2,1)S(1)} %collective-permute-done.10.refs_1_), channel_id=1, source_target_pairs={{0,1},{1,0},{2,3},{3,2},{4,5},{5,4},{6,7},{7,6},{8,9},{9,8},{10,11... | collective-permute-start | bytes 786440 | tf_op jit(solution)/shard_map/ppermute | solution.py:102

commit v17 on v14

--- a/solution.py
+++ b/solution.py
@@ -201,18 +201,19 @@
 
         all_heads(one)
 
-    def out_copy(step):
-        span = STEP_HEADS * GROUP * dim
-        here = pl.ds(pl.multiple_of(step * span, span), span)
-        return pltpu.make_async_copy(out_refs[0].at[:, here], result_ref.at[:, here], sems.at[step])
+    def out_copy(head):
+        span = GROUP * dim
+        here = pl.ds(pl.multiple_of(head * span, span), span)
+        return pltpu.make_async_copy(out_refs[0].at[:, here], result_ref.at[:, here], sems.at[head])
 
     def all_heads(one):
         @pl.loop(0, KV_HEADS // STEP_HEADS)
         def _(step):
             for index in range(STEP_HEADS):
-                one(step * STEP_HEADS + index)
-            if last:
-                out_copy(step).start()
+                head = step * STEP_HEADS + index
+                one(head)
+                if last:
+                    out_copy(head).start()
 
     near = tok * sum(piece[0] == 0 for piece in pieces)
     near = min(-(-near // dim) * dim, len(pieces) * tok)
@@ -236,9 +237,9 @@
 
     if last:
 
-        @pl.loop(0, KV_HEADS // STEP_HEADS)
-        def _(step):
-            out_copy(step).wait()
+        @pl.loop(0, KV_HEADS)
+        def _(head):
+            out_copy(head).wait()
 
 
 def solution(mesh):
@@ -250,7 +251,7 @@
         tok, columns = query_rows.shape
         dim = key_rows.shape[1] // KV_HEADS
         rows = GROUP * tok
-        query_rows, key_rows, value_rows = (
+        query_rows, *own = (
             pltpu.with_memory_space_constraint(array, pltpu.HBM)
             for array in (query_rows, key_rows, value_rows)
         )
@@ -258,7 +259,6 @@
         state_shapes = [
             jax.ShapeDtypeStruct((KV_HEADS, rows, size), jnp.float32) for size in (2 * dim, dim)
         ]
-        steps = KV_HEADS // STEP_HEADS
 
         arrays, found = {}, {}
 
@@ -278,7 +278,7 @@
             scratch = []
             if last:
                 scratch += [pltpu.VMEM((tok, columns), query_rows.dtype)]
-                scratch += [pltpu.SemaphoreType.DMA((steps,))]
+                scratch += [pltpu.SemaphoreType.DMA((KV_HEADS,))]
             if 0 in levels or len(levels) > 1:
                 scratch += [pltpu.VMEM((tok, keys), jnp.float32)]
             return pl.pallas_call(
@@ -307,12 +307,14 @@
         while len(batches) > 8:
             batches = [sum(batches[at : at + 2], []) for at in range(0, len(batches), 2)]
 
-        keep("z0", stack([key_rows, value_rows], "pack"), [(0, 0, 0)])
+        keep("z0", stack(own, "pack"), [(0, 0, 0)])
         queries = fetch(query_rows)
         state = []
         for dz in range(depth):
             block = arrays[f"z{dz}"]
-            if dz + 1 < depth:
+            if dz == 0:
+                parts = [z_forward(array, grid, 1) for array in (key_rows, value_rows)]
+            elif dz + 1 < depth:
                 keep(f"z{dz + 1}", z_forward(block, grid, dz + 1), [(dz + 1, 0, 0)])
             if width == 2:
                 keep(f"y{dz}", y_swap(block, grid), [(dz, 1, 0)])
@@ -321,7 +323,10 @@
             keep(f"c{dz}", core_swap(block, grid), [(dz, 0, 1)])
             if dz and width == 2:
                 keep(f"d{dz}", core_swap(arrays[f"y{dz - 1}"], grid), [(dz - 1, 1, 1)])
-            if dz + 1 < depth:
+            if dz == 0:
+                parts, state, queries = lax.optimization_barrier((parts, state, queries))
+                keep("z1", stack(parts, "pack"), [(1, 0, 0)])
+            elif dz + 1 < depth:
                 tied = [f"z{dz + 1}"]
                 values, state, queries = lax.optimization_barrier(
                     ([arrays[name] for name in tied], state, queries)

time: 40.5 us -> 39.7 us (0.980)
  waiting for transfers between devices: 5.74 us -> 3.28 us
  starting transfers between devices: 13.7 us -> 15.4 us
    ppermute x3 -> x4, waiting for transfers between devices: 4.19 us -> 1.75 us  [z_forward(): return lax.ppermute(block, 'tp', pairs)]
    ppermute x3 -> x4, starting transfers between devices: 2.25 us -> 3.48 us  [z_forward(): return lax.ppermute(block, 'tp', pairs)]
    ppermute x8, starting transfers between devices: 8.83 us -> 9.26 us  [core_swap(): lax.ppermute(blocks, 'tp', [(at, at ^ 1) for at in range(depth * width *...]
    pallas_call x1 -> x2, Pallas kernels: 0.98 us -> 1.01 us  [stack(): pl.pallas_call(kernel, out_shape=jax.ShapeDtypeStruct((count, *arrays[0]....]
  transfers between devices with their start and end apart: 15 -> 16, of which waited for: 4 -> 4; matrix products, arithmetic and copies ran while one was open for 0% -> 0% of each run, Pallas kernels for 35% -> 38%
where the time goes in v17:
time: 39.7 us; the launch traced here: 39.1 us
  Pallas kernels  20.4 us (51%)
  starting transfers between devices  15.4 us (39%)
  waiting for transfers between devices  3.28 us (8%)
    pallas_call x4, Pallas kernels, phase(): pl.pallas_call(functools.partial(attend_kernel, grid, sources, bool(state...  17.8 us
    ppermute x8, starting transfers between devices, core_swap(): lax.ppermute(blocks, 'tp', [(at, at ^ 1) for at in range(depth * width *...  9.26 us
    ppermute x4, starting transfers between devices, z_forward(): return lax.ppermute(block, 'tp', pairs)  3.48 us
    ppermute x4, starting transfers between devices, y_swap(): lax.ppermute(block, 'tp', [(at, at ^ cores) for at in range(depth * width...  2.62 us
    ppermute x4, waiting for transfers between devices, z_forward(): return lax.ppermute(block, 'tp', pairs)  1.75 us
    pallas_call x1, Pallas kernels, fetch(): pl.pallas_call(kernel, out_shape=jax.ShapeDtypeStruct(array.shape, array....  1.6 us
    ppermute x8, waiting for transfers between devices, core_swap(): lax.ppermute(blocks, 'tp', [(at, at ^ 1) for at in range(depth * width *...  1.17 us
    pallas_call x2, Pallas kernels, stack(): pl.pallas_call(kernel, out_shape=jax.ShapeDtypeStruct((count, *arrays[0]....  1.01 us
  transfers between devices with their start and end apart: 16, of which 4 were waited for; matrix products, arithmetic and copies ran while one was open for 0% of the time, Pallas kernels for 38%

profile of v17, /device:TPU:25, one launch (start us, length us, event | category | flops | bytes accessed | tf_op | source)
XLA Modules:
  0.0 39.1 jit_solution(15489159617369735822)
XLA Ops:
  0.0 1.2 %collective-permute-start.1 = (bf16[64,1024]{1,0:T(8,128)(2,1)}, bf16[64,1024]{1,0:T(8,128)(2,1)S(1)}, u32[]{:S(2)}, u32[]{:S(2)}) collective-permute-start(bf16[64,1024]{1,0:T(8,128)(2,1)} %refs_1_.1), channel_id=1, source_target_pairs={{0,4},{1,5},{2,6},{3,7},{4,8},{5,9},{6,10},{7,11},{8,12},{9,13},{1... | collective-permute-start | bytes 393224 | tf_op jit(solution)/shard_map/ppermute | solution.py:75
  1.2 1.0 %pack.3.refs_3_ = bf16[2,64,1024]{2,1,0:T(8,128)(2,1)S(1)} custom-call(bf16[64,1024]{1,0:T(8,128)(2,1)} %refs_0_.1, bf16[64,1024]{1,0:T(8,128)(2,1)} %refs_1_.1), custom_call_target="tpu_custom_call" | custom-call | tf_op jit(solution)/shard_map/pack/pallas_call | solution.py:41
  2.2 1.3 %collective-permute-start.4 = (bf16[2,64,1024]{2,1,0:T(8,128)(2,1)S(1)}, bf16[2,64,1024]{2,1,0:T(8,128)(2,1)S(1)}, u32[]{:S(2)}, u32[]{:S(2)}) collective-permute-start(bf16[2,64,1024]{2,1,0:T(8,128)(2,1)S(1)} %pack.3.refs_3_), channel_id=1, source_target_pairs={{0,2},{1,3},{2,0},{3,1},{4,6},{5,7},{6,4},{7,5},{8,10},{9,11},{10,... | collective-permute-start | bytes 786440 | tf_op jit(solution)/shard_map/ppermute | solution.py:80
  3.5 1.5 %collective-permute-start.3 = (bf16[2,64,1024]{2,1,0:T(8,128)(2,1)S(1)}, bf16[2,64,1024]{2,1,0:T(8,128)(2,1)S(1)}, u32[]{:S(2)}, u32[]{:S(2)}) collective-permute-start(bf16[2,64,1024]{2,1,0:T(8,128)(2,1)S(1)} %pack.3.refs_3_), channel_id=1, source_target_pairs={{0,1},{1,0},{2,3},{3,2},{4,5},{5,4},{6,7},{7,6},{8,9},{9,8},{10,11... | collective-permute-start | bytes 786440 | tf_op jit(solution)/shard_map/ppermute | solution.py:87
  5.1 1.6 %fetch.1.query_ref = bf16[64,16384]{1,0:T(8,128)(2,1)S(1)} custom-call(bf16[64,16384]{1,0:T(8,128)(2,1)} %array_ref.1), custom_call_target="tpu_custom_call" | custom-call | tf_op jit(solution)/shard_map/fetch/pallas_call | solution.py:57
  6.7 0.0 collective-permute-done.refs_0_
  6.7 0.7 %collective-permute-done.1.refs_1_ = bf16[64,1024]{1,0:T(8,128)(2,1)S(1)} collective-permute-done((bf16[64,1024]{1,0:T(8,128)(2,1)}, bf16[64,1024]{1,0:T(8,128)(2,1)S(1)}, u32[]{:S(2)}, u32[]{:S(2)}) %collective-permute-start.1) | collective-permute-done | bytes 131104 | tf_op jit(solution)/shard_map/ppermute | solution.py:75
  7.4 2.2 %collective-permute-start.2 = (bf16[2,64,1024]{2,1,0:T(8,128)(2,1)S(1)}, bf16[2,64,1024]{2,1,0:T(8,128)(2,1)S(1)}, u32[]{:S(2)}, u32[]{:S(2)}) collective-permute-start(bf16[2,64,1024]{2,1,0:T(8,128)(2,1)S(1)} %pack.2.refs_0_), channel_id=1, source_target_pairs={{0,4},{1,5},{2,6},{3,7},{4,8},{5,9},{6,10},{7,11},{8,12},{9,13},{1... | collective-permute-start | bytes 786440 | tf_op jit(solution)/shard_map/ppermute | solution.py:75
  9.6 1.0 %collective-permute-start.7 = (bf16[2,64,1024]{2,1,0:T(8,128)(2,1)S(1)}, bf16[2,64,1024]{2,1,0:T(8,128)(2,1)S(1)}, u32[]{:S(2)}, u32[]{:S(2)}) collective-permute-start(bf16[2,64,1024]{2,1,0:T(8,128)(2,1)S(1)} %pack.2.refs_0_), channel_id=1, source_target_pairs={{0,2},{1,3},{2,0},{3,1},{4,6},{5,7},{6,4},{7,5},{8,10},{9,11},{10,... | collective-permute-start | bytes 786440 | tf_op jit(solution)/shard_map/ppermute | solution.py:80
  10.6 2.0 %collective-permute-start.6 = (bf16[2,64,1024]{2,1,0:T(8,128)(2,1)S(1)}, bf16[2,64,1024]{2,1,0:T(8,128)(2,1)S(1)}, u32[]{:S(2)}, u32[]{:S(2)}) collective-permute-start(bf16[2,64,1024]{2,1,0:T(8,128)(2,1)S(1)} %pack.2.refs_0_), channel_id=1, source_target_pairs={{0,1},{1,0},{2,3},{3,2},{4,5},{5,4},{6,7},{7,6},{8,9},{9,8},{10,11... | collective-permute-start | bytes 786440 | tf_op jit(solution)/shard_map/ppermute | solution.py:87
  12.6 0.0 collective-permute-start.8
  12.6 0.0 collective-permute-done.3.refs_1_
  12.6 3.7 %attend.3 = (f32[8,1024,256]{2,1,0:T(8,128)S(1)}, f32[8,1024,128]{2,1,0:T(8,128)S(1)}) custom-call(bf16[64,16384]{1,0:T(8,128)(2,1)S(1)} %fetch.1.query_ref, bf16[2,64,1024]{2,1,0:T(8,128)(2,1)S(1)} %pack.2.refs_0_, bf16[2,64,1024]{2,1,0:T(8,128)(2,1)S(1)} %collective-permute-done.3.refs_1_, bf16[2,64,1024]{2,1,0:T(8,128)(2,1)S(1)} %collective-permute-done.4.refs_2_, ...), custom_call_target="tpu_custom_call" | custom-call | flops 1000 | bytes 1000 | tf_op jit(solution)/shard_map/attend/pallas_call | solution.py:284
  16.3 0.0 collective-permute-done.2.refs_0_
  16.3 0.1 collective-permute-start.5
  16.4 0.3 collective-permute-start.12
  16.7 0.0 collective-permute-done.7.refs_2_
  16.7 1.6 %collective-permute-start.11 = (bf16[2,64,1024]{2,1,0:T(8,128)(2,1)S(1)}, bf16[2,64,1024]{2,1,0:T(8,128)(2,1)S(1)}, u32[]{:S(2)}, u32[]{:S(2)}) collective-permute-start(bf16[2,64,1024]{2,1,0:T(8,128)(2,1)S(1)} %collective-permute-done.2.refs_0_), channel_id=1, source_target_pairs={{0,1},{1,0},{2,3},{3,2},{4,5},{5,4},{6,7},{7,6},{8,9},{9,8},{10,11... | collective-permute-start | bytes 786440 | tf_op jit(solution)/shard_map/ppermute | solution.py:87
  18.3 0.0 collective-permute-start.13
  18.3 0.0 collective-permute-done.8.refs_3_
  18.3 4.4 %attend.4 = (f32[8,1024,256]{2,1,0:T(8,128)S(1)}, f32[8,1024,128]{2,1,0:T(8,128)S(1)}) custom-call(bf16[64,16384]{1,0:T(8,128)(2,1)S(1)} %fetch.1.query_ref, bf16[2,64,1024]{2,1,0:T(8,128)(2,1)S(1)} %collective-permute-done.2.refs_0_, bf16[2,64,1024]{2,1,0:T(8,128)(2,1)S(1)} %collective-permute-done.6.refs_1_, ...), custom_call_target="tpu_custom_call", output_to_operand_aliasing={{0}: (5, {}), {1}: (6, {})} | custom-call | flops 1000 | bytes 1000 | tf_op jit(solution)/shard_map/attend/pallas_call | solution.py:284
  22.7 1.0 %collective-permute-done.5.refs_0_ = bf16[2,64,1024]{2,1,0:T(8,128)(2,1)S(1)} collective-permute-done((bf16[2,64,1024]{2,1,0:T(8,128)(2,1)S(1)}, bf16[2,64,1024]{2,1,0:T(8,128)(2,1)S(1)}, u32[]{:S(2)}, u32[]{:S(2)}) %collective-permute-start.5) | collective-permute-done | bytes 262176 | tf_op jit(solution)/shard_map/ppermute | solution.py:75
  23.8 0.0 collective-permute-start.10
  23.8 1.8 %collective-permute-start.9 = (bf16[2,64,1024]{2,1,0:T(8,128)(2,1)S(1)}, bf16[2,64,1024]{2,1,0:T(8,128)(2,1)S(1)}, u32[]{:S(2)}, u32[]{:S(2)}) collective-permute-start(bf16[2,64,1024]{2,1,0:T(8,128)(2,1)S(1)} %collective-permute-done.5.refs_0_), channel_id=1, source_target_pairs={{0,1},{1,0},{2,3},{3,2},{4,5},{5,4},{6,7},{7,6},{8,9},{9,8},{10,11... | collective-permute-start | bytes 786440 | tf_op jit(solution)/shard_map/ppermute | solution.py:87
  25.6 0.0 collective-permute-done.12.refs_2_
  25.6 0.0 collective-permute-start.14
  25.6 0.0 collective-permute-done.11.refs_1_
  25.6 4.2 %attend.5 = (f32[8,1024,256]{2,1,0:T(8,128)S(1)}, f32[8,1024,128]{2,1,0:T(8,128)S(1)}) custom-call(bf16[64,16384]{1,0:T(8,128)(2,1)S(1)} %fetch.1.query_ref, bf16[2,64,1024]{2,1,0:T(8,128)(2,1)S(1)} %collective-permute-done.5.refs_0_, bf16[2,64,1024]{2,1,0:T(8,128)(2,1)S(1)} %collective-permute-done.11.refs_1_, ...), custom_call_target="tpu_custom_call", output_to_operand_aliasing={{0}: (5, {}), {1}: (6, {})} | custom-call | flops 1000 | bytes 1000 | tf_op jit(solution)/shard_map/attend/pallas_call | solution.py:284
  29.9 0.4 collective-permute-done.10.refs_1_
  30.2 2.3 %collective-permute-start.15 = (bf16[2,64,1024]{2,1,0:T(8,128)(2,1)S(1)}, bf16[2,64,1024]{2,1,0:T(8,128)(2,1)S(1)}, u32[]{:S(2)}, u32[]{:S(2)}) collective-permute-start(bf16[2,64,1024]{2,1,0:T(8,128)(2,1)S(1)} %collective-permute-done.10.refs_1_), channel_id=1, source_target_pairs={{0,1},{1,0},{2,3},{3,2},{4,5},{5,4},{6,7},{7,6},{8,9},{9,8},{10,11... | collective-permute-start | bytes 786440 | tf_op jit(solution)/shard_map/ppermute | solution.py:87
  32.5 1.2 %collective-permute-done.15.refs_3_ = bf16[2,64,1024]{2,1,0:T(8,128)(2,1)S(1)} collective-permute-done((bf16[2,64,1024]{2,1,0:T(8,128)(2,1)S(1)}, bf16[2,64,1024]{2,1,0:T(8,128)(2,1)S(1)}, u32[]{:S(2)}, u32[]{:S(2)}) %collective-permute-start.15) | collective-permute-done | bytes 262176 | tf_op jit(solution)/shard_map/ppermute | solution.py:87
  33.6 5.5 %attend_last.1 = bf16[64,16384]{1,0:T(8,128)(2,1)} custom-call(bf16[64,16384]{1,0:T(8,128)(2,1)S(1)} %fetch.1.query_ref, bf16[2,64,1024]{2,1,0:T(8,128)(2,1)S(1)} %collective-permute-done.9.refs_0_, bf16[2,64,1024]{2,1,0:T(8,128)(2,1)S(1)} %collective-permute-done.10.refs_1_, bf16[2,64,1024]{2,1,0:T(8,128)(2,1)S(1)} %collective-permute-done.14.refs_2_, ...), custom_call_target="tpu_custom_call" | custom-call | flops 1000 | bytes 1000 | tf_op jit(solution)/shard_map/attend_last/pallas_call | solution.py:284
  (7 shorter events, 0.0 us)
Async XLA Ops:
  0.0 6.7 %collective-permute-start = (bf16[64,1024]{1,0:T(8,128)(2,1)}, bf16[64,1024]{1,0:T(8,128)(2,1)S(1)}, u32[]{:S(2)}, u32[]{:S(2)}) collective-permute-start(bf16[64,1024]{1,0:T(8,128)(2,1)} %refs_0_.1), channel_id=1, source_target_pairs={{0,4},{1,5},{2,6},{3,7},{4,8},{5,9},{6,10},{7,11},{8,12},{9,13},{1... | collective-permute-start | bytes 393224 | tf_op jit(solution)/shard_map/ppermute | solution.py:75
  0.0 7.4 %collective-permute-start.1 = (bf16[64,1024]{1,0:T(8,128)(2,1)}, bf16[64,1024]{1,0:T(8,128)(2,1)S(1)}, u32[]{:S(2)}, u32[]{:S(2)}) collective-permute-start(bf16[64,1024]{1,0:T(8,128)(2,1)} %refs_1_.1), channel_id=1, source_target_pairs={{0,4},{1,5},{2,6},{3,7},{4,8},{5,9},{6,10},{7,11},{8,12},{9,13},{1... | collective-permute-start | bytes 393224 | tf_op jit(solution)/shard_map/ppermute | solution.py:75
  2.2 10.4 %collective-permute-start.4 = (bf16[2,64,1024]{2,1,0:T(8,128)(2,1)S(1)}, bf16[2,64,1024]{2,1,0:T(8,128)(2,1)S(1)}, u32[]{:S(2)}, u32[]{:S(2)}) collective-permute-start(bf16[2,64,1024]{2,1,0:T(8,128)(2,1)S(1)} %pack.3.refs_3_), channel_id=1, source_target_pairs={{0,2},{1,3},{2,0},{3,1},{4,6},{5,7},{6,4},{7,5},{8,10},{9,11},{10,... | collective-permute-start | bytes 786440 | tf_op jit(solution)/shard_map/ppermute | solution.py:80
  3.5 9.1 %collective-permute-start.3 = (bf16[2,64,1024]{2,1,0:T(8,128)(2,1)S(1)}, bf16[2,64,1024]{2,1,0:T(8,128)(2,1)S(1)}, u32[]{:S(2)}, u32[]{:S(2)}) collective-permute-start(bf16[2,64,1024]{2,1,0:T(8,128)(2,1)S(1)} %pack.3.refs_3_), channel_id=1, source_target_pairs={{0,1},{1,0},{2,3},{3,2},{4,5},{5,4},{6,7},{7,6},{8,9},{9,8},{10,11... | collective-permute-start | bytes 786440 | tf_op jit(solution)/shard_map/ppermute | solution.py:87
  7.4 8.9 %collective-permute-start.2 = (bf16[2,64,1024]{2,1,0:T(8,128)(2,1)S(1)}, bf16[2,64,1024]{2,1,0:T(8,128)(2,1)S(1)}, u32[]{:S(2)}, u32[]{:S(2)}) collective-permute-start(bf16[2,64,1024]{2,1,0:T(8,128)(2,1)S(1)} %pack.2.refs_0_), channel_id=1, source_target_pairs={{0,4},{1,5},{2,6},{3,7},{4,8},{5,9},{6,10},{7,11},{8,12},{9,13},{1... | collective-permute-start | bytes 786440 | tf_op jit(solution)/shard_map/ppermute | solution.py:75
  9.6 7.1 %collective-permute-start.7 = (bf16[2,64,1024]{2,1,0:T(8,128)(2,1)S(1)}, bf16[2,64,1024]{2,1,0:T(8,128)(2,1)S(1)}, u32[]{:S(2)}, u32[]{:S(2)}) collective-permute-start(bf16[2,64,1024]{2,1,0:T(8,128)(2,1)S(1)} %pack.2.refs_0_), channel_id=1, source_target_pairs={{0,2},{1,3},{2,0},{3,1},{4,6},{5,7},{6,4},{7,5},{8,10},{9,11},{10,... | collective-permute-start | bytes 786440 | tf_op jit(solution)/shard_map/ppermute | solution.py:80
  10.6 7.7 %collective-permute-start.6 = (bf16[2,64,1024]{2,1,0:T(8,128)(2,1)S(1)}, bf16[2,64,1024]{2,1,0:T(8,128)(2,1)S(1)}, u32[]{:S(2)}, u32[]{:S(2)}) collective-permute-start(bf16[2,64,1024]{2,1,0:T(8,128)(2,1)S(1)} %pack.2.refs_0_), channel_id=1, source_target_pairs={{0,1},{1,0},{2,3},{3,2},{4,5},{5,4},{6,7},{7,6},{8,9},{9,8},{10,11... | collective-permute-start | bytes 786440 | tf_op jit(solution)/shard_map/ppermute | solution.py:87
  12.6 5.7 %collective-permute-start.8 = (bf16[2,64,1024]{2,1,0:T(8,128)(2,1)S(1)}, bf16[2,64,1024]{2,1,0:T(8,128)(2,1)S(1)}, u32[]{:S(2)}, u32[]{:S(2)}) collective-permute-start(bf16[2,64,1024]{2,1,0:T(8,128)(2,1)S(1)} %collective-permute-done.4.refs_2_), channel_id=1, source_target_pairs={{0,1},{1,0},{2,3},{3,2},{4,5},{5,4},{6,7},{7,6},{8,9},{9,8},{10,11... | collective-permute-start | bytes 786440 | tf_op jit(solution)/shard_map/ppermute | solution.py:87
  16.3 7.4 %collective-permute-start.5 = (bf16[2,64,1024]{2,1,0:T(8,128)(2,1)S(1)}, bf16[2,64,1024]{2,1,0:T(8,128)(2,1)S(1)}, u32[]{:S(2)}, u32[]{:S(2)}) collective-permute-start(bf16[2,64,1024]{2,1,0:T(8,128)(2,1)S(1)} %collective-permute-done.2.refs_0_), channel_id=1, source_target_pairs={{0,4},{1,5},{2,6},{3,7},{4,0},{5,1},{6,2},{7,3},{8,12},{9,13},{10,... | collective-permute-start | bytes 786440 | tf_op jit(solution)/shard_map/ppermute | solution.py:75
  16.4 9.2 %collective-permute-start.12 = (bf16[2,64,1024]{2,1,0:T(8,128)(2,1)S(1)}, bf16[2,64,1024]{2,1,0:T(8,128)(2,1)S(1)}, u32[]{:S(2)}, u32[]{:S(2)}) collective-permute-start(bf16[2,64,1024]{2,1,0:T(8,128)(2,1)S(1)} %collective-permute-done.2.refs_0_), channel_id=1, source_target_pairs={{0,2},{1,3},{2,0},{3,1},{4,6},{5,7},{6,4},{7,5},{8,10},{9,11},{10,... | collective-permute-start | bytes 786440 | tf_op jit(solution)/shard_map/ppermute | solution.py:80
  16.7 8.9 %collective-permute-start.11 = (bf16[2,64,1024]{2,1,0:T(8,128)(2,1)S(1)}, bf16[2,64,1024]{2,1,0:T(8,128)(2,1)S(1)}, u32[]{:S(2)}, u32[]{:S(2)}) collective-permute-start(bf16[2,64,1024]{2,1,0:T(8,128)(2,1)S(1)} %collective-permute-done.2.refs_0_), channel_id=1, source_target_pairs={{0,1},{1,0},{2,3},{3,2},{4,5},{5,4},{6,7},{7,6},{8,9},{9,8},{10,11... | collective-permute-start | bytes 786440 | tf_op jit(solution)/shard_map/ppermute | solution.py:87
  18.3 7.3 %collective-permute-start.13 = (bf16[2,64,1024]{2,1,0:T(8,128)(2,1)S(1)}, bf16[2,64,1024]{2,1,0:T(8,128)(2,1)S(1)}, u32[]{:S(2)}, u32[]{:S(2)}) collective-permute-start(bf16[2,64,1024]{2,1,0:T(8,128)(2,1)S(1)} %collective-permute-done.7.refs_2_), channel_id=1, source_target_pairs={{0,1},{1,0},{2,3},{3,2},{4,5},{5,4},{6,7},{7,6},{8,9},{9,8},{10,11... | collective-permute-start | bytes 786440 | tf_op jit(solution)/shard_map/ppermute | solution.py:87
  23.8 6.5 %collective-permute-start.10 = (bf16[2,64,1024]{2,1,0:T(8,128)(2,1)S(1)}, bf16[2,64,1024]{2,1,0:T(8,128)(2,1)S(1)}, u32[]{:S(2)}, u32[]{:S(2)}) collective-permute-start(bf16[2,64,1024]{2,1,0:T(8,128)(2,1)S(1)} %collective-permute-done.5.refs_0_), channel_id=1, source_target_pairs={{0,2},{1,3},{2,0},{3,1},{4,6},{5,7},{6,4},{7,5},{8,10},{9,11},{10,... | collective-permute-start | bytes 786440 | tf_op jit(solution)/shard_map/ppermute | solution.py:80
  23.8 8.7 %collective-permute-start.9 = (bf16[2,64,1024]{2,1,0:T(8,128)(2,1)S(1)}, bf16[2,64,1024]{2,1,0:T(8,128)(2,1)S(1)}, u32[]{:S(2)}, u32[]{:S(2)}) collective-permute-start(bf16[2,64,1024]{2,1,0:T(8,128)(2,1)S(1)} %collective-permute-done.5.refs_0_), channel_id=1, source_target_pairs={{0,1},{1,0},{2,3},{3,2},{4,5},{5,4},{6,7},{7,6},{8,9},{9,8},{10,11... | collective-permute-start | bytes 786440 | tf_op jit(solution)/shard_map/ppermute | solution.py:87
  25.6 6.9 %collective-permute-start.14 = (bf16[2,64,1024]{2,1,0:T(8,128)(2,1)S(1)}, bf16[2,64,1024]{2,1,0:T(8,128)(2,1)S(1)}, u32[]{:S(2)}, u32[]{:S(2)}) collective-permute-start(bf16[2,64,1024]{2,1,0:T(8,128)(2,1)S(1)} %collective-permute-done.12.refs_2_), channel_id=1, source_target_pairs={{0,1},{1,0},{2,3},{3,2},{4,5},{5,4},{6,7},{7,6},{8,9},{9,8},{10,11... | collective-permute-start | bytes 786440 | tf_op jit(solution)/shard_map/ppermute | solution.py:87
  30.2 3.4 %collective-permute-start.15 = (bf16[2,64,1024]{2,1,0:T(8,128)(2,1)S(1)}, bf16[2,64,1024]{2,1,0:T(8,128)(2,1)S(1)}, u32[]{:S(2)}, u32[]{:S(2)}) collective-permute-start(bf16[2,64,1024]{2,1,0:T(8,128)(2,1)S(1)} %collective-permute-done.10.refs_1_), channel_id=1, source_target_pairs={{0,1},{1,0},{2,3},{3,2},{4,5},{5,4},{6,7},{7,6},{8,9},{9,8},{10,11... | collective-permute-start | bytes 786440 | tf_op jit(solution)/shard_map/ppermute | solution.py:87

commit v18 on v17

--- a/solution.py
+++ b/solution.py
@@ -131,6 +131,8 @@
             bias_ref[:, at * tok : (at + 1) * tok] = jnp.where(limit <= row, 0.0, masked_score)
 
     def column(index):
+        if isinstance(index, int):
+            return pl.ds(index * dim, dim)
         return pl.ds(pl.multiple_of(index * dim, dim), dim)
 
     def emit(head, part, sums, peak):
@@ -203,17 +205,21 @@
 
     def out_copy(head):
         span = GROUP * dim
-        here = pl.ds(pl.multiple_of(head * span, span), span)
+        start = head * span if isinstance(head, int) else pl.multiple_of(head * span, span)
+        here = pl.ds(start, span)
         return pltpu.make_async_copy(out_refs[0].at[:, here], result_ref.at[:, here], sems.at[head])
 
     def all_heads(one):
+        if last:
+            for head in range(KV_HEADS):
+                one(head)
+                out_copy(head).start()
+            return
+
         @pl.loop(0, KV_HEADS // STEP_HEADS)
         def _(step):
             for index in range(STEP_HEADS):
-                head = step * STEP_HEADS + index
-                one(head)
-                if last:
-                    out_copy(head).start()
+                one(step * STEP_HEADS + index)
 
     near = tok * sum(piece[0] == 0 for piece in pieces)
     near = min(-(-near // dim) * dim, len(pieces) * tok)

time: 39.7 us -> 39.6 us (level)
  the two profiles are of different devices: /device:TPU:25 before, /device:TPU:0 now
where the time goes in v18:
time: 39.6 us; the launch traced here: 39.5 us
  Pallas kernels  14.1 us (36%)
  waiting for transfers between devices  13.4 us (34%)
  starting transfers between devices  11.7 us (30%)
    pallas_call x4, Pallas kernels, phase(): pl.pallas_call(functools.partial(attend_kernel, grid, sources, bool(state...  11.5 us
    ppermute x4, waiting for transfers between devices, z_forward(): return lax.ppermute(block, 'tp', pairs)  6.35 us
    ppermute x4, starting transfers between devices, y_swap(): lax.ppermute(block, 'tp', [(at, at ^ cores) for at in range(depth * width...  5.52 us
    ppermute x4, waiting for transfers between devices, y_swap(): lax.ppermute(block, 'tp', [(at, at ^ cores) for at in range(depth * width...  5.48 us
    ppermute x4, starting transfers between devices, z_forward(): return lax.ppermute(block, 'tp', pairs)  4.66 us
    pallas_call x1, Pallas kernels, fetch(): pl.pallas_call(kernel, out_shape=jax.ShapeDtypeStruct(array.shape, array....  1.6 us
    ppermute x8, waiting for transfers between devices, core_swap(): lax.ppermute(blocks, 'tp', [(at, at ^ 1) for at in range(depth * width *...  1.54 us
    ppermute x8, starting transfers between devices, core_swap(): lax.ppermute(blocks, 'tp', [(at, at ^ 1) for at in range(depth * width *...  1.53 us
  transfers between devices with their start and end apart: 16, of which 6 were waited for; matrix products, arithmetic and copies ran while one was open for 0% of the time, Pallas kernels for 31%

profile of v18, /device:TPU:0, one launch (start us, length us, event | category | flops | bytes accessed | tf_op | source)
XLA Modules:
  0.0 39.5 jit_solution(2326737666476240881)
XLA Ops:
  0.0 3.0 %collective-permute-start = (bf16[64,1024]{1,0:T(8,128)(2,1)}, bf16[64,1024]{1,0:T(8,128)(2,1)S(1)}, u32[]{:S(2)}, u32[]{:S(2)}) collective-permute-start(bf16[64,1024]{1,0:T(8,128)(2,1)} %refs_0_.1), channel_id=1, source_target_pairs={{0,4},{1,5},{2,6},{3,7},{4,8},{5,9},{6,10},{7,11},{8,12},{9,13},{1... | collective-permute-start | bytes 393224 | tf_op jit(solution)/shard_map/ppermute | solution.py:75
  3.0 1.6 %collective-permute-start.1 = (bf16[64,1024]{1,0:T(8,128)(2,1)}, bf16[64,1024]{1,0:T(8,128)(2,1)S(1)}, u32[]{:S(2)}, u32[]{:S(2)}) collective-permute-start(bf16[64,1024]{1,0:T(8,128)(2,1)} %refs_1_.1), channel_id=1, source_target_pairs={{0,4},{1,5},{2,6},{3,7},{4,8},{5,9},{6,10},{7,11},{8,12},{9,13},{1... | collective-permute-start | bytes 393224 | tf_op jit(solution)/shard_map/ppermute | solution.py:75
  4.6 1.0 %pack.3.refs_3_ = bf16[2,64,1024]{2,1,0:T(8,128)(2,1)S(1)} custom-call(bf16[64,1024]{1,0:T(8,128)(2,1)} %refs_0_.1, bf16[64,1024]{1,0:T(8,128)(2,1)} %refs_1_.1), custom_call_target="tpu_custom_call" | custom-call | tf_op jit(solution)/shard_map/pack/pallas_call | solution.py:41
  5.6 1.6 %collective-permute-start.4 = (bf16[2,64,1024]{2,1,0:T(8,128)(2,1)S(1)}, bf16[2,64,1024]{2,1,0:T(8,128)(2,1)S(1)}, u32[]{:S(2)}, u32[]{:S(2)}) collective-permute-start(bf16[2,64,1024]{2,1,0:T(8,128)(2,1)S(1)} %pack.3.refs_3_), channel_id=1, source_target_pairs={{0,2},{1,3},{2,0},{3,1},{4,6},{5,7},{6,4},{7,5},{8,10},{9,11},{10,... | collective-permute-start | bytes 786440 | tf_op jit(solution)/shard_map/ppermute | solution.py:80
  7.2 0.0 collective-permute-start.3
  7.2 1.6 %fetch.1.query_ref = bf16[64,16384]{1,0:T(8,128)(2,1)S(1)} custom-call(bf16[64,16384]{1,0:T(8,128)(2,1)} %array_ref.1), custom_call_target="tpu_custom_call" | custom-call | tf_op jit(solution)/shard_map/fetch/pallas_call | solution.py:57
  8.8 0.8 %collective-permute-done.refs_0_ = bf16[64,1024]{1,0:T(8,128)(2,1)S(1)} collective-permute-done((bf16[64,1024]{1,0:T(8,128)(2,1)}, bf16[64,1024]{1,0:T(8,128)(2,1)S(1)}, u32[]{:S(2)}, u32[]{:S(2)}) %collective-permute-start) | collective-permute-done | bytes 131104 | tf_op jit(solution)/shard_map/ppermute | solution.py:75
  9.6 2.0 %collective-permute-done.1.refs_1_ = bf16[64,1024]{1,0:T(8,128)(2,1)S(1)} collective-permute-done((bf16[64,1024]{1,0:T(8,128)(2,1)}, bf16[64,1024]{1,0:T(8,128)(2,1)S(1)}, u32[]{:S(2)}, u32[]{:S(2)}) %collective-permute-start.1) | collective-permute-done | bytes 131104 | tf_op jit(solution)/shard_map/ppermute | solution.py:75
  11.6 0.1 collective-permute-start.2
  11.7 1.6 %collective-permute-start.7 = (bf16[2,64,1024]{2,1,0:T(8,128)(2,1)S(1)}, bf16[2,64,1024]{2,1,0:T(8,128)(2,1)S(1)}, u32[]{:S(2)}, u32[]{:S(2)}) collective-permute-start(bf16[2,64,1024]{2,1,0:T(8,128)(2,1)S(1)} %pack.2.refs_0_), channel_id=1, source_target_pairs={{0,2},{1,3},{2,0},{3,1},{4,6},{5,7},{6,4},{7,5},{8,10},{9,11},{10,... | collective-permute-start | bytes 786440 | tf_op jit(solution)/shard_map/ppermute | solution.py:80
  13.2 0.0 collective-permute-start.6
  13.2 0.0 collective-permute-done.4.refs_2_
  13.2 0.5 %collective-permute-start.8 = (bf16[2,64,1024]{2,1,0:T(8,128)(2,1)S(1)}, bf16[2,64,1024]{2,1,0:T(8,128)(2,1)S(1)}, u32[]{:S(2)}, u32[]{:S(2)}) collective-permute-start(bf16[2,64,1024]{2,1,0:T(8,128)(2,1)S(1)} %collective-permute-done.4.refs_2_), channel_id=1, source_target_pairs={{0,1},{1,0},{2,3},{3,2},{4,5},{5,4},{6,7},{7,6},{8,9},{9,8},{10,11... | collective-permute-start | bytes 786440 | tf_op jit(solution)/shard_map/ppermute | solution.py:87
  13.8 0.0 collective-permute-done.3.refs_1_
  13.8 3.7 %attend.3 = (f32[8,1024,256]{2,1,0:T(8,128)S(1)}, f32[8,1024,128]{2,1,0:T(8,128)S(1)}) custom-call(bf16[64,16384]{1,0:T(8,128)(2,1)S(1)} %fetch.1.query_ref, bf16[2,64,1024]{2,1,0:T(8,128)(2,1)S(1)} %pack.2.refs_0_, bf16[2,64,1024]{2,1,0:T(8,128)(2,1)S(1)} %collective-permute-done.3.refs_1_, bf16[2,64,1024]{2,1,0:T(8,128)(2,1)S(1)} %collective-permute-done.4.refs_2_, ...), custom_call_target="tpu_custom_call" | custom-call | flops 1000 | bytes 1000 | tf_op jit(solution)/shard_map/attend/pallas_call | solution.py:290
  17.4 3.5 %collective-permute-done.2.refs_0_ = bf16[2,64,1024]{2,1,0:T(8,128)(2,1)S(1)} collective-permute-done((bf16[2,64,1024]{2,1,0:T(8,128)(2,1)S(1)}, bf16[2,64,1024]{2,1,0:T(8,128)(2,1)S(1)}, u32[]{:S(2)}, u32[]{:S(2)}) %collective-permute-start.2) | collective-permute-done | bytes 262176 | tf_op jit(solution)/shard_map/ppermute | solution.py:75
  20.9 0.0 collective-permute-start.5
  20.9 1.3 %collective-permute-start.12 = (bf16[2,64,1024]{2,1,0:T(8,128)(2,1)S(1)}, bf16[2,64,1024]{2,1,0:T(8,128)(2,1)S(1)}, u32[]{:S(2)}, u32[]{:S(2)}) collective-permute-start(bf16[2,64,1024]{2,1,0:T(8,128)(2,1)S(1)} %collective-permute-done.2.refs_0_), channel_id=1, source_target_pairs={{0,2},{1,3},{2,0},{3,1},{4,6},{5,7},{6,4},{7,5},{8,10},{9,11},{10,... | collective-permute-start | bytes 786440 | tf_op jit(solution)/shard_map/ppermute | solution.py:80
  22.2 0.0 collective-permute-done.7.refs_2_
  22.2 0.0 collective-permute-start.11
  22.2 0.0 collective-permute-done.6.refs_1_
  22.2 0.5 %collective-permute-start.13 = (bf16[2,64,1024]{2,1,0:T(8,128)(2,1)S(1)}, bf16[2,64,1024]{2,1,0:T(8,128)(2,1)S(1)}, u32[]{:S(2)}, u32[]{:S(2)}) collective-permute-start(bf16[2,64,1024]{2,1,0:T(8,128)(2,1)S(1)} %collective-permute-done.7.refs_2_), channel_id=1, source_target_pairs={{0,1},{1,0},{2,3},{3,2},{4,5},{5,4},{6,7},{7,6},{8,9},{9,8},{10,11... | collective-permute-start | bytes 786440 | tf_op jit(solution)/shard_map/ppermute | solution.py:87
  22.7 0.0 collective-permute-done.8.refs_3_
  22.7 4.7 %attend.4 = (f32[8,1024,256]{2,1,0:T(8,128)S(1)}, f32[8,1024,128]{2,1,0:T(8,128)S(1)}) custom-call(bf16[64,16384]{1,0:T(8,128)(2,1)S(1)} %fetch.1.query_ref, bf16[2,64,1024]{2,1,0:T(8,128)(2,1)S(1)} %collective-permute-done.2.refs_0_, bf16[2,64,1024]{2,1,0:T(8,128)(2,1)S(1)} %collective-permute-done.6.refs_1_, ...), custom_call_target="tpu_custom_call", output_to_operand_aliasing={{0}: (5, {}), {1}: (6, {})} | custom-call | flops 1000 | bytes 1000 | tf_op jit(solution)/shard_map/attend/pallas_call | solution.py:290
  27.4 0.1 collective-permute-done.5.refs_0_
  27.5 1.1 %collective-permute-start.10 = (bf16[2,64,1024]{2,1,0:T(8,128)(2,1)S(1)}, bf16[2,64,1024]{2,1,0:T(8,128)(2,1)S(1)}, u32[]{:S(2)}, u32[]{:S(2)}) collective-permute-start(bf16[2,64,1024]{2,1,0:T(8,128)(2,1)S(1)} %collective-permute-done.5.refs_0_), channel_id=1, source_target_pairs={{0,2},{1,3},{2,0},{3,1},{4,6},{5,7},{6,4},{7,5},{8,10},{9,11},{10,... | collective-permute-start | bytes 786440 | tf_op jit(solution)/shard_map/ppermute | solution.py:80
  28.6 0.5 %collective-permute-start.14 = (bf16[2,64,1024]{2,1,0:T(8,128)(2,1)S(1)}, bf16[2,64,1024]{2,1,0:T(8,128)(2,1)S(1)}, u32[]{:S(2)}, u32[]{:S(2)}) collective-permute-start(bf16[2,64,1024]{2,1,0:T(8,128)(2,1)S(1)} %collective-permute-done.12.refs_2_), channel_id=1, source_target_pairs={{0,1},{1,0},{2,3},{3,2},{4,5},{5,4},{6,7},{7,6},{8,9},{9,8},{10,11... | collective-permute-start | bytes 786440 | tf_op jit(solution)/shard_map/ppermute | solution.py:87
  29.1 0.0 collective-permute-done.13.refs_3_
  29.1 1.2 %attend.5 = (f32[8,1024,256]{2,1,0:T(8,128)S(1)}, f32[8,1024,128]{2,1,0:T(8,128)S(1)}) custom-call(bf16[64,16384]{1,0:T(8,128)(2,1)S(1)} %fetch.1.query_ref, bf16[2,64,1024]{2,1,0:T(8,128)(2,1)S(1)} %collective-permute-done.5.refs_0_, bf16[2,64,1024]{2,1,0:T(8,128)(2,1)S(1)} %collective-permute-done.11.refs_1_, ...), custom_call_target="tpu_custom_call", output_to_operand_aliasing={{0}: (5, {}), {1}: (6, {})} | custom-call | flops 1000 | bytes 1000 | tf_op jit(solution)/shard_map/attend/pallas_call | solution.py:290
  30.3 5.5 %collective-permute-done.10.refs_1_ = bf16[2,64,1024]{2,1,0:T(8,128)(2,1)S(1)} collective-permute-done((bf16[2,64,1024]{2,1,0:T(8,128)(2,1)S(1)}, bf16[2,64,1024]{2,1,0:T(8,128)(2,1)S(1)}, u32[]{:S(2)}, u32[]{:S(2)}) %collective-permute-start.10) | collective-permute-done | bytes 262176 | tf_op jit(solution)/shard_map/ppermute | solution.py:80
  35.8 1.5 %collective-permute-done.15.refs_3_ = bf16[2,64,1024]{2,1,0:T(8,128)(2,1)S(1)} collective-permute-done((bf16[2,64,1024]{2,1,0:T(8,128)(2,1)S(1)}, bf16[2,64,1024]{2,1,0:T(8,128)(2,1)S(1)}, u32[]{:S(2)}, u32[]{:S(2)}) %collective-permute-start.15) | collective-permute-done | bytes 262176 | tf_op jit(solution)/shard_map/ppermute | solution.py:87
  37.3 2.0 %attend_last.1 = bf16[64,16384]{1,0:T(8,128)(2,1)} custom-call(bf16[64,16384]{1,0:T(8,128)(2,1)S(1)} %fetch.1.query_ref, bf16[2,64,1024]{2,1,0:T(8,128)(2,1)S(1)} %collective-permute-done.9.refs_0_, bf16[2,64,1024]{2,1,0:T(8,128)(2,1)S(1)} %collective-permute-done.10.refs_1_, bf16[2,64,1024]{2,1,0:T(8,128)(2,1)S(1)} %collective-permute-done.14.refs_2_, ...), custom_call_target="tpu_custom_call" | custom-call | flops 1000 | bytes 1000 | tf_op jit(solution)/shard_map/attend_last/pallas_call | solution.py:290
  (7 shorter events, 0.0 us)
Async XLA Ops:
  0.0 9.6 %collective-permute-start = (bf16[64,1024]{1,0:T(8,128)(2,1)}, bf16[64,1024]{1,0:T(8,128)(2,1)S(1)}, u32[]{:S(2)}, u32[]{:S(2)}) collective-permute-start(bf16[64,1024]{1,0:T(8,128)(2,1)} %refs_0_.1), channel_id=1, source_target_pairs={{0,4},{1,5},{2,6},{3,7},{4,8},{5,9},{6,10},{7,11},{8,12},{9,13},{1... | collective-permute-start | bytes 393224 | tf_op jit(solution)/shard_map/ppermute | solution.py:75
  3.0 8.5 %collective-permute-start.1 = (bf16[64,1024]{1,0:T(8,128)(2,1)}, bf16[64,1024]{1,0:T(8,128)(2,1)S(1)}, u32[]{:S(2)}, u32[]{:S(2)}) collective-permute-start(bf16[64,1024]{1,0:T(8,128)(2,1)} %refs_1_.1), channel_id=1, source_target_pairs={{0,4},{1,5},{2,6},{3,7},{4,8},{5,9},{6,10},{7,11},{8,12},{9,13},{1... | collective-permute-start | bytes 393224 | tf_op jit(solution)/shard_map/ppermute | solution.py:75
  5.6 7.6 %collective-permute-start.4 = (bf16[2,64,1024]{2,1,0:T(8,128)(2,1)S(1)}, bf16[2,64,1024]{2,1,0:T(8,128)(2,1)S(1)}, u32[]{:S(2)}, u32[]{:S(2)}) collective-permute-start(bf16[2,64,1024]{2,1,0:T(8,128)(2,1)S(1)} %pack.3.refs_3_), channel_id=1, source_target_pairs={{0,2},{1,3},{2,0},{3,1},{4,6},{5,7},{6,4},{7,5},{8,10},{9,11},{10,... | collective-permute-start | bytes 786440 | tf_op jit(solution)/shard_map/ppermute | solution.py:80
  7.2 6.6 %collective-permute-start.3 = (bf16[2,64,1024]{2,1,0:T(8,128)(2,1)S(1)}, bf16[2,64,1024]{2,1,0:T(8,128)(2,1)S(1)}, u32[]{:S(2)}, u32[]{:S(2)}) collective-permute-start(bf16[2,64,1024]{2,1,0:T(8,128)(2,1)S(1)} %pack.3.refs_3_), channel_id=1, source_target_pairs={{0,1},{1,0},{2,3},{3,2},{4,5},{5,4},{6,7},{7,6},{8,9},{9,8},{10,11... | collective-permute-start | bytes 786440 | tf_op jit(solution)/shard_map/ppermute | solution.py:87
  11.6 9.3 %collective-permute-start.2 = (bf16[2,64,1024]{2,1,0:T(8,128)(2,1)S(1)}, bf16[2,64,1024]{2,1,0:T(8,128)(2,1)S(1)}, u32[]{:S(2)}, u32[]{:S(2)}) collective-permute-start(bf16[2,64,1024]{2,1,0:T(8,128)(2,1)S(1)} %pack.2.refs_0_), channel_id=1, source_target_pairs={{0,4},{1,5},{2,6},{3,7},{4,8},{5,9},{6,10},{7,11},{8,12},{9,13},{1... | collective-permute-start | bytes 786440 | tf_op jit(solution)/shard_map/ppermute | solution.py:75
  11.7 10.6 %collective-permute-start.7 = (bf16[2,64,1024]{2,1,0:T(8,128)(2,1)S(1)}, bf16[2,64,1024]{2,1,0:T(8,128)(2,1)S(1)}, u32[]{:S(2)}, u32[]{:S(2)}) collective-permute-start(bf16[2,64,1024]{2,1,0:T(8,128)(2,1)S(1)} %pack.2.refs_0_), channel_id=1, source_target_pairs={{0,2},{1,3},{2,0},{3,1},{4,6},{5,7},{6,4},{7,5},{8,10},{9,11},{10,... | collective-permute-start | bytes 786440 | tf_op jit(solution)/shard_map/ppermute | solution.py:80
  13.2 9.0 %collective-permute-start.6 = (bf16[2,64,1024]{2,1,0:T(8,128)(2,1)S(1)}, bf16[2,64,1024]{2,1,0:T(8,128)(2,1)S(1)}, u32[]{:S(2)}, u32[]{:S(2)}) collective-permute-start(bf16[2,64,1024]{2,1,0:T(8,128)(2,1)S(1)} %pack.2.refs_0_), channel_id=1, source_target_pairs={{0,1},{1,0},{2,3},{3,2},{4,5},{5,4},{6,7},{7,6},{8,9},{9,8},{10,11... | collective-permute-start | bytes 786440 | tf_op jit(solution)/shard_map/ppermute | solution.py:87
  13.2 9.5 %collective-permute-start.8 = (bf16[2,64,1024]{2,1,0:T(8,128)(2,1)S(1)}, bf16[2,64,1024]{2,1,0:T(8,128)(2,1)S(1)}, u32[]{:S(2)}, u32[]{:S(2)}) collective-permute-start(bf16[2,64,1024]{2,1,0:T(8,128)(2,1)S(1)} %collective-permute-done.4.refs_2_), channel_id=1, source_target_pairs={{0,1},{1,0},{2,3},{3,2},{4,5},{5,4},{6,7},{7,6},{8,9},{9,8},{10,11... | collective-permute-start | bytes 786440 | tf_op jit(solution)/shard_map/ppermute | solution.py:87
  20.9 6.6 %collective-permute-start.5 = (bf16[2,64,1024]{2,1,0:T(8,128)(2,1)S(1)}, bf16[2,64,1024]{2,1,0:T(8,128)(2,1)S(1)}, u32[]{:S(2)}, u32[]{:S(2)}) collective-permute-start(bf16[2,64,1024]{2,1,0:T(8,128)(2,1)S(1)} %collective-permute-done.2.refs_0_), channel_id=1, source_target_pairs={{0,4},{1,5},{2,6},{3,7},{4,0},{5,1},{6,2},{7,3},{8,12},{9,13},{10,... | collective-permute-start | bytes 786440 | tf_op jit(solution)/shard_map/ppermute | solution.py:75
  20.9 7.6 %collective-permute-start.12 = (bf16[2,64,1024]{2,1,0:T(8,128)(2,1)S(1)}, bf16[2,64,1024]{2,1,0:T(8,128)(2,1)S(1)}, u32[]{:S(2)}, u32[]{:S(2)}) collective-permute-start(bf16[2,64,1024]{2,1,0:T(8,128)(2,1)S(1)} %collective-permute-done.2.refs_0_), channel_id=1, source_target_pairs={{0,2},{1,3},{2,0},{3,1},{4,6},{5,7},{6,4},{7,5},{8,10},{9,11},{10,... | collective-permute-start | bytes 786440 | tf_op jit(solution)/shard_map/ppermute | solution.py:80
  22.2 6.9 %collective-permute-start.11 = (bf16[2,64,1024]{2,1,0:T(8,128)(2,1)S(1)}, bf16[2,64,1024]{2,1,0:T(8,128)(2,1)S(1)}, u32[]{:S(2)}, u32[]{:S(2)}) collective-permute-start(bf16[2,64,1024]{2,1,0:T(8,128)(2,1)S(1)} %collective-permute-done.2.refs_0_), channel_id=1, source_target_pairs={{0,1},{1,0},{2,3},{3,2},{4,5},{5,4},{6,7},{7,6},{8,9},{9,8},{10,11... | collective-permute-start | bytes 786440 | tf_op jit(solution)/shard_map/ppermute | solution.py:87
  22.2 6.9 %collective-permute-start.13 = (bf16[2,64,1024]{2,1,0:T(8,128)(2,1)S(1)}, bf16[2,64,1024]{2,1,0:T(8,128)(2,1)S(1)}, u32[]{:S(2)}, u32[]{:S(2)}) collective-permute-start(bf16[2,64,1024]{2,1,0:T(8,128)(2,1)S(1)} %collective-permute-done.7.refs_2_), channel_id=1, source_target_pairs={{0,1},{1,0},{2,3},{3,2},{4,5},{5,4},{6,7},{7,6},{8,9},{9,8},{10,11... | collective-permute-start | bytes 786440 | tf_op jit(solution)/shard_map/ppermute | solution.py:87
  27.5 8.3 %collective-permute-start.10 = (bf16[2,64,1024]{2,1,0:T(8,128)(2,1)S(1)}, bf16[2,64,1024]{2,1,0:T(8,128)(2,1)S(1)}, u32[]{:S(2)}, u32[]{:S(2)}) collective-permute-start(bf16[2,64,1024]{2,1,0:T(8,128)(2,1)S(1)} %collective-permute-done.5.refs_0_), channel_id=1, source_target_pairs={{0,2},{1,3},{2,0},{3,1},{4,6},{5,7},{6,4},{7,5},{8,10},{9,11},{10,... | collective-permute-start | bytes 786440 | tf_op jit(solution)/shard_map/ppermute | solution.py:80
  28.6 7.2 %collective-permute-start.9 = (bf16[2,64,1024]{2,1,0:T(8,128)(2,1)S(1)}, bf16[2,64,1024]{2,1,0:T(8,128)(2,1)S(1)}, u32[]{:S(2)}, u32[]{:S(2)}) collective-permute-start(bf16[2,64,1024]{2,1,0:T(8,128)(2,1)S(1)} %collective-permute-done.5.refs_0_), channel_id=1, source_target_pairs={{0,1},{1,0},{2,3},{3,2},{4,5},{5,4},{6,7},{7,6},{8,9},{9,8},{10,11... | collective-permute-start | bytes 786440 | tf_op jit(solution)/shard_map/ppermute | solution.py:87
  28.6 7.2 %collective-permute-start.14 = (bf16[2,64,1024]{2,1,0:T(8,128)(2,1)S(1)}, bf16[2,64,1024]{2,1,0:T(8,128)(2,1)S(1)}, u32[]{:S(2)}, u32[]{:S(2)}) collective-permute-start(bf16[2,64,1024]{2,1,0:T(8,128)(2,1)S(1)} %collective-permute-done.12.refs_2_), channel_id=1, source_target_pairs={{0,1},{1,0},{2,3},{3,2},{4,5},{5,4},{6,7},{7,6},{8,9},{9,8},{10,11... | collective-permute-start | bytes 786440 | tf_op jit(solution)/shard_map/ppermute | solution.py:87
  35.8 1.5 %collective-permute-start.15 = (bf16[2,64,1024]{2,1,0:T(8,128)(2,1)S(1)}, bf16[2,64,1024]{2,1,0:T(8,128)(2,1)S(1)}, u32[]{:S(2)}, u32[]{:S(2)}) collective-permute-start(bf16[2,64,1024]{2,1,0:T(8,128)(2,1)S(1)} %collective-permute-done.10.refs_1_), channel_id=1, source_target_pairs={{0,1},{1,0},{2,3},{3,2},{4,5},{5,4},{6,7},{7,6},{8,9},{9,8},{10,11... | collective-permute-start | bytes 786440 | tf_op jit(solution)/shard_map/ppermute | solution.py:87

commit v19 on v18

--- a/solution.py
+++ b/solution.py
@@ -65,14 +65,24 @@
     )(array)
 
 
-def z_forward(block, grid, dz):
+def z_forward(block, grid, dz, groups):
     depth, width, cores = grid
     side = width * cores
+    count = depth * side
     pairs = []
-    for z in range(depth):
-        target = z ^ 1 if dz == depth - 1 and depth % 2 == 0 else (z + 1) % depth
-        pairs += [(z * side + at, target * side + at) for at in range(side)]
-    return lax.ppermute(block, "tp", pairs)
+    for group in range(groups):
+        for at in range(count):
+            z, place_in = divmod(at, side)
+            target_group = group
+            if dz == depth - 1 and depth % 2 == 0:
+                target = z ^ 1
+            elif groups % 2 or z >= dz - 1:
+                lowest = 0 if groups % 2 else dz - 1
+                target = z + 1 if z + 1 < depth else lowest
+            else:
+                target, target_group = z, group ^ 1
+            pairs.append((group * count + at, target_group * count + target * side + place_in))
+    return lax.ppermute(block, ("groups", "tp"), pairs)
 
 
 def y_swap(block, grid):
@@ -251,6 +261,7 @@
 def solution(mesh):
     grid = chip_grid(mesh.shape["tp"])
     depth, width, cores = grid
+    groups = mesh.shape["groups"]
     assert cores == 2 and depth > 2
 
     def body(query_rows, key_rows, value_rows):
@@ -319,9 +330,9 @@
         for dz in range(depth):
             block = arrays[f"z{dz}"]
             if dz == 0:
-                parts = [z_forward(array, grid, 1) for array in (key_rows, value_rows)]
+                parts = [z_forward(array, grid, 1, groups) for array in (key_rows, value_rows)]
             elif dz + 1 < depth:
-                keep(f"z{dz + 1}", z_forward(block, grid, dz + 1), [(dz + 1, 0, 0)])
+                keep(f"z{dz + 1}", z_forward(block, grid, dz + 1, groups), [(dz + 1, 0, 0)])
             if width == 2:
                 keep(f"y{dz}", y_swap(block, grid), [(dz, 1, 0)])
             if dz and all(place in found for place in batches[0]):

time: 39.6 us -> 39.2 us (0.990)
  the two profiles are of different devices: /device:TPU:0 before, /device:TPU:17 now
where the time goes in v19:
time: 39.2 us; the launch traced here: 39.1 us
  Pallas kernels  20.6 us (53%)
  starting transfers between devices  15.4 us (39%)
  waiting for transfers between devices  2.89 us (7%)
    pallas_call x4, Pallas kernels, phase(): pl.pallas_call(functools.partial(attend_kernel, grid, sources, bool(state...  18 us
    ppermute x8, starting transfers between devices, core_swap(): lax.ppermute(blocks, 'tp', [(at, at ^ 1) for at in range(depth * width *...  8.03 us
    ppermute x4, starting transfers between devices, y_swap(): lax.ppermute(block, 'tp', [(at, at ^ cores) for at in range(depth * width...  4.39 us
    ppermute x4, starting transfers between devices, z_forward(): return lax.ppermute(block, ('groups', 'tp'), pairs)  2.94 us
    pallas_call x1, Pallas kernels, fetch(): pl.pallas_call(kernel, out_shape=jax.ShapeDtypeStruct(array.shape, array....  1.6 us
    ppermute x8, waiting for transfers between devices, core_swap(): lax.ppermute(blocks, 'tp', [(at, at ^ 1) for at in range(depth * width *...  1.17 us
    pallas_call x2, Pallas kernels, stack(): pl.pallas_call(kernel, out_shape=jax.ShapeDtypeStruct((count, *arrays[0]....  1.01 us
    ppermute x4, waiting for transfers between devices, y_swap(): lax.ppermute(block, 'tp', [(at, at ^ cores) for at in range(depth * width...  1 us
  transfers between devices with their start and end apart: 16, of which 3 were waited for; matrix products, arithmetic and copies ran while one was open for 0% of the time, Pallas kernels for 39%

profile of v19, /device:TPU:17, one launch (start us, length us, event | category | flops | bytes accessed | tf_op | source)
XLA Modules:
  0.0 39.1 jit_solution(14056535573629103257)
XLA Ops:
  0.0 1.3 %collective-permute-start = (bf16[64,1024]{1,0:T(8,128)(2,1)}, bf16[64,1024]{1,0:T(8,128)(2,1)S(1)}, u32[]{:S(2)}, u32[]{:S(2)}) collective-permute-start(bf16[64,1024]{1,0:T(8,128)(2,1)} %refs_0_.1), channel_id=1, source_target_pairs={{0,4},{1,5},{2,6},{3,7},{4,8},{5,9},{6,10},{7,11},{8,12},{9,13},{1... | collective-permute-start | bytes 393224 | tf_op jit(solution)/shard_map/ppermute | solution.py:85
  1.3 0.0 collective-permute-start.1
  1.3 1.0 %pack.3.refs_3_ = bf16[2,64,1024]{2,1,0:T(8,128)(2,1)S(1)} custom-call(bf16[64,1024]{1,0:T(8,128)(2,1)} %refs_0_.1, bf16[64,1024]{1,0:T(8,128)(2,1)} %refs_1_.1), custom_call_target="tpu_custom_call" | custom-call | tf_op jit(solution)/shard_map/pack/pallas_call | solution.py:41
  2.3 1.3 %collective-permute-start.4 = (bf16[2,64,1024]{2,1,0:T(8,128)(2,1)S(1)}, bf16[2,64,1024]{2,1,0:T(8,128)(2,1)S(1)}, u32[]{:S(2)}, u32[]{:S(2)}) collective-permute-start(bf16[2,64,1024]{2,1,0:T(8,128)(2,1)S(1)} %pack.3.refs_3_), channel_id=1, source_target_pairs={{0,2},{1,3},{2,0},{3,1},{4,6},{5,7},{6,4},{7,5},{8,10},{9,11},{10,... | collective-permute-start | bytes 786440 | tf_op jit(solution)/shard_map/ppermute | solution.py:90
  3.6 1.4 %collective-permute-start.3 = (bf16[2,64,1024]{2,1,0:T(8,128)(2,1)S(1)}, bf16[2,64,1024]{2,1,0:T(8,128)(2,1)S(1)}, u32[]{:S(2)}, u32[]{:S(2)}) collective-permute-start(bf16[2,64,1024]{2,1,0:T(8,128)(2,1)S(1)} %pack.3.refs_3_), channel_id=1, source_target_pairs={{0,1},{1,0},{2,3},{3,2},{4,5},{5,4},{6,7},{7,6},{8,9},{9,8},{10,11... | collective-permute-start | bytes 786440 | tf_op jit(solution)/shard_map/ppermute | solution.py:97
  5.1 1.6 %fetch.1.query_ref = bf16[64,16384]{1,0:T(8,128)(2,1)S(1)} custom-call(bf16[64,16384]{1,0:T(8,128)(2,1)} %array_ref.1), custom_call_target="tpu_custom_call" | custom-call | tf_op jit(solution)/shard_map/fetch/pallas_call | solution.py:57
  6.7 0.0 collective-permute-done.refs_0_
  6.7 0.7 %collective-permute-done.1.refs_1_ = bf16[64,1024]{1,0:T(8,128)(2,1)S(1)} collective-permute-done((bf16[64,1024]{1,0:T(8,128)(2,1)}, bf16[64,1024]{1,0:T(8,128)(2,1)S(1)}, u32[]{:S(2)}, u32[]{:S(2)}) %collective-permute-start.1) | collective-permute-done | bytes 131104 | tf_op jit(solution)/shard_map/ppermute | solution.py:85
  7.4 1.3 %collective-permute-start.2 = (bf16[2,64,1024]{2,1,0:T(8,128)(2,1)S(1)}, bf16[2,64,1024]{2,1,0:T(8,128)(2,1)S(1)}, u32[]{:S(2)}, u32[]{:S(2)}) collective-permute-start(bf16[2,64,1024]{2,1,0:T(8,128)(2,1)S(1)} %pack.2.refs_0_), channel_id=1, source_target_pairs={{0,16},{1,17},{2,18},{3,19},{4,8},{5,9},{6,10},{7,11},{8,12},{9,13... | collective-permute-start | bytes 786440 | tf_op jit(solution)/shard_map/ppermute | solution.py:85
  8.8 1.2 %collective-permute-start.7 = (bf16[2,64,1024]{2,1,0:T(8,128)(2,1)S(1)}, bf16[2,64,1024]{2,1,0:T(8,128)(2,1)S(1)}, u32[]{:S(2)}, u32[]{:S(2)}) collective-permute-start(bf16[2,64,1024]{2,1,0:T(8,128)(2,1)S(1)} %pack.2.refs_0_), channel_id=1, source_target_pairs={{0,2},{1,3},{2,0},{3,1},{4,6},{5,7},{6,4},{7,5},{8,10},{9,11},{10,... | collective-permute-start | bytes 786440 | tf_op jit(solution)/shard_map/ppermute | solution.py:90
  10.0 2.1 %collective-permute-start.6 = (bf16[2,64,1024]{2,1,0:T(8,128)(2,1)S(1)}, bf16[2,64,1024]{2,1,0:T(8,128)(2,1)S(1)}, u32[]{:S(2)}, u32[]{:S(2)}) collective-permute-start(bf16[2,64,1024]{2,1,0:T(8,128)(2,1)S(1)} %pack.2.refs_0_), channel_id=1, source_target_pairs={{0,1},{1,0},{2,3},{3,2},{4,5},{5,4},{6,7},{7,6},{8,9},{9,8},{10,11... | collective-permute-start | bytes 786440 | tf_op jit(solution)/shard_map/ppermute | solution.py:97
  12.1 0.0 collective-permute-done.4.refs_2_
  12.1 0.0 collective-permute-start.8
  12.1 0.0 collective-permute-done.3.refs_1_
  12.1 3.7 %attend.3 = (f32[8,1024,256]{2,1,0:T(8,128)S(1)}, f32[8,1024,128]{2,1,0:T(8,128)S(1)}) custom-call(bf16[64,16384]{1,0:T(8,128)(2,1)S(1)} %fetch.1.query_ref, bf16[2,64,1024]{2,1,0:T(8,128)(2,1)S(1)} %pack.2.refs_0_, bf16[2,64,1024]{2,1,0:T(8,128)(2,1)S(1)} %collective-permute-done.3.refs_1_, bf16[2,64,1024]{2,1,0:T(8,128)(2,1)S(1)} %collective-permute-done.4.refs_2_, ...), custom_call_target="tpu_custom_call" | custom-call | flops 1000 | bytes 1000 | tf_op jit(solution)/shard_map/attend/pallas_call | solution.py:301
  15.8 0.3 collective-permute-start.5
  16.1 1.6 %collective-permute-start.12 = (bf16[2,64,1024]{2,1,0:T(8,128)(2,1)S(1)}, bf16[2,64,1024]{2,1,0:T(8,128)(2,1)S(1)}, u32[]{:S(2)}, u32[]{:S(2)}) collective-permute-start(bf16[2,64,1024]{2,1,0:T(8,128)(2,1)S(1)} %collective-permute-done.2.refs_0_), channel_id=1, source_target_pairs={{0,2},{1,3},{2,0},{3,1},{4,6},{5,7},{6,4},{7,5},{8,10},{9,11},{10,... | collective-permute-start | bytes 786440 | tf_op jit(solution)/shard_map/ppermute | solution.py:90
  17.6 0.0 collective-permute-done.7.refs_2_
  17.6 1.6 %collective-permute-start.11 = (bf16[2,64,1024]{2,1,0:T(8,128)(2,1)S(1)}, bf16[2,64,1024]{2,1,0:T(8,128)(2,1)S(1)}, u32[]{:S(2)}, u32[]{:S(2)}) collective-permute-start(bf16[2,64,1024]{2,1,0:T(8,128)(2,1)S(1)} %collective-permute-done.2.refs_0_), channel_id=1, source_target_pairs={{0,1},{1,0},{2,3},{3,2},{4,5},{5,4},{6,7},{7,6},{8,9},{9,8},{10,11... | collective-permute-start | bytes 786440 | tf_op jit(solution)/shard_map/ppermute | solution.py:97
  19.3 0.1 collective-permute-start.13
  19.4 4.4 %attend.4 = (f32[8,1024,256]{2,1,0:T(8,128)S(1)}, f32[8,1024,128]{2,1,0:T(8,128)S(1)}) custom-call(bf16[64,16384]{1,0:T(8,128)(2,1)S(1)} %fetch.1.query_ref, bf16[2,64,1024]{2,1,0:T(8,128)(2,1)S(1)} %collective-permute-done.2.refs_0_, bf16[2,64,1024]{2,1,0:T(8,128)(2,1)S(1)} %collective-permute-done.6.refs_1_, ...), custom_call_target="tpu_custom_call", output_to_operand_aliasing={{0}: (5, {}), {1}: (6, {})} | custom-call | flops 1000 | bytes 1000 | tf_op jit(solution)/shard_map/attend/pallas_call | solution.py:301
  23.8 0.3 collective-permute-start.10
  24.1 1.1 %collective-permute-start.9 = (bf16[2,64,1024]{2,1,0:T(8,128)(2,1)S(1)}, bf16[2,64,1024]{2,1,0:T(8,128)(2,1)S(1)}, u32[]{:S(2)}, u32[]{:S(2)}) collective-permute-start(bf16[2,64,1024]{2,1,0:T(8,128)(2,1)S(1)} %collective-permute-done.5.refs_0_), channel_id=1, source_target_pairs={{0,1},{1,0},{2,3},{3,2},{4,5},{5,4},{6,7},{7,6},{8,9},{9,8},{10,11... | collective-permute-start | bytes 786440 | tf_op jit(solution)/shard_map/ppermute | solution.py:97
  25.2 0.0 collective-permute-done.12.refs_2_
  25.2 0.0 collective-permute-start.14
  25.2 0.0 collective-permute-done.13.refs_3_
  25.2 4.7 %attend.5 = (f32[8,1024,256]{2,1,0:T(8,128)S(1)}, f32[8,1024,128]{2,1,0:T(8,128)S(1)}) custom-call(bf16[64,16384]{1,0:T(8,128)(2,1)S(1)} %fetch.1.query_ref, bf16[2,64,1024]{2,1,0:T(8,128)(2,1)S(1)} %collective-permute-done.5.refs_0_, bf16[2,64,1024]{2,1,0:T(8,128)(2,1)S(1)} %collective-permute-done.11.refs_1_, ...), custom_call_target="tpu_custom_call", output_to_operand_aliasing={{0}: (5, {}), {1}: (6, {})} | custom-call | flops 1000 | bytes 1000 | tf_op jit(solution)/shard_map/attend/pallas_call | solution.py:301
  29.9 1.0 %collective-permute-done.10.refs_1_ = bf16[2,64,1024]{2,1,0:T(8,128)(2,1)S(1)} collective-permute-done((bf16[2,64,1024]{2,1,0:T(8,128)(2,1)S(1)}, bf16[2,64,1024]{2,1,0:T(8,128)(2,1)S(1)}, u32[]{:S(2)}, u32[]{:S(2)}) %collective-permute-start.10) | collective-permute-done | bytes 262176 | tf_op jit(solution)/shard_map/ppermute | solution.py:90
  30.9 1.7 %collective-permute-start.15 = (bf16[2,64,1024]{2,1,0:T(8,128)(2,1)S(1)}, bf16[2,64,1024]{2,1,0:T(8,128)(2,1)S(1)}, u32[]{:S(2)}, u32[]{:S(2)}) collective-permute-start(bf16[2,64,1024]{2,1,0:T(8,128)(2,1)S(1)} %collective-permute-done.10.refs_1_), channel_id=1, source_target_pairs={{0,1},{1,0},{2,3},{3,2},{4,5},{5,4},{6,7},{7,6},{8,9},{9,8},{10,11... | collective-permute-start | bytes 786440 | tf_op jit(solution)/shard_map/ppermute | solution.py:97
  32.6 0.0 collective-permute-done.14.refs_2_
  32.6 1.2 %collective-permute-done.15.refs_3_ = bf16[2,64,1024]{2,1,0:T(8,128)(2,1)S(1)} collective-permute-done((bf16[2,64,1024]{2,1,0:T(8,128)(2,1)S(1)}, bf16[2,64,1024]{2,1,0:T(8,128)(2,1)S(1)}, u32[]{:S(2)}, u32[]{:S(2)}) %collective-permute-start.15) | collective-permute-done | bytes 262176 | tf_op jit(solution)/shard_map/ppermute | solution.py:97
  33.7 5.2 %attend_last.1 = bf16[64,16384]{1,0:T(8,128)(2,1)} custom-call(bf16[64,16384]{1,0:T(8,128)(2,1)S(1)} %fetch.1.query_ref, bf16[2,64,1024]{2,1,0:T(8,128)(2,1)S(1)} %collective-permute-done.9.refs_0_, bf16[2,64,1024]{2,1,0:T(8,128)(2,1)S(1)} %collective-permute-done.10.refs_1_, bf16[2,64,1024]{2,1,0:T(8,128)(2,1)S(1)} %collective-permute-done.14.refs_2_, ...), custom_call_target="tpu_custom_call" | custom-call | flops 1000 | bytes 1000 | tf_op jit(solution)/shard_map/attend_last/pallas_call | solution.py:301
  (7 shorter events, 0.0 us)
Async XLA Ops:
  0.0 6.7 %collective-permute-start = (bf16[64,1024]{1,0:T(8,128)(2,1)}, bf16[64,1024]{1,0:T(8,128)(2,1)S(1)}, u32[]{:S(2)}, u32[]{:S(2)}) collective-permute-start(bf16[64,1024]{1,0:T(8,128)(2,1)} %refs_0_.1), channel_id=1, source_target_pairs={{0,4},{1,5},{2,6},{3,7},{4,8},{5,9},{6,10},{7,11},{8,12},{9,13},{1... | collective-permute-start | bytes 393224 | tf_op jit(solution)/shard_map/ppermute | solution.py:85
  1.3 6.1 %collective-permute-start.1 = (bf16[64,1024]{1,0:T(8,128)(2,1)}, bf16[64,1024]{1,0:T(8,128)(2,1)S(1)}, u32[]{:S(2)}, u32[]{:S(2)}) collective-permute-start(bf16[64,1024]{1,0:T(8,128)(2,1)} %refs_1_.1), channel_id=1, source_target_pairs={{0,4},{1,5},{2,6},{3,7},{4,8},{5,9},{6,10},{7,11},{8,12},{9,13},{1... | collective-permute-start | bytes 393224 | tf_op jit(solution)/shard_map/ppermute | solution.py:85
  2.3 9.8 %collective-permute-start.4 = (bf16[2,64,1024]{2,1,0:T(8,128)(2,1)S(1)}, bf16[2,64,1024]{2,1,0:T(8,128)(2,1)S(1)}, u32[]{:S(2)}, u32[]{:S(2)}) collective-permute-start(bf16[2,64,1024]{2,1,0:T(8,128)(2,1)S(1)} %pack.3.refs_3_), channel_id=1, source_target_pairs={{0,2},{1,3},{2,0},{3,1},{4,6},{5,7},{6,4},{7,5},{8,10},{9,11},{10,... | collective-permute-start | bytes 786440 | tf_op jit(solution)/shard_map/ppermute | solution.py:90
  3.6 8.5 %collective-permute-start.3 = (bf16[2,64,1024]{2,1,0:T(8,128)(2,1)S(1)}, bf16[2,64,1024]{2,1,0:T(8,128)(2,1)S(1)}, u32[]{:S(2)}, u32[]{:S(2)}) collective-permute-start(bf16[2,64,1024]{2,1,0:T(8,128)(2,1)S(1)} %pack.3.refs_3_), channel_id=1, source_target_pairs={{0,1},{1,0},{2,3},{3,2},{4,5},{5,4},{6,7},{7,6},{8,9},{9,8},{10,11... | collective-permute-start | bytes 786440 | tf_op jit(solution)/shard_map/ppermute | solution.py:97
  7.4 8.4 %collective-permute-start.2 = (bf16[2,64,1024]{2,1,0:T(8,128)(2,1)S(1)}, bf16[2,64,1024]{2,1,0:T(8,128)(2,1)S(1)}, u32[]{:S(2)}, u32[]{:S(2)}) collective-permute-start(bf16[2,64,1024]{2,1,0:T(8,128)(2,1)S(1)} %pack.2.refs_0_), channel_id=1, source_target_pairs={{0,16},{1,17},{2,18},{3,19},{4,8},{5,9},{6,10},{7,11},{8,12},{9,13... | collective-permute-start | bytes 786440 | tf_op jit(solution)/shard_map/ppermute | solution.py:85
  8.8 8.9 %collective-permute-start.7 = (bf16[2,64,1024]{2,1,0:T(8,128)(2,1)S(1)}, bf16[2,64,1024]{2,1,0:T(8,128)(2,1)S(1)}, u32[]{:S(2)}, u32[]{:S(2)}) collective-permute-start(bf16[2,64,1024]{2,1,0:T(8,128)(2,1)S(1)} %pack.2.refs_0_), channel_id=1, source_target_pairs={{0,2},{1,3},{2,0},{3,1},{4,6},{5,7},{6,4},{7,5},{8,10},{9,11},{10,... | collective-permute-start | bytes 786440 | tf_op jit(solution)/shard_map/ppermute | solution.py:90
  10.0 9.3 %collective-permute-start.6 = (bf16[2,64,1024]{2,1,0:T(8,128)(2,1)S(1)}, bf16[2,64,1024]{2,1,0:T(8,128)(2,1)S(1)}, u32[]{:S(2)}, u32[]{:S(2)}) collective-permute-start(bf16[2,64,1024]{2,1,0:T(8,128)(2,1)S(1)} %pack.2.refs_0_), channel_id=1, source_target_pairs={{0,1},{1,0},{2,3},{3,2},{4,5},{5,4},{6,7},{7,6},{8,9},{9,8},{10,11... | collective-permute-start | bytes 786440 | tf_op jit(solution)/shard_map/ppermute | solution.py:97
  12.1 7.3 %collective-permute-start.8 = (bf16[2,64,1024]{2,1,0:T(8,128)(2,1)S(1)}, bf16[2,64,1024]{2,1,0:T(8,128)(2,1)S(1)}, u32[]{:S(2)}, u32[]{:S(2)}) collective-permute-start(bf16[2,64,1024]{2,1,0:T(8,128)(2,1)S(1)} %collective-permute-done.4.refs_2_), channel_id=1, source_target_pairs={{0,1},{1,0},{2,3},{3,2},{4,5},{5,4},{6,7},{7,6},{8,9},{9,8},{10,11... | collective-permute-start | bytes 786440 | tf_op jit(solution)/shard_map/ppermute | solution.py:97
  15.8 7.9 %collective-permute-start.5 = (bf16[2,64,1024]{2,1,0:T(8,128)(2,1)S(1)}, bf16[2,64,1024]{2,1,0:T(8,128)(2,1)S(1)}, u32[]{:S(2)}, u32[]{:S(2)}) collective-permute-start(bf16[2,64,1024]{2,1,0:T(8,128)(2,1)S(1)} %collective-permute-done.2.refs_0_), channel_id=1, source_target_pairs={{0,4},{1,5},{2,6},{3,7},{4,0},{5,1},{6,2},{7,3},{8,12},{9,13},{10,... | collective-permute-start | bytes 786440 | tf_op jit(solution)/shard_map/ppermute | solution.py:85
  16.1 9.1 %collective-permute-start.12 = (bf16[2,64,1024]{2,1,0:T(8,128)(2,1)S(1)}, bf16[2,64,1024]{2,1,0:T(8,128)(2,1)S(1)}, u32[]{:S(2)}, u32[]{:S(2)}) collective-permute-start(bf16[2,64,1024]{2,1,0:T(8,128)(2,1)S(1)} %collective-permute-done.2.refs_0_), channel_id=1, source_target_pairs={{0,2},{1,3},{2,0},{3,1},{4,6},{5,7},{6,4},{7,5},{8,10},{9,11},{10,... | collective-permute-start | bytes 786440 | tf_op jit(solution)/shard_map/ppermute | solution.py:90
  17.6 7.5 %collective-permute-start.11 = (bf16[2,64,1024]{2,1,0:T(8,128)(2,1)S(1)}, bf16[2,64,1024]{2,1,0:T(8,128)(2,1)S(1)}, u32[]{:S(2)}, u32[]{:S(2)}) collective-permute-start(bf16[2,64,1024]{2,1,0:T(8,128)(2,1)S(1)} %collective-permute-done.2.refs_0_), channel_id=1, source_target_pairs={{0,1},{1,0},{2,3},{3,2},{4,5},{5,4},{6,7},{7,6},{8,9},{9,8},{10,11... | collective-permute-start | bytes 786440 | tf_op jit(solution)/shard_map/ppermute | solution.py:97
  19.3 5.9 %collective-permute-start.13 = (bf16[2,64,1024]{2,1,0:T(8,128)(2,1)S(1)}, bf16[2,64,1024]{2,1,0:T(8,128)(2,1)S(1)}, u32[]{:S(2)}, u32[]{:S(2)}) collective-permute-start(bf16[2,64,1024]{2,1,0:T(8,128)(2,1)S(1)} %collective-permute-done.7.refs_2_), channel_id=1, source_target_pairs={{0,1},{1,0},{2,3},{3,2},{4,5},{5,4},{6,7},{7,6},{8,9},{9,8},{10,11... | collective-permute-start | bytes 786440 | tf_op jit(solution)/shard_map/ppermute | solution.py:97
  23.8 7.1 %collective-permute-start.10 = (bf16[2,64,1024]{2,1,0:T(8,128)(2,1)S(1)}, bf16[2,64,1024]{2,1,0:T(8,128)(2,1)S(1)}, u32[]{:S(2)}, u32[]{:S(2)}) collective-permute-start(bf16[2,64,1024]{2,1,0:T(8,128)(2,1)S(1)} %collective-permute-done.5.refs_0_), channel_id=1, source_target_pairs={{0,2},{1,3},{2,0},{3,1},{4,6},{5,7},{6,4},{7,5},{8,10},{9,11},{10,... | collective-permute-start | bytes 786440 | tf_op jit(solution)/shard_map/ppermute | solution.py:90
  24.1 8.5 %collective-permute-start.9 = (bf16[2,64,1024]{2,1,0:T(8,128)(2,1)S(1)}, bf16[2,64,1024]{2,1,0:T(8,128)(2,1)S(1)}, u32[]{:S(2)}, u32[]{:S(2)}) collective-permute-start(bf16[2,64,1024]{2,1,0:T(8,128)(2,1)S(1)} %collective-permute-done.5.refs_0_), channel_id=1, source_target_pairs={{0,1},{1,0},{2,3},{3,2},{4,5},{5,4},{6,7},{7,6},{8,9},{9,8},{10,11... | collective-permute-start | bytes 786440 | tf_op jit(solution)/shard_map/ppermute | solution.py:97
  25.2 7.4 %collective-permute-start.14 = (bf16[2,64,1024]{2,1,0:T(8,128)(2,1)S(1)}, bf16[2,64,1024]{2,1,0:T(8,128)(2,1)S(1)}, u32[]{:S(2)}, u32[]{:S(2)}) collective-permute-start(bf16[2,64,1024]{2,1,0:T(8,128)(2,1)S(1)} %collective-permute-done.12.refs_2_), channel_id=1, source_target_pairs={{0,1},{1,0},{2,3},{3,2},{4,5},{5,4},{6,7},{7,6},{8,9},{9,8},{10,11... | collective-permute-start | bytes 786440 | tf_op jit(solution)/shard_map/ppermute | solution.py:97
  30.9 2.8 %collective-permute-start.15 = (bf16[2,64,1024]{2,1,0:T(8,128)(2,1)S(1)}, bf16[2,64,1024]{2,1,0:T(8,128)(2,1)S(1)}, u32[]{:S(2)}, u32[]{:S(2)}) collective-permute-start(bf16[2,64,1024]{2,1,0:T(8,128)(2,1)S(1)} %collective-permute-done.10.refs_1_), channel_id=1, source_target_pairs={{0,1},{1,0},{2,3},{3,2},{4,5},{5,4},{6,7},{7,6},{8,9},{9,8},{10,11... | collective-permute-start | bytes 786440 | tf_op jit(solution)/shard_map/ppermute | solution.py:97

commit v20 on v19

--- a/solution.py
+++ b/solution.py
@@ -320,7 +320,9 @@
         batches[0].append((0, 0, 0))
         final = [(depth - 1, 0, 1)]
         if width == 2:
-            final += [(depth - 1, 1, 0), (depth - 2, 1, 1), (depth - 1, 1, 1)]
+            final += [(depth - 1, 0, 0), (depth - 1, 1, 0), (depth - 1, 1, 1)]
+            batches[-1].remove((depth - 1, 0, 0))
+            batches[-1].append((depth - 2, 1, 1))
         while len(batches) > 8:
             batches = [sum(batches[at : at + 2], []) for at in range(0, len(batches), 2)]
 
@@ -335,11 +337,17 @@
                 keep(f"z{dz + 1}", z_forward(block, grid, dz + 1, groups), [(dz + 1, 0, 0)])
             if width == 2:
                 keep(f"y{dz}", y_swap(block, grid), [(dz, 1, 0)])
-            if dz and all(place in found for place in batches[0]):
-                state = phase(batches.pop(0), state)
             keep(f"c{dz}", core_swap(block, grid), [(dz, 0, 1)])
             if dz and width == 2:
-                keep(f"d{dz}", core_swap(arrays[f"y{dz - 1}"], grid), [(dz - 1, 1, 1)])
+                swapped = arrays[f"y{dz - 1}"]
+                if dz + 1 == depth:
+                    swapped, _ = lax.optimization_barrier((swapped, block))
+                    swapped = stack([core_swap(swapped[half], grid) for half in range(2)], "pack")
+                else:
+                    swapped = core_swap(swapped, grid)
+                keep(f"d{dz}", swapped, [(dz - 1, 1, 1)])
+            if dz and batches and all(place in found for place in batches[0]):
+                state = phase(batches.pop(0), state)
             if dz == 0:
                 parts, state, queries = lax.optimization_barrier((parts, state, queries))
                 keep("z1", stack(parts, "pack"), [(1, 0, 0)])
@@ -353,6 +361,7 @@
             block, state = lax.optimization_barrier((arrays[f"y{depth - 1}"], state))
             arrays[f"y{depth - 1}"] = block
             keep("c", core_swap(block, grid), [(depth - 1, 1, 1)])
+        assert not batches
         return phase(final, state, last=True)
 
     spec = P(("groups", "tp"), None)

time: 39.2 us -> 38.2 us (0.974)
  the two profiles are of different devices: /device:TPU:17 before, /device:TPU:25 now
where the time goes in v20:
time: 38.2 us; the launch traced here: 37.5 us
  Pallas kernels  19.6 us (51%)
  starting transfers between devices  14.7 us (38%)
  waiting for transfers between devices  2.88 us (8%)
    pallas_call x4, Pallas kernels, phase(): pl.pallas_call(functools.partial(attend_kernel, grid, sources, bool(state...  16.9 us
    ppermute x9, starting transfers between devices, core_swap(): lax.ppermute(blocks, 'tp', [(at, at ^ 1) for at in range(depth * width *...  8.64 us
    ppermute x4, starting transfers between devices, z_forward(): return lax.ppermute(block, ('groups', 'tp'), pairs)  3.33 us
    ppermute x4, starting transfers between devices, y_swap(): lax.ppermute(block, 'tp', [(at, at ^ cores) for at in range(depth * width...  2.77 us
    ppermute x9, waiting for transfers between devices, core_swap(): lax.ppermute(blocks, 'tp', [(at, at ^ 1) for at in range(depth * width *...  2.15 us
    pallas_call x1, Pallas kernels, fetch(): pl.pallas_call(kernel, out_shape=jax.ShapeDtypeStruct(array.shape, array....  1.6 us
    pallas_call x3, Pallas kernels, stack(): pl.pallas_call(kernel, out_shape=jax.ShapeDtypeStruct((count, *arrays[0]....  1.03 us
  transfers between devices with their start and end apart: 17, of which 3 were waited for; matrix products, arithmetic and copies ran while one was open for 0% of the time, Pallas kernels for 40%

profile of v20, /device:TPU:25, one launch (start us, length us, event | category | flops | bytes accessed | tf_op | source)
XLA Modules:
  0.0 37.5 jit_solution(2008667854683326204)
XLA Ops:
  0.0 1.2 %collective-permute-start.1 = (bf16[64,1024]{1,0:T(8,128)(2,1)}, bf16[64,1024]{1,0:T(8,128)(2,1)S(1)}, u32[]{:S(2)}, u32[]{:S(2)}) collective-permute-start(bf16[64,1024]{1,0:T(8,128)(2,1)} %refs_1_.1), channel_id=1, source_target_pairs={{0,4},{1,5},{2,6},{3,7},{4,8},{5,9},{6,10},{7,11},{8,12},{9,13},{1... | collective-permute-start | bytes 393224 | tf_op jit(solution)/shard_map/ppermute | solution.py:85
  1.2 1.0 %pack.4.refs_3_ = bf16[2,64,1024]{2,1,0:T(8,128)(2,1)S(1)} custom-call(bf16[64,1024]{1,0:T(8,128)(2,1)} %refs_0_.1, bf16[64,1024]{1,0:T(8,128)(2,1)} %refs_1_.1), custom_call_target="tpu_custom_call" | custom-call | tf_op jit(solution)/shard_map/pack/pallas_call | solution.py:41
  2.2 1.3 %collective-permute-start.4 = (bf16[2,64,1024]{2,1,0:T(8,128)(2,1)S(1)}, bf16[2,64,1024]{2,1,0:T(8,128)(2,1)S(1)}, u32[]{:S(2)}, u32[]{:S(2)}) collective-permute-start(bf16[2,64,1024]{2,1,0:T(8,128)(2,1)S(1)} %pack.4.refs_3_), channel_id=1, source_target_pairs={{0,2},{1,3},{2,0},{3,1},{4,6},{5,7},{6,4},{7,5},{8,10},{9,11},{10,... | collective-permute-start | bytes 786440 | tf_op jit(solution)/shard_map/ppermute | solution.py:90
  3.5 1.5 %collective-permute-start.3 = (bf16[2,64,1024]{2,1,0:T(8,128)(2,1)S(1)}, bf16[2,64,1024]{2,1,0:T(8,128)(2,1)S(1)}, u32[]{:S(2)}, u32[]{:S(2)}) collective-permute-start(bf16[2,64,1024]{2,1,0:T(8,128)(2,1)S(1)} %pack.4.refs_3_), channel_id=1, source_target_pairs={{0,1},{1,0},{2,3},{3,2},{4,5},{5,4},{6,7},{7,6},{8,9},{9,8},{10,11... | collective-permute-start | bytes 786440 | tf_op jit(solution)/shard_map/ppermute | solution.py:97
  5.1 1.6 %fetch.1.query_ref = bf16[64,16384]{1,0:T(8,128)(2,1)S(1)} custom-call(bf16[64,16384]{1,0:T(8,128)(2,1)} %array_ref.1), custom_call_target="tpu_custom_call" | custom-call | tf_op jit(solution)/shard_map/fetch/pallas_call | solution.py:57
  6.7 0.0 collective-permute-done.refs_0_
  6.7 0.7 %collective-permute-done.1.refs_1_ = bf16[64,1024]{1,0:T(8,128)(2,1)S(1)} collective-permute-done((bf16[64,1024]{1,0:T(8,128)(2,1)}, bf16[64,1024]{1,0:T(8,128)(2,1)S(1)}, u32[]{:S(2)}, u32[]{:S(2)}) %collective-permute-start.1) | collective-permute-done | bytes 131104 | tf_op jit(solution)/shard_map/ppermute | solution.py:85
  7.4 0.8 %collective-permute-start.2 = (bf16[2,64,1024]{2,1,0:T(8,128)(2,1)S(1)}, bf16[2,64,1024]{2,1,0:T(8,128)(2,1)S(1)}, u32[]{:S(2)}, u32[]{:S(2)}) collective-permute-start(bf16[2,64,1024]{2,1,0:T(8,128)(2,1)S(1)} %pack.3.refs_0_), channel_id=1, source_target_pairs={{0,16},{1,17},{2,18},{3,19},{4,8},{5,9},{6,10},{7,11},{8,12},{9,13... | collective-permute-start | bytes 786440 | tf_op jit(solution)/shard_map/ppermute | solution.py:85
  8.2 0.6 %collective-permute-start.7 = (bf16[2,64,1024]{2,1,0:T(8,128)(2,1)S(1)}, bf16[2,64,1024]{2,1,0:T(8,128)(2,1)S(1)}, u32[]{:S(2)}, u32[]{:S(2)}) collective-permute-start(bf16[2,64,1024]{2,1,0:T(8,128)(2,1)S(1)} %pack.3.refs_0_), channel_id=1, source_target_pairs={{0,2},{1,3},{2,0},{3,1},{4,6},{5,7},{6,4},{7,5},{8,10},{9,11},{10,... | collective-permute-start | bytes 786440 | tf_op jit(solution)/shard_map/ppermute | solution.py:90
  8.8 2.1 %collective-permute-start.6 = (bf16[2,64,1024]{2,1,0:T(8,128)(2,1)S(1)}, bf16[2,64,1024]{2,1,0:T(8,128)(2,1)S(1)}, u32[]{:S(2)}, u32[]{:S(2)}) collective-permute-start(bf16[2,64,1024]{2,1,0:T(8,128)(2,1)S(1)} %pack.3.refs_0_), channel_id=1, source_target_pairs={{0,1},{1,0},{2,3},{3,2},{4,5},{5,4},{6,7},{7,6},{8,9},{9,8},{10,11... | collective-permute-start | bytes 786440 | tf_op jit(solution)/shard_map/ppermute | solution.py:97
  10.9 0.2 collective-permute-start.8
  11.0 0.0 collective-permute-done.3.refs_1_
  11.0 3.7 %attend.3 = (f32[8,1024,256]{2,1,0:T(8,128)S(1)}, f32[8,1024,128]{2,1,0:T(8,128)S(1)}) custom-call(bf16[64,16384]{1,0:T(8,128)(2,1)S(1)} %fetch.1.query_ref, bf16[2,64,1024]{2,1,0:T(8,128)(2,1)S(1)} %pack.3.refs_0_, bf16[2,64,1024]{2,1,0:T(8,128)(2,1)S(1)} %collective-permute-done.3.refs_1_, bf16[2,64,1024]{2,1,0:T(8,128)(2,1)S(1)} %collective-permute-done.4.refs_2_, ...), custom_call_target="tpu_custom_call" | custom-call | flops 1000 | bytes 1000 | tf_op jit(solution)/shard_map/attend/pallas_call | solution.py:301
  14.7 1.3 %collective-permute-start.5 = (bf16[2,64,1024]{2,1,0:T(8,128)(2,1)S(1)}, bf16[2,64,1024]{2,1,0:T(8,128)(2,1)S(1)}, u32[]{:S(2)}, u32[]{:S(2)}) collective-permute-start(bf16[2,64,1024]{2,1,0:T(8,128)(2,1)S(1)} %collective-permute-done.2.refs_0_), channel_id=1, source_target_pairs={{0,4},{1,5},{2,6},{3,7},{4,0},{5,1},{6,2},{7,3},{8,12},{9,13},{10,... | collective-permute-start | bytes 786440 | tf_op jit(solution)/shard_map/ppermute | solution.py:85
  16.1 0.4 collective-permute-start.12
  16.4 1.7 %collective-permute-start.11 = (bf16[2,64,1024]{2,1,0:T(8,128)(2,1)S(1)}, bf16[2,64,1024]{2,1,0:T(8,128)(2,1)S(1)}, u32[]{:S(2)}, u32[]{:S(2)}) collective-permute-start(bf16[2,64,1024]{2,1,0:T(8,128)(2,1)S(1)} %collective-permute-done.2.refs_0_), channel_id=1, source_target_pairs={{0,1},{1,0},{2,3},{3,2},{4,5},{5,4},{6,7},{7,6},{8,9},{9,8},{10,11... | collective-permute-start | bytes 786440 | tf_op jit(solution)/shard_map/ppermute | solution.py:97
  18.2 0.0 collective-permute-done.6.refs_1_
  18.2 0.1 collective-permute-start.13
  18.2 0.0 collective-permute-done.8.refs_3_
  18.2 4.4 %attend.4 = (f32[8,1024,256]{2,1,0:T(8,128)S(1)}, f32[8,1024,128]{2,1,0:T(8,128)S(1)}) custom-call(bf16[64,16384]{1,0:T(8,128)(2,1)S(1)} %fetch.1.query_ref, bf16[2,64,1024]{2,1,0:T(8,128)(2,1)S(1)} %collective-permute-done.2.refs_0_, bf16[2,64,1024]{2,1,0:T(8,128)(2,1)S(1)} %collective-permute-done.6.refs_1_, ...), custom_call_target="tpu_custom_call", output_to_operand_aliasing={{0}: (5, {}), {1}: (6, {})} | custom-call | flops 1000 | bytes 1000 | tf_op jit(solution)/shard_map/attend/pallas_call | solution.py:301
  22.6 0.0 collective-permute-done.5.refs_1_
  22.6 0.5 %collective-permute-start.10 = (bf16[2,64,1024]{2,1,0:T(8,128)(2,1)S(1)}, bf16[2,64,1024]{2,1,0:T(8,128)(2,1)S(1)}, u32[]{:S(2)}, u32[]{:S(2)}) collective-permute-start(bf16[2,64,1024]{2,1,0:T(8,128)(2,1)S(1)} %collective-permute-done.5.refs_1_), channel_id=1, source_target_pairs={{0,2},{1,3},{2,0},{3,1},{4,6},{5,7},{6,4},{7,5},{8,10},{9,11},{10,... | collective-permute-start | bytes 786440 | tf_op jit(solution)/shard_map/ppermute | solution.py:90
  23.1 0.0 collective-permute-done.12.refs_1_
  23.2 2.3 %collective-permute-start.15 = (bf16[64,1024]{1,0:T(8,128)(2,1)S(1)}, bf16[64,1024]{1,0:T(8,128)(2,1)S(1)}, u32[]{:S(2)}, u32[]{:S(2)}) collective-permute-start(bf16[64,1024]{1,0:T(8,128)(2,1)S(1)} %get-tuple-element.47), channel_id=1, source_target_pairs={{0,1},{1,0},{2,3},{3,2},{4,5},{5,4},{6,7},{7,6},{8,9},{9,8},{10,11... | collective-permute-start | bytes 393224 | tf_op jit(solution)/shard_map/ppermute | solution.py:97
  25.4 0.1 collective-permute-start.14
  25.5 0.9 %collective-permute-done.15.refs_1_ = bf16[64,1024]{1,0:T(8,128)(2,1)S(1)} collective-permute-done((bf16[64,1024]{1,0:T(8,128)(2,1)S(1)}, bf16[64,1024]{1,0:T(8,128)(2,1)S(1)}, u32[]{:S(2)}, u32[]{:S(2)}) %collective-permute-start.15) | collective-permute-done | bytes 131104 | tf_op jit(solution)/shard_map/ppermute | solution.py:97
  26.4 0.4 collective-permute-start.9
  26.8 0.0 collective-permute-done.14.refs_0_
  26.8 4.2 %attend.5 = (f32[8,1024,256]{2,1,0:T(8,128)S(1)}, f32[8,1024,128]{2,1,0:T(8,128)S(1)}) custom-call(bf16[64,16384]{1,0:T(8,128)(2,1)S(1)} %fetch.1.query_ref, bf16[2,64,1024]{2,1,0:T(8,128)(2,1)S(1)} %collective-permute-done.11.refs_0_, bf16[2,64,1024]{2,1,0:T(8,128)(2,1)S(1)} %collective-permute-done.12.refs_1_, ...), custom_call_target="tpu_custom_call", output_to_operand_aliasing={{0}: (5, {}), {1}: (6, {})} | custom-call | flops 1000 | bytes 1000 | tf_op jit(solution)/shard_map/attend/pallas_call | solution.py:301
  31.1 0.4 collective-permute-start.16
  31.4 1.2 %collective-permute-done.16.refs_3_ = bf16[2,64,1024]{2,1,0:T(8,128)(2,1)S(1)} collective-permute-done((bf16[2,64,1024]{2,1,0:T(8,128)(2,1)S(1)}, bf16[2,64,1024]{2,1,0:T(8,128)(2,1)S(1)}, u32[]{:S(2)}, u32[]{:S(2)}) %collective-permute-start.16) | collective-permute-done | bytes 262176 | tf_op jit(solution)/shard_map/ppermute | solution.py:97
  32.7 4.7 %attend_last.1 = bf16[64,16384]{1,0:T(8,128)(2,1)} custom-call(bf16[64,16384]{1,0:T(8,128)(2,1)S(1)} %fetch.1.query_ref, bf16[2,64,1024]{2,1,0:T(8,128)(2,1)S(1)} %collective-permute-done.9.refs_0_, bf16[2,64,1024]{2,1,0:T(8,128)(2,1)S(1)} %collective-permute-done.5.refs_1_, bf16[2,64,1024]{2,1,0:T(8,128)(2,1)S(1)} %collective-permute-done.10.refs_2_, ...), custom_call_target="tpu_custom_call" | custom-call | flops 1000 | bytes 1000 | tf_op jit(solution)/shard_map/attend_last/pallas_call | solution.py:301
  (11 shorter events, 0.1 us)
Async XLA Ops:
  0.0 6.7 %collective-permute-start = (bf16[64,1024]{1,0:T(8,128)(2,1)}, bf16[64,1024]{1,0:T(8,128)(2,1)S(1)}, u32[]{:S(2)}, u32[]{:S(2)}) collective-permute-start(bf16[64,1024]{1,0:T(8,128)(2,1)} %refs_0_.1), channel_id=1, source_target_pairs={{0,4},{1,5},{2,6},{3,7},{4,8},{5,9},{6,10},{7,11},{8,12},{9,13},{1... | collective-permute-start | bytes 393224 | tf_op jit(solution)/shard_map/ppermute | solution.py:85
  0.0 7.4 %collective-permute-start.1 = (bf16[64,1024]{1,0:T(8,128)(2,1)}, bf16[64,1024]{1,0:T(8,128)(2,1)S(1)}, u32[]{:S(2)}, u32[]{:S(2)}) collective-permute-start(bf16[64,1024]{1,0:T(8,128)(2,1)} %refs_1_.1), channel_id=1, source_target_pairs={{0,4},{1,5},{2,6},{3,7},{4,8},{5,9},{6,10},{7,11},{8,12},{9,13},{1... | collective-permute-start | bytes 393224 | tf_op jit(solution)/shard_map/ppermute | solution.py:85
  2.2 8.6 %collective-permute-start.4 = (bf16[2,64,1024]{2,1,0:T(8,128)(2,1)S(1)}, bf16[2,64,1024]{2,1,0:T(8,128)(2,1)S(1)}, u32[]{:S(2)}, u32[]{:S(2)}) collective-permute-start(bf16[2,64,1024]{2,1,0:T(8,128)(2,1)S(1)} %pack.4.refs_3_), channel_id=1, source_target_pairs={{0,2},{1,3},{2,0},{3,1},{4,6},{5,7},{6,4},{7,5},{8,10},{9,11},{10,... | collective-permute-start | bytes 786440 | tf_op jit(solution)/shard_map/ppermute | solution.py:90
  3.5 7.5 %collective-permute-start.3 = (bf16[2,64,1024]{2,1,0:T(8,128)(2,1)S(1)}, bf16[2,64,1024]{2,1,0:T(8,128)(2,1)S(1)}, u32[]{:S(2)}, u32[]{:S(2)}) collective-permute-start(bf16[2,64,1024]{2,1,0:T(8,128)(2,1)S(1)} %pack.4.refs_3_), channel_id=1, source_target_pairs={{0,1},{1,0},{2,3},{3,2},{4,5},{5,4},{6,7},{7,6},{8,9},{9,8},{10,11... | collective-permute-start | bytes 786440 | tf_op jit(solution)/shard_map/ppermute | solution.py:97
  7.4 7.3 %collective-permute-start.2 = (bf16[2,64,1024]{2,1,0:T(8,128)(2,1)S(1)}, bf16[2,64,1024]{2,1,0:T(8,128)(2,1)S(1)}, u32[]{:S(2)}, u32[]{:S(2)}) collective-permute-start(bf16[2,64,1024]{2,1,0:T(8,128)(2,1)S(1)} %pack.3.refs_0_), channel_id=1, source_target_pairs={{0,16},{1,17},{2,18},{3,19},{4,8},{5,9},{6,10},{7,11},{8,12},{9,13... | collective-permute-start | bytes 786440 | tf_op jit(solution)/shard_map/ppermute | solution.py:85
  8.2 8.3 %collective-permute-start.7 = (bf16[2,64,1024]{2,1,0:T(8,128)(2,1)S(1)}, bf16[2,64,1024]{2,1,0:T(8,128)(2,1)S(1)}, u32[]{:S(2)}, u32[]{:S(2)}) collective-permute-start(bf16[2,64,1024]{2,1,0:T(8,128)(2,1)S(1)} %pack.3.refs_0_), channel_id=1, source_target_pairs={{0,2},{1,3},{2,0},{3,1},{4,6},{5,7},{6,4},{7,5},{8,10},{9,11},{10,... | collective-permute-start | bytes 786440 | tf_op jit(solution)/shard_map/ppermute | solution.py:90
  8.8 9.4 %collective-permute-start.6 = (bf16[2,64,1024]{2,1,0:T(8,128)(2,1)S(1)}, bf16[2,64,1024]{2,1,0:T(8,128)(2,1)S(1)}, u32[]{:S(2)}, u32[]{:S(2)}) collective-permute-start(bf16[2,64,1024]{2,1,0:T(8,128)(2,1)S(1)} %pack.3.refs_0_), channel_id=1, source_target_pairs={{0,1},{1,0},{2,3},{3,2},{4,5},{5,4},{6,7},{7,6},{8,9},{9,8},{10,11... | collective-permute-start | bytes 786440 | tf_op jit(solution)/shard_map/ppermute | solution.py:97
  10.9 7.4 %collective-permute-start.8 = (bf16[2,64,1024]{2,1,0:T(8,128)(2,1)S(1)}, bf16[2,64,1024]{2,1,0:T(8,128)(2,1)S(1)}, u32[]{:S(2)}, u32[]{:S(2)}) collective-permute-start(bf16[2,64,1024]{2,1,0:T(8,128)(2,1)S(1)} %collective-permute-done.4.refs_2_), channel_id=1, source_target_pairs={{0,1},{1,0},{2,3},{3,2},{4,5},{5,4},{6,7},{7,6},{8,9},{9,8},{10,11... | collective-permute-start | bytes 786440 | tf_op jit(solution)/shard_map/ppermute | solution.py:97
  14.7 7.9 %collective-permute-start.5 = (bf16[2,64,1024]{2,1,0:T(8,128)(2,1)S(1)}, bf16[2,64,1024]{2,1,0:T(8,128)(2,1)S(1)}, u32[]{:S(2)}, u32[]{:S(2)}) collective-permute-start(bf16[2,64,1024]{2,1,0:T(8,128)(2,1)S(1)} %collective-permute-done.2.refs_0_), channel_id=1, source_target_pairs={{0,4},{1,5},{2,6},{3,7},{4,0},{5,1},{6,2},{7,3},{8,12},{9,13},{10,... | collective-permute-start | bytes 786440 | tf_op jit(solution)/shard_map/ppermute | solution.py:85
  16.1 7.1 %collective-permute-start.12 = (bf16[2,64,1024]{2,1,0:T(8,128)(2,1)S(1)}, bf16[2,64,1024]{2,1,0:T(8,128)(2,1)S(1)}, u32[]{:S(2)}, u32[]{:S(2)}) collective-permute-start(bf16[2,64,1024]{2,1,0:T(8,128)(2,1)S(1)} %collective-permute-done.2.refs_0_), channel_id=1, source_target_pairs={{0,2},{1,3},{2,0},{3,1},{4,6},{5,7},{6,4},{7,5},{8,10},{9,11},{10,... | collective-permute-start | bytes 786440 | tf_op jit(solution)/shard_map/ppermute | solution.py:90
  16.4 10.4 %collective-permute-start.11 = (bf16[2,64,1024]{2,1,0:T(8,128)(2,1)S(1)}, bf16[2,64,1024]{2,1,0:T(8,128)(2,1)S(1)}, u32[]{:S(2)}, u32[]{:S(2)}) collective-permute-start(bf16[2,64,1024]{2,1,0:T(8,128)(2,1)S(1)} %collective-permute-done.2.refs_0_), channel_id=1, source_target_pairs={{0,1},{1,0},{2,3},{3,2},{4,5},{5,4},{6,7},{7,6},{8,9},{9,8},{10,11... | collective-permute-start | bytes 786440 | tf_op jit(solution)/shard_map/ppermute | solution.py:97
  18.2 8.7 %collective-permute-start.13 = (bf16[2,64,1024]{2,1,0:T(8,128)(2,1)S(1)}, bf16[2,64,1024]{2,1,0:T(8,128)(2,1)S(1)}, u32[]{:S(2)}, u32[]{:S(2)}) collective-permute-start(bf16[2,64,1024]{2,1,0:T(8,128)(2,1)S(1)} %collective-permute-done.7.refs_2_), channel_id=1, source_target_pairs={{0,1},{1,0},{2,3},{3,2},{4,5},{5,4},{6,7},{7,6},{8,9},{9,8},{10,11... | collective-permute-start | bytes 786440 | tf_op jit(solution)/shard_map/ppermute | solution.py:97
  22.6 8.4 %collective-permute-start.10 = (bf16[2,64,1024]{2,1,0:T(8,128)(2,1)S(1)}, bf16[2,64,1024]{2,1,0:T(8,128)(2,1)S(1)}, u32[]{:S(2)}, u32[]{:S(2)}) collective-permute-start(bf16[2,64,1024]{2,1,0:T(8,128)(2,1)S(1)} %collective-permute-done.5.refs_1_), channel_id=1, source_target_pairs={{0,2},{1,3},{2,0},{3,1},{4,6},{5,7},{6,4},{7,5},{8,10},{9,11},{10,... | collective-permute-start | bytes 786440 | tf_op jit(solution)/shard_map/ppermute | solution.py:90
  23.2 3.3 %collective-permute-start.15 = (bf16[64,1024]{1,0:T(8,128)(2,1)S(1)}, bf16[64,1024]{1,0:T(8,128)(2,1)S(1)}, u32[]{:S(2)}, u32[]{:S(2)}) collective-permute-start(bf16[64,1024]{1,0:T(8,128)(2,1)S(1)} %get-tuple-element.47), channel_id=1, source_target_pairs={{0,1},{1,0},{2,3},{3,2},{4,5},{5,4},{6,7},{7,6},{8,9},{9,8},{10,11... | collective-permute-start | bytes 393224 | tf_op jit(solution)/shard_map/ppermute | solution.py:97
  25.4 1.4 %collective-permute-start.14 = (bf16[64,1024]{1,0:T(8,128)(2,1)S(1)}, bf16[64,1024]{1,0:T(8,128)(2,1)S(1)}, u32[]{:S(2)}, u32[]{:S(2)}) collective-permute-start(bf16[64,1024]{1,0:T(8,128)(2,1)S(1)} %get-tuple-element.48), channel_id=1, source_target_pairs={{0,1},{1,0},{2,3},{3,2},{4,5},{5,4},{6,7},{7,6},{8,9},{9,8},{10,11... | collective-permute-start | bytes 393224 | tf_op jit(solution)/shard_map/ppermute | solution.py:97
  26.4 5.0 %collective-permute-start.9 = (bf16[2,64,1024]{2,1,0:T(8,128)(2,1)S(1)}, bf16[2,64,1024]{2,1,0:T(8,128)(2,1)S(1)}, u32[]{:S(2)}, u32[]{:S(2)}) collective-permute-start(bf16[2,64,1024]{2,1,0:T(8,128)(2,1)S(1)} %collective-permute-done.5.refs_1_), channel_id=1, source_target_pairs={{0,1},{1,0},{2,3},{3,2},{4,5},{5,4},{6,7},{7,6},{8,9},{9,8},{10,11... | collective-permute-start | bytes 786440 | tf_op jit(solution)/shard_map/ppermute | solution.py:97
  31.1 1.6 %collective-permute-start.16 = (bf16[2,64,1024]{2,1,0:T(8,128)(2,1)S(1)}, bf16[2,64,1024]{2,1,0:T(8,128)(2,1)S(1)}, u32[]{:S(2)}, u32[]{:S(2)}) collective-permute-start(bf16[2,64,1024]{2,1,0:T(8,128)(2,1)S(1)} %collective-permute-done.10.refs_2_), channel_id=1, source_target_pairs={{0,1},{1,0},{2,3},{3,2},{4,5},{5,4},{6,7},{7,6},{8,9},{9,8},{10,11... | collective-permute-start | bytes 786440 | tf_op jit(solution)/shard_map/ppermute | solution.py:97

commit v21 on v20

--- a/solution.py
+++ b/solution.py
@@ -85,11 +85,13 @@
     return lax.ppermute(block, ("groups", "tp"), pairs)
 
 
-def y_swap(block, grid):
-    depth, width, cores = grid
-    return lax.ppermute(
-        block, "tp", [(at, at ^ cores) for at in range(depth * width * cores)]
-    )
+def y_swap(block, grid, dz):
+    depth, width, cores = grid
+    pairs = []
+    for at in range(depth * width * cores):
+        served = at // (width * cores) >= dz
+        pairs.append((at, at ^ cores if served else at ^ 1))
+    return lax.ppermute(block, "tp", pairs)
 
 
 def core_swap(blocks, grid):
@@ -336,7 +338,7 @@
             elif dz + 1 < depth:
                 keep(f"z{dz + 1}", z_forward(block, grid, dz + 1, groups), [(dz + 1, 0, 0)])
             if width == 2:
-                keep(f"y{dz}", y_swap(block, grid), [(dz, 1, 0)])
+                keep(f"y{dz}", y_swap(block, grid, dz), [(dz, 1, 0)])
             keep(f"c{dz}", core_swap(block, grid), [(dz, 0, 1)])
             if dz and width == 2:
                 swapped = arrays[f"y{dz - 1}"]

time: 38.2 us -> 37.6 us (0.984); the launches traced: 37.5 us -> 37.5 us
  no operation moved by 1% of the time
where the time goes in v21:
time: 37.6 us; the launch traced here: 37.5 us
  Pallas kernels  19.6 us (52%)
  starting transfers between devices  14.7 us (39%)
  waiting for transfers between devices  2.88 us (8%)
    pallas_call x4, Pallas kernels, phase(): pl.pallas_call(functools.partial(attend_kernel, grid, sources, bool(state...  16.9 us
    ppermute x9, starting transfers between devices, core_swap(): lax.ppermute(blocks, 'tp', [(at, at ^ 1) for at in range(depth * width *...  8.64 us
    ppermute x4, starting transfers between devices, z_forward(): return lax.ppermute(block, ('groups', 'tp'), pairs)  3.33 us
    ppermute x4, starting transfers between devices, y_swap(): return lax.ppermute(block, 'tp', pairs)  2.77 us
    ppermute x9, waiting for transfers between devices, core_swap(): lax.ppermute(blocks, 'tp', [(at, at ^ 1) for at in range(depth * width *...  2.15 us
    pallas_call x1, Pallas kernels, fetch(): pl.pallas_call(kernel, out_shape=jax.ShapeDtypeStruct(array.shape, array....  1.6 us
    pallas_call x3, Pallas kernels, stack(): pl.pallas_call(kernel, out_shape=jax.ShapeDtypeStruct((count, *arrays[0]....  1.03 us
  transfers between devices with their start and end apart: 17, of which 3 were waited for; matrix products, arithmetic and copies ran while one was open for 0% of the time, Pallas kernels for 40%

profile of v21, /device:TPU:25, one launch (start us, length us, event | category | flops | bytes accessed | tf_op | source)
XLA Modules:
  0.0 37.5 jit_solution(6899543980474744009)
XLA Ops:
  0.0 1.2 %collective-permute-start.1 = (bf16[64,1024]{1,0:T(8,128)(2,1)}, bf16[64,1024]{1,0:T(8,128)(2,1)S(1)}, u32[]{:S(2)}, u32[]{:S(2)}) collective-permute-start(bf16[64,1024]{1,0:T(8,128)(2,1)} %refs_1_.1), channel_id=1, source_target_pairs={{0,4},{1,5},{2,6},{3,7},{4,8},{5,9},{6,10},{7,11},{8,12},{9,13},{1... | collective-permute-start | bytes 393224 | tf_op jit(solution)/shard_map/ppermute | solution.py:85
  1.2 1.0 %pack.4.refs_3_ = bf16[2,64,1024]{2,1,0:T(8,128)(2,1)S(1)} custom-call(bf16[64,1024]{1,0:T(8,128)(2,1)} %refs_0_.1, bf16[64,1024]{1,0:T(8,128)(2,1)} %refs_1_.1), custom_call_target="tpu_custom_call" | custom-call | tf_op jit(solution)/shard_map/pack/pallas_call | solution.py:41
  2.2 1.3 %collective-permute-start.4 = (bf16[2,64,1024]{2,1,0:T(8,128)(2,1)S(1)}, bf16[2,64,1024]{2,1,0:T(8,128)(2,1)S(1)}, u32[]{:S(2)}, u32[]{:S(2)}) collective-permute-start(bf16[2,64,1024]{2,1,0:T(8,128)(2,1)S(1)} %pack.4.refs_3_), channel_id=1, source_target_pairs={{0,2},{1,3},{2,0},{3,1},{4,6},{5,7},{6,4},{7,5},{8,10},{9,11},{10,... | collective-permute-start | bytes 786440 | tf_op jit(solution)/shard_map/ppermute | solution.py:94
  3.5 1.5 %collective-permute-start.3 = (bf16[2,64,1024]{2,1,0:T(8,128)(2,1)S(1)}, bf16[2,64,1024]{2,1,0:T(8,128)(2,1)S(1)}, u32[]{:S(2)}, u32[]{:S(2)}) collective-permute-start(bf16[2,64,1024]{2,1,0:T(8,128)(2,1)S(1)} %pack.4.refs_3_), channel_id=1, source_target_pairs={{0,1},{1,0},{2,3},{3,2},{4,5},{5,4},{6,7},{7,6},{8,9},{9,8},{10,11... | collective-permute-start | bytes 786440 | tf_op jit(solution)/shard_map/ppermute | solution.py:99
  5.1 1.6 %fetch.1.query_ref = bf16[64,16384]{1,0:T(8,128)(2,1)S(1)} custom-call(bf16[64,16384]{1,0:T(8,128)(2,1)} %array_ref.1), custom_call_target="tpu_custom_call" | custom-call | tf_op jit(solution)/shard_map/fetch/pallas_call | solution.py:57
  6.7 0.0 collective-permute-done.refs_0_
  6.7 0.7 %collective-permute-done.1.refs_1_ = bf16[64,1024]{1,0:T(8,128)(2,1)S(1)} collective-permute-done((bf16[64,1024]{1,0:T(8,128)(2,1)}, bf16[64,1024]{1,0:T(8,128)(2,1)S(1)}, u32[]{:S(2)}, u32[]{:S(2)}) %collective-permute-start.1) | collective-permute-done | bytes 131104 | tf_op jit(solution)/shard_map/ppermute | solution.py:85
  7.4 0.8 %collective-permute-start.2 = (bf16[2,64,1024]{2,1,0:T(8,128)(2,1)S(1)}, bf16[2,64,1024]{2,1,0:T(8,128)(2,1)S(1)}, u32[]{:S(2)}, u32[]{:S(2)}) collective-permute-start(bf16[2,64,1024]{2,1,0:T(8,128)(2,1)S(1)} %pack.3.refs_0_), channel_id=1, source_target_pairs={{0,16},{1,17},{2,18},{3,19},{4,8},{5,9},{6,10},{7,11},{8,12},{9,13... | collective-permute-start | bytes 786440 | tf_op jit(solution)/shard_map/ppermute | solution.py:85
  8.2 0.6 %collective-permute-start.7 = (bf16[2,64,1024]{2,1,0:T(8,128)(2,1)S(1)}, bf16[2,64,1024]{2,1,0:T(8,128)(2,1)S(1)}, u32[]{:S(2)}, u32[]{:S(2)}) collective-permute-start(bf16[2,64,1024]{2,1,0:T(8,128)(2,1)S(1)} %pack.3.refs_0_), channel_id=1, source_target_pairs={{0,1},{1,0},{2,3},{3,2},{4,6},{5,7},{6,4},{7,5},{8,10},{9,11},{10,... | collective-permute-start | bytes 786440 | tf_op jit(solution)/shard_map/ppermute | solution.py:94
  8.8 2.1 %collective-permute-start.6 = (bf16[2,64,1024]{2,1,0:T(8,128)(2,1)S(1)}, bf16[2,64,1024]{2,1,0:T(8,128)(2,1)S(1)}, u32[]{:S(2)}, u32[]{:S(2)}) collective-permute-start(bf16[2,64,1024]{2,1,0:T(8,128)(2,1)S(1)} %pack.3.refs_0_), channel_id=1, source_target_pairs={{0,1},{1,0},{2,3},{3,2},{4,5},{5,4},{6,7},{7,6},{8,9},{9,8},{10,11... | collective-permute-start | bytes 786440 | tf_op jit(solution)/shard_map/ppermute | solution.py:99
  10.9 0.2 collective-permute-start.8
  11.0 0.0 collective-permute-done.3.refs_1_
  11.0 3.7 %attend.3 = (f32[8,1024,256]{2,1,0:T(8,128)S(1)}, f32[8,1024,128]{2,1,0:T(8,128)S(1)}) custom-call(bf16[64,16384]{1,0:T(8,128)(2,1)S(1)} %fetch.1.query_ref, bf16[2,64,1024]{2,1,0:T(8,128)(2,1)S(1)} %pack.3.refs_0_, bf16[2,64,1024]{2,1,0:T(8,128)(2,1)S(1)} %collective-permute-done.3.refs_1_, bf16[2,64,1024]{2,1,0:T(8,128)(2,1)S(1)} %collective-permute-done.4.refs_2_, ...), custom_call_target="tpu_custom_call" | custom-call | flops 1000 | bytes 1000 | tf_op jit(solution)/shard_map/attend/pallas_call | solution.py:303
  14.7 1.3 %collective-permute-start.5 = (bf16[2,64,1024]{2,1,0:T(8,128)(2,1)S(1)}, bf16[2,64,1024]{2,1,0:T(8,128)(2,1)S(1)}, u32[]{:S(2)}, u32[]{:S(2)}) collective-permute-start(bf16[2,64,1024]{2,1,0:T(8,128)(2,1)S(1)} %collective-permute-done.2.refs_0_), channel_id=1, source_target_pairs={{0,4},{1,5},{2,6},{3,7},{4,0},{5,1},{6,2},{7,3},{8,12},{9,13},{10,... | collective-permute-start | bytes 786440 | tf_op jit(solution)/shard_map/ppermute | solution.py:85
  16.1 0.4 collective-permute-start.12
  16.4 1.7 %collective-permute-start.11 = (bf16[2,64,1024]{2,1,0:T(8,128)(2,1)S(1)}, bf16[2,64,1024]{2,1,0:T(8,128)(2,1)S(1)}, u32[]{:S(2)}, u32[]{:S(2)}) collective-permute-start(bf16[2,64,1024]{2,1,0:T(8,128)(2,1)S(1)} %collective-permute-done.2.refs_0_), channel_id=1, source_target_pairs={{0,1},{1,0},{2,3},{3,2},{4,5},{5,4},{6,7},{7,6},{8,9},{9,8},{10,11... | collective-permute-start | bytes 786440 | tf_op jit(solution)/shard_map/ppermute | solution.py:99
  18.2 0.0 collective-permute-done.6.refs_1_
  18.2 0.1 collective-permute-start.13
  18.2 0.0 collective-permute-done.8.refs_3_
  18.2 4.4 %attend.4 = (f32[8,1024,256]{2,1,0:T(8,128)S(1)}, f32[8,1024,128]{2,1,0:T(8,128)S(1)}) custom-call(bf16[64,16384]{1,0:T(8,128)(2,1)S(1)} %fetch.1.query_ref, bf16[2,64,1024]{2,1,0:T(8,128)(2,1)S(1)} %collective-permute-done.2.refs_0_, bf16[2,64,1024]{2,1,0:T(8,128)(2,1)S(1)} %collective-permute-done.6.refs_1_, ...), custom_call_target="tpu_custom_call", output_to_operand_aliasing={{0}: (5, {}), {1}: (6, {})} | custom-call | flops 1000 | bytes 1000 | tf_op jit(solution)/shard_map/attend/pallas_call | solution.py:303
  22.6 0.0 collective-permute-done.5.refs_1_
  22.6 0.5 %collective-permute-start.10 = (bf16[2,64,1024]{2,1,0:T(8,128)(2,1)S(1)}, bf16[2,64,1024]{2,1,0:T(8,128)(2,1)S(1)}, u32[]{:S(2)}, u32[]{:S(2)}) collective-permute-start(bf16[2,64,1024]{2,1,0:T(8,128)(2,1)S(1)} %collective-permute-done.5.refs_1_), channel_id=1, source_target_pairs={{0,1},{1,0},{2,3},{3,2},{4,5},{5,4},{6,7},{7,6},{8,9},{9,8},{10,11... | collective-permute-start | bytes 786440 | tf_op jit(solution)/shard_map/ppermute | solution.py:94
  23.1 0.0 collective-permute-done.12.refs_1_
  23.2 2.3 %collective-permute-start.15 = (bf16[64,1024]{1,0:T(8,128)(2,1)S(1)}, bf16[64,1024]{1,0:T(8,128)(2,1)S(1)}, u32[]{:S(2)}, u32[]{:S(2)}) collective-permute-start(bf16[64,1024]{1,0:T(8,128)(2,1)S(1)} %get-tuple-element.47), channel_id=1, source_target_pairs={{0,1},{1,0},{2,3},{3,2},{4,5},{5,4},{6,7},{7,6},{8,9},{9,8},{10,11... | collective-permute-start | bytes 393224 | tf_op jit(solution)/shard_map/ppermute | solution.py:99
  25.4 0.1 collective-permute-start.14
  25.5 0.9 %collective-permute-done.15.refs_1_ = bf16[64,1024]{1,0:T(8,128)(2,1)S(1)} collective-permute-done((bf16[64,1024]{1,0:T(8,128)(2,1)S(1)}, bf16[64,1024]{1,0:T(8,128)(2,1)S(1)}, u32[]{:S(2)}, u32[]{:S(2)}) %collective-permute-start.15) | collective-permute-done | bytes 131104 | tf_op jit(solution)/shard_map/ppermute | solution.py:99
  26.4 0.4 collective-permute-start.9
  26.8 0.0 collective-permute-done.14.refs_0_
  26.8 4.2 %attend.5 = (f32[8,1024,256]{2,1,0:T(8,128)S(1)}, f32[8,1024,128]{2,1,0:T(8,128)S(1)}) custom-call(bf16[64,16384]{1,0:T(8,128)(2,1)S(1)} %fetch.1.query_ref, bf16[2,64,1024]{2,1,0:T(8,128)(2,1)S(1)} %collective-permute-done.11.refs_0_, bf16[2,64,1024]{2,1,0:T(8,128)(2,1)S(1)} %collective-permute-done.12.refs_1_, ...), custom_call_target="tpu_custom_call", output_to_operand_aliasing={{0}: (5, {}), {1}: (6, {})} | custom-call | flops 1000 | bytes 1000 | tf_op jit(solution)/shard_map/attend/pallas_call | solution.py:303
  31.1 0.4 collective-permute-start.16
  31.4 1.2 %collective-permute-done.16.refs_3_ = bf16[2,64,1024]{2,1,0:T(8,128)(2,1)S(1)} collective-permute-done((bf16[2,64,1024]{2,1,0:T(8,128)(2,1)S(1)}, bf16[2,64,1024]{2,1,0:T(8,128)(2,1)S(1)}, u32[]{:S(2)}, u32[]{:S(2)}) %collective-permute-start.16) | collective-permute-done | bytes 262176 | tf_op jit(solution)/shard_map/ppermute | solution.py:99
  32.7 4.7 %attend_last.1 = bf16[64,16384]{1,0:T(8,128)(2,1)} custom-call(bf16[64,16384]{1,0:T(8,128)(2,1)S(1)} %fetch.1.query_ref, bf16[2,64,1024]{2,1,0:T(8,128)(2,1)S(1)} %collective-permute-done.9.refs_0_, bf16[2,64,1024]{2,1,0:T(8,128)(2,1)S(1)} %collective-permute-done.5.refs_1_, bf16[2,64,1024]{2,1,0:T(8,128)(2,1)S(1)} %collective-permute-done.10.refs_2_, ...), custom_call_target="tpu_custom_call" | custom-call | flops 1000 | bytes 1000 | tf_op jit(solution)/shard_map/attend_last/pallas_call | solution.py:303
  (11 shorter events, 0.1 us)
Async XLA Ops:
  0.0 6.7 %collective-permute-start = (bf16[64,1024]{1,0:T(8,128)(2,1)}, bf16[64,1024]{1,0:T(8,128)(2,1)S(1)}, u32[]{:S(2)}, u32[]{:S(2)}) collective-permute-start(bf16[64,1024]{1,0:T(8,128)(2,1)} %refs_0_.1), channel_id=1, source_target_pairs={{0,4},{1,5},{2,6},{3,7},{4,8},{5,9},{6,10},{7,11},{8,12},{9,13},{1... | collective-permute-start | bytes 393224 | tf_op jit(solution)/shard_map/ppermute | solution.py:85
  0.0 7.4 %collective-permute-start.1 = (bf16[64,1024]{1,0:T(8,128)(2,1)}, bf16[64,1024]{1,0:T(8,128)(2,1)S(1)}, u32[]{:S(2)}, u32[]{:S(2)}) collective-permute-start(bf16[64,1024]{1,0:T(8,128)(2,1)} %refs_1_.1), channel_id=1, source_target_pairs={{0,4},{1,5},{2,6},{3,7},{4,8},{5,9},{6,10},{7,11},{8,12},{9,13},{1... | collective-permute-start | bytes 393224 | tf_op jit(solution)/shard_map/ppermute | solution.py:85
  2.2 8.6 %collective-permute-start.4 = (bf16[2,64,1024]{2,1,0:T(8,128)(2,1)S(1)}, bf16[2,64,1024]{2,1,0:T(8,128)(2,1)S(1)}, u32[]{:S(2)}, u32[]{:S(2)}) collective-permute-start(bf16[2,64,1024]{2,1,0:T(8,128)(2,1)S(1)} %pack.4.refs_3_), channel_id=1, source_target_pairs={{0,2},{1,3},{2,0},{3,1},{4,6},{5,7},{6,4},{7,5},{8,10},{9,11},{10,... | collective-permute-start | bytes 786440 | tf_op jit(solution)/shard_map/ppermute | solution.py:94
  3.5 7.5 %collective-permute-start.3 = (bf16[2,64,1024]{2,1,0:T(8,128)(2,1)S(1)}, bf16[2,64,1024]{2,1,0:T(8,128)(2,1)S(1)}, u32[]{:S(2)}, u32[]{:S(2)}) collective-permute-start(bf16[2,64,1024]{2,1,0:T(8,128)(2,1)S(1)} %pack.4.refs_3_), channel_id=1, source_target_pairs={{0,1},{1,0},{2,3},{3,2},{4,5},{5,4},{6,7},{7,6},{8,9},{9,8},{10,11... | collective-permute-start | bytes 786440 | tf_op jit(solution)/shard_map/ppermute | solution.py:99
  7.4 7.3 %collective-permute-start.2 = (bf16[2,64,1024]{2,1,0:T(8,128)(2,1)S(1)}, bf16[2,64,1024]{2,1,0:T(8,128)(2,1)S(1)}, u32[]{:S(2)}, u32[]{:S(2)}) collective-permute-start(bf16[2,64,1024]{2,1,0:T(8,128)(2,1)S(1)} %pack.3.refs_0_), channel_id=1, source_target_pairs={{0,16},{1,17},{2,18},{3,19},{4,8},{5,9},{6,10},{7,11},{8,12},{9,13... | collective-permute-start | bytes 786440 | tf_op jit(solution)/shard_map/ppermute | solution.py:85
  8.2 8.3 %collective-permute-start.7 = (bf16[2,64,1024]{2,1,0:T(8,128)(2,1)S(1)}, bf16[2,64,1024]{2,1,0:T(8,128)(2,1)S(1)}, u32[]{:S(2)}, u32[]{:S(2)}) collective-permute-start(bf16[2,64,1024]{2,1,0:T(8,128)(2,1)S(1)} %pack.3.refs_0_), channel_id=1, source_target_pairs={{0,1},{1,0},{2,3},{3,2},{4,6},{5,7},{6,4},{7,5},{8,10},{9,11},{10,... | collective-permute-start | bytes 786440 | tf_op jit(solution)/shard_map/ppermute | solution.py:94
  8.8 9.4 %collective-permute-start.6 = (bf16[2,64,1024]{2,1,0:T(8,128)(2,1)S(1)}, bf16[2,64,1024]{2,1,0:T(8,128)(2,1)S(1)}, u32[]{:S(2)}, u32[]{:S(2)}) collective-permute-start(bf16[2,64,1024]{2,1,0:T(8,128)(2,1)S(1)} %pack.3.refs_0_), channel_id=1, source_target_pairs={{0,1},{1,0},{2,3},{3,2},{4,5},{5,4},{6,7},{7,6},{8,9},{9,8},{10,11... | collective-permute-start | bytes 786440 | tf_op jit(solution)/shard_map/ppermute | solution.py:99
  10.9 7.4 %collective-permute-start.8 = (bf16[2,64,1024]{2,1,0:T(8,128)(2,1)S(1)}, bf16[2,64,1024]{2,1,0:T(8,128)(2,1)S(1)}, u32[]{:S(2)}, u32[]{:S(2)}) collective-permute-start(bf16[2,64,1024]{2,1,0:T(8,128)(2,1)S(1)} %collective-permute-done.4.refs_2_), channel_id=1, source_target_pairs={{0,1},{1,0},{2,3},{3,2},{4,5},{5,4},{6,7},{7,6},{8,9},{9,8},{10,11... | collective-permute-start | bytes 786440 | tf_op jit(solution)/shard_map/ppermute | solution.py:99
  14.7 7.9 %collective-permute-start.5 = (bf16[2,64,1024]{2,1,0:T(8,128)(2,1)S(1)}, bf16[2,64,1024]{2,1,0:T(8,128)(2,1)S(1)}, u32[]{:S(2)}, u32[]{:S(2)}) collective-permute-start(bf16[2,64,1024]{2,1,0:T(8,128)(2,1)S(1)} %collective-permute-done.2.refs_0_), channel_id=1, source_target_pairs={{0,4},{1,5},{2,6},{3,7},{4,0},{5,1},{6,2},{7,3},{8,12},{9,13},{10,... | collective-permute-start | bytes 786440 | tf_op jit(solution)/shard_map/ppermute | solution.py:85
  16.1 7.1 %collective-permute-start.12 = (bf16[2,64,1024]{2,1,0:T(8,128)(2,1)S(1)}, bf16[2,64,1024]{2,1,0:T(8,128)(2,1)S(1)}, u32[]{:S(2)}, u32[]{:S(2)}) collective-permute-start(bf16[2,64,1024]{2,1,0:T(8,128)(2,1)S(1)} %collective-permute-done.2.refs_0_), channel_id=1, source_target_pairs={{0,1},{1,0},{2,3},{3,2},{4,5},{5,4},{6,7},{7,6},{8,10},{9,11},{10,... | collective-permute-start | bytes 786440 | tf_op jit(solution)/shard_map/ppermute | solution.py:94
  16.4 10.4 %collective-permute-start.11 = (bf16[2,64,1024]{2,1,0:T(8,128)(2,1)S(1)}, bf16[2,64,1024]{2,1,0:T(8,128)(2,1)S(1)}, u32[]{:S(2)}, u32[]{:S(2)}) collective-permute-start(bf16[2,64,1024]{2,1,0:T(8,128)(2,1)S(1)} %collective-permute-done.2.refs_0_), channel_id=1, source_target_pairs={{0,1},{1,0},{2,3},{3,2},{4,5},{5,4},{6,7},{7,6},{8,9},{9,8},{10,11... | collective-permute-start | bytes 786440 | tf_op jit(solution)/shard_map/ppermute | solution.py:99
  18.2 8.7 %collective-permute-start.13 = (bf16[2,64,1024]{2,1,0:T(8,128)(2,1)S(1)}, bf16[2,64,1024]{2,1,0:T(8,128)(2,1)S(1)}, u32[]{:S(2)}, u32[]{:S(2)}) collective-permute-start(bf16[2,64,1024]{2,1,0:T(8,128)(2,1)S(1)} %collective-permute-done.7.refs_2_), channel_id=1, source_target_pairs={{0,1},{1,0},{2,3},{3,2},{4,5},{5,4},{6,7},{7,6},{8,9},{9,8},{10,11... | collective-permute-start | bytes 786440 | tf_op jit(solution)/shard_map/ppermute | solution.py:99
  22.6 8.4 %collective-permute-start.10 = (bf16[2,64,1024]{2,1,0:T(8,128)(2,1)S(1)}, bf16[2,64,1024]{2,1,0:T(8,128)(2,1)S(1)}, u32[]{:S(2)}, u32[]{:S(2)}) collective-permute-start(bf16[2,64,1024]{2,1,0:T(8,128)(2,1)S(1)} %collective-permute-done.5.refs_1_), channel_id=1, source_target_pairs={{0,1},{1,0},{2,3},{3,2},{4,5},{5,4},{6,7},{7,6},{8,9},{9,8},{10,11... | collective-permute-start | bytes 786440 | tf_op jit(solution)/shard_map/ppermute | solution.py:94
  23.2 3.3 %collective-permute-start.15 = (bf16[64,1024]{1,0:T(8,128)(2,1)S(1)}, bf16[64,1024]{1,0:T(8,128)(2,1)S(1)}, u32[]{:S(2)}, u32[]{:S(2)}) collective-permute-start(bf16[64,1024]{1,0:T(8,128)(2,1)S(1)} %get-tuple-element.47), channel_id=1, source_target_pairs={{0,1},{1,0},{2,3},{3,2},{4,5},{5,4},{6,7},{7,6},{8,9},{9,8},{10,11... | collective-permute-start | bytes 393224 | tf_op jit(solution)/shard_map/ppermute | solution.py:99
  25.4 1.4 %collective-permute-start.14 = (bf16[64,1024]{1,0:T(8,128)(2,1)S(1)}, bf16[64,1024]{1,0:T(8,128)(2,1)S(1)}, u32[]{:S(2)}, u32[]{:S(2)}) collective-permute-start(bf16[64,1024]{1,0:T(8,128)(2,1)S(1)} %get-tuple-element.48), channel_id=1, source_target_pairs={{0,1},{1,0},{2,3},{3,2},{4,5},{5,4},{6,7},{7,6},{8,9},{9,8},{10,11... | collective-permute-start | bytes 393224 | tf_op jit(solution)/shard_map/ppermute | solution.py:99
  26.4 5.0 %collective-permute-start.9 = (bf16[2,64,1024]{2,1,0:T(8,128)(2,1)S(1)}, bf16[2,64,1024]{2,1,0:T(8,128)(2,1)S(1)}, u32[]{:S(2)}, u32[]{:S(2)}) collective-permute-start(bf16[2,64,1024]{2,1,0:T(8,128)(2,1)S(1)} %collective-permute-done.5.refs_1_), channel_id=1, source_target_pairs={{0,1},{1,0},{2,3},{3,2},{4,5},{5,4},{6,7},{7,6},{8,9},{9,8},{10,11... | collective-permute-start | bytes 786440 | tf_op jit(solution)/shard_map/ppermute | solution.py:99
  31.1 1.6 %collective-permute-start.16 = (bf16[2,64,1024]{2,1,0:T(8,128)(2,1)S(1)}, bf16[2,64,1024]{2,1,0:T(8,128)(2,1)S(1)}, u32[]{:S(2)}, u32[]{:S(2)}) collective-permute-start(bf16[2,64,1024]{2,1,0:T(8,128)(2,1)S(1)} %collective-permute-done.10.refs_2_), channel_id=1, source_target_pairs={{0,1},{1,0},{2,3},{3,2},{4,5},{5,4},{6,7},{7,6},{8,9},{9,8},{10,11... | collective-permute-start | bytes 786440 | tf_op jit(solution)/shard_map/ppermute | solution.py:99
